TPU v7x, 512 devices: a whole 4x8x8 slice. The times are simulated.
512 devices in a mesh: ctx: 64 (over y, x, core), cand: 8 (over z).
Axes of the slice: x: 4, y: 8, z: 8, core: 2. Of those that a mesh axis runs over, the one named last changes fastest.
Arguments:
- memory: bfloat16 [16384, 8192], P('ctx', 'cand'), may hold values from -60 to 60
- kv_weight: bfloat16 [2048, 8192], P('ctx', 'cand'), may hold values from -0.06629126 to 0.06629126
- queries: bfloat16 [512, 8192], P('cand', 'ctx'), may hold values from -64 to 64
Outputs:
- attended: bfloat16 [512, 8192], P('cand', 'ctx')
All inputs are finite; a program needn't handle non-finite values.
Results may differ from a plain program's by a relative error of at most 0.012.
The roundings to bfloat16 on the way count: a program that leaves them out, or rounds other values in their place, can miss the bound.
Values may be sent and summed in bfloat16 or wider, within the bound.
No kernel may reach another device: no remote copies, remote signals or barrier semaphores. Data moves between devices by JAX's collectives and lax.ppermute only.
A program may use at most 64 MiB of HBM per device.

v0:
```python
import jax
import jax.numpy as jnp
from jax import lax
from jax.sharding import PartitionSpec as P

QH = 64
KVH = 8
HD = 128


def body(memory, kv_weight, queries):
    tok_rows = memory.shape[0]
    cand_rows = queries.shape[0]
    ctx_count = lax.axis_size("ctx")
    partial_kv = lax.dot_general(
        memory,
        lax.all_gather(kv_weight, "ctx", axis=0, tiled=True),
        (((1,), (1,)), ((), ())),
        preferred_element_type=jnp.float32,
    )
    kv_all = lax.psum(partial_kv, "cand").astype(jnp.bfloat16)
    keys = kv_all[:, : KVH * HD].reshape(tok_rows, KVH, HD)
    values = kv_all[:, KVH * HD :].reshape(tok_rows, KVH, HD)
    query_all = lax.all_gather(queries, "ctx", axis=1, tiled=True)
    group = QH // KVH
    query_grouped = query_all.reshape(cand_rows, KVH, group, HD)
    scores = jnp.einsum(
        "ckgd,tkd->kgct", query_grouped, keys, preferred_element_type=jnp.float32
    ) * HD ** (-0.5)
    local_max = jnp.max(scores, axis=3)
    expo = jnp.exp(scores - local_max[..., None])
    local_total = jnp.sum(expo, axis=3).reshape(QH, cand_rows)
    weights = expo.astype(jnp.bfloat16)
    local_out = jnp.einsum(
        "kgct,tkd->kgcd", weights, values, preferred_element_type=jnp.float32
    ).reshape(QH, cand_rows, HD)
    local_max = local_max.reshape(QH, cand_rows)
    owned = QH // ctx_count
    top = lax.pmax(local_max, "ctx")
    factor = jnp.exp(local_max - top)
    numer, denom = (
        lax.psum_scatter(factor[..., None] * local_out, "ctx", scatter_dimension=0, tiled=True),
        lax.psum_scatter(factor * local_total, "ctx", scatter_dimension=0, tiled=True),
    )
    result = (numer / denom[..., None]).astype(jnp.bfloat16)
    return jnp.transpose(result, (1, 0, 2)).reshape(cand_rows, owned * HD)


def solution(mesh):
    return jax.shard_map(
        body,
        mesh=mesh,
        in_specs=(P("ctx", "cand"), P("ctx", "cand"), P("cand", "ctx")),
        out_specs=P("cand", "ctx"),
        check_vma=False,
    )
```

profile of v0, /device:TPU:1, one launch (start us, length us, event | category | flops | bytes accessed | tf_op | source)
XLA Modules:
  0.0 760.2 jit_solution(16658249204560734399)
XLA Ops:
  6.5 0.0 copy-start
  6.5 0.0 all-gather.5.cloned.1.call-start
  6.5 0.7 all-gather.5.cloned.1.call-update
  7.3 0.0 all-gather.3.cloned.1.call-start
  7.3 0.7 all-gather.3.cloned.1.call-update
  8.0 0.0 reduce-scatter.4.cloned.1.call-start
  8.1 84.1 %all-gather.5.cloned.1.call-done = bf16[64,8192]{1,0:T(8,128)(2,1)} async-done(((bf16[64,128]{1,0:T(8,128)(2,1)}), bf16[64,8192]{1,0:T(8,128)(2,1)}) %all-gather.5.cloned.1.call-update) | async-done | bytes 1048592 | tf_op jit(solution)/shard_map/all_gather | solution.py:24
  92.2 1.5 copy.19
  93.7 85.6 %all-gather.3.cloned.1.call-done = bf16[2048,1024]{1,0:T(8,128)(2,1)} async-done(((bf16[32,1024]{1,0:T(8,128)(2,1)}), bf16[2048,1024]{1,0:T(8,128)(2,1)}) %all-gather.3.cloned.1.call-update) | async-done | bytes 4194320 | tf_op jit(solution)/shard_map/all_gather | solution.py:17
  179.2 0.0 copy-done
  179.2 4.8 fusion.13
  184.0 60.5 %all-reduce.3 = bf16[256,2048]{1,0:T(8,128)(2,1)S(1)} all-reduce(f32[256,2048]{1,0:T(8,128)} %fusion.13), channel_id=1, replica_groups=mesh['ctx'=64,'cand'=8] {'cand'}, use_global_device_ids=true, to_apply=%region_0.0 | all-reduce | flops 524288 | bytes 3145728 | tf_op jit(solution)/shard_map/psum | solution.py:21
  244.5 0.1 slice_bitcast_fusion
  244.6 0.1 copy.18
  244.7 1.2 bitcast_reduce_fusion
  245.9 0.0 copy-start.1
  245.9 1.9 copy-done.1
  247.8 1.4 fusion.1
  249.2 249.7 %pmax.7 = f32[64,64]{1,0:T(8,128)S(1)} all-reduce(f32[64,64]{1,0:T(8,128)S(1)} %bitcast.41), channel_id=1, replica_groups=mesh['ctx'=64,'cand'=8] {'ctx'}, use_global_device_ids=true, to_apply=%region_2.0 | all-reduce | flops 4096 | bytes 32768 | tf_op jit(solution)/shard_map/pmax | solution.py:39
  498.9 0.1 copy.20
  499.0 2.8 fusion.3
  501.9 2.0 bitcast_multiply_fusion
  503.8 0.0 reduce-scatter.4.cloned.1.call-update
  503.9 1.3 dynamic-slice
  505.1 246.4 %all-reduce.1 = f32[64,64]{1,0:T(8,128)S(1)} all-reduce(f32[64,64]{1,0:T(8,128)S(1)} %get-tuple-element.5), channel_id=3, replica_groups=mesh['ctx'=64,'cand'=8] {'ctx'}, use_global_device_ids=true, to_apply=%region_5.0.clone | all-reduce | flops 4096 | bytes 32768
  751.5 0.7 dynamic-slice_bitcast_fusion
  752.2 0.0 reduce-scatter.4.cloned.1.call-done
  752.2 1.4 fusion.11
  (1 shorter events, 0.0 us)
Async XLA Ops:
  6.5 172.7 %copy-start = (bf16[256,1024]{1,0:T(8,128)(2,1)S(1)}, bf16[256,1024]{1,0:T(8,128)(2,1)}, u32[]{:S(2)}) copy-start(bf16[256,1024]{1,0:T(8,128)(2,1)} %param.3) | copy-start | bytes 1572868
  6.5 85.6 %all-gather.5.cloned.1.call-start = ((), (), s32[]{:S(2)}) async-start(), calls=%async_computation.2 | async-start | bytes 1064960 | tf_op jit(solution)/shard_map/all_gather | solution.py:24
  7.3 172.0 %all-gather.3.cloned.1.call-start = ((), (), s32[]{:S(2)}) async-start(), calls=%async_computation.1 | async-start | bytes 4259840 | tf_op jit(solution)/shard_map/all_gather | solution.py:17
  8.0 744.2 %reduce-scatter.4.cloned.1.call-start = ((), (), s32[]{:S(2)}) async-start(), calls=%async_computation.3 | async-start | bytes 2129920
  245.9 1.9 copy-start.1
Sparse Core Ops, SparseCore 0:
  10.6 81.5 all-gather.4
  95.5 83.6 all-gather.2
  504.0 141.5 reduce-scatter.3
where the time goes:
time: 762 us; the launch traced here: 760 us
  blocking collectives  557 us (73%)
  waiting for transfers between devices  171 us (22%)
  between operations  13.2 us (2%)
  matrix products  8.8 us (1%)
    pmax x1, blocking collectives, body(): top = lax.pmax(local_max, 'ctx')  250 us
    unnamed x1, blocking collectives  246 us
    all_gather x1, waiting for transfers between devices, body(): lax.all_gather(kv_weight, 'ctx', axis=0, tiled=True)  85.6 us
    all_gather x1, waiting for transfers between devices, body(): query_all = lax.all_gather(queries, 'ctx', axis=1, tiled=True)  84.1 us
    psum x1, blocking collectives, body(): kv_all = lax.psum(partial_kv, 'cand').astype(jnp.bfloat16)  60.5 us
  transfers between devices with their start and end apart: 3, of which 2 were waited for; matrix products, arithmetic and copies ran while one was open for 0% of the time, Pallas kernels for 0%

commit v1 on v0

v1 whole, which is shorter than its diff:
```python
import jax
import jax.numpy as jnp
from jax import lax
from jax.experimental import pallas as pl
from jax.experimental.pallas import tpu as pltpu
from jax.sharding import Mesh, PartitionSpec as P

HD = 128
NT = (((1,), (1,)), ((), ()))
NN = (((1,), (0,)), ((), ()))


def spread(value, axis):
    count = lax.axis_size(axis)
    copies = jnp.broadcast_to(value[None], (count,) + value.shape)
    return lax.all_to_all(copies, axis, 0, 0, tiled=True)


def place(y, x, c, z):
    return ((y * 4 + x) * 2 + c) * 8 + z


def weight_moves():
    moves = []
    for y in range(8):
        for x in range(4):
            for c in range(2):
                shard = y * 8 + x * 2 + c
                kind, head, quarter = shard // 32, shard // 4 % 8, shard % 4
                for z in range(8):
                    moves.append((place(y, x, c, z), place(kind * 4 + quarter, z // 2, z % 2, head)))
    return moves


def query_moves():
    return [
        (place(y, x, c, z), place(x * 2 + c, z // 2, z % 2, y))
        for y in range(8)
        for x in range(4)
        for c in range(2)
        for z in range(8)
    ]


ALL = ("y", "x", "c", "z")
RIGHT = [(i, (i + 1) % 4) for i in range(4)]
LEFT = [(i, (i - 1) % 4) for i in range(4)]
SWAP = [(0, 1), (1, 0)]


def project_kernel(core_ref, mem_a, mem_b, w_a, w_b, out_ref, acc):
    step = pl.program_id(0)
    part = lax.dot_general(mem_a[...], w_a[...], NT, preferred_element_type=jnp.float32)
    part += lax.dot_general(mem_b[...], w_b[...], NT, preferred_element_type=jnp.float32)

    @pl.when(step == 0)
    def _():
        acc[...] = part

    @pl.when(step > 0)
    def _():
        acc[...] += part

    @pl.when(step == pl.num_programs(0) - 1)
    def _():
        out_ref[...] = acc[...].astype(out_ref.dtype)


def project(core, mem_all, w_a, w_b):
    tok, feat = 256, mem_all.shape[1]
    return pl.pallas_call(
        project_kernel,
        out_shape=jax.ShapeDtypeStruct((tok, 2 * HD), jnp.bfloat16),
        grid_spec=pltpu.PrefetchScalarGridSpec(
            num_scalar_prefetch=1,
            grid=(4,),
            in_specs=[
                pl.BlockSpec((tok, feat), lambda j, core: (2 * j + core[0], 0)),
                pl.BlockSpec((tok, feat), lambda j, core: (2 * j + 1 - core[0], 0)),
                pl.BlockSpec((2 * HD, feat), lambda j, core: (j, 0)),
                pl.BlockSpec((2 * HD, feat), lambda j, core: (j, 0)),
            ],
            out_specs=pl.BlockSpec((tok, 2 * HD), lambda j, core: (0, 0)),
            scratch_shapes=[pltpu.VMEM((tok, 2 * HD), jnp.float32)],
        ),
        compiler_params=pltpu.CompilerParams(vmem_limit_bytes=24 << 20),
        cost_estimate=pl.CostEstimate(flops=2 * 256 * 256 * 8192, bytes_accessed=8 << 20, transcendentals=0),
    )(core, mem_all, mem_all, w_a, w_b)


def attend_kernel(q_ref, own, other, left, right, opp_a, opp_b, out_ref):
    blocks = [(own, 0), (other, 0), (left, 0), (left, 256), (right, 0), (right, 256), (opp_a, 0), (opp_b, 0)]
    query = q_ref[...]
    top = total = acc = None
    for ref, start in blocks:
        keys = ref[start : start + 256, :HD]
        values = ref[start : start + 256, HD:]
        scores = lax.dot_general(query, keys, NT, preferred_element_type=jnp.float32) * HD ** (-0.5)
        block_max = jnp.max(scores, axis=1, keepdims=True)
        expo = jnp.exp(scores - block_max)
        block_total = jnp.sum(expo, axis=1, keepdims=True)
        block_out = lax.dot_general(expo.astype(jnp.bfloat16), values, NN, preferred_element_type=jnp.float32)
        if top is None:
            top, total, acc = block_max, block_total, block_out
        else:
            new_top = jnp.maximum(top, block_max)
            keep, add = jnp.exp(top - new_top), jnp.exp(block_max - new_top)
            total = total * keep + block_total * add
            acc = acc * keep + block_out * add
            top = new_top
    tops = jnp.concatenate([top[h * 64 : h * 64 + 64] for h in range(8)], axis=1)
    totals = jnp.concatenate([total[h * 64 : h * 64 + 64] for h in range(8)], axis=1)
    stats = jnp.concatenate([tops, totals], axis=0).T
    for h in range(8):
        out_ref[h, :64, :] = acc[h * 64 : h * 64 + 64]
        out_ref[h, 64:, :] = jnp.broadcast_to(stats[h : h + 1], (8, HD))


def attend(query, pieces):
    return pl.pallas_call(
        attend_kernel,
        out_shape=jax.ShapeDtypeStruct((8, 72, HD), jnp.float32),
        compiler_params=pltpu.CompilerParams(vmem_limit_bytes=24 << 20),
        cost_estimate=pl.CostEstimate(
            flops=4 * 512 * 2048 * HD, bytes_accessed=2 << 20, transcendentals=512 * 2048
        ),
    )(query, *pieces)


def merge_kernel(part_ref, out_ref):
    stats = jnp.concatenate([part_ref[j, 64:65, :] for j in range(8)], axis=0).T
    tops, totals = stats[:64], stats[64:]
    top = jnp.max(tops, axis=1, keepdims=True)
    factor = jnp.exp(tops - top)
    denom = jnp.sum(factor * totals, axis=1, keepdims=True)
    numer = factor[:, :1] * part_ref[0, :64, :]
    for j in range(1, 8):
        numer += factor[:, j : j + 1] * part_ref[j, :64, :]
    out_ref[...] = (numer / denom).astype(out_ref.dtype)


def merge(parts):
    return pl.pallas_call(
        merge_kernel,
        out_shape=jax.ShapeDtypeStruct((64, HD), jnp.bfloat16),
    )(parts)


def body(memory, kv_weight, queries):
    core = lax.axis_index("c")
    mem_all = lax.all_gather(memory, "z", axis=0, tiled=True)

    rows = lax.ppermute(kv_weight, ALL, weight_moves())
    query = lax.ppermute(queries, ALL, query_moves())
    rows = spread(rows, "y").reshape(2 * HD, -1)
    w_a = spread(rows, "x").reshape(8 * HD, -1)
    w_b = lax.ppermute(w_a, "c", SWAP)
    query = spread(query, "y").reshape(512, HD)

    own = project(core.astype(jnp.int32)[None], mem_all, w_a, w_b)
    other = lax.ppermute(own, "c", SWAP)
    pair = jnp.concatenate([own, other], axis=0)
    left = lax.ppermute(pair, "x", RIGHT)
    right = lax.ppermute(pair, "x", LEFT)
    opp_a = lax.ppermute(left[:256], "x", RIGHT)
    opp_b = lax.ppermute(right[256:], "x", LEFT)

    parts = attend(query, (own, other, left, right, opp_a, opp_b))
    parts = lax.all_to_all(parts, "y", 0, 0, tiled=True)
    result = merge(parts)
    return lax.ppermute(result, ALL, [(b, a) for a, b in query_moves()])


def solution(mesh):
    fine = Mesh(mesh.devices.reshape(8, 4, 2, 8), ALL)
    ctx = ("y", "x", "c")
    return jax.shard_map(
        body,
        mesh=fine,
        in_specs=(P(ctx, "z"), P(ctx, "z"), P("z", ctx)),
        out_specs=P("z", ctx),
        check_vma=False,
    )
```

time: 762 us -> 170 us (0.22)
  the two profiles are of different devices: /device:TPU:1 before, /device:TPU:22 now
where the time goes in v1:
time: 170 us; the launch traced here: 169 us
  blocking collectives  65 us (38%)
  starting transfers between devices  50 us (29%)
  waiting for transfers between devices  28.6 us (17%)
  between operations  13.5 us (8%)
  Pallas kernels  8.12 us (5%)
  local copies, waits for them, and re-layouts  3.8 us (2%)
    all_to_all x2, blocking collectives, spread(): return lax.all_to_all(copies, axis, 0, 0, tiled=True)  49.7 us
    all_to_all x1, blocking collectives, body(): parts = lax.all_to_all(parts, 'y', 0, 0, tiled=True)  15.3 us
    ppermute x1, starting transfers between devices, body(): rows = lax.ppermute(kv_weight, ALL, weight_moves())  10.8 us
    ppermute x1, starting transfers between devices, body(): query = lax.ppermute(queries, ALL, query_moves())  9.64 us
    ppermute x1, waiting for transfers between devices, body(): return lax.ppermute(result, ALL, [(b, a) for a, b in query_moves()])  8.97 us
    all_to_all x1, starting transfers between devices, spread(): return lax.all_to_all(copies, axis, 0, 0, tiled=True)  7.4 us
    ppermute x1, starting transfers between devices, body(): opp_a = lax.ppermute(left[:256], 'x', RIGHT)  5.64 us
    ppermute x1, waiting for transfers between devices, body(): opp_b = lax.ppermute(right[256:], 'x', LEFT)  5.6 us
  transfers between devices with their start and end apart: 11, of which 7 were waited for; matrix products, arithmetic and copies ran while one was open for 1% of the time, Pallas kernels for 0%

profile of v1, /device:TPU:22, one launch (start us, length us, event | category | flops | bytes accessed | tf_op | source)
XLA Modules:
  0.0 169.1 jit_solution(2215335947397202670)
XLA Ops:
  6.5 0.0 all-gather.2.cloned.1.call-start
  6.5 0.7 all-gather.2.cloned.1.call-update
  7.3 10.8 %collective-permute-start.1 = (bf16[32,1024]{1,0:T(8,128)(2,1)}, bf16[32,1024]{1,0:T(8,128)(2,1)S(1)}, u32[]{:S(2)}, u32[]{:S(2)}) collective-permute-start(bf16[32,1024]{1,0:T(8,128)(2,1)} %param.4), channel_id=1, source_target_pairs={{0,0},{1,8},{2,16},{3,24},{4,32},{5,40},{6,48},{7,56},{8,64},{9,72... | collective-permute-start | bytes 196616 | tf_op jit(solution)/shard_map/ppermute | solution.py:153
  18.1 5.1 %collective-permute-done.1 = bf16[32,1024]{1,0:T(8,128)(2,1)S(1)} collective-permute-done((bf16[32,1024]{1,0:T(8,128)(2,1)}, bf16[32,1024]{1,0:T(8,128)(2,1)S(1)}, u32[]{:S(2)}, u32[]{:S(2)}) %collective-permute-start.1) | collective-permute-done | bytes 65568 | tf_op jit(solution)/shard_map/ppermute | solution.py:153
  23.2 22.5 %all_to_all.20 = bf16[8,32,1024]{2,1,0:T(8,128)(2,1)S(1)} all-to-all(bf16[8,32,1024]{2,1,0:T(8,128)(2,1)S(1)} %broadcast_in_dim.24), channel_id=1, replica_groups=mesh['y'=8,'x'=4,'c'=2,'z'=8] {'y'}, dimensions={0} | all-to-all | bytes 1048576 | tf_op jit(solution)/shard_map/all_to_all | solution.py:16
  45.8 0.3 broadcast_in_dim.26
  46.0 27.1 %all_to_all.21 = bf16[4,256,1024]{2,1,0:T(8,128)(2,1)S(1)} all-to-all(bf16[4,256,1024]{2,1,0:T(8,128)(2,1)S(1)} %broadcast_in_dim.26), channel_id=1, replica_groups=mesh['y'=8,'x'=4,'c'=2,'z'=8] {'x'}, dimensions={0} | all-to-all | bytes 4194304 | tf_op jit(solution)/shard_map/all_to_all | solution.py:16
  73.2 1.9 %collective-permute-start.2 = (bf16[1024,1024]{1,0:T(8,128)(2,1)S(1)}, bf16[1024,1024]{1,0:T(8,128)(2,1)}, u32[]{:S(2)}, u32[]{:S(2)}) collective-permute-start(bf16[1024,1024]{1,0:T(8,128)(2,1)S(1)} %bitcast.4), channel_id=1, source_target_pairs={{0,8},{8,0},{1,9},{9,1},{2,10},{10,2},{3,11},{11,3},{4,12},{12,4},... | collective-permute-start | bytes 6291464 | tf_op jit(solution)/shard_map/ppermute | solution.py:157
  75.1 4.3 %collective-permute-done.2.w_b = bf16[1024,1024]{1,0:T(8,128)(2,1)} collective-permute-done((bf16[1024,1024]{1,0:T(8,128)(2,1)S(1)}, bf16[1024,1024]{1,0:T(8,128)(2,1)}, u32[]{:S(2)}, u32[]{:S(2)}) %collective-permute-start.2) | collective-permute-done | bytes 2097184 | tf_op jit(solution)/shard_map/ppermute | solution.py:157
  79.3 2.2 %copy-done = bf16[2048,1024]{1,0:T(8,128)(2,1)S(1)} copy-done((bf16[2048,1024]{1,0:T(8,128)(2,1)S(1)}, bf16[2048,1024]{1,0:T(8,128)(2,1)}, u32[]{:S(2)}) %copy-start) | copy-done | bytes 4194328
  81.5 3.7 %shard_map.37.own = bf16[256,256]{1,0:T(8,128)(2,1)S(1)} custom-call(s32[1]{0:T(128)} %bitcast.1.core_ref, bf16[2048,1024]{1,0:T(8,128)(2,1)S(1)} %copy-done, bf16[2048,1024]{1,0:T(8,128)(2,1)S(1)} %copy-done, bf16[1024,1024]{1,0:T(8,128)(2,1)S(1)} %bitcast.5, bf16[1024,1024]{1,0:T(8,128)(2,1)} %collective-permute-done.2.w_b), custom_call_target="tpu_custom_call" | custom-call | flops 1073741824 | bytes 8388608 | tf_op jit(solution)/shard_map/pallas_call | solution.py:71
  85.2 2.0 %collective-permute-start.3 = (bf16[256,256]{1,0:T(8,128)(2,1)S(1)}, bf16[256,256]{1,0:T(8,128)(2,1)S(1)}, u32[]{:S(2)}, u32[]{:S(2)}) collective-permute-start(bf16[256,256]{1,0:T(8,128)(2,1)S(1)} %shard_map.37.own), channel_id=1, source_target_pairs={{0,8},{8,0},{1,9},{9,1},{2,10},{10,2},{3,11},{11,3},{4,12},{12,4},... | collective-permute-start | bytes 393224 | tf_op jit(solution)/shard_map/ppermute | solution.py:161
  87.2 1.2 collective-permute-done.3.other
  88.5 4.0 %collective-permute-start.4 = (bf16[512,256]{1,0:T(8,128)(2,1)S(1)}, bf16[512,256]{1,0:T(8,128)(2,1)S(1)}, u32[]{:S(2)}, u32[]{:S(2)}) collective-permute-start(bf16[512,256]{1,0:T(8,128)(2,1)S(1)} %pad_maximum_fusion), channel_id=1, source_target_pairs={{0,16},{16,32},{32,48},{48,0},{1,17},{17,33},{33,49},{49,1},{2,18}... | collective-permute-start | bytes 786440 | tf_op jit(solution)/shard_map/ppermute | solution.py:163
  92.4 1.9 %collective-permute-start.5 = (bf16[512,256]{1,0:T(8,128)(2,1)S(1)}, bf16[512,256]{1,0:T(8,128)(2,1)S(1)}, u32[]{:S(2)}, u32[]{:S(2)}) collective-permute-start(bf16[512,256]{1,0:T(8,128)(2,1)S(1)} %pad_maximum_fusion), channel_id=1, source_target_pairs={{0,48},{16,0},{32,16},{48,32},{1,49},{17,1},{33,17},{49,33},{2,50}... | collective-permute-start | bytes 786440 | tf_op jit(solution)/shard_map/ppermute | solution.py:164
  94.4 9.6 %collective-permute-start = (bf16[64,128]{1,0:T(8,128)(2,1)S(1)}, bf16[64,128]{1,0:T(8,128)(2,1)S(1)}, u32[]{:S(2)}, u32[]{:S(2)}) collective-permute-start(bf16[64,128]{1,0:T(8,128)(2,1)S(1)} %copy-done.1), channel_id=1, source_target_pairs={{0,0},{1,8},{2,16},{3,24},{4,32},{5,40},{6,48},{7,56},{8,64},{9,72... | collective-permute-start | bytes 49160 | tf_op jit(solution)/shard_map/ppermute | solution.py:154
  104.0 2.3 %collective-permute-done = bf16[64,128]{1,0:T(8,128)(2,1)S(1)} collective-permute-done((bf16[64,128]{1,0:T(8,128)(2,1)S(1)}, bf16[64,128]{1,0:T(8,128)(2,1)S(1)}, u32[]{:S(2)}, u32[]{:S(2)}) %collective-permute-start) | collective-permute-done | bytes 16416 | tf_op jit(solution)/shard_map/ppermute | solution.py:154
  106.3 0.7 broadcast_in_dim.10
  107.0 7.4 %all-to-all-start = ((bf16[8,64,128]{2,1,0:T(8,128)(2,1)}), bf16[8,64,128]{2,1,0:T(8,128)(2,1)S(1)}, u32[]{:S(2)}, u32[]{:S(2)}) async-start(bf16[8,64,128]{2,1,0:T(8,128)(2,1)} %broadcast_in_dim.10), calls=%async_computation | async-start | bytes 262144 | tf_op jit(solution)/shard_map/all_to_all | solution.py:16
  114.4 0.0 collective-permute-done.4.left
  114.4 5.6 %collective-permute-start.6 = (bf16[256,256]{1,0:T(8,128)(2,1)S(1)}, bf16[256,256]{1,0:T(8,128)(2,1)S(1)}, u32[]{:S(2)}, u32[]{:S(2)}) collective-permute-start(bf16[256,256]{1,0:T(8,128)(2,1)S(1)} %slice.8), channel_id=1, source_target_pairs={{0,16},{16,32},{32,48},{48,0},{1,17},{17,33},{33,49},{49,1},{2,18}... | collective-permute-start | bytes 393224 | tf_op jit(solution)/shard_map/ppermute | solution.py:165
  120.1 0.0 collective-permute-done.5.right
  120.1 1.9 %collective-permute-start.7 = (bf16[256,256]{1,0:T(8,128)(2,1)S(1)}, bf16[256,256]{1,0:T(8,128)(2,1)S(1)}, u32[]{:S(2)}, u32[]{:S(2)}) collective-permute-start(bf16[256,256]{1,0:T(8,128)(2,1)S(1)} %slice.9), channel_id=1, source_target_pairs={{0,48},{16,0},{32,16},{48,32},{1,49},{17,1},{33,17},{49,33},{2,50}... | collective-permute-start | bytes 393224 | tf_op jit(solution)/shard_map/ppermute | solution.py:166
  122.0 0.0 all-to-all-done
  122.0 0.5 collective-permute-done.6.opp_a
  122.6 5.6 %collective-permute-done.7.opp_b = bf16[256,256]{1,0:T(8,128)(2,1)S(1)} collective-permute-done((bf16[256,256]{1,0:T(8,128)(2,1)S(1)}, bf16[256,256]{1,0:T(8,128)(2,1)S(1)}, u32[]{:S(2)}, u32[]{:S(2)}) %collective-permute-start.7) | collective-permute-done | bytes 131104 | tf_op jit(solution)/shard_map/ppermute | solution.py:166
  128.2 2.3 %shard_map.38 = f32[8,72,128]{2,1,0:T(8,128)S(1)} custom-call(bf16[512,128]{1,0:T(8,128)(2,1)S(1)} %bitcast.6, bf16[256,256]{1,0:T(8,128)(2,1)S(1)} %shard_map.37.own, bf16[256,256]{1,0:T(8,128)(2,1)S(1)} %collective-permute-done.3.other, bf16[512,256]{1,0:T(8,128)(2,1)S(1)} %collective-permute-done.4.left, ...), custom_call_target="tpu_custom_call" | custom-call | flops 536870912 | bytes 2097152 | tf_op jit(solution)/shard_map/pallas_call | solution.py:120
  130.5 15.3 %all_to_all.22.part_ref = f32[8,72,128]{2,1,0:T(8,128)} all-to-all(f32[8,72,128]{2,1,0:T(8,128)S(1)} %shard_map.38), channel_id=1, replica_groups=mesh['y'=8,'x'=4,'c'=2,'z'=8] {'y'}, dimensions={0} | all-to-all | bytes 589824 | tf_op jit(solution)/shard_map/all_to_all | solution.py:169
  145.8 2.1 %shard_map.39 = bf16[64,128]{1,0:T(8,128)(2,1)} custom-call(f32[8,72,128]{2,1,0:T(8,128)} %all_to_all.22.part_ref), custom_call_target="tpu_custom_call" | custom-call | tf_op jit(solution)/shard_map/pallas_call | solution.py:143
  148.0 4.7 %collective-permute-start.8 = (bf16[64,128]{1,0:T(8,128)(2,1)}, bf16[64,128]{1,0:T(8,128)(2,1)S(1)}, u32[]{:S(2)}, u32[]{:S(2)}) collective-permute-start(bf16[64,128]{1,0:T(8,128)(2,1)} %shard_map.39), channel_id=1, source_target_pairs={{0,0},{8,1},{16,2},{24,3},{32,4},{40,5},{48,6},{56,7},{64,8},{72,9... | collective-permute-start | bytes 49160 | tf_op jit(solution)/shard_map/ppermute | solution.py:171
  152.6 9.0 %collective-permute-done.8 = bf16[64,128]{1,0:T(8,128)(2,1)S(1)} collective-permute-done((bf16[64,128]{1,0:T(8,128)(2,1)}, bf16[64,128]{1,0:T(8,128)(2,1)S(1)}, u32[]{:S(2)}, u32[]{:S(2)}) %collective-permute-start.8) | collective-permute-done | bytes 16416 | tf_op jit(solution)/shard_map/ppermute | solution.py:171
  161.6 0.6 copy.5
  (8 shorter events, 0.1 us)
Async XLA Ops:
  6.5 72.8 %all-gather.2.cloned.1.call-start = ((), (), s32[]{:S(2)}) async-start(), calls=%async_computation.4 | async-start | bytes 4718592 | tf_op jit(solution)/shard_map/all_gather | solution.py:151
  7.3 15.9 %collective-permute-start.1 = (bf16[32,1024]{1,0:T(8,128)(2,1)}, bf16[32,1024]{1,0:T(8,128)(2,1)S(1)}, u32[]{:S(2)}, u32[]{:S(2)}) collective-permute-start(bf16[32,1024]{1,0:T(8,128)(2,1)} %param.4), channel_id=1, source_target_pairs={{0,0},{1,8},{2,16},{3,24},{4,32},{5,40},{6,48},{7,56},{8,64},{9,72... | collective-permute-start | bytes 196616 | tf_op jit(solution)/shard_map/ppermute | solution.py:153
  73.2 6.2 %collective-permute-start.2 = (bf16[1024,1024]{1,0:T(8,128)(2,1)S(1)}, bf16[1024,1024]{1,0:T(8,128)(2,1)}, u32[]{:S(2)}, u32[]{:S(2)}) collective-permute-start(bf16[1024,1024]{1,0:T(8,128)(2,1)S(1)} %bitcast.4), channel_id=1, source_target_pairs={{0,8},{8,0},{1,9},{9,1},{2,10},{10,2},{3,11},{11,3},{4,12},{12,4},... | collective-permute-start | bytes 6291464 | tf_op jit(solution)/shard_map/ppermute | solution.py:157
  79.3 2.2 %copy-start = (bf16[2048,1024]{1,0:T(8,128)(2,1)S(1)}, bf16[2048,1024]{1,0:T(8,128)(2,1)}, u32[]{:S(2)}) copy-start(bf16[2048,1024]{1,0:T(8,128)(2,1)} %all-gather.2.cloned.1.call-done.mem_a.mem_b) | copy-start | bytes 12582916
  81.5 12.8 %copy-start.1 = (bf16[64,128]{1,0:T(8,128)(2,1)S(1)}, bf16[64,128]{1,0:T(8,128)(2,1)}, u32[]{:S(2)}) copy-start(bf16[64,128]{1,0:T(8,128)(2,1)} %param.5) | copy-start | bytes 49156
  85.2 3.2 %collective-permute-start.3 = (bf16[256,256]{1,0:T(8,128)(2,1)S(1)}, bf16[256,256]{1,0:T(8,128)(2,1)S(1)}, u32[]{:S(2)}, u32[]{:S(2)}) collective-permute-start(bf16[256,256]{1,0:T(8,128)(2,1)S(1)} %shard_map.37.own), channel_id=1, source_target_pairs={{0,8},{8,0},{1,9},{9,1},{2,10},{10,2},{3,11},{11,3},{4,12},{12,4},... | collective-permute-start | bytes 393224 | tf_op jit(solution)/shard_map/ppermute | solution.py:161
  88.5 25.9 %collective-permute-start.4 = (bf16[512,256]{1,0:T(8,128)(2,1)S(1)}, bf16[512,256]{1,0:T(8,128)(2,1)S(1)}, u32[]{:S(2)}, u32[]{:S(2)}) collective-permute-start(bf16[512,256]{1,0:T(8,128)(2,1)S(1)} %pad_maximum_fusion), channel_id=1, source_target_pairs={{0,16},{16,32},{32,48},{48,0},{1,17},{17,33},{33,49},{49,1},{2,18}... | collective-permute-start | bytes 786440 | tf_op jit(solution)/shard_map/ppermute | solution.py:163
  92.4 27.6 %collective-permute-start.5 = (bf16[512,256]{1,0:T(8,128)(2,1)S(1)}, bf16[512,256]{1,0:T(8,128)(2,1)S(1)}, u32[]{:S(2)}, u32[]{:S(2)}) collective-permute-start(bf16[512,256]{1,0:T(8,128)(2,1)S(1)} %pad_maximum_fusion), channel_id=1, source_target_pairs={{0,48},{16,0},{32,16},{48,32},{1,49},{17,1},{33,17},{49,33},{2,50}... | collective-permute-start | bytes 786440 | tf_op jit(solution)/shard_map/ppermute | solution.py:164
  94.4 11.9 %collective-permute-start = (bf16[64,128]{1,0:T(8,128)(2,1)S(1)}, bf16[64,128]{1,0:T(8,128)(2,1)S(1)}, u32[]{:S(2)}, u32[]{:S(2)}) collective-permute-start(bf16[64,128]{1,0:T(8,128)(2,1)S(1)} %copy-done.1), channel_id=1, source_target_pairs={{0,0},{1,8},{2,16},{3,24},{4,32},{5,40},{6,48},{7,56},{8,64},{9,72... | collective-permute-start | bytes 49160 | tf_op jit(solution)/shard_map/ppermute | solution.py:154
  107.0 15.0 %all-to-all-start = ((bf16[8,64,128]{2,1,0:T(8,128)(2,1)}), bf16[8,64,128]{2,1,0:T(8,128)(2,1)S(1)}, u32[]{:S(2)}, u32[]{:S(2)}) async-start(bf16[8,64,128]{2,1,0:T(8,128)(2,1)} %broadcast_in_dim.10), calls=%async_computation | async-start | bytes 262144 | tf_op jit(solution)/shard_map/all_to_all | solution.py:16
  114.4 8.1 %collective-permute-start.6 = (bf16[256,256]{1,0:T(8,128)(2,1)S(1)}, bf16[256,256]{1,0:T(8,128)(2,1)S(1)}, u32[]{:S(2)}, u32[]{:S(2)}) collective-permute-start(bf16[256,256]{1,0:T(8,128)(2,1)S(1)} %slice.8), channel_id=1, source_target_pairs={{0,16},{16,32},{32,48},{48,0},{1,17},{17,33},{33,49},{49,1},{2,18}... | collective-permute-start | bytes 393224 | tf_op jit(solution)/shard_map/ppermute | solution.py:165
  120.1 8.1 %collective-permute-start.7 = (bf16[256,256]{1,0:T(8,128)(2,1)S(1)}, bf16[256,256]{1,0:T(8,128)(2,1)S(1)}, u32[]{:S(2)}, u32[]{:S(2)}) collective-permute-start(bf16[256,256]{1,0:T(8,128)(2,1)S(1)} %slice.9), channel_id=1, source_target_pairs={{0,48},{16,0},{32,16},{48,32},{1,49},{17,1},{33,17},{49,33},{2,50}... | collective-permute-start | bytes 393224 | tf_op jit(solution)/shard_map/ppermute | solution.py:166
  148.0 13.6 %collective-permute-start.8 = (bf16[64,128]{1,0:T(8,128)(2,1)}, bf16[64,128]{1,0:T(8,128)(2,1)S(1)}, u32[]{:S(2)}, u32[]{:S(2)}) collective-permute-start(bf16[64,128]{1,0:T(8,128)(2,1)} %shard_map.39), channel_id=1, source_target_pairs={{0,0},{8,1},{16,2},{24,3},{32,4},{40,5},{48,6},{56,7},{64,8},{72,9... | collective-permute-start | bytes 49160 | tf_op jit(solution)/shard_map/ppermute | solution.py:171
Sparse Core Ops, SparseCore 0:
  9.4 62.6 all-gather.1

commit v2 on v1

--- a/solution.py
+++ b/solution.py
@@ -34,62 +34,61 @@
 
 def query_moves():
     return [
-        (place(y, x, c, z), place(x * 2 + c, z // 2, z % 2, y))
-        for y in range(8)
-        for x in range(4)
-        for c in range(2)
-        for z in range(8)
+        (place(y, x, c, z), place(z, x, c, y)) for y in range(8) for x in range(4) for c in range(2) for z in range(8)
     ]
 
 
 ALL = ("y", "x", "c", "z")
-RIGHT = [(i, (i + 1) % 4) for i in range(4)]
-LEFT = [(i, (i - 1) % 4) for i in range(4)]
+def shift(count, away):
+    return [(i, (i + away) % count) for i in range(count)]
+
+
 SWAP = [(0, 1), (1, 0)]
 
 
-def project_kernel(core_ref, mem_a, mem_b, w_a, w_b, out_ref, acc):
-    step = pl.program_id(0)
-    part = lax.dot_general(mem_a[...], w_a[...], NT, preferred_element_type=jnp.float32)
-    part += lax.dot_general(mem_b[...], w_b[...], NT, preferred_element_type=jnp.float32)
-
-    @pl.when(step == 0)
-    def _():
-        acc[...] = part
-
-    @pl.when(step > 0)
-    def _():
-        acc[...] += part
-
-    @pl.when(step == pl.num_programs(0) - 1)
-    def _():
-        out_ref[...] = acc[...].astype(out_ref.dtype)
-
-
-def project(core, mem_all, w_a, w_b):
-    tok, feat = 256, mem_all.shape[1]
+def project_kernel(*refs):
+    mem, mem_a, mem_b, w_refs, (out_ref, held, sems) = refs[:7], refs[7], refs[8], refs[9:19], refs[19:]
+    x, core, z = lax.axis_index("x"), lax.axis_index("c"), lax.axis_index("z")
+    copies = []
+    for swapped in range(2):
+        half = core if swapped == 0 else 1 - core
+        own, left, right, opp_k, opp_v = w_refs[5 * swapped : 5 * swapped + 5]
+        for away, ref in ((0, own), (3, left), (1, right)):
+            copies.append((ref, held.at[lax.rem(x + away, 4) * 2 + half]))
+        opposite = lax.rem(x + 2, 4) * 2 + half
+        copies.append((opp_k, held.at[opposite, pl.ds(0, HD)]))
+        copies.append((opp_v, held.at[opposite, pl.ds(HD, HD)]))
+    copies = [pltpu.make_async_copy(src, dst, sems.at[j]) for j, (src, dst) in enumerate(copies)]
+    for copy in copies:
+        copy.start()
+    for copy in copies:
+        copy.wait()
+    total = None
+    for ref, away in zip(mem, (0, 7, 6, 5, 1, 2, 3)):
+        w_rows = held[lax.rem(z + away, 8)]
+        part = lax.dot_general(ref[...], w_rows, NT, preferred_element_type=jnp.float32)
+        total = part if total is None else total + part
+    w_rows = held[lax.rem(z + 4, 8)]
+    for start, ref in ((0, mem_a), (128, mem_b)):
+        part = lax.dot_general(ref[...], w_rows, NT, preferred_element_type=jnp.float32)
+        out_ref[start : start + 128] = (total[start : start + 128] + part).astype(out_ref.dtype)
+
+
+def project(mem, w_pieces):
+    vmem = pl.BlockSpec(memory_space=pltpu.VMEM)
     return pl.pallas_call(
         project_kernel,
-        out_shape=jax.ShapeDtypeStruct((tok, 2 * HD), jnp.bfloat16),
-        grid_spec=pltpu.PrefetchScalarGridSpec(
-            num_scalar_prefetch=1,
-            grid=(4,),
-            in_specs=[
-                pl.BlockSpec((tok, feat), lambda j, core: (2 * j + core[0], 0)),
-                pl.BlockSpec((tok, feat), lambda j, core: (2 * j + 1 - core[0], 0)),
-                pl.BlockSpec((2 * HD, feat), lambda j, core: (j, 0)),
-                pl.BlockSpec((2 * HD, feat), lambda j, core: (j, 0)),
-            ],
-            out_specs=pl.BlockSpec((tok, 2 * HD), lambda j, core: (0, 0)),
-            scratch_shapes=[pltpu.VMEM((tok, 2 * HD), jnp.float32)],
-        ),
+        out_shape=jax.ShapeDtypeStruct((256, 2 * HD), jnp.bfloat16),
+        in_specs=[vmem] * 9 + [pl.BlockSpec(memory_space=pl.ANY)] * 10,
+        out_specs=vmem,
+        scratch_shapes=[pltpu.VMEM((8, 2 * HD, 8 * HD), jnp.bfloat16), pltpu.SemaphoreType.DMA((10,))],
         compiler_params=pltpu.CompilerParams(vmem_limit_bytes=24 << 20),
         cost_estimate=pl.CostEstimate(flops=2 * 256 * 256 * 8192, bytes_accessed=8 << 20, transcendentals=0),
-    )(core, mem_all, mem_all, w_a, w_b)
-
-
-def attend_kernel(q_ref, own, other, left, right, opp_a, opp_b, out_ref):
-    blocks = [(own, 0), (other, 0), (left, 0), (left, 256), (right, 0), (right, 256), (opp_a, 0), (opp_b, 0)]
+    )(*mem, *w_pieces)
+
+
+def attend_kernel(q_ref, own, other, out_ref):
+    blocks = [(ref, start) for ref in (own, other) for start in range(0, 1024, 256)]
     query = q_ref[...]
     top = total = acc = None
     for ref, start in blocks:
@@ -116,7 +115,7 @@
         out_ref[h, 64:, :] = jnp.broadcast_to(stats[h : h + 1], (8, HD))
 
 
-def attend(query, pieces):
+def attend(query, own, other):
     return pl.pallas_call(
         attend_kernel,
         out_shape=jax.ShapeDtypeStruct((8, 72, HD), jnp.float32),
@@ -124,7 +123,7 @@
         cost_estimate=pl.CostEstimate(
             flops=4 * 512 * 2048 * HD, bytes_accessed=2 << 20, transcendentals=512 * 2048
         ),
-    )(query, *pieces)
+    )(query, own, other)
 
 
 def merge_kernel(part_ref, out_ref):
@@ -146,29 +145,47 @@
     )(parts)
 
 
+def ring(value):
+    half = value.shape[0] // 2
+    left = lax.ppermute(value, "x", shift(4, 1))
+    right = lax.ppermute(value, "x", shift(4, -1))
+    opp_a = lax.ppermute(left[:half], "x", shift(4, 1))
+    opp_b = lax.ppermute(right[half:], "x", shift(4, -1))
+    return value, left, right, opp_a, opp_b
+
+
+def ring_z(value, after):
+    ups = [lax.ppermute(value, "z", shift(8, 1))]
+    downs = [lax.ppermute(value, "z", shift(8, -1))]
+    ups[0], downs[0], after = lax.optimization_barrier((ups[0], downs[0], after))
+    for _ in range(2):
+        ups.append(lax.ppermute(ups[-1], "z", shift(8, 1)))
+        downs.append(lax.ppermute(downs[-1], "z", shift(8, -1)))
+    opp_a = lax.ppermute(ups[2][:128], "z", shift(8, 1))
+    opp_b = lax.ppermute(downs[2][128:], "z", shift(8, -1))
+    return (value, *ups, *downs, opp_a, opp_b), after
+
+
+def swap(value):
+    return lax.ppermute(value, "c", SWAP)
+
+
 def body(memory, kv_weight, queries):
-    core = lax.axis_index("c")
-    mem_all = lax.all_gather(memory, "z", axis=0, tiled=True)
-
     rows = lax.ppermute(kv_weight, ALL, weight_moves())
     query = lax.ppermute(queries, ALL, query_moves())
-    rows = spread(rows, "y").reshape(2 * HD, -1)
-    w_a = spread(rows, "x").reshape(8 * HD, -1)
-    w_b = lax.ppermute(w_a, "c", SWAP)
-    query = spread(query, "y").reshape(512, HD)
-
-    own = project(core.astype(jnp.int32)[None], mem_all, w_a, w_b)
-    other = lax.ppermute(own, "c", SWAP)
-    pair = jnp.concatenate([own, other], axis=0)
-    left = lax.ppermute(pair, "x", RIGHT)
-    right = lax.ppermute(pair, "x", LEFT)
-    opp_a = lax.ppermute(left[:256], "x", RIGHT)
-    opp_b = lax.ppermute(right[256:], "x", LEFT)
-
-    parts = attend(query, (own, other, left, right, opp_a, opp_b))
+    both = jnp.concatenate([rows, query.reshape(8, 8 * HD)], axis=0)
+    mem, both = ring_z(memory, both)
+    both = spread(both, "y")
+    rows = both[:, :32].reshape(2 * HD, 8 * HD)
+    query = both[:, 32:].reshape(512, HD)
+    w_pieces = ring(rows)
+    own = project(mem, (*w_pieces, *map(swap, w_pieces)))
+
+    own = lax.all_gather(own, "x", axis=0, tiled=True)
+    parts = attend(query, own, swap(own))
     parts = lax.all_to_all(parts, "y", 0, 0, tiled=True)
     result = merge(parts)
-    return lax.ppermute(result, ALL, [(b, a) for a, b in query_moves()])
+    return lax.ppermute(result, ALL, query_moves())
 
 
 def solution(mesh):

time: 170 us -> 152 us (0.89)
  the two profiles are of different devices: /device:TPU:22 before, /device:TPU:256 now
where the time goes in v2:
time: 152 us; the launch traced here: 151 us
  starting transfers between devices  70.3 us (46%)
  waiting for transfers between devices  38.3 us (25%)
  blocking collectives  32.2 us (21%)
  Pallas kernels  6.31 us (4%)
  local copies, waits for them, and re-layouts  3.69 us (2%)
    all_to_all x1, blocking collectives, body(): parts = lax.all_to_all(parts, 'y', 0, 0, tiled=True)  19.2 us
    all_gather x1, blocking collectives, body(): own = lax.all_gather(own, 'x', axis=0, tiled=True)  13 us
    ppermute x2, waiting for transfers between devices, ring_z(): ups.append(lax.ppermute(ups[-1], 'z', shift(8, 1)))  12.2 us
    ppermute x6, starting transfers between devices, swap(): return lax.ppermute(value, 'c', SWAP)  12 us
    ppermute x1, waiting for transfers between devices, body(): return lax.ppermute(result, ALL, query_moves())  11.8 us
    ppermute x1, waiting for transfers between devices, body(): query = lax.ppermute(queries, ALL, query_moves())  10.3 us
    ppermute x2, starting transfers between devices, ring_z(): downs.append(lax.ppermute(downs[-1], 'z', shift(8, -1)))  9.16 us
    ppermute x1, starting transfers between devices, body(): rows = lax.ppermute(kv_weight, ALL, weight_moves())  7.11 us
  transfers between devices with their start and end apart: 22, of which 8 were waited for; matrix products, arithmetic and copies ran while one was open for 1% of the time, Pallas kernels for 0%

profile of v2, /device:TPU:256, one launch (start us, length us, event | category | flops | bytes accessed | tf_op | source)
XLA Modules:
  0.0 151.1 jit_solution(9379702966112213517)
XLA Ops:
  0.0 3.4 %collective-permute-start = (bf16[256,1024]{1,0:T(8,128)(2,1)}, bf16[256,1024]{1,0:T(8,128)(2,1)S(1)}, u32[]{:S(2)}, u32[]{:S(2)}) collective-permute-start(bf16[256,1024]{1,0:T(8,128)(2,1)} %refs_0_.1), channel_id=1, source_target_pairs={{0,1},{1,2},{2,3},{3,4},{4,5},{5,6},{6,7},{7,0},{8,9},{9,10},{10,1... | collective-permute-start | bytes 1572872 | tf_op jit(solution)/shard_map/ppermute | solution.py:158
  3.4 3.7 %collective-permute-start.1 = (bf16[256,1024]{1,0:T(8,128)(2,1)}, bf16[256,1024]{1,0:T(8,128)(2,1)S(1)}, u32[]{:S(2)}, u32[]{:S(2)}) collective-permute-start(bf16[256,1024]{1,0:T(8,128)(2,1)} %refs_0_.1), channel_id=1, source_target_pairs={{0,7},{1,0},{2,1},{3,2},{4,3},{5,4},{6,5},{7,6},{8,15},{9,8},{10,9... | collective-permute-start | bytes 1572872 | tf_op jit(solution)/shard_map/ppermute | solution.py:159
  7.1 7.1 %collective-permute-start.2 = (bf16[32,1024]{1,0:T(8,128)(2,1)}, bf16[32,1024]{1,0:T(8,128)(2,1)S(1)}, u32[]{:S(2)}, u32[]{:S(2)}) collective-permute-start(bf16[32,1024]{1,0:T(8,128)(2,1)} %param.4), channel_id=1, source_target_pairs={{0,0},{1,8},{2,16},{3,24},{4,32},{5,40},{6,48},{7,56},{8,64},{9,72... | collective-permute-start | bytes 196616 | tf_op jit(solution)/shard_map/ppermute | solution.py:174
  14.2 4.3 %collective-permute-start.3 = (bf16[64,128]{1,0:T(8,128)(2,1)}, bf16[64,128]{1,0:T(8,128)(2,1)S(1)}, u32[]{:S(2)}, u32[]{:S(2)}) collective-permute-start(bf16[64,128]{1,0:T(8,128)(2,1)} %param.5), channel_id=1, source_target_pairs={{0,0},{1,64},{2,128},{3,192},{4,256},{5,320},{6,384},{7,448},{8,8}... | collective-permute-start | bytes 49160 | tf_op jit(solution)/shard_map/ppermute | solution.py:175
  18.5 10.3 %collective-permute-done.3 = bf16[64,128]{1,0:T(8,128)(2,1)S(1)} collective-permute-done((bf16[64,128]{1,0:T(8,128)(2,1)}, bf16[64,128]{1,0:T(8,128)(2,1)S(1)}, u32[]{:S(2)}, u32[]{:S(2)}) %collective-permute-start.3) | collective-permute-done | bytes 16416 | tf_op jit(solution)/shard_map/ppermute | solution.py:175
  29.7 4.2 %all-to-all-start = ((bf16[8,40,1024]{2,1,0:T(8,128)(2,1)}), bf16[8,40,1024]{2,1,0:T(8,128)(2,1)}, u32[]{:S(2)}, u32[]{:S(2)}) async-start(bf16[8,40,1024]{2,1,0:T(8,128)(2,1)} %broadcast_in_dim.2), calls=%async_computation | async-start | bytes 1310720 | tf_op jit(solution)/shard_map/all_to_all | solution.py:16
  34.0 3.0 %collective-permute-start.4 = (bf16[256,1024]{1,0:T(8,128)(2,1)S(1)}, bf16[256,1024]{1,0:T(8,128)(2,1)S(1)}, u32[]{:S(2)}, u32[]{:S(2)}) collective-permute-start(bf16[256,1024]{1,0:T(8,128)(2,1)S(1)} %collective-permute-done.refs_1_), channel_id=1, source_target_pairs={{0,1},{1,2},{2,3},{3,4},{4,5},{5,6},{6,7},{7,0},{8,9},{9,10},{10,1... | collective-permute-start | bytes 1572872 | tf_op jit(solution)/shard_map/ppermute | solution.py:162
  37.0 4.0 %collective-permute-start.6 = (bf16[256,1024]{1,0:T(8,128)(2,1)S(1)}, bf16[256,1024]{1,0:T(8,128)(2,1)S(1)}, u32[]{:S(2)}, u32[]{:S(2)}) collective-permute-start(bf16[256,1024]{1,0:T(8,128)(2,1)S(1)} %collective-permute-done.1.refs_4_), channel_id=1, source_target_pairs={{0,7},{1,0},{2,1},{3,2},{4,3},{5,4},{6,5},{7,6},{8,15},{9,8},{10,9... | collective-permute-start | bytes 1572872 | tf_op jit(solution)/shard_map/ppermute | solution.py:163
  41.0 10.0 %collective-permute-done.4.refs_2_ = bf16[256,1024]{1,0:T(8,128)(2,1)S(1)} collective-permute-done((bf16[256,1024]{1,0:T(8,128)(2,1)S(1)}, bf16[256,1024]{1,0:T(8,128)(2,1)S(1)}, u32[]{:S(2)}, u32[]{:S(2)}) %collective-permute-start.4) | collective-permute-done | bytes 524320 | tf_op jit(solution)/shard_map/ppermute | solution.py:162
  51.0 1.9 %collective-permute-start.5 = (bf16[256,1024]{1,0:T(8,128)(2,1)S(1)}, bf16[256,1024]{1,0:T(8,128)(2,1)S(1)}, u32[]{:S(2)}, u32[]{:S(2)}) collective-permute-start(bf16[256,1024]{1,0:T(8,128)(2,1)S(1)} %collective-permute-done.4.refs_2_), channel_id=1, source_target_pairs={{0,1},{1,2},{2,3},{3,4},{4,5},{5,6},{6,7},{7,0},{8,9},{9,10},{10,1... | collective-permute-start | bytes 1572872 | tf_op jit(solution)/shard_map/ppermute | solution.py:162
  52.9 5.1 %collective-permute-start.7 = (bf16[256,1024]{1,0:T(8,128)(2,1)S(1)}, bf16[256,1024]{1,0:T(8,128)(2,1)S(1)}, u32[]{:S(2)}, u32[]{:S(2)}) collective-permute-start(bf16[256,1024]{1,0:T(8,128)(2,1)S(1)} %collective-permute-done.6.refs_5_), channel_id=1, source_target_pairs={{0,7},{1,0},{2,1},{3,2},{4,3},{5,4},{6,5},{7,6},{8,15},{9,8},{10,9... | collective-permute-start | bytes 1572872 | tf_op jit(solution)/shard_map/ppermute | solution.py:163
  59.2 1.9 %collective-permute-start.11 = (bf16[256,1024]{1,0:T(8,128)(2,1)S(1)}, bf16[256,1024]{1,0:T(8,128)(2,1)S(1)}, u32[]{:S(2)}, u32[]{:S(2)}) collective-permute-start(bf16[256,1024]{1,0:T(8,128)(2,1)S(1)} %bitcast.1), channel_id=1, source_target_pairs={{0,48},{16,0},{32,16},{48,32},{1,49},{17,1},{33,17},{49,33},{2,50}... | collective-permute-start | bytes 1572872 | tf_op jit(solution)/shard_map/ppermute | solution.py:151
  61.1 3.9 %collective-permute-start.10 = (bf16[256,1024]{1,0:T(8,128)(2,1)S(1)}, bf16[256,1024]{1,0:T(8,128)(2,1)S(1)}, u32[]{:S(2)}, u32[]{:S(2)}) collective-permute-start(bf16[256,1024]{1,0:T(8,128)(2,1)S(1)} %bitcast.2), channel_id=1, source_target_pairs={{0,16},{16,32},{32,48},{48,0},{1,17},{17,33},{33,49},{49,1},{2,18}... | collective-permute-start | bytes 1572872 | tf_op jit(solution)/shard_map/ppermute | solution.py:150
  65.0 2.2 %collective-permute-done.5.refs_3_ = bf16[256,1024]{1,0:T(8,128)(2,1)S(1)} collective-permute-done((bf16[256,1024]{1,0:T(8,128)(2,1)S(1)}, bf16[256,1024]{1,0:T(8,128)(2,1)S(1)}, u32[]{:S(2)}, u32[]{:S(2)}) %collective-permute-start.5) | collective-permute-done | bytes 524320 | tf_op jit(solution)/shard_map/ppermute | solution.py:162
  67.2 1.9 %collective-permute-start.8 = (bf16[128,1024]{1,0:T(8,128)(2,1)S(1)}, bf16[128,1024]{1,0:T(8,128)(2,1)S(1)}, u32[]{:S(2)}, u32[]{:S(2)}) collective-permute-start(bf16[128,1024]{1,0:T(8,128)(2,1)S(1)} %slice.25), channel_id=1, source_target_pairs={{0,1},{1,2},{2,3},{3,4},{4,5},{5,6},{6,7},{7,0},{8,9},{9,10},{10,1... | collective-permute-start | bytes 786440 | tf_op jit(solution)/shard_map/ppermute | solution.py:164
  69.2 5.3 %collective-permute-start.9 = (bf16[128,1024]{1,0:T(8,128)(2,1)S(1)}, bf16[128,1024]{1,0:T(8,128)(2,1)S(1)}, u32[]{:S(2)}, u32[]{:S(2)}) collective-permute-start(bf16[128,1024]{1,0:T(8,128)(2,1)S(1)} %slice.26), channel_id=1, source_target_pairs={{0,7},{1,0},{2,1},{3,2},{4,3},{5,4},{6,5},{7,6},{8,15},{9,8},{10,9... | collective-permute-start | bytes 786440 | tf_op jit(solution)/shard_map/ppermute | solution.py:165
  74.5 1.9 %collective-permute-start.14 = (bf16[256,1024]{1,0:T(8,128)(2,1)S(1)}, bf16[256,1024]{1,0:T(8,128)(2,1)S(1)}, u32[]{:S(2)}, u32[]{:S(2)}) collective-permute-start(bf16[256,1024]{1,0:T(8,128)(2,1)S(1)} %bitcast.3), channel_id=1, source_target_pairs={{0,8},{8,0},{1,9},{9,1},{2,10},{10,2},{3,11},{11,3},{4,12},{12,4},... | collective-permute-start | bytes 1572872 | tf_op jit(solution)/shard_map/ppermute | solution.py:170
  76.4 1.9 %collective-permute-start.13 = (bf16[128,1024]{1,0:T(8,128)(2,1)S(1)}, bf16[128,1024]{1,0:T(8,128)(2,1)S(1)}, u32[]{:S(2)}, u32[]{:S(2)}) collective-permute-start(bf16[128,1024]{1,0:T(8,128)(2,1)S(1)} %slice.29), channel_id=1, source_target_pairs={{0,48},{16,0},{32,16},{48,32},{1,49},{17,1},{33,17},{49,33},{2,50}... | collective-permute-start | bytes 786440 | tf_op jit(solution)/shard_map/ppermute | solution.py:153
  78.4 3.9 %collective-permute-start.12 = (bf16[128,1024]{1,0:T(8,128)(2,1)S(1)}, bf16[128,1024]{1,0:T(8,128)(2,1)S(1)}, u32[]{:S(2)}, u32[]{:S(2)}) collective-permute-start(bf16[128,1024]{1,0:T(8,128)(2,1)S(1)} %slice.28), channel_id=1, source_target_pairs={{0,16},{16,32},{32,48},{48,0},{1,17},{17,33},{33,49},{49,1},{2,18}... | collective-permute-start | bytes 786440 | tf_op jit(solution)/shard_map/ppermute | solution.py:152
  82.4 2.1 %collective-permute-start.16 = (bf16[256,1024]{1,0:T(8,128)(2,1)S(1)}, bf16[256,1024]{1,0:T(8,128)(2,1)S(1)}, u32[]{:S(2)}, u32[]{:S(2)}) collective-permute-start(bf16[256,1024]{1,0:T(8,128)(2,1)S(1)} %collective-permute-done.11.refs_11_), channel_id=1, source_target_pairs={{0,8},{8,0},{1,9},{9,1},{2,10},{10,2},{3,11},{11,3},{4,12},{12,4},... | collective-permute-start | bytes 1572872 | tf_op jit(solution)/shard_map/ppermute | solution.py:170
  84.5 2.2 %collective-permute-start.15 = (bf16[256,1024]{1,0:T(8,128)(2,1)S(1)}, bf16[256,1024]{1,0:T(8,128)(2,1)S(1)}, u32[]{:S(2)}, u32[]{:S(2)}) collective-permute-start(bf16[256,1024]{1,0:T(8,128)(2,1)S(1)} %collective-permute-done.10.refs_10_), channel_id=1, source_target_pairs={{0,8},{8,0},{1,9},{9,1},{2,10},{10,2},{3,11},{11,3},{4,12},{12,4},... | collective-permute-start | bytes 1572872 | tf_op jit(solution)/shard_map/ppermute | solution.py:170
  87.3 1.9 %collective-permute-start.18 = (bf16[128,1024]{1,0:T(8,128)(2,1)S(1)}, bf16[128,1024]{1,0:T(8,128)(2,1)S(1)}, u32[]{:S(2)}, u32[]{:S(2)}) collective-permute-start(bf16[128,1024]{1,0:T(8,128)(2,1)S(1)} %collective-permute-done.13.refs_13_), channel_id=1, source_target_pairs={{0,8},{8,0},{1,9},{9,1},{2,10},{10,2},{3,11},{11,3},{4,12},{12,4},... | collective-permute-start | bytes 786440 | tf_op jit(solution)/shard_map/ppermute | solution.py:170
  90.2 1.9 %collective-permute-start.17 = (bf16[128,1024]{1,0:T(8,128)(2,1)S(1)}, bf16[128,1024]{1,0:T(8,128)(2,1)S(1)}, u32[]{:S(2)}, u32[]{:S(2)}) collective-permute-start(bf16[128,1024]{1,0:T(8,128)(2,1)S(1)} %collective-permute-done.12.refs_12_), channel_id=1, source_target_pairs={{0,8},{8,0},{1,9},{9,1},{2,10},{10,2},{3,11},{11,3},{4,12},{12,4},... | collective-permute-start | bytes 786440 | tf_op jit(solution)/shard_map/ppermute | solution.py:170
  92.2 1.5 collective-permute-done.17.refs_17_
  93.7 1.8 %shard_map.37 = bf16[256,256]{1,0:T(8,128)(2,1)S(1)} custom-call(bf16[256,1024]{1,0:T(8,128)(2,1)S(1)} %copy-done, bf16[256,1024]{1,0:T(8,128)(2,1)S(1)} %collective-permute-done.refs_1_, bf16[256,1024]{1,0:T(8,128)(2,1)S(1)} %collective-permute-done.4.refs_2_, bf16[256,1024]{1,0:T(8,128)(2,1)S(1)} %collective-permute-done.5.refs_3_, ...), custom_call_target="tpu_custom_call" | custom-call | flops 1073741824 | bytes 8388608 | tf_op jit(solution)/shard_map/pallas_call | solution.py:79
  95.5 13.0 %all_gather.3.own = bf16[1024,256]{1,0:T(8,128)(2,1)S(1)} all-gather(bf16[256,256]{1,0:T(8,128)(2,1)S(1)} %shard_map.37), channel_id=1, replica_groups=mesh['y'=8,'x'=4,'c'=2,'z'=8] {'x'}, dimensions={0}, use_global_device_ids=true | all-gather | bytes 655360 | tf_op jit(solution)/shard_map/all_gather | solution.py:184
  108.5 1.9 %collective-permute-start.19 = (bf16[1024,256]{1,0:T(8,128)(2,1)S(1)}, bf16[1024,256]{1,0:T(8,128)(2,1)S(1)}, u32[]{:S(2)}, u32[]{:S(2)}) collective-permute-start(bf16[1024,256]{1,0:T(8,128)(2,1)S(1)} %all_gather.3.own), channel_id=1, source_target_pairs={{0,8},{8,0},{1,9},{9,1},{2,10},{10,2},{3,11},{11,3},{4,12},{12,4},... | collective-permute-start | bytes 1572872 | tf_op jit(solution)/shard_map/ppermute | solution.py:170
  112.3 2.3 %shard_map.38 = f32[8,72,128]{2,1,0:T(8,128)S(1)} custom-call(bf16[512,128]{1,0:T(8,128)(2,1)S(1)} %reshape.11.q_ref, bf16[1024,256]{1,0:T(8,128)(2,1)S(1)} %all_gather.3.own, bf16[1024,256]{1,0:T(8,128)(2,1)S(1)} %collective-permute-done.19.other), custom_call_target="tpu_custom_call" | custom-call | flops 536870912 | bytes 2097152 | tf_op jit(solution)/shard_map/pallas_call | solution.py:119
  114.6 19.2 %all_to_all.10.part_ref = f32[8,72,128]{2,1,0:T(8,128)} all-to-all(f32[8,72,128]{2,1,0:T(8,128)S(1)} %shard_map.38), channel_id=1, replica_groups=mesh['y'=8,'x'=4,'c'=2,'z'=8] {'y'}, dimensions={0} | all-to-all | bytes 589824 | tf_op jit(solution)/shard_map/all_to_all | solution.py:186
  133.9 2.1 %shard_map.39 = bf16[64,128]{1,0:T(8,128)(2,1)} custom-call(f32[8,72,128]{2,1,0:T(8,128)} %all_to_all.10.part_ref), custom_call_target="tpu_custom_call" | custom-call | tf_op jit(solution)/shard_map/pallas_call | solution.py:142
  136.0 2.7 %collective-permute-start.20 = (bf16[64,128]{1,0:T(8,128)(2,1)}, bf16[64,128]{1,0:T(8,128)(2,1)S(1)}, u32[]{:S(2)}, u32[]{:S(2)}) collective-permute-start(bf16[64,128]{1,0:T(8,128)(2,1)} %shard_map.39), channel_id=1, source_target_pairs={{0,0},{1,64},{2,128},{3,192},{4,256},{5,320},{6,384},{7,448},{8,8}... | collective-permute-start | bytes 49160 | tf_op jit(solution)/shard_map/ppermute | solution.py:188
  138.7 11.8 %collective-permute-done.20 = bf16[64,128]{1,0:T(8,128)(2,1)S(1)} collective-permute-done((bf16[64,128]{1,0:T(8,128)(2,1)}, bf16[64,128]{1,0:T(8,128)(2,1)S(1)}, u32[]{:S(2)}, u32[]{:S(2)}) %collective-permute-start.20) | collective-permute-done | bytes 16416 | tf_op jit(solution)/shard_map/ppermute | solution.py:188
  (30 shorter events, 6.2 us)
Async XLA Ops:
  0.0 28.8 %collective-permute-start = (bf16[256,1024]{1,0:T(8,128)(2,1)}, bf16[256,1024]{1,0:T(8,128)(2,1)S(1)}, u32[]{:S(2)}, u32[]{:S(2)}) collective-permute-start(bf16[256,1024]{1,0:T(8,128)(2,1)} %refs_0_.1), channel_id=1, source_target_pairs={{0,1},{1,2},{2,3},{3,4},{4,5},{5,6},{6,7},{7,0},{8,9},{9,10},{10,1... | collective-permute-start | bytes 1572872 | tf_op jit(solution)/shard_map/ppermute | solution.py:158
  3.4 25.4 %collective-permute-start.1 = (bf16[256,1024]{1,0:T(8,128)(2,1)}, bf16[256,1024]{1,0:T(8,128)(2,1)S(1)}, u32[]{:S(2)}, u32[]{:S(2)}) collective-permute-start(bf16[256,1024]{1,0:T(8,128)(2,1)} %refs_0_.1), channel_id=1, source_target_pairs={{0,7},{1,0},{2,1},{3,2},{4,3},{5,4},{6,5},{7,6},{8,15},{9,8},{10,9... | collective-permute-start | bytes 1572872 | tf_op jit(solution)/shard_map/ppermute | solution.py:159
  7.1 21.7 %collective-permute-start.2 = (bf16[32,1024]{1,0:T(8,128)(2,1)}, bf16[32,1024]{1,0:T(8,128)(2,1)S(1)}, u32[]{:S(2)}, u32[]{:S(2)}) collective-permute-start(bf16[32,1024]{1,0:T(8,128)(2,1)} %param.4), channel_id=1, source_target_pairs={{0,0},{1,8},{2,16},{3,24},{4,32},{5,40},{6,48},{7,56},{8,64},{9,72... | collective-permute-start | bytes 196616 | tf_op jit(solution)/shard_map/ppermute | solution.py:174
  14.2 14.6 %collective-permute-start.3 = (bf16[64,128]{1,0:T(8,128)(2,1)}, bf16[64,128]{1,0:T(8,128)(2,1)S(1)}, u32[]{:S(2)}, u32[]{:S(2)}) collective-permute-start(bf16[64,128]{1,0:T(8,128)(2,1)} %param.5), channel_id=1, source_target_pairs={{0,0},{1,64},{2,128},{3,192},{4,256},{5,320},{6,384},{7,448},{8,8}... | collective-permute-start | bytes 49160 | tf_op jit(solution)/shard_map/ppermute | solution.py:175
  29.7 28.3 %all-to-all-start = ((bf16[8,40,1024]{2,1,0:T(8,128)(2,1)}), bf16[8,40,1024]{2,1,0:T(8,128)(2,1)}, u32[]{:S(2)}, u32[]{:S(2)}) async-start(bf16[8,40,1024]{2,1,0:T(8,128)(2,1)} %broadcast_in_dim.2), calls=%async_computation | async-start | bytes 1310720 | tf_op jit(solution)/shard_map/all_to_all | solution.py:16
  34.0 17.0 %collective-permute-start.4 = (bf16[256,1024]{1,0:T(8,128)(2,1)S(1)}, bf16[256,1024]{1,0:T(8,128)(2,1)S(1)}, u32[]{:S(2)}, u32[]{:S(2)}) collective-permute-start(bf16[256,1024]{1,0:T(8,128)(2,1)S(1)} %collective-permute-done.refs_1_), channel_id=1, source_target_pairs={{0,1},{1,2},{2,3},{3,4},{4,5},{5,6},{6,7},{7,0},{8,9},{9,10},{10,1... | collective-permute-start | bytes 1572872 | tf_op jit(solution)/shard_map/ppermute | solution.py:162
  37.0 15.9 %collective-permute-start.6 = (bf16[256,1024]{1,0:T(8,128)(2,1)S(1)}, bf16[256,1024]{1,0:T(8,128)(2,1)S(1)}, u32[]{:S(2)}, u32[]{:S(2)}) collective-permute-start(bf16[256,1024]{1,0:T(8,128)(2,1)S(1)} %collective-permute-done.1.refs_4_), channel_id=1, source_target_pairs={{0,7},{1,0},{2,1},{3,2},{4,3},{5,4},{6,5},{7,6},{8,15},{9,8},{10,9... | collective-permute-start | bytes 1572872 | tf_op jit(solution)/shard_map/ppermute | solution.py:163
  51.0 16.2 %collective-permute-start.5 = (bf16[256,1024]{1,0:T(8,128)(2,1)S(1)}, bf16[256,1024]{1,0:T(8,128)(2,1)S(1)}, u32[]{:S(2)}, u32[]{:S(2)}) collective-permute-start(bf16[256,1024]{1,0:T(8,128)(2,1)S(1)} %collective-permute-done.4.refs_2_), channel_id=1, source_target_pairs={{0,1},{1,2},{2,3},{3,4},{4,5},{5,6},{6,7},{7,0},{8,9},{9,10},{10,1... | collective-permute-start | bytes 1572872 | tf_op jit(solution)/shard_map/ppermute | solution.py:162
  52.9 16.2 %collective-permute-start.7 = (bf16[256,1024]{1,0:T(8,128)(2,1)S(1)}, bf16[256,1024]{1,0:T(8,128)(2,1)S(1)}, u32[]{:S(2)}, u32[]{:S(2)}) collective-permute-start(bf16[256,1024]{1,0:T(8,128)(2,1)S(1)} %collective-permute-done.6.refs_5_), channel_id=1, source_target_pairs={{0,7},{1,0},{2,1},{3,2},{4,3},{5,4},{6,5},{7,6},{8,15},{9,8},{10,9... | collective-permute-start | bytes 1572872 | tf_op jit(solution)/shard_map/ppermute | solution.py:163
  59.2 17.2 %collective-permute-start.11 = (bf16[256,1024]{1,0:T(8,128)(2,1)S(1)}, bf16[256,1024]{1,0:T(8,128)(2,1)S(1)}, u32[]{:S(2)}, u32[]{:S(2)}) collective-permute-start(bf16[256,1024]{1,0:T(8,128)(2,1)S(1)} %bitcast.1), channel_id=1, source_target_pairs={{0,48},{16,0},{32,16},{48,32},{1,49},{17,1},{33,17},{49,33},{2,50}... | collective-permute-start | bytes 1572872 | tf_op jit(solution)/shard_map/ppermute | solution.py:151
  61.1 17.3 %collective-permute-start.10 = (bf16[256,1024]{1,0:T(8,128)(2,1)S(1)}, bf16[256,1024]{1,0:T(8,128)(2,1)S(1)}, u32[]{:S(2)}, u32[]{:S(2)}) collective-permute-start(bf16[256,1024]{1,0:T(8,128)(2,1)S(1)} %bitcast.2), channel_id=1, source_target_pairs={{0,16},{16,32},{32,48},{48,0},{1,17},{17,33},{33,49},{49,1},{2,18}... | collective-permute-start | bytes 1572872 | tf_op jit(solution)/shard_map/ppermute | solution.py:150
  67.2 15.1 %collective-permute-start.8 = (bf16[128,1024]{1,0:T(8,128)(2,1)S(1)}, bf16[128,1024]{1,0:T(8,128)(2,1)S(1)}, u32[]{:S(2)}, u32[]{:S(2)}) collective-permute-start(bf16[128,1024]{1,0:T(8,128)(2,1)S(1)} %slice.25), channel_id=1, source_target_pairs={{0,1},{1,2},{2,3},{3,4},{4,5},{5,6},{6,7},{7,0},{8,9},{9,10},{10,1... | collective-permute-start | bytes 786440 | tf_op jit(solution)/shard_map/ppermute | solution.py:164
  69.2 24.5 %copy-start = (bf16[256,1024]{1,0:T(8,128)(2,1)S(1)}, bf16[256,1024]{1,0:T(8,128)(2,1)}, u32[]{:S(2)}) copy-start(bf16[256,1024]{1,0:T(8,128)(2,1)} %refs_0_.1) | copy-start | bytes 1572868
  69.2 15.3 %collective-permute-start.9 = (bf16[128,1024]{1,0:T(8,128)(2,1)S(1)}, bf16[128,1024]{1,0:T(8,128)(2,1)S(1)}, u32[]{:S(2)}, u32[]{:S(2)}) collective-permute-start(bf16[128,1024]{1,0:T(8,128)(2,1)S(1)} %slice.26), channel_id=1, source_target_pairs={{0,7},{1,0},{2,1},{3,2},{4,3},{5,4},{6,5},{7,6},{8,15},{9,8},{10,9... | collective-permute-start | bytes 786440 | tf_op jit(solution)/shard_map/ppermute | solution.py:165
  74.5 17.7 %collective-permute-start.14 = (bf16[256,1024]{1,0:T(8,128)(2,1)S(1)}, bf16[256,1024]{1,0:T(8,128)(2,1)S(1)}, u32[]{:S(2)}, u32[]{:S(2)}) collective-permute-start(bf16[256,1024]{1,0:T(8,128)(2,1)S(1)} %bitcast.3), channel_id=1, source_target_pairs={{0,8},{8,0},{1,9},{9,1},{2,10},{10,2},{3,11},{11,3},{4,12},{12,4},... | collective-permute-start | bytes 1572872 | tf_op jit(solution)/shard_map/ppermute | solution.py:170
  76.4 10.9 %collective-permute-start.13 = (bf16[128,1024]{1,0:T(8,128)(2,1)S(1)}, bf16[128,1024]{1,0:T(8,128)(2,1)S(1)}, u32[]{:S(2)}, u32[]{:S(2)}) collective-permute-start(bf16[128,1024]{1,0:T(8,128)(2,1)S(1)} %slice.29), channel_id=1, source_target_pairs={{0,48},{16,0},{32,16},{48,32},{1,49},{17,1},{33,17},{49,33},{2,50}... | collective-permute-start | bytes 786440 | tf_op jit(solution)/shard_map/ppermute | solution.py:153
  78.4 11.8 %collective-permute-start.12 = (bf16[128,1024]{1,0:T(8,128)(2,1)S(1)}, bf16[128,1024]{1,0:T(8,128)(2,1)S(1)}, u32[]{:S(2)}, u32[]{:S(2)}) collective-permute-start(bf16[128,1024]{1,0:T(8,128)(2,1)S(1)} %slice.28), channel_id=1, source_target_pairs={{0,16},{16,32},{32,48},{48,0},{1,17},{17,33},{33,49},{49,1},{2,18}... | collective-permute-start | bytes 786440 | tf_op jit(solution)/shard_map/ppermute | solution.py:152
  82.4 11.3 %collective-permute-start.16 = (bf16[256,1024]{1,0:T(8,128)(2,1)S(1)}, bf16[256,1024]{1,0:T(8,128)(2,1)S(1)}, u32[]{:S(2)}, u32[]{:S(2)}) collective-permute-start(bf16[256,1024]{1,0:T(8,128)(2,1)S(1)} %collective-permute-done.11.refs_11_), channel_id=1, source_target_pairs={{0,8},{8,0},{1,9},{9,1},{2,10},{10,2},{3,11},{11,3},{4,12},{12,4},... | collective-permute-start | bytes 1572872 | tf_op jit(solution)/shard_map/ppermute | solution.py:170
  84.5 9.2 %collective-permute-start.15 = (bf16[256,1024]{1,0:T(8,128)(2,1)S(1)}, bf16[256,1024]{1,0:T(8,128)(2,1)S(1)}, u32[]{:S(2)}, u32[]{:S(2)}) collective-permute-start(bf16[256,1024]{1,0:T(8,128)(2,1)S(1)} %collective-permute-done.10.refs_10_), channel_id=1, source_target_pairs={{0,8},{8,0},{1,9},{9,1},{2,10},{10,2},{3,11},{11,3},{4,12},{12,4},... | collective-permute-start | bytes 1572872 | tf_op jit(solution)/shard_map/ppermute | solution.py:170
  87.3 4.9 %collective-permute-start.18 = (bf16[128,1024]{1,0:T(8,128)(2,1)S(1)}, bf16[128,1024]{1,0:T(8,128)(2,1)S(1)}, u32[]{:S(2)}, u32[]{:S(2)}) collective-permute-start(bf16[128,1024]{1,0:T(8,128)(2,1)S(1)} %collective-permute-done.13.refs_13_), channel_id=1, source_target_pairs={{0,8},{8,0},{1,9},{9,1},{2,10},{10,2},{3,11},{11,3},{4,12},{12,4},... | collective-permute-start | bytes 786440 | tf_op jit(solution)/shard_map/ppermute | solution.py:170
  90.2 3.4 %collective-permute-start.17 = (bf16[128,1024]{1,0:T(8,128)(2,1)S(1)}, bf16[128,1024]{1,0:T(8,128)(2,1)S(1)}, u32[]{:S(2)}, u32[]{:S(2)}) collective-permute-start(bf16[128,1024]{1,0:T(8,128)(2,1)S(1)} %collective-permute-done.12.refs_12_), channel_id=1, source_target_pairs={{0,8},{8,0},{1,9},{9,1},{2,10},{10,2},{3,11},{11,3},{4,12},{12,4},... | collective-permute-start | bytes 786440 | tf_op jit(solution)/shard_map/ppermute | solution.py:170
  108.5 3.8 %collective-permute-start.19 = (bf16[1024,256]{1,0:T(8,128)(2,1)S(1)}, bf16[1024,256]{1,0:T(8,128)(2,1)S(1)}, u32[]{:S(2)}, u32[]{:S(2)}) collective-permute-start(bf16[1024,256]{1,0:T(8,128)(2,1)S(1)} %all_gather.3.own), channel_id=1, source_target_pairs={{0,8},{8,0},{1,9},{9,1},{2,10},{10,2},{3,11},{11,3},{4,12},{12,4},... | collective-permute-start | bytes 1572872 | tf_op jit(solution)/shard_map/ppermute | solution.py:170
  136.0 14.5 %collective-permute-start.20 = (bf16[64,128]{1,0:T(8,128)(2,1)}, bf16[64,128]{1,0:T(8,128)(2,1)S(1)}, u32[]{:S(2)}, u32[]{:S(2)}) collective-permute-start(bf16[64,128]{1,0:T(8,128)(2,1)} %shard_map.39), channel_id=1, source_target_pairs={{0,0},{1,64},{2,128},{3,192},{4,256},{5,320},{6,384},{7,448},{8,8}... | collective-permute-start | bytes 49160 | tf_op jit(solution)/shard_map/ppermute | solution.py:188

commit v3 on v2

--- a/solution.py
+++ b/solution.py
@@ -47,44 +47,37 @@
 
 
 def project_kernel(*refs):
-    mem, mem_a, mem_b, w_refs, (out_ref, held, sems) = refs[:7], refs[7], refs[8], refs[9:19], refs[19:]
-    x, core, z = lax.axis_index("x"), lax.axis_index("c"), lax.axis_index("z")
-    copies = []
-    for swapped in range(2):
-        half = core if swapped == 0 else 1 - core
-        own, left, right, opp_k, opp_v = w_refs[5 * swapped : 5 * swapped + 5]
-        for away, ref in ((0, own), (3, left), (1, right)):
-            copies.append((ref, held.at[lax.rem(x + away, 4) * 2 + half]))
-        opposite = lax.rem(x + 2, 4) * 2 + half
-        copies.append((opp_k, held.at[opposite, pl.ds(0, HD)]))
-        copies.append((opp_v, held.at[opposite, pl.ds(HD, HD)]))
-    copies = [pltpu.make_async_copy(src, dst, sems.at[j]) for j, (src, dst) in enumerate(copies)]
-    for copy in copies:
-        copy.start()
-    for copy in copies:
-        copy.wait()
-    total = None
-    for ref, away in zip(mem, (0, 7, 6, 5, 1, 2, 3)):
-        w_rows = held[lax.rem(z + away, 8)]
-        part = lax.dot_general(ref[...], w_rows, NT, preferred_element_type=jnp.float32)
-        total = part if total is None else total + part
-    w_rows = held[lax.rem(z + 4, 8)]
-    for start, ref in ((0, mem_a), (128, mem_b)):
-        part = lax.dot_general(ref[...], w_rows, NT, preferred_element_type=jnp.float32)
-        out_ref[start : start + 128] = (total[start : start + 128] + part).astype(out_ref.dtype)
+    mem, (mem_a, mem_b, w_a, w_b, out_ref) = refs[:7], refs[7:]
+    core, z = lax.axis_index("c"), lax.axis_index("z")
+
+    def run(even, odd):
+        def rows(away):
+            return (even, odd)[away % 2][lax.rem(z + away, 8) // 2]
+
+        total = None
+        for ref, away in zip(mem, (0, 7, 6, 5, 1, 2, 3)):
+            part = lax.dot_general(ref[...], rows(away), NT, preferred_element_type=jnp.float32)
+            total = part if total is None else total + part
+        for start, ref in ((0, mem_a), (128, mem_b)):
+            part = lax.dot_general(ref[...], rows(4), NT, preferred_element_type=jnp.float32)
+            out_ref[start : start + 128] = (total[start : start + 128] + part).astype(out_ref.dtype)
+
+    @pl.when(lax.rem(z, 2) == core)
+    def _():
+        run(w_a, w_b)
+
+    @pl.when(lax.rem(z, 2) != core)
+    def _():
+        run(w_b, w_a)
 
 
-def project(mem, w_pieces):
-    vmem = pl.BlockSpec(memory_space=pltpu.VMEM)
+def project(mem, w_a, w_b):
     return pl.pallas_call(
         project_kernel,
         out_shape=jax.ShapeDtypeStruct((256, 2 * HD), jnp.bfloat16),
-        in_specs=[vmem] * 9 + [pl.BlockSpec(memory_space=pl.ANY)] * 10,
-        out_specs=vmem,
-        scratch_shapes=[pltpu.VMEM((8, 2 * HD, 8 * HD), jnp.bfloat16), pltpu.SemaphoreType.DMA((10,))],
-        compiler_params=pltpu.CompilerParams(vmem_limit_bytes=24 << 20),
+        compiler_params=pltpu.CompilerParams(vmem_limit_bytes=32 << 20),
         cost_estimate=pl.CostEstimate(flops=2 * 256 * 256 * 8192, bytes_accessed=8 << 20, transcendentals=0),
-    )(*mem, *w_pieces)
+    )(*mem, w_a, w_b)
 
 
 def attend_kernel(q_ref, own, other, out_ref):
@@ -145,25 +138,8 @@
     )(parts)
 
 
-def ring(value):
-    half = value.shape[0] // 2
-    left = lax.ppermute(value, "x", shift(4, 1))
-    right = lax.ppermute(value, "x", shift(4, -1))
-    opp_a = lax.ppermute(left[:half], "x", shift(4, 1))
-    opp_b = lax.ppermute(right[half:], "x", shift(4, -1))
-    return value, left, right, opp_a, opp_b
-
-
-def ring_z(value, after):
-    ups = [lax.ppermute(value, "z", shift(8, 1))]
-    downs = [lax.ppermute(value, "z", shift(8, -1))]
-    ups[0], downs[0], after = lax.optimization_barrier((ups[0], downs[0], after))
-    for _ in range(2):
-        ups.append(lax.ppermute(ups[-1], "z", shift(8, 1)))
-        downs.append(lax.ppermute(downs[-1], "z", shift(8, -1)))
-    opp_a = lax.ppermute(ups[2][:128], "z", shift(8, 1))
-    opp_b = lax.ppermute(downs[2][128:], "z", shift(8, -1))
-    return (value, *ups, *downs, opp_a, opp_b), after
+def step_z(ups, downs):
+    return lax.ppermute(ups, "z", shift(8, 1)), lax.ppermute(downs, "z", shift(8, -1))
 
 
 def swap(value):
@@ -173,13 +149,19 @@
 def body(memory, kv_weight, queries):
     rows = lax.ppermute(kv_weight, ALL, weight_moves())
     query = lax.ppermute(queries, ALL, query_moves())
-    both = jnp.concatenate([rows, query.reshape(8, 8 * HD)], axis=0)
-    mem, both = ring_z(memory, both)
-    both = spread(both, "y")
+    memory, rows, query = lax.optimization_barrier((memory, rows, query))
+    both = spread(jnp.concatenate([rows, query.reshape(8, 8 * HD)], axis=0), "y")
+    ring = [step_z(memory, memory)]
+    ring.append(step_z(*ring[0]))
+    both, ring[1] = lax.optimization_barrier((both, ring[1]))
     rows = both[:, :32].reshape(2 * HD, 8 * HD)
     query = both[:, 32:].reshape(512, HD)
-    w_pieces = ring(rows)
-    own = project(mem, (*w_pieces, *map(swap, w_pieces)))
+    w_a = spread(rows, "x")
+    ring.append(step_z(*ring[1]))
+    w_a, ring[2] = lax.optimization_barrier((w_a, ring[2]))
+    ups, downs = zip(*ring)
+    opposite = step_z(ups[2][:128], downs[2][128:])
+    own = project((memory, *ups, *downs, *opposite), w_a, swap(w_a))
 
     own = lax.all_gather(own, "x", axis=0, tiled=True)
     parts = attend(query, own, swap(own))

time: 152 us -> 169 us (1.11)
  the two profiles are of different devices: /device:TPU:256 before, /device:TPU:32 now
where the time goes in v3:
time: 169 us; the launch traced here: 168 us
  starting transfers between devices  70.5 us (42%)
  waiting for transfers between devices  52.7 us (31%)
  blocking collectives  28.1 us (17%)
  local copies, waits for them, and re-layouts  9.86 us (6%)
  Pallas kernels  6.91 us (4%)
    ppermute x4, waiting for transfers between devices, step_z(): lax.ppermute(downs, 'z', shift(8, -1))  19.4 us
    ppermute x4, starting transfers between devices, step_z(): lax.ppermute(downs, 'z', shift(8, -1))  17.9 us
    all_to_all x2, starting transfers between devices, spread(): return lax.all_to_all(copies, axis, 0, 0, tiled=True)  16.5 us
    ppermute x4, waiting for transfers between devices, step_z(): lax.ppermute(ups, 'z', shift(8, 1))  15 us
    all_to_all x1, blocking collectives, body(): parts = lax.all_to_all(parts, 'y', 0, 0, tiled=True)  14.6 us
    all_gather x1, blocking collectives, body(): own = lax.all_gather(own, 'x', axis=0, tiled=True)  13.4 us
    ppermute x1, starting transfers between devices, body(): query = lax.ppermute(queries, ALL, query_moves())  10.9 us
    ppermute x1, starting transfers between devices, body(): return lax.ppermute(result, ALL, query_moves())  10.1 us
  transfers between devices with their start and end apart: 15, of which 11 were waited for; matrix products, arithmetic and copies ran while one was open for 0% of the time, Pallas kernels for 0%

profile of v3, /device:TPU:32, one launch (start us, length us, event | category | flops | bytes accessed | tf_op | source)
XLA Modules:
  0.0 168.3 jit_solution(13515004161659256958)
XLA Ops:
  0.0 1.6 collective-permute-start
  1.6 10.9 %collective-permute-start.1 = (bf16[64,128]{1,0:T(8,128)(2,1)}, bf16[64,128]{1,0:T(8,128)(2,1)S(1)}, u32[]{:S(2)}, u32[]{:S(2)}) collective-permute-start(bf16[64,128]{1,0:T(8,128)(2,1)} %param.5), channel_id=1, source_target_pairs={{0,0},{1,64},{2,128},{3,192},{4,256},{5,320},{6,384},{7,448},{8,8}... | collective-permute-start | bytes 49160 | tf_op jit(solution)/shard_map/ppermute | solution.py:151
  12.5 3.8 %collective-permute-done.1 = bf16[64,128]{1,0:T(8,128)(2,1)S(1)} collective-permute-done((bf16[64,128]{1,0:T(8,128)(2,1)}, bf16[64,128]{1,0:T(8,128)(2,1)S(1)}, u32[]{:S(2)}, u32[]{:S(2)}) %collective-permute-start.1) | collective-permute-done | bytes 16416 | tf_op jit(solution)/shard_map/ppermute | solution.py:151
  17.3 12.9 %all-to-all-start = ((bf16[8,40,1024]{2,1,0:T(8,128)(2,1)}), bf16[8,40,1024]{2,1,0:T(8,128)(2,1)S(1)}, u32[]{:S(2)}, u32[]{:S(2)}) async-start(bf16[8,40,1024]{2,1,0:T(8,128)(2,1)} %broadcast_in_dim.6), calls=%async_computation | async-start | bytes 1310720 | tf_op jit(solution)/shard_map/all_to_all | solution.py:16
  30.2 5.1 %collective-permute-start.4 = (bf16[256,1024]{1,0:T(8,128)(2,1)S(1)}, bf16[256,1024]{1,0:T(8,128)(2,1)S(1)}, u32[]{:S(2)}, u32[]{:S(2)}) collective-permute-start(bf16[256,1024]{1,0:T(8,128)(2,1)S(1)} %copy-done), channel_id=1, source_target_pairs={{0,7},{1,0},{2,1},{3,2},{4,3},{5,4},{6,5},{7,6},{8,15},{9,8},{10,9... | collective-permute-start | bytes 1572872 | tf_op jit(solution)/shard_map/ppermute | solution.py:142
  35.3 1.9 %collective-permute-start.2 = (bf16[256,1024]{1,0:T(8,128)(2,1)S(1)}, bf16[256,1024]{1,0:T(8,128)(2,1)S(1)}, u32[]{:S(2)}, u32[]{:S(2)}) collective-permute-start(bf16[256,1024]{1,0:T(8,128)(2,1)S(1)} %copy-done), channel_id=1, source_target_pairs={{0,1},{1,2},{2,3},{3,4},{4,5},{5,6},{6,7},{7,0},{8,9},{9,10},{10,1... | collective-permute-start | bytes 1572872 | tf_op jit(solution)/shard_map/ppermute | solution.py:142
  37.3 7.9 %collective-permute-done.4.refs_4_ = bf16[256,1024]{1,0:T(8,128)(2,1)S(1)} collective-permute-done((bf16[256,1024]{1,0:T(8,128)(2,1)S(1)}, bf16[256,1024]{1,0:T(8,128)(2,1)S(1)}, u32[]{:S(2)}, u32[]{:S(2)}) %collective-permute-start.4) | collective-permute-done | bytes 524320 | tf_op jit(solution)/shard_map/ppermute | solution.py:142
  45.2 5.6 %collective-permute-start.5 = (bf16[256,1024]{1,0:T(8,128)(2,1)S(1)}, bf16[256,1024]{1,0:T(8,128)(2,1)S(1)}, u32[]{:S(2)}, u32[]{:S(2)}) collective-permute-start(bf16[256,1024]{1,0:T(8,128)(2,1)S(1)} %collective-permute-done.4.refs_4_), channel_id=1, source_target_pairs={{0,7},{1,0},{2,1},{3,2},{4,3},{5,4},{6,5},{7,6},{8,15},{9,8},{10,9... | collective-permute-start | bytes 1572872 | tf_op jit(solution)/shard_map/ppermute | solution.py:142
  51.6 1.9 %collective-permute-start.3 = (bf16[256,1024]{1,0:T(8,128)(2,1)S(1)}, bf16[256,1024]{1,0:T(8,128)(2,1)}, u32[]{:S(2)}, u32[]{:S(2)}) collective-permute-start(bf16[256,1024]{1,0:T(8,128)(2,1)S(1)} %collective-permute-done.2.refs_1_), channel_id=1, source_target_pairs={{0,1},{1,2},{2,3},{3,4},{4,5},{5,6},{6,7},{7,0},{8,9},{9,10},{10,1... | collective-permute-start | bytes 1572872 | tf_op jit(solution)/shard_map/ppermute | solution.py:142
  54.3 5.4 %collective-permute-done.5.refs_5_ = bf16[256,1024]{1,0:T(8,128)(2,1)S(1)} collective-permute-done((bf16[256,1024]{1,0:T(8,128)(2,1)S(1)}, bf16[256,1024]{1,0:T(8,128)(2,1)S(1)}, u32[]{:S(2)}, u32[]{:S(2)}) %collective-permute-start.5) | collective-permute-done | bytes 524320 | tf_op jit(solution)/shard_map/ppermute | solution.py:142
  60.5 5.4 %collective-permute-done.3.refs_2_ = bf16[256,1024]{1,0:T(8,128)(2,1)} collective-permute-done((bf16[256,1024]{1,0:T(8,128)(2,1)S(1)}, bf16[256,1024]{1,0:T(8,128)(2,1)}, u32[]{:S(2)}, u32[]{:S(2)}) %collective-permute-start.3) | collective-permute-done | bytes 524320 | tf_op jit(solution)/shard_map/ppermute | solution.py:142
  66.0 1.6 broadcast_in_dim.15
  67.6 3.6 %all-to-all-start.1 = ((bf16[4,256,1024]{2,1,0:T(8,128)(2,1)}), bf16[4,256,1024]{2,1,0:T(8,128)(2,1)S(1)}, u32[]{:S(2)}, u32[]{:S(2)}) async-start(bf16[4,256,1024]{2,1,0:T(8,128)(2,1)} %broadcast_in_dim.15), calls=%async_computation.1 | async-start | bytes 4194304 | tf_op jit(solution)/shard_map/all_to_all | solution.py:16
  71.2 1.9 %collective-permute-start.6 = (bf16[256,1024]{1,0:T(8,128)(2,1)}, bf16[256,1024]{1,0:T(8,128)(2,1)S(1)}, u32[]{:S(2)}, u32[]{:S(2)}) collective-permute-start(bf16[256,1024]{1,0:T(8,128)(2,1)} %collective-permute-done.3.refs_2_), channel_id=1, source_target_pairs={{0,1},{1,2},{2,3},{3,4},{4,5},{5,6},{6,7},{7,0},{8,9},{9,10},{10,1... | collective-permute-start | bytes 1572872 | tf_op jit(solution)/shard_map/ppermute | solution.py:142
  73.1 5.1 %collective-permute-start.7 = (bf16[256,1024]{1,0:T(8,128)(2,1)}, bf16[256,1024]{1,0:T(8,128)(2,1)S(1)}, u32[]{:S(2)}, u32[]{:S(2)}) collective-permute-start(bf16[256,1024]{1,0:T(8,128)(2,1)} %copy-done.6), channel_id=1, source_target_pairs={{0,7},{1,0},{2,1},{3,2},{4,3},{5,4},{6,5},{7,6},{8,15},{9,8},{10,9... | collective-permute-start | bytes 1572872 | tf_op jit(solution)/shard_map/ppermute | solution.py:142
  78.3 6.5 %collective-permute-done.6.refs_3_ = bf16[256,1024]{1,0:T(8,128)(2,1)S(1)} collective-permute-done((bf16[256,1024]{1,0:T(8,128)(2,1)}, bf16[256,1024]{1,0:T(8,128)(2,1)S(1)}, u32[]{:S(2)}, u32[]{:S(2)}) %collective-permute-start.6) | collective-permute-done | bytes 524320 | tf_op jit(solution)/shard_map/ppermute | solution.py:142
  84.7 1.3 collective-permute-done.7.refs_6_
  86.0 8.3 %all-to-all-done.1.refs_9_ = bf16[4,256,1024]{2,1,0:T(8,128)(2,1)S(1)} async-done(((bf16[4,256,1024]{2,1,0:T(8,128)(2,1)}), bf16[4,256,1024]{2,1,0:T(8,128)(2,1)S(1)}, u32[]{:S(2)}, u32[]{:S(2)}) %all-to-all-start.1) | async-done | bytes 2097184 | tf_op jit(solution)/shard_map/all_to_all | solution.py:16
  94.3 1.9 %collective-permute-start.10 = (bf16[4,256,1024]{2,1,0:T(8,128)(2,1)S(1)}, bf16[4,256,1024]{2,1,0:T(8,128)(2,1)S(1)}, u32[]{:S(2)}, u32[]{:S(2)}) collective-permute-start(bf16[4,256,1024]{2,1,0:T(8,128)(2,1)S(1)} %all-to-all-done.1.refs_9_), channel_id=1, source_target_pairs={{0,8},{8,0},{1,9},{9,1},{2,10},{10,2},{3,11},{11,3},{4,12},{12,4},... | collective-permute-start | bytes 6291464 | tf_op jit(solution)/shard_map/ppermute | solution.py:146
  96.3 2.1 %collective-permute-start.9 = (bf16[128,1024]{1,0:T(8,128)(2,1)S(1)}, bf16[128,1024]{1,0:T(8,128)(2,1)S(1)}, u32[]{:S(2)}, u32[]{:S(2)}) collective-permute-start(bf16[128,1024]{1,0:T(8,128)(2,1)S(1)} %slice.15), channel_id=1, source_target_pairs={{0,7},{1,0},{2,1},{3,2},{4,3},{5,4},{6,5},{7,6},{8,15},{9,8},{10,9... | collective-permute-start | bytes 786440 | tf_op jit(solution)/shard_map/ppermute | solution.py:142
  98.4 3.9 %collective-permute-start.8 = (bf16[128,1024]{1,0:T(8,128)(2,1)S(1)}, bf16[128,1024]{1,0:T(8,128)(2,1)S(1)}, u32[]{:S(2)}, u32[]{:S(2)}) collective-permute-start(bf16[128,1024]{1,0:T(8,128)(2,1)S(1)} %slice.14), channel_id=1, source_target_pairs={{0,1},{1,2},{2,3},{3,4},{4,5},{5,6},{6,7},{7,0},{8,9},{9,10},{10,1... | collective-permute-start | bytes 786440 | tf_op jit(solution)/shard_map/ppermute | solution.py:142
  102.3 4.7 %collective-permute-done.9.refs_8_ = bf16[128,1024]{1,0:T(8,128)(2,1)S(1)} collective-permute-done((bf16[128,1024]{1,0:T(8,128)(2,1)S(1)}, bf16[128,1024]{1,0:T(8,128)(2,1)S(1)}, u32[]{:S(2)}, u32[]{:S(2)}) %collective-permute-start.9) | collective-permute-done | bytes 262176 | tf_op jit(solution)/shard_map/ppermute | solution.py:142
  107.0 3.1 %collective-permute-done.8.refs_7_ = bf16[128,1024]{1,0:T(8,128)(2,1)S(1)} collective-permute-done((bf16[128,1024]{1,0:T(8,128)(2,1)S(1)}, bf16[128,1024]{1,0:T(8,128)(2,1)S(1)}, u32[]{:S(2)}, u32[]{:S(2)}) %collective-permute-start.8) | collective-permute-done | bytes 262176 | tf_op jit(solution)/shard_map/ppermute | solution.py:142
  114.4 2.5 %shard_map.37 = bf16[256,256]{1,0:T(8,128)(2,1)S(1)} custom-call(bf16[256,1024]{1,0:T(8,128)(2,1)S(1)} %copy-done.1, bf16[256,1024]{1,0:T(8,128)(2,1)S(1)} %copy-done.5, bf16[256,1024]{1,0:T(8,128)(2,1)} %collective-permute-done.3.refs_2_, bf16[256,1024]{1,0:T(8,128)(2,1)S(1)} %collective-permute-done.6.refs_3_, bf16[256,1024]{1,0:T(8,128)(2,1)S(1)} %copy-done.3, ...), custom_call_target="tpu_custom_call" | custom-call | flops 1073741824 | bytes 8388608 | tf_op jit(solution)/shard_map/pallas_call | solution.py:75
  116.8 13.4 %all_gather.3.own = bf16[1024,256]{1,0:T(8,128)(2,1)S(1)} all-gather(bf16[256,256]{1,0:T(8,128)(2,1)S(1)} %shard_map.37), channel_id=1, replica_groups=mesh['y'=8,'x'=4,'c'=2,'z'=8] {'x'}, dimensions={0}, use_global_device_ids=true | all-gather | bytes 655360 | tf_op jit(solution)/shard_map/all_gather | solution.py:166
  130.3 1.9 %collective-permute-start.11 = (bf16[1024,256]{1,0:T(8,128)(2,1)S(1)}, bf16[1024,256]{1,0:T(8,128)(2,1)S(1)}, u32[]{:S(2)}, u32[]{:S(2)}) collective-permute-start(bf16[1024,256]{1,0:T(8,128)(2,1)S(1)} %all_gather.3.own), channel_id=1, source_target_pairs={{0,8},{8,0},{1,9},{9,1},{2,10},{10,2},{3,11},{11,3},{4,12},{12,4},... | collective-permute-start | bytes 1572872 | tf_op jit(solution)/shard_map/ppermute | solution.py:146
  132.3 1.8 %collective-permute-done.11.other = bf16[1024,256]{1,0:T(8,128)(2,1)S(1)} collective-permute-done((bf16[1024,256]{1,0:T(8,128)(2,1)S(1)}, bf16[1024,256]{1,0:T(8,128)(2,1)S(1)}, u32[]{:S(2)}, u32[]{:S(2)}) %collective-permute-start.11) | collective-permute-done | bytes 524320 | tf_op jit(solution)/shard_map/ppermute | solution.py:146
  134.1 2.3 %shard_map.38 = f32[8,72,128]{2,1,0:T(8,128)S(1)} custom-call(bf16[512,128]{1,0:T(8,128)(2,1)S(1)} %reshape.9.q_ref, bf16[1024,256]{1,0:T(8,128)(2,1)S(1)} %all_gather.3.own, bf16[1024,256]{1,0:T(8,128)(2,1)S(1)} %collective-permute-done.11.other), custom_call_target="tpu_custom_call" | custom-call | flops 536870912 | bytes 2097152 | tf_op jit(solution)/shard_map/pallas_call | solution.py:112
  136.4 14.6 %all_to_all.15.part_ref = f32[8,72,128]{2,1,0:T(8,128)} all-to-all(f32[8,72,128]{2,1,0:T(8,128)S(1)} %shard_map.38), channel_id=1, replica_groups=mesh['y'=8,'x'=4,'c'=2,'z'=8] {'y'}, dimensions={0} | all-to-all | bytes 589824 | tf_op jit(solution)/shard_map/all_to_all | solution.py:168
  151.0 2.1 %shard_map.39 = bf16[64,128]{1,0:T(8,128)(2,1)} custom-call(f32[8,72,128]{2,1,0:T(8,128)} %all_to_all.15.part_ref), custom_call_target="tpu_custom_call" | custom-call | tf_op jit(solution)/shard_map/pallas_call | solution.py:135
  153.1 10.1 %collective-permute-start.12 = (bf16[64,128]{1,0:T(8,128)(2,1)}, bf16[64,128]{1,0:T(8,128)(2,1)S(1)}, u32[]{:S(2)}, u32[]{:S(2)}) collective-permute-start(bf16[64,128]{1,0:T(8,128)(2,1)} %shard_map.39), channel_id=1, source_target_pairs={{0,0},{1,64},{2,128},{3,192},{4,256},{5,320},{6,384},{7,448},{8,8}... | collective-permute-start | bytes 49160 | tf_op jit(solution)/shard_map/ppermute | solution.py:170
  163.3 4.4 %collective-permute-done.12 = bf16[64,128]{1,0:T(8,128)(2,1)S(1)} collective-permute-done((bf16[64,128]{1,0:T(8,128)(2,1)}, bf16[64,128]{1,0:T(8,128)(2,1)S(1)}, u32[]{:S(2)}, u32[]{:S(2)}) %collective-permute-start.12) | collective-permute-done | bytes 16416 | tf_op jit(solution)/shard_map/ppermute | solution.py:170
  (32 shorter events, 8.3 us)
Async XLA Ops:
  0.0 30.2 %copy-start = (bf16[256,1024]{1,0:T(8,128)(2,1)S(1)}, bf16[256,1024]{1,0:T(8,128)(2,1)}, u32[]{:S(2)}) copy-start(bf16[256,1024]{1,0:T(8,128)(2,1)} %refs_0_) | copy-start | bytes 1572868
  0.0 16.3 %collective-permute-start = (bf16[32,1024]{1,0:T(8,128)(2,1)}, bf16[32,1024]{1,0:T(8,128)(2,1)S(1)}, u32[]{:S(2)}, u32[]{:S(2)}) collective-permute-start(bf16[32,1024]{1,0:T(8,128)(2,1)} %param.4), channel_id=1, source_target_pairs={{0,0},{1,8},{2,16},{3,24},{4,32},{5,40},{6,48},{7,56},{8,64},{9,72... | collective-permute-start | bytes 196616 | tf_op jit(solution)/shard_map/ppermute | solution.py:150
  1.6 14.7 %collective-permute-start.1 = (bf16[64,128]{1,0:T(8,128)(2,1)}, bf16[64,128]{1,0:T(8,128)(2,1)S(1)}, u32[]{:S(2)}, u32[]{:S(2)}) collective-permute-start(bf16[64,128]{1,0:T(8,128)(2,1)} %param.5), channel_id=1, source_target_pairs={{0,0},{1,64},{2,128},{3,192},{4,256},{5,320},{6,384},{7,448},{8,8}... | collective-permute-start | bytes 49160 | tf_op jit(solution)/shard_map/ppermute | solution.py:151
  17.3 48.6 %all-to-all-start = ((bf16[8,40,1024]{2,1,0:T(8,128)(2,1)}), bf16[8,40,1024]{2,1,0:T(8,128)(2,1)S(1)}, u32[]{:S(2)}, u32[]{:S(2)}) async-start(bf16[8,40,1024]{2,1,0:T(8,128)(2,1)} %broadcast_in_dim.6), calls=%async_computation | async-start | bytes 1310720 | tf_op jit(solution)/shard_map/all_to_all | solution.py:16
  30.2 15.0 %collective-permute-start.4 = (bf16[256,1024]{1,0:T(8,128)(2,1)S(1)}, bf16[256,1024]{1,0:T(8,128)(2,1)S(1)}, u32[]{:S(2)}, u32[]{:S(2)}) collective-permute-start(bf16[256,1024]{1,0:T(8,128)(2,1)S(1)} %copy-done), channel_id=1, source_target_pairs={{0,7},{1,0},{2,1},{3,2},{4,3},{5,4},{6,5},{7,6},{8,15},{9,8},{10,9... | collective-permute-start | bytes 1572872 | tf_op jit(solution)/shard_map/ppermute | solution.py:142
  35.3 16.2 %collective-permute-start.2 = (bf16[256,1024]{1,0:T(8,128)(2,1)S(1)}, bf16[256,1024]{1,0:T(8,128)(2,1)S(1)}, u32[]{:S(2)}, u32[]{:S(2)}) collective-permute-start(bf16[256,1024]{1,0:T(8,128)(2,1)S(1)} %copy-done), channel_id=1, source_target_pairs={{0,1},{1,2},{2,3},{3,4},{4,5},{5,6},{6,7},{7,0},{8,9},{9,10},{10,1... | collective-permute-start | bytes 1572872 | tf_op jit(solution)/shard_map/ppermute | solution.py:142
  45.2 14.5 %collective-permute-start.5 = (bf16[256,1024]{1,0:T(8,128)(2,1)S(1)}, bf16[256,1024]{1,0:T(8,128)(2,1)S(1)}, u32[]{:S(2)}, u32[]{:S(2)}) collective-permute-start(bf16[256,1024]{1,0:T(8,128)(2,1)S(1)} %collective-permute-done.4.refs_4_), channel_id=1, source_target_pairs={{0,7},{1,0},{2,1},{3,2},{4,3},{5,4},{6,5},{7,6},{8,15},{9,8},{10,9... | collective-permute-start | bytes 1572872 | tf_op jit(solution)/shard_map/ppermute | solution.py:142
  50.8 0.8 copy-start.2
  51.6 14.3 %collective-permute-start.3 = (bf16[256,1024]{1,0:T(8,128)(2,1)S(1)}, bf16[256,1024]{1,0:T(8,128)(2,1)}, u32[]{:S(2)}, u32[]{:S(2)}) collective-permute-start(bf16[256,1024]{1,0:T(8,128)(2,1)S(1)} %collective-permute-done.2.refs_1_), channel_id=1, source_target_pairs={{0,1},{1,2},{2,3},{3,4},{4,5},{5,6},{6,7},{7,0},{8,9},{9,10},{10,1... | collective-permute-start | bytes 1572872 | tf_op jit(solution)/shard_map/ppermute | solution.py:142
  53.5 0.8 copy-start.4
  59.7 0.8 copy-start.6
  65.9 1.7 copy-start.8
  67.6 26.8 %all-to-all-start.1 = ((bf16[4,256,1024]{2,1,0:T(8,128)(2,1)}), bf16[4,256,1024]{2,1,0:T(8,128)(2,1)S(1)}, u32[]{:S(2)}, u32[]{:S(2)}) async-start(bf16[4,256,1024]{2,1,0:T(8,128)(2,1)} %broadcast_in_dim.15), calls=%async_computation.1 | async-start | bytes 4194304 | tf_op jit(solution)/shard_map/all_to_all | solution.py:16
  71.2 13.5 %collective-permute-start.6 = (bf16[256,1024]{1,0:T(8,128)(2,1)}, bf16[256,1024]{1,0:T(8,128)(2,1)S(1)}, u32[]{:S(2)}, u32[]{:S(2)}) collective-permute-start(bf16[256,1024]{1,0:T(8,128)(2,1)} %collective-permute-done.3.refs_2_), channel_id=1, source_target_pairs={{0,1},{1,2},{2,3},{3,4},{4,5},{5,6},{6,7},{7,0},{8,9},{9,10},{10,1... | collective-permute-start | bytes 1572872 | tf_op jit(solution)/shard_map/ppermute | solution.py:142
  73.1 12.9 %collective-permute-start.7 = (bf16[256,1024]{1,0:T(8,128)(2,1)}, bf16[256,1024]{1,0:T(8,128)(2,1)S(1)}, u32[]{:S(2)}, u32[]{:S(2)}) collective-permute-start(bf16[256,1024]{1,0:T(8,128)(2,1)} %copy-done.6), channel_id=1, source_target_pairs={{0,7},{1,0},{2,1},{3,2},{4,3},{5,4},{6,5},{7,6},{8,15},{9,8},{10,9... | collective-permute-start | bytes 1572872 | tf_op jit(solution)/shard_map/ppermute | solution.py:142
  94.3 15.9 %collective-permute-start.10 = (bf16[4,256,1024]{2,1,0:T(8,128)(2,1)S(1)}, bf16[4,256,1024]{2,1,0:T(8,128)(2,1)S(1)}, u32[]{:S(2)}, u32[]{:S(2)}) collective-permute-start(bf16[4,256,1024]{2,1,0:T(8,128)(2,1)S(1)} %all-to-all-done.1.refs_9_), channel_id=1, source_target_pairs={{0,8},{8,0},{1,9},{9,1},{2,10},{10,2},{3,11},{11,3},{4,12},{12,4},... | collective-permute-start | bytes 6291464 | tf_op jit(solution)/shard_map/ppermute | solution.py:146
  96.3 35.9 %slice-start = ((bf16[8,40,1024]{2,1,0:T(8,128)(2,1)}), bf16[8,8,1024]{2,1,0:T(8,128)(2,1)S(1)}, s32[]{:S(2)}) async-start(bf16[8,40,1024]{2,1,0:T(8,128)(2,1)} %copy-done.8), calls=%async_computation.3 | async-start | bytes 262144 | tf_op jit(solution)/shard_map/slice | solution.py:158
  96.3 10.7 %collective-permute-start.9 = (bf16[128,1024]{1,0:T(8,128)(2,1)S(1)}, bf16[128,1024]{1,0:T(8,128)(2,1)S(1)}, u32[]{:S(2)}, u32[]{:S(2)}) collective-permute-start(bf16[128,1024]{1,0:T(8,128)(2,1)S(1)} %slice.15), channel_id=1, source_target_pairs={{0,7},{1,0},{2,1},{3,2},{4,3},{5,4},{6,5},{7,6},{8,15},{9,8},{10,9... | collective-permute-start | bytes 786440 | tf_op jit(solution)/shard_map/ppermute | solution.py:142
  98.4 11.8 %collective-permute-start.8 = (bf16[128,1024]{1,0:T(8,128)(2,1)S(1)}, bf16[128,1024]{1,0:T(8,128)(2,1)S(1)}, u32[]{:S(2)}, u32[]{:S(2)}) collective-permute-start(bf16[128,1024]{1,0:T(8,128)(2,1)S(1)} %slice.14), channel_id=1, source_target_pairs={{0,1},{1,2},{2,3},{3,4},{4,5},{5,6},{6,7},{7,0},{8,9},{9,10},{10,1... | collective-permute-start | bytes 786440 | tf_op jit(solution)/shard_map/ppermute | solution.py:142
  110.2 1.0 copy-start.1
  111.2 1.0 copy-start.3
  112.3 1.0 copy-start.5
  113.3 1.0 copy-start.7
  130.3 3.8 %collective-permute-start.11 = (bf16[1024,256]{1,0:T(8,128)(2,1)S(1)}, bf16[1024,256]{1,0:T(8,128)(2,1)S(1)}, u32[]{:S(2)}, u32[]{:S(2)}) collective-permute-start(bf16[1024,256]{1,0:T(8,128)(2,1)S(1)} %all_gather.3.own), channel_id=1, source_target_pairs={{0,8},{8,0},{1,9},{9,1},{2,10},{10,2},{3,11},{11,3},{4,12},{12,4},... | collective-permute-start | bytes 1572872 | tf_op jit(solution)/shard_map/ppermute | solution.py:146
  153.1 14.5 %collective-permute-start.12 = (bf16[64,128]{1,0:T(8,128)(2,1)}, bf16[64,128]{1,0:T(8,128)(2,1)S(1)}, u32[]{:S(2)}, u32[]{:S(2)}) collective-permute-start(bf16[64,128]{1,0:T(8,128)(2,1)} %shard_map.39), channel_id=1, source_target_pairs={{0,0},{1,64},{2,128},{3,192},{4,256},{5,320},{6,384},{7,448},{8,8}... | collective-permute-start | bytes 49160 | tf_op jit(solution)/shard_map/ppermute | solution.py:170

commit v4 on v3

--- a/solution.py
+++ b/solution.py
@@ -32,7 +32,7 @@
     return moves
 
 
-def query_moves():
+def exchange_moves():
     return [
         (place(y, x, c, z), place(z, x, c, y)) for y in range(8) for x in range(4) for c in range(2) for z in range(8)
     ]
@@ -47,20 +47,24 @@
 
 
 def project_kernel(*refs):
-    mem, (mem_a, mem_b, w_a, w_b, out_ref) = refs[:7], refs[7:]
+    mem, (mem_a, mem_b, w_a, w_b, out_ref, held, sems) = refs[:7], refs[7:]
     core, z = lax.axis_index("c"), lax.axis_index("z")
+    copies = [pltpu.make_async_copy(ref, held.at[j], sems.at[j]) for j, ref in enumerate(mem)]
+    copies.append(pltpu.make_async_copy(mem_a, held.at[7, pl.ds(0, 128)], sems.at[7]))
+    copies.append(pltpu.make_async_copy(mem_b, held.at[7, pl.ds(128, 128)], sems.at[8]))
+    for copy in copies:
+        copy.start()
 
     def run(even, odd):
-        def rows(away):
-            return (even, odd)[away % 2][lax.rem(z + away, 8) // 2]
-
         total = None
-        for ref, away in zip(mem, (0, 7, 6, 5, 1, 2, 3)):
-            part = lax.dot_general(ref[...], rows(away), NT, preferred_element_type=jnp.float32)
+        for j, away in enumerate((0, 7, 6, 5, 1, 2, 3, 4)):
+            copies[j].wait()
+            if j == 7:
+                copies[8].wait()
+            rows = (even, odd)[away % 2][lax.rem(z + away, 8) // 2]
+            part = lax.dot_general(held[j], rows, NT, preferred_element_type=jnp.float32)
             total = part if total is None else total + part
-        for start, ref in ((0, mem_a), (128, mem_b)):
-            part = lax.dot_general(ref[...], rows(4), NT, preferred_element_type=jnp.float32)
-            out_ref[start : start + 128] = (total[start : start + 128] + part).astype(out_ref.dtype)
+        out_ref[...] = total.astype(out_ref.dtype)
 
     @pl.when(lax.rem(z, 2) == core)
     def _():
@@ -72,10 +76,14 @@
 
 
 def project(mem, w_a, w_b):
+    vmem = pl.BlockSpec(memory_space=pltpu.VMEM)
     return pl.pallas_call(
         project_kernel,
         out_shape=jax.ShapeDtypeStruct((256, 2 * HD), jnp.bfloat16),
-        compiler_params=pltpu.CompilerParams(vmem_limit_bytes=32 << 20),
+        in_specs=[pl.BlockSpec(memory_space=pl.ANY)] * 9 + [vmem] * 2,
+        out_specs=vmem,
+        scratch_shapes=[pltpu.VMEM((8, 256, 8 * HD), jnp.bfloat16), pltpu.SemaphoreType.DMA((9,))],
+        compiler_params=pltpu.CompilerParams(vmem_limit_bytes=50 << 20),
         cost_estimate=pl.CostEstimate(flops=2 * 256 * 256 * 8192, bytes_accessed=8 << 20, transcendentals=0),
     )(*mem, w_a, w_b)
 
@@ -112,7 +120,7 @@
     return pl.pallas_call(
         attend_kernel,
         out_shape=jax.ShapeDtypeStruct((8, 72, HD), jnp.float32),
-        compiler_params=pltpu.CompilerParams(vmem_limit_bytes=24 << 20),
+        compiler_params=pltpu.CompilerParams(vmem_limit_bytes=16 << 20),
         cost_estimate=pl.CostEstimate(
             flops=4 * 512 * 2048 * HD, bytes_accessed=2 << 20, transcendentals=512 * 2048
         ),
@@ -148,26 +156,23 @@
 
 def body(memory, kv_weight, queries):
     rows = lax.ppermute(kv_weight, ALL, weight_moves())
-    query = lax.ppermute(queries, ALL, query_moves())
-    memory, rows, query = lax.optimization_barrier((memory, rows, query))
-    both = spread(jnp.concatenate([rows, query.reshape(8, 8 * HD)], axis=0), "y")
     ring = [step_z(memory, memory)]
+    rows = spread(rows, "y").reshape(2 * HD, 8 * HD)
     ring.append(step_z(*ring[0]))
-    both, ring[1] = lax.optimization_barrier((both, ring[1]))
-    rows = both[:, :32].reshape(2 * HD, 8 * HD)
-    query = both[:, 32:].reshape(512, HD)
+    rows, ring[1] = lax.optimization_barrier((rows, ring[1]))
     w_a = spread(rows, "x")
     ring.append(step_z(*ring[1]))
-    w_a, ring[2] = lax.optimization_barrier((w_a, ring[2]))
+    w_a, ring[2], queries = lax.optimization_barrier((w_a, ring[2], queries))
     ups, downs = zip(*ring)
     opposite = step_z(ups[2][:128], downs[2][128:])
+    query = spread(queries, "z").reshape(512, HD)
+    opposite, query = lax.optimization_barrier((opposite, query))
     own = project((memory, *ups, *downs, *opposite), w_a, swap(w_a))
 
+    own = lax.ppermute(own, ALL, exchange_moves())
     own = lax.all_gather(own, "x", axis=0, tiled=True)
     parts = attend(query, own, swap(own))
-    parts = lax.all_to_all(parts, "y", 0, 0, tiled=True)
-    result = merge(parts)
-    return lax.ppermute(result, ALL, query_moves())
+    return merge(lax.all_to_all(parts, "z", 0, 0, tiled=True))
 
 
 def solution(mesh):

time: 169 us -> 173 us (1.024)
  the two profiles are of different devices: /device:TPU:32 before, /device:TPU:1 now
where the time goes in v4:
time: 173 us; the launch traced here: 171 us
  starting transfers between devices  70.1 us (41%)
  blocking collectives  56.4 us (33%)
  waiting for transfers between devices  30.1 us (17%)
  Pallas kernels  9.98 us (6%)
  local copies, waits for them, and re-layouts  4.78 us (3%)
    all_to_all x1, blocking collectives, body(): return merge(lax.all_to_all(parts, 'z', 0, 0, tiled=True))  31.6 us
    ppermute x4, starting transfers between devices, step_z(): lax.ppermute(downs, 'z', shift(8, -1))  25.5 us
    all_to_all x2, starting transfers between devices, spread(): return lax.all_to_all(copies, axis, 0, 0, tiled=True)  16.6 us
    all_to_all x2, waiting for transfers between devices, spread(): return lax.all_to_all(copies, axis, 0, 0, tiled=True)  16.5 us
    all_to_all x1, blocking collectives, spread(): return lax.all_to_all(copies, axis, 0, 0, tiled=True)  13.4 us
    ppermute x2, starting transfers between devices, swap(): return lax.ppermute(value, 'c', SWAP)  12.3 us
    all_gather x1, blocking collectives, body(): own = lax.all_gather(own, 'x', axis=0, tiled=True)  11.4 us
    ppermute x4, starting transfers between devices, step_z(): lax.ppermute(ups, 'z', shift(8, 1))  11 us
  transfers between devices with their start and end apart: 14, of which 6 were waited for; matrix products, arithmetic and copies ran while one was open for 1% of the time, Pallas kernels for 0%

profile of v4, /device:TPU:1, one launch (start us, length us, event | category | flops | bytes accessed | tf_op | source)
XLA Modules:
  0.0 171.4 jit_solution(12123148687461299759)
XLA Ops:
  0.0 4.8 %collective-permute-start.1 = (bf16[256,1024]{1,0:T(8,128)(2,1)}, bf16[256,1024]{1,0:T(8,128)(2,1)S(1)}, u32[]{:S(2)}, u32[]{:S(2)}) collective-permute-start(bf16[256,1024]{1,0:T(8,128)(2,1)} %refs_0_.1), channel_id=1, source_target_pairs={{0,1},{1,2},{2,3},{3,4},{4,5},{5,6},{6,7},{7,0},{8,9},{9,10},{10,1... | collective-permute-start | bytes 1572872 | tf_op jit(solution)/shard_map/ppermute | solution.py:150
  4.8 8.6 %collective-permute-start.3 = (bf16[256,1024]{1,0:T(8,128)(2,1)}, bf16[256,1024]{1,0:T(8,128)(2,1)S(1)}, u32[]{:S(2)}, u32[]{:S(2)}) collective-permute-start(bf16[256,1024]{1,0:T(8,128)(2,1)} %refs_0_.1), channel_id=1, source_target_pairs={{0,7},{1,0},{2,1},{3,2},{4,3},{5,4},{6,5},{7,6},{8,15},{9,8},{10,9... | collective-permute-start | bytes 1572872 | tf_op jit(solution)/shard_map/ppermute | solution.py:150
  13.4 4.0 %collective-permute-start = (bf16[32,1024]{1,0:T(8,128)(2,1)}, bf16[32,1024]{1,0:T(8,128)(2,1)S(1)}, u32[]{:S(2)}, u32[]{:S(2)}) collective-permute-start(bf16[32,1024]{1,0:T(8,128)(2,1)} %param.4), channel_id=1, source_target_pairs={{0,0},{1,8},{2,16},{3,24},{4,32},{5,40},{6,48},{7,56},{8,64},{9,72... | collective-permute-start | bytes 196616 | tf_op jit(solution)/shard_map/ppermute | solution.py:158
  17.5 4.7 %collective-permute-done = bf16[32,1024]{1,0:T(8,128)(2,1)S(1)} collective-permute-done((bf16[32,1024]{1,0:T(8,128)(2,1)}, bf16[32,1024]{1,0:T(8,128)(2,1)S(1)}, u32[]{:S(2)}, u32[]{:S(2)}) %collective-permute-start) | collective-permute-done | bytes 65568 | tf_op jit(solution)/shard_map/ppermute | solution.py:158
  22.2 0.9 broadcast_in_dim.6
  23.1 6.8 %all-to-all-start = ((bf16[8,32,1024]{2,1,0:T(8,128)(2,1)}), bf16[8,32,1024]{2,1,0:T(8,128)(2,1)S(1)}, u32[]{:S(2)}, u32[]{:S(2)}) async-start(bf16[8,32,1024]{2,1,0:T(8,128)(2,1)} %broadcast_in_dim.6), calls=%async_computation | async-start | bytes 1048576 | tf_op jit(solution)/shard_map/all_to_all | solution.py:16
  29.9 0.0 collective-permute-done.1.refs_1_
  29.9 1.9 %collective-permute-start.2 = (bf16[256,1024]{1,0:T(8,128)(2,1)S(1)}, bf16[256,1024]{1,0:T(8,128)(2,1)S(1)}, u32[]{:S(2)}, u32[]{:S(2)}) collective-permute-start(bf16[256,1024]{1,0:T(8,128)(2,1)S(1)} %collective-permute-done.1.refs_1_), channel_id=1, source_target_pairs={{0,1},{1,2},{2,3},{3,4},{4,5},{5,6},{6,7},{7,0},{8,9},{9,10},{10,1... | collective-permute-start | bytes 1572872 | tf_op jit(solution)/shard_map/ppermute | solution.py:150
  31.9 8.9 %collective-permute-start.4 = (bf16[256,1024]{1,0:T(8,128)(2,1)S(1)}, bf16[256,1024]{1,0:T(8,128)(2,1)S(1)}, u32[]{:S(2)}, u32[]{:S(2)}) collective-permute-start(bf16[256,1024]{1,0:T(8,128)(2,1)S(1)} %collective-permute-done.3.refs_4_), channel_id=1, source_target_pairs={{0,7},{1,0},{2,1},{3,2},{4,3},{5,4},{6,5},{7,6},{8,15},{9,8},{10,9... | collective-permute-start | bytes 1572872 | tf_op jit(solution)/shard_map/ppermute | solution.py:150
  40.7 7.2 %all-to-all-done = bf16[8,32,1024]{2,1,0:T(8,128)(2,1)S(1)} async-done(((bf16[8,32,1024]{2,1,0:T(8,128)(2,1)}), bf16[8,32,1024]{2,1,0:T(8,128)(2,1)S(1)}, u32[]{:S(2)}, u32[]{:S(2)}) %all-to-all-start) | async-done | bytes 524320 | tf_op jit(solution)/shard_map/all_to_all | solution.py:16
  48.0 0.0 collective-permute-done.2.refs_2_
  48.0 1.6 broadcast_in_dim.7
  49.6 9.8 %all-to-all-start.1 = ((bf16[4,256,1024]{2,1,0:T(8,128)(2,1)}), bf16[4,256,1024]{2,1,0:T(8,128)(2,1)}, u32[]{:S(2)}, u32[]{:S(2)}) async-start(bf16[4,256,1024]{2,1,0:T(8,128)(2,1)} %broadcast_in_dim.7), calls=%async_computation.1 | async-start | bytes 4194304 | tf_op jit(solution)/shard_map/all_to_all | solution.py:16
  59.4 2.3 %collective-permute-start.5 = (bf16[256,1024]{1,0:T(8,128)(2,1)S(1)}, bf16[256,1024]{1,0:T(8,128)(2,1)S(1)}, u32[]{:S(2)}, u32[]{:S(2)}) collective-permute-start(bf16[256,1024]{1,0:T(8,128)(2,1)S(1)} %collective-permute-done.2.refs_2_), channel_id=1, source_target_pairs={{0,1},{1,2},{2,3},{3,4},{4,5},{5,6},{6,7},{7,0},{8,9},{9,10},{10,1... | collective-permute-start | bytes 1572872 | tf_op jit(solution)/shard_map/ppermute | solution.py:150
  61.7 4.2 %collective-permute-start.6 = (bf16[256,1024]{1,0:T(8,128)(2,1)S(1)}, bf16[256,1024]{1,0:T(8,128)(2,1)}, u32[]{:S(2)}, u32[]{:S(2)}) collective-permute-start(bf16[256,1024]{1,0:T(8,128)(2,1)S(1)} %collective-permute-done.4.refs_5_), channel_id=1, source_target_pairs={{0,7},{1,0},{2,1},{3,2},{4,3},{5,4},{6,5},{7,6},{8,15},{9,8},{10,9... | collective-permute-start | bytes 1572872 | tf_op jit(solution)/shard_map/ppermute | solution.py:150
  65.9 6.3 %collective-permute-done.5.refs_3_ = bf16[256,1024]{1,0:T(8,128)(2,1)S(1)} collective-permute-done((bf16[256,1024]{1,0:T(8,128)(2,1)S(1)}, bf16[256,1024]{1,0:T(8,128)(2,1)S(1)}, u32[]{:S(2)}, u32[]{:S(2)}) %collective-permute-start.5) | collective-permute-done | bytes 524320 | tf_op jit(solution)/shard_map/ppermute | solution.py:150
  72.2 1.0 collective-permute-done.6.refs_6_
  73.2 9.3 %all-to-all-done.1.refs_9_ = bf16[4,256,1024]{2,1,0:T(8,128)(2,1)} async-done(((bf16[4,256,1024]{2,1,0:T(8,128)(2,1)}), bf16[4,256,1024]{2,1,0:T(8,128)(2,1)}, u32[]{:S(2)}, u32[]{:S(2)}) %all-to-all-start.1) | async-done | bytes 2097184 | tf_op jit(solution)/shard_map/all_to_all | solution.py:16
  82.4 6.4 %collective-permute-start.9 = (bf16[4,256,1024]{2,1,0:T(8,128)(2,1)}, bf16[4,256,1024]{2,1,0:T(8,128)(2,1)S(1)}, u32[]{:S(2)}, u32[]{:S(2)}) collective-permute-start(bf16[4,256,1024]{2,1,0:T(8,128)(2,1)} %all-to-all-done.1.refs_9_), channel_id=1, source_target_pairs={{0,8},{8,0},{1,9},{9,1},{2,10},{10,2},{3,11},{11,3},{4,12},{12,4},... | collective-permute-start | bytes 6291464 | tf_op jit(solution)/shard_map/ppermute | solution.py:154
  88.9 1.0 slice.7
  89.9 3.9 %collective-permute-start.8 = (bf16[128,1024]{1,0:T(8,128)(2,1)S(1)}, bf16[128,1024]{1,0:T(8,128)(2,1)S(1)}, u32[]{:S(2)}, u32[]{:S(2)}) collective-permute-start(bf16[128,1024]{1,0:T(8,128)(2,1)S(1)} %slice.7), channel_id=1, source_target_pairs={{0,7},{1,0},{2,1},{3,2},{4,3},{5,4},{6,5},{7,6},{8,15},{9,8},{10,9... | collective-permute-start | bytes 786440 | tf_op jit(solution)/shard_map/ppermute | solution.py:150
  93.8 1.9 %collective-permute-start.7 = (bf16[128,1024]{1,0:T(8,128)(2,1)S(1)}, bf16[128,1024]{1,0:T(8,128)(2,1)S(1)}, u32[]{:S(2)}, u32[]{:S(2)}) collective-permute-start(bf16[128,1024]{1,0:T(8,128)(2,1)S(1)} %slice.6), channel_id=1, source_target_pairs={{0,1},{1,2},{2,3},{3,4},{4,5},{5,6},{6,7},{7,0},{8,9},{9,10},{10,1... | collective-permute-start | bytes 786440 | tf_op jit(solution)/shard_map/ppermute | solution.py:150
  95.7 13.4 %all_to_all.20 = bf16[8,64,128]{2,1,0:T(8,128)(2,1)S(1)} all-to-all(bf16[8,64,128]{2,1,0:T(8,128)(2,1)S(1)} %broadcast_in_dim.8), channel_id=1, replica_groups=mesh['y'=8,'x'=4,'c'=2,'z'=8] {'z'}, dimensions={0} | all-to-all | bytes 262144 | tf_op jit(solution)/shard_map/all_to_all | solution.py:16
  109.2 1.3 copy-done.1
  110.5 5.5 %shard_map.37 = bf16[256,256]{1,0:T(8,128)(2,1)S(1)} custom-call(bf16[256,1024]{1,0:T(8,128)(2,1)S(1)} %copy-done, bf16[256,1024]{1,0:T(8,128)(2,1)S(1)} %collective-permute-done.1.refs_1_, bf16[256,1024]{1,0:T(8,128)(2,1)S(1)} %collective-permute-done.2.refs_2_, bf16[256,1024]{1,0:T(8,128)(2,1)S(1)} %collective-permute-done.5.refs_3_, ...), custom_call_target="tpu_custom_call" | custom-call | flops 1073741824 | bytes 8388608 | tf_op jit(solution)/shard_map/pallas_call | solution.py:80
  116.0 0.7 collective-permute-start.10
  116.7 11.4 %all_gather.3.own = bf16[1024,256]{1,0:T(8,128)(2,1)S(1)} all-gather(bf16[256,256]{1,0:T(8,128)(2,1)S(1)} %collective-permute-done.10), channel_id=1, replica_groups=mesh['y'=8,'x'=4,'c'=2,'z'=8] {'x'}, dimensions={0}, use_global_device_ids=true | all-gather | bytes 655360 | tf_op jit(solution)/shard_map/all_gather | solution.py:173
  128.1 5.8 %collective-permute-start.11 = (bf16[1024,256]{1,0:T(8,128)(2,1)S(1)}, bf16[1024,256]{1,0:T(8,128)(2,1)S(1)}, u32[]{:S(2)}, u32[]{:S(2)}) collective-permute-start(bf16[1024,256]{1,0:T(8,128)(2,1)S(1)} %all_gather.3.own), channel_id=1, source_target_pairs={{0,8},{8,0},{1,9},{9,1},{2,10},{10,2},{3,11},{11,3},{4,12},{12,4},... | collective-permute-start | bytes 1572872 | tf_op jit(solution)/shard_map/ppermute | solution.py:154
  133.9 1.5 collective-permute-done.11.other
  135.4 2.3 %shard_map.38 = f32[8,72,128]{2,1,0:T(8,128)S(1)} custom-call(bf16[512,128]{1,0:T(8,128)(2,1)S(1)} %bitcast.2, bf16[1024,256]{1,0:T(8,128)(2,1)S(1)} %all_gather.3.own, bf16[1024,256]{1,0:T(8,128)(2,1)S(1)} %collective-permute-done.11.other), custom_call_target="tpu_custom_call" | custom-call | flops 536870912 | bytes 2097152 | tf_op jit(solution)/shard_map/pallas_call | solution.py:120
  137.7 31.6 %all_to_all.21.part_ref = f32[8,72,128]{2,1,0:T(8,128)} all-to-all(f32[8,72,128]{2,1,0:T(8,128)S(1)} %shard_map.38), channel_id=1, replica_groups=mesh['y'=8,'x'=4,'c'=2,'z'=8] {'z'}, dimensions={0} | all-to-all | bytes 589824 | tf_op jit(solution)/shard_map/all_to_all | solution.py:175
  169.3 2.1 %shard_map.39 = bf16[64,128]{1,0:T(8,128)(2,1)} custom-call(f32[8,72,128]{2,1,0:T(8,128)} %all_to_all.21.part_ref), custom_call_target="tpu_custom_call" | custom-call | tf_op jit(solution)/shard_map/pallas_call | solution.py:143
  (13 shorter events, 0.1 us)
Async XLA Ops:
  0.0 29.9 %collective-permute-start.1 = (bf16[256,1024]{1,0:T(8,128)(2,1)}, bf16[256,1024]{1,0:T(8,128)(2,1)S(1)}, u32[]{:S(2)}, u32[]{:S(2)}) collective-permute-start(bf16[256,1024]{1,0:T(8,128)(2,1)} %refs_0_.1), channel_id=1, source_target_pairs={{0,1},{1,2},{2,3},{3,4},{4,5},{5,6},{6,7},{7,0},{8,9},{9,10},{10,1... | collective-permute-start | bytes 1572872 | tf_op jit(solution)/shard_map/ppermute | solution.py:150
  4.8 27.0 %collective-permute-start.3 = (bf16[256,1024]{1,0:T(8,128)(2,1)}, bf16[256,1024]{1,0:T(8,128)(2,1)S(1)}, u32[]{:S(2)}, u32[]{:S(2)}) collective-permute-start(bf16[256,1024]{1,0:T(8,128)(2,1)} %refs_0_.1), channel_id=1, source_target_pairs={{0,7},{1,0},{2,1},{3,2},{4,3},{5,4},{6,5},{7,6},{8,15},{9,8},{10,9... | collective-permute-start | bytes 1572872 | tf_op jit(solution)/shard_map/ppermute | solution.py:150
  13.4 8.8 %collective-permute-start = (bf16[32,1024]{1,0:T(8,128)(2,1)}, bf16[32,1024]{1,0:T(8,128)(2,1)S(1)}, u32[]{:S(2)}, u32[]{:S(2)}) collective-permute-start(bf16[32,1024]{1,0:T(8,128)(2,1)} %param.4), channel_id=1, source_target_pairs={{0,0},{1,8},{2,16},{3,24},{4,32},{5,40},{6,48},{7,56},{8,64},{9,72... | collective-permute-start | bytes 196616 | tf_op jit(solution)/shard_map/ppermute | solution.py:158
  23.1 24.9 %all-to-all-start = ((bf16[8,32,1024]{2,1,0:T(8,128)(2,1)}), bf16[8,32,1024]{2,1,0:T(8,128)(2,1)S(1)}, u32[]{:S(2)}, u32[]{:S(2)}) async-start(bf16[8,32,1024]{2,1,0:T(8,128)(2,1)} %broadcast_in_dim.6), calls=%async_computation | async-start | bytes 1048576 | tf_op jit(solution)/shard_map/all_to_all | solution.py:16
  29.9 18.1 %collective-permute-start.2 = (bf16[256,1024]{1,0:T(8,128)(2,1)S(1)}, bf16[256,1024]{1,0:T(8,128)(2,1)S(1)}, u32[]{:S(2)}, u32[]{:S(2)}) collective-permute-start(bf16[256,1024]{1,0:T(8,128)(2,1)S(1)} %collective-permute-done.1.refs_1_), channel_id=1, source_target_pairs={{0,1},{1,2},{2,3},{3,4},{4,5},{5,6},{6,7},{7,0},{8,9},{9,10},{10,1... | collective-permute-start | bytes 1572872 | tf_op jit(solution)/shard_map/ppermute | solution.py:150
  31.9 16.1 %collective-permute-start.4 = (bf16[256,1024]{1,0:T(8,128)(2,1)S(1)}, bf16[256,1024]{1,0:T(8,128)(2,1)S(1)}, u32[]{:S(2)}, u32[]{:S(2)}) collective-permute-start(bf16[256,1024]{1,0:T(8,128)(2,1)S(1)} %collective-permute-done.3.refs_4_), channel_id=1, source_target_pairs={{0,7},{1,0},{2,1},{3,2},{4,3},{5,4},{6,5},{7,6},{8,15},{9,8},{10,9... | collective-permute-start | bytes 1572872 | tf_op jit(solution)/shard_map/ppermute | solution.py:150
  49.6 46.1 %copy-start.2 = (bf16[64,128]{1,0:T(8,128)(2,1)S(1)}, bf16[64,128]{1,0:T(8,128)(2,1)}, u32[]{:S(2)}) copy-start(bf16[64,128]{1,0:T(8,128)(2,1)} %param.5) | copy-start | bytes 49156
  49.6 60.9 %copy-start = (bf16[256,1024]{1,0:T(8,128)(2,1)S(1)}, bf16[256,1024]{1,0:T(8,128)(2,1)}, u32[]{:S(2)}) copy-start(bf16[256,1024]{1,0:T(8,128)(2,1)} %refs_0_.1) | copy-start | bytes 1572868
  49.6 32.9 %all-to-all-start.1 = ((bf16[4,256,1024]{2,1,0:T(8,128)(2,1)}), bf16[4,256,1024]{2,1,0:T(8,128)(2,1)}, u32[]{:S(2)}, u32[]{:S(2)}) async-start(bf16[4,256,1024]{2,1,0:T(8,128)(2,1)} %broadcast_in_dim.7), calls=%async_computation.1 | async-start | bytes 4194304 | tf_op jit(solution)/shard_map/all_to_all | solution.py:16
  59.4 12.8 %collective-permute-start.5 = (bf16[256,1024]{1,0:T(8,128)(2,1)S(1)}, bf16[256,1024]{1,0:T(8,128)(2,1)S(1)}, u32[]{:S(2)}, u32[]{:S(2)}) collective-permute-start(bf16[256,1024]{1,0:T(8,128)(2,1)S(1)} %collective-permute-done.2.refs_2_), channel_id=1, source_target_pairs={{0,1},{1,2},{2,3},{3,4},{4,5},{5,6},{6,7},{7,0},{8,9},{9,10},{10,1... | collective-permute-start | bytes 1572872 | tf_op jit(solution)/shard_map/ppermute | solution.py:150
  61.7 11.4 %collective-permute-start.6 = (bf16[256,1024]{1,0:T(8,128)(2,1)S(1)}, bf16[256,1024]{1,0:T(8,128)(2,1)}, u32[]{:S(2)}, u32[]{:S(2)}) collective-permute-start(bf16[256,1024]{1,0:T(8,128)(2,1)S(1)} %collective-permute-done.4.refs_5_), channel_id=1, source_target_pairs={{0,7},{1,0},{2,1},{3,2},{4,3},{5,4},{6,5},{7,6},{8,15},{9,8},{10,9... | collective-permute-start | bytes 1572872 | tf_op jit(solution)/shard_map/ppermute | solution.py:150
  82.4 26.7 %collective-permute-start.9 = (bf16[4,256,1024]{2,1,0:T(8,128)(2,1)}, bf16[4,256,1024]{2,1,0:T(8,128)(2,1)S(1)}, u32[]{:S(2)}, u32[]{:S(2)}) collective-permute-start(bf16[4,256,1024]{2,1,0:T(8,128)(2,1)} %all-to-all-done.1.refs_9_), channel_id=1, source_target_pairs={{0,8},{8,0},{1,9},{9,1},{2,10},{10,2},{3,11},{11,3},{4,12},{12,4},... | collective-permute-start | bytes 6291464 | tf_op jit(solution)/shard_map/ppermute | solution.py:154
  89.9 19.3 %collective-permute-start.8 = (bf16[128,1024]{1,0:T(8,128)(2,1)S(1)}, bf16[128,1024]{1,0:T(8,128)(2,1)S(1)}, u32[]{:S(2)}, u32[]{:S(2)}) collective-permute-start(bf16[128,1024]{1,0:T(8,128)(2,1)S(1)} %slice.7), channel_id=1, source_target_pairs={{0,7},{1,0},{2,1},{3,2},{4,3},{5,4},{6,5},{7,6},{8,15},{9,8},{10,9... | collective-permute-start | bytes 786440 | tf_op jit(solution)/shard_map/ppermute | solution.py:150
  93.8 15.4 %collective-permute-start.7 = (bf16[128,1024]{1,0:T(8,128)(2,1)S(1)}, bf16[128,1024]{1,0:T(8,128)(2,1)S(1)}, u32[]{:S(2)}, u32[]{:S(2)}) collective-permute-start(bf16[128,1024]{1,0:T(8,128)(2,1)S(1)} %slice.6), channel_id=1, source_target_pairs={{0,1},{1,2},{2,3},{3,4},{4,5},{5,6},{6,7},{7,0},{8,9},{9,10},{10,1... | collective-permute-start | bytes 786440 | tf_op jit(solution)/shard_map/ppermute | solution.py:150
  109.2 1.3 copy-start.1
  116.0 0.7 collective-permute-start.10
  128.1 7.3 %collective-permute-start.11 = (bf16[1024,256]{1,0:T(8,128)(2,1)S(1)}, bf16[1024,256]{1,0:T(8,128)(2,1)S(1)}, u32[]{:S(2)}, u32[]{:S(2)}) collective-permute-start(bf16[1024,256]{1,0:T(8,128)(2,1)S(1)} %all_gather.3.own), channel_id=1, source_target_pairs={{0,8},{8,0},{1,9},{9,1},{2,10},{10,2},{3,11},{11,3},{4,12},{12,4},... | collective-permute-start | bytes 1572872 | tf_op jit(solution)/shard_map/ppermute | solution.py:154

commit v5 on v2

--- a/solution.py
+++ b/solution.py
@@ -46,45 +46,44 @@
 SWAP = [(0, 1), (1, 0)]
 
 
-def project_kernel(*refs):
-    mem, mem_a, mem_b, w_refs, (out_ref, held, sems) = refs[:7], refs[7], refs[8], refs[9:19], refs[19:]
-    x, core, z = lax.axis_index("x"), lax.axis_index("c"), lax.axis_index("z")
+def project_kernel(mem_ref, *refs):
+    w_refs, (out_ref, held, sems) = refs[:10], refs[10:]
+    x, core = lax.axis_index("x"), lax.axis_index("c")
+    order = [(swapped, away) for away in (0, 3, 1, 2) for swapped in (0, 1)]
     copies = []
-    for swapped in range(2):
+    for j, (swapped, away) in enumerate(order):
         half = core if swapped == 0 else 1 - core
+        share = lax.rem(x + away, 4) * 2 + half
+        copies.append(pltpu.make_async_copy(mem_ref.at[share], held.at[j], sems.at[j]))
+        copies[j].start()
+    keys = values = None
+    for j, (swapped, away) in enumerate(order):
         own, left, right, opp_k, opp_v = w_refs[5 * swapped : 5 * swapped + 5]
-        for away, ref in ((0, own), (3, left), (1, right)):
-            copies.append((ref, held.at[lax.rem(x + away, 4) * 2 + half]))
-        opposite = lax.rem(x + 2, 4) * 2 + half
-        copies.append((opp_k, held.at[opposite, pl.ds(0, HD)]))
-        copies.append((opp_v, held.at[opposite, pl.ds(HD, HD)]))
-    copies = [pltpu.make_async_copy(src, dst, sems.at[j]) for j, (src, dst) in enumerate(copies)]
-    for copy in copies:
-        copy.start()
-    for copy in copies:
-        copy.wait()
-    total = None
-    for ref, away in zip(mem, (0, 7, 6, 5, 1, 2, 3)):
-        w_rows = held[lax.rem(z + away, 8)]
-        part = lax.dot_general(ref[...], w_rows, NT, preferred_element_type=jnp.float32)
-        total = part if total is None else total + part
-    w_rows = held[lax.rem(z + 4, 8)]
-    for start, ref in ((0, mem_a), (128, mem_b)):
-        part = lax.dot_general(ref[...], w_rows, NT, preferred_element_type=jnp.float32)
-        out_ref[start : start + 128] = (total[start : start + 128] + part).astype(out_ref.dtype)
+        if away == 2:
+            k_rows, v_rows = opp_k[...], opp_v[...]
+        else:
+            ref = {0: own, 3: left, 1: right}[away]
+            k_rows, v_rows = ref[:HD], ref[HD:]
+        copies[j].wait()
+        k_part = lax.dot_general(held[j], k_rows, NT, preferred_element_type=jnp.float32)
+        v_part = lax.dot_general(held[j], v_rows, NT, preferred_element_type=jnp.float32)
+        keys = k_part if keys is None else keys + k_part
+        values = v_part if values is None else values + v_part
+    out_ref[:, :HD] = keys.astype(out_ref.dtype)
+    out_ref[:, HD:] = values.astype(out_ref.dtype)
 
 
-def project(mem, w_pieces):
+def project(mem_all, w_pieces):
     vmem = pl.BlockSpec(memory_space=pltpu.VMEM)
     return pl.pallas_call(
         project_kernel,
         out_shape=jax.ShapeDtypeStruct((256, 2 * HD), jnp.bfloat16),
-        in_specs=[vmem] * 9 + [pl.BlockSpec(memory_space=pl.ANY)] * 10,
+        in_specs=[pl.BlockSpec(memory_space=pl.ANY)] + [vmem] * 10,
         out_specs=vmem,
-        scratch_shapes=[pltpu.VMEM((8, 2 * HD, 8 * HD), jnp.bfloat16), pltpu.SemaphoreType.DMA((10,))],
-        compiler_params=pltpu.CompilerParams(vmem_limit_bytes=24 << 20),
+        scratch_shapes=[pltpu.VMEM(mem_all.shape, jnp.bfloat16), pltpu.SemaphoreType.DMA((8,))],
+        compiler_params=pltpu.CompilerParams(vmem_limit_bytes=50 << 20),
         cost_estimate=pl.CostEstimate(flops=2 * 256 * 256 * 8192, bytes_accessed=8 << 20, transcendentals=0),
-    )(*mem, *w_pieces)
+    )(mem_all, *w_pieces)
 
 
 def attend_kernel(q_ref, own, other, out_ref):
@@ -154,32 +153,19 @@
     return value, left, right, opp_a, opp_b
 
 
-def ring_z(value, after):
-    ups = [lax.ppermute(value, "z", shift(8, 1))]
-    downs = [lax.ppermute(value, "z", shift(8, -1))]
-    ups[0], downs[0], after = lax.optimization_barrier((ups[0], downs[0], after))
-    for _ in range(2):
-        ups.append(lax.ppermute(ups[-1], "z", shift(8, 1)))
-        downs.append(lax.ppermute(downs[-1], "z", shift(8, -1)))
-    opp_a = lax.ppermute(ups[2][:128], "z", shift(8, 1))
-    opp_b = lax.ppermute(downs[2][128:], "z", shift(8, -1))
-    return (value, *ups, *downs, opp_a, opp_b), after
-
-
 def swap(value):
     return lax.ppermute(value, "c", SWAP)
 
 
 def body(memory, kv_weight, queries):
+    mem_all = lax.all_gather(memory, "z", axis=0)
     rows = lax.ppermute(kv_weight, ALL, weight_moves())
     query = lax.ppermute(queries, ALL, query_moves())
-    both = jnp.concatenate([rows, query.reshape(8, 8 * HD)], axis=0)
-    mem, both = ring_z(memory, both)
-    both = spread(both, "y")
+    both = spread(jnp.concatenate([rows, query.reshape(8, 8 * HD)], axis=0), "y")
     rows = both[:, :32].reshape(2 * HD, 8 * HD)
     query = both[:, 32:].reshape(512, HD)
     w_pieces = ring(rows)
-    own = project(mem, (*w_pieces, *map(swap, w_pieces)))
+    own = project(mem_all, (*w_pieces, *map(swap, w_pieces)))
 
     own = lax.all_gather(own, "x", axis=0, tiled=True)
     parts = attend(query, own, swap(own))

time: 152 us -> 152 us (level)
  the two profiles are of different devices: /device:TPU:256 before, /device:TPU:178 now
where the time goes in v5:
time: 152 us; the launch traced here: 151 us
  blocking collectives  50.7 us (33%)
  starting transfers between devices  45.7 us (30%)
  waiting for transfers between devices  28.4 us (19%)
  between operations  13.6 us (9%)
  Pallas kernels  9.48 us (6%)
  local copies, waits for them, and re-layouts  3.29 us (2%)
    all_to_all x1, blocking collectives, spread(): return lax.all_to_all(copies, axis, 0, 0, tiled=True)  20.9 us
    all_gather x1, blocking collectives, body(): own = lax.all_gather(own, 'x', axis=0, tiled=True)  15.2 us
    all_to_all x1, blocking collectives, body(): parts = lax.all_to_all(parts, 'y', 0, 0, tiled=True)  14.5 us
    ppermute x6, starting transfers between devices, swap(): return lax.ppermute(value, 'c', SWAP)  12 us
    ppermute x1, waiting for transfers between devices, body(): return lax.ppermute(result, ALL, query_moves())  8.58 us
    ppermute x1, waiting for transfers between devices, body(): query = lax.ppermute(queries, ALL, query_moves())  7.5 us
    ppermute x1, starting transfers between devices, body(): rows = lax.ppermute(kv_weight, ALL, weight_moves())  7.3 us
    ppermute x1, starting transfers between devices, body(): query = lax.ppermute(queries, ALL, query_moves())  7.17 us
  transfers between devices with their start and end apart: 14, of which 7 were waited for; matrix products, arithmetic and copies ran while one was open for 0% of the time, Pallas kernels for 0%

profile of v5, /device:TPU:178, one launch (start us, length us, event | category | flops | bytes accessed | tf_op | source)
XLA Modules:
  0.0 151.1 jit_solution(8880977422435511113)
XLA Ops:
  6.5 0.7 all-gather.3.cloned.1.call-update
  7.3 7.3 %collective-permute-start = (bf16[32,1024]{1,0:T(8,128)(2,1)}, bf16[32,1024]{1,0:T(8,128)(2,1)S(1)}, u32[]{:S(2)}, u32[]{:S(2)}) collective-permute-start(bf16[32,1024]{1,0:T(8,128)(2,1)} %param.4), channel_id=1, source_target_pairs={{0,0},{1,8},{2,16},{3,24},{4,32},{5,40},{6,48},{7,56},{8,64},{9,72... | collective-permute-start | bytes 196616 | tf_op jit(solution)/shard_map/ppermute | solution.py:162
  14.6 7.2 %collective-permute-start.1 = (bf16[64,128]{1,0:T(8,128)(2,1)}, bf16[64,128]{1,0:T(8,128)(2,1)S(1)}, u32[]{:S(2)}, u32[]{:S(2)}) collective-permute-start(bf16[64,128]{1,0:T(8,128)(2,1)} %param.5), channel_id=1, source_target_pairs={{0,0},{1,64},{2,128},{3,192},{4,256},{5,320},{6,384},{7,448},{8,8}... | collective-permute-start | bytes 49160 | tf_op jit(solution)/shard_map/ppermute | solution.py:163
  21.7 7.5 %collective-permute-done.1 = bf16[64,128]{1,0:T(8,128)(2,1)S(1)} collective-permute-done((bf16[64,128]{1,0:T(8,128)(2,1)}, bf16[64,128]{1,0:T(8,128)(2,1)S(1)}, u32[]{:S(2)}, u32[]{:S(2)}) %collective-permute-start.1) | collective-permute-done | bytes 16416 | tf_op jit(solution)/shard_map/ppermute | solution.py:163
  29.3 0.1 broadcast_in_dim.2
  29.4 20.9 %all_to_all.10 = bf16[8,40,1024]{2,1,0:T(8,128)(2,1)S(1)} all-to-all(bf16[8,40,1024]{2,1,0:T(8,128)(2,1)S(1)} %broadcast_in_dim.2), channel_id=1, replica_groups=mesh['y'=8,'x'=4,'c'=2,'z'=8] {'y'}, dimensions={0} | all-to-all | bytes 1310720 | tf_op jit(solution)/shard_map/all_to_all | solution.py:16
  50.3 4.1 %collective-permute-start.3 = (bf16[256,1024]{1,0:T(8,128)(2,1)S(1)}, bf16[256,1024]{1,0:T(8,128)(2,1)S(1)}, u32[]{:S(2)}, u32[]{:S(2)}) collective-permute-start(bf16[256,1024]{1,0:T(8,128)(2,1)S(1)} %bitcast.2), channel_id=1, source_target_pairs={{0,48},{16,0},{32,16},{48,32},{1,49},{17,1},{33,17},{49,33},{2,50}... | collective-permute-start | bytes 1572872 | tf_op jit(solution)/shard_map/ppermute | solution.py:150
  54.4 2.8 %collective-permute-start.2 = (bf16[256,1024]{1,0:T(8,128)(2,1)S(1)}, bf16[256,1024]{1,0:T(8,128)(2,1)S(1)}, u32[]{:S(2)}, u32[]{:S(2)}) collective-permute-start(bf16[256,1024]{1,0:T(8,128)(2,1)S(1)} %bitcast.3), channel_id=1, source_target_pairs={{0,16},{16,32},{32,48},{48,0},{1,17},{17,33},{33,49},{49,1},{2,18}... | collective-permute-start | bytes 1572872 | tf_op jit(solution)/shard_map/ppermute | solution.py:149
  57.2 1.9 %collective-permute-start.6 = (bf16[256,1024]{1,0:T(8,128)(2,1)S(1)}, bf16[256,1024]{1,0:T(8,128)(2,1)S(1)}, u32[]{:S(2)}, u32[]{:S(2)}) collective-permute-start(bf16[256,1024]{1,0:T(8,128)(2,1)S(1)} %bitcast.4), channel_id=1, source_target_pairs={{0,8},{8,0},{1,9},{9,1},{2,10},{10,2},{3,11},{11,3},{4,12},{12,4},... | collective-permute-start | bytes 1572872 | tf_op jit(solution)/shard_map/ppermute | solution.py:157
  59.2 6.3 %collective-permute-done.3.refs_2_ = bf16[256,1024]{1,0:T(8,128)(2,1)S(1)} collective-permute-done((bf16[256,1024]{1,0:T(8,128)(2,1)S(1)}, bf16[256,1024]{1,0:T(8,128)(2,1)S(1)}, u32[]{:S(2)}, u32[]{:S(2)}) %collective-permute-start.3) | collective-permute-done | bytes 524320 | tf_op jit(solution)/shard_map/ppermute | solution.py:150
  65.4 4.5 %collective-permute-start.5 = (bf16[128,1024]{1,0:T(8,128)(2,1)S(1)}, bf16[128,1024]{1,0:T(8,128)(2,1)S(1)}, u32[]{:S(2)}, u32[]{:S(2)}) collective-permute-start(bf16[128,1024]{1,0:T(8,128)(2,1)S(1)} %slice.19), channel_id=1, source_target_pairs={{0,48},{16,0},{32,16},{48,32},{1,49},{17,1},{33,17},{49,33},{2,50}... | collective-permute-start | bytes 786440 | tf_op jit(solution)/shard_map/ppermute | solution.py:152
  69.9 0.4 collective-permute-done.2.refs_1_
  70.4 1.9 %collective-permute-start.4 = (bf16[128,1024]{1,0:T(8,128)(2,1)S(1)}, bf16[128,1024]{1,0:T(8,128)(2,1)S(1)}, u32[]{:S(2)}, u32[]{:S(2)}) collective-permute-start(bf16[128,1024]{1,0:T(8,128)(2,1)S(1)} %slice.18), channel_id=1, source_target_pairs={{0,16},{16,32},{32,48},{48,0},{1,17},{17,33},{33,49},{49,1},{2,18}... | collective-permute-start | bytes 786440 | tf_op jit(solution)/shard_map/ppermute | solution.py:151
  72.3 1.9 %collective-permute-start.8 = (bf16[256,1024]{1,0:T(8,128)(2,1)S(1)}, bf16[256,1024]{1,0:T(8,128)(2,1)S(1)}, u32[]{:S(2)}, u32[]{:S(2)}) collective-permute-start(bf16[256,1024]{1,0:T(8,128)(2,1)S(1)} %collective-permute-done.3.refs_2_), channel_id=1, source_target_pairs={{0,8},{8,0},{1,9},{9,1},{2,10},{10,2},{3,11},{11,3},{4,12},{12,4},... | collective-permute-start | bytes 1572872 | tf_op jit(solution)/shard_map/ppermute | solution.py:157
  74.2 2.4 %collective-permute-start.7 = (bf16[256,1024]{1,0:T(8,128)(2,1)S(1)}, bf16[256,1024]{1,0:T(8,128)(2,1)S(1)}, u32[]{:S(2)}, u32[]{:S(2)}) collective-permute-start(bf16[256,1024]{1,0:T(8,128)(2,1)S(1)} %collective-permute-done.2.refs_1_), channel_id=1, source_target_pairs={{0,8},{8,0},{1,9},{9,1},{2,10},{10,2},{3,11},{11,3},{4,12},{12,4},... | collective-permute-start | bytes 1572872 | tf_op jit(solution)/shard_map/ppermute | solution.py:157
  76.7 1.9 %collective-permute-start.10 = (bf16[128,1024]{1,0:T(8,128)(2,1)S(1)}, bf16[128,1024]{1,0:T(8,128)(2,1)S(1)}, u32[]{:S(2)}, u32[]{:S(2)}) collective-permute-start(bf16[128,1024]{1,0:T(8,128)(2,1)S(1)} %collective-permute-done.5.refs_4_), channel_id=1, source_target_pairs={{0,8},{8,0},{1,9},{9,1},{2,10},{10,2},{3,11},{11,3},{4,12},{12,4},... | collective-permute-start | bytes 786440 | tf_op jit(solution)/shard_map/ppermute | solution.py:157
  78.6 1.6 %collective-permute-done.4.refs_3_ = bf16[128,1024]{1,0:T(8,128)(2,1)S(1)} collective-permute-done((bf16[128,1024]{1,0:T(8,128)(2,1)S(1)}, bf16[128,1024]{1,0:T(8,128)(2,1)S(1)}, u32[]{:S(2)}, u32[]{:S(2)}) %collective-permute-start.4) | collective-permute-done | bytes 262176 | tf_op jit(solution)/shard_map/ppermute | solution.py:151
  80.2 1.9 %collective-permute-start.9 = (bf16[128,1024]{1,0:T(8,128)(2,1)S(1)}, bf16[128,1024]{1,0:T(8,128)(2,1)S(1)}, u32[]{:S(2)}, u32[]{:S(2)}) collective-permute-start(bf16[128,1024]{1,0:T(8,128)(2,1)S(1)} %collective-permute-done.4.refs_3_), channel_id=1, source_target_pairs={{0,8},{8,0},{1,9},{9,1},{2,10},{10,2},{3,11},{11,3},{4,12},{12,4},... | collective-permute-start | bytes 786440 | tf_op jit(solution)/shard_map/ppermute | solution.py:157
  82.1 1.5 collective-permute-done.9.refs_8_
  83.6 0.7 copy-done
  84.3 0.8 copy-done.3
  85.1 0.9 copy-done.1
  86.1 5.0 %shard_map.37 = bf16[256,256]{1,0:T(8,128)(2,1)S(1)} custom-call(bf16[8,256,1024]{2,1,0:T(8,128)(2,1)} %bitcast.6, bf16[256,1024]{1,0:T(8,128)(2,1)S(1)} %bitcast.5, bf16[256,1024]{1,0:T(8,128)(2,1)S(1)} %collective-permute-done.2.refs_1_, bf16[256,1024]{1,0:T(8,128)(2,1)S(1)} %collective-permute-done.3.refs_2_, ...), custom_call_target="tpu_custom_call" | custom-call | flops 1073741824 | bytes 8388608 | tf_op jit(solution)/shard_map/pallas_call | solution.py:78
  91.1 15.2 %all_gather.11.own = bf16[1024,256]{1,0:T(8,128)(2,1)S(1)} all-gather(bf16[256,256]{1,0:T(8,128)(2,1)S(1)} %shard_map.37), channel_id=1, replica_groups=mesh['y'=8,'x'=4,'c'=2,'z'=8] {'x'}, dimensions={0}, use_global_device_ids=true | all-gather | bytes 655360 | tf_op jit(solution)/shard_map/all_gather | solution.py:170
  106.3 1.9 %collective-permute-start.11 = (bf16[1024,256]{1,0:T(8,128)(2,1)S(1)}, bf16[1024,256]{1,0:T(8,128)(2,1)S(1)}, u32[]{:S(2)}, u32[]{:S(2)}) collective-permute-start(bf16[1024,256]{1,0:T(8,128)(2,1)S(1)} %all_gather.11.own), channel_id=1, source_target_pairs={{0,8},{8,0},{1,9},{9,1},{2,10},{10,2},{3,11},{11,3},{4,12},{12,4},... | collective-permute-start | bytes 1572872 | tf_op jit(solution)/shard_map/ppermute | solution.py:157
  108.3 1.8 %collective-permute-done.11.other = bf16[1024,256]{1,0:T(8,128)(2,1)S(1)} collective-permute-done((bf16[1024,256]{1,0:T(8,128)(2,1)S(1)}, bf16[1024,256]{1,0:T(8,128)(2,1)S(1)}, u32[]{:S(2)}, u32[]{:S(2)}) %collective-permute-start.11) | collective-permute-done | bytes 524320 | tf_op jit(solution)/shard_map/ppermute | solution.py:157
  110.1 2.3 %shard_map.38 = f32[8,72,128]{2,1,0:T(8,128)S(1)} custom-call(bf16[512,128]{1,0:T(8,128)(2,1)S(1)} %reshape.11.q_ref, bf16[1024,256]{1,0:T(8,128)(2,1)S(1)} %all_gather.11.own, bf16[1024,256]{1,0:T(8,128)(2,1)S(1)} %collective-permute-done.11.other), custom_call_target="tpu_custom_call" | custom-call | flops 536870912 | bytes 2097152 | tf_op jit(solution)/shard_map/pallas_call | solution.py:118
  112.5 14.5 %all_to_all.11.part_ref = f32[8,72,128]{2,1,0:T(8,128)} all-to-all(f32[8,72,128]{2,1,0:T(8,128)S(1)} %shard_map.38), channel_id=1, replica_groups=mesh['y'=8,'x'=4,'c'=2,'z'=8] {'y'}, dimensions={0} | all-to-all | bytes 589824 | tf_op jit(solution)/shard_map/all_to_all | solution.py:172
  127.0 2.1 %shard_map.39 = bf16[64,128]{1,0:T(8,128)(2,1)} custom-call(f32[8,72,128]{2,1,0:T(8,128)} %all_to_all.11.part_ref), custom_call_target="tpu_custom_call" | custom-call | tf_op jit(solution)/shard_map/pallas_call | solution.py:141
  129.1 6.0 %collective-permute-start.12 = (bf16[64,128]{1,0:T(8,128)(2,1)}, bf16[64,128]{1,0:T(8,128)(2,1)S(1)}, u32[]{:S(2)}, u32[]{:S(2)}) collective-permute-start(bf16[64,128]{1,0:T(8,128)(2,1)} %shard_map.39), channel_id=1, source_target_pairs={{0,0},{1,64},{2,128},{3,192},{4,256},{5,320},{6,384},{7,448},{8,8}... | collective-permute-start | bytes 49160 | tf_op jit(solution)/shard_map/ppermute | solution.py:174
  135.1 8.6 %collective-permute-done.12 = bf16[64,128]{1,0:T(8,128)(2,1)S(1)} collective-permute-done((bf16[64,128]{1,0:T(8,128)(2,1)}, bf16[64,128]{1,0:T(8,128)(2,1)S(1)}, u32[]{:S(2)}, u32[]{:S(2)}) %collective-permute-start.12) | collective-permute-done | bytes 16416 | tf_op jit(solution)/shard_map/ppermute | solution.py:174
  143.7 0.6 copy.5
  (21 shorter events, 0.2 us)
Async XLA Ops:
  6.5 78.6 %all-gather.3.cloned.1.call-start = ((), (), s32[]{:S(2)}) async-start(), calls=%async_computation.2 | async-start | bytes 4718592 | tf_op jit(solution)/shard_map/all_gather | solution.py:161
  7.3 22.0 %collective-permute-start = (bf16[32,1024]{1,0:T(8,128)(2,1)}, bf16[32,1024]{1,0:T(8,128)(2,1)S(1)}, u32[]{:S(2)}, u32[]{:S(2)}) collective-permute-start(bf16[32,1024]{1,0:T(8,128)(2,1)} %param.4), channel_id=1, source_target_pairs={{0,0},{1,8},{2,16},{3,24},{4,32},{5,40},{6,48},{7,56},{8,64},{9,72... | collective-permute-start | bytes 196616 | tf_op jit(solution)/shard_map/ppermute | solution.py:162
  14.6 14.7 %collective-permute-start.1 = (bf16[64,128]{1,0:T(8,128)(2,1)}, bf16[64,128]{1,0:T(8,128)(2,1)S(1)}, u32[]{:S(2)}, u32[]{:S(2)}) collective-permute-start(bf16[64,128]{1,0:T(8,128)(2,1)} %param.5), channel_id=1, source_target_pairs={{0,0},{1,64},{2,128},{3,192},{4,256},{5,320},{6,384},{7,448},{8,8}... | collective-permute-start | bytes 49160 | tf_op jit(solution)/shard_map/ppermute | solution.py:163
  50.3 34.0 %copy-start.2 = (bf16[8,40,1024]{2,1,0:T(8,128)(2,1)}, bf16[8,40,1024]{2,1,0:T(8,128)(2,1)S(1)}, u32[]{:S(2)}) copy-start(bf16[8,40,1024]{2,1,0:T(8,128)(2,1)S(1)} %all_to_all.10) | copy-start | bytes 1966084
  50.3 15.1 %collective-permute-start.3 = (bf16[256,1024]{1,0:T(8,128)(2,1)S(1)}, bf16[256,1024]{1,0:T(8,128)(2,1)S(1)}, u32[]{:S(2)}, u32[]{:S(2)}) collective-permute-start(bf16[256,1024]{1,0:T(8,128)(2,1)S(1)} %bitcast.2), channel_id=1, source_target_pairs={{0,48},{16,0},{32,16},{48,32},{1,49},{17,1},{33,17},{49,33},{2,50}... | collective-permute-start | bytes 1572872 | tf_op jit(solution)/shard_map/ppermute | solution.py:150
  54.4 16.0 %collective-permute-start.2 = (bf16[256,1024]{1,0:T(8,128)(2,1)S(1)}, bf16[256,1024]{1,0:T(8,128)(2,1)S(1)}, u32[]{:S(2)}, u32[]{:S(2)}) collective-permute-start(bf16[256,1024]{1,0:T(8,128)(2,1)S(1)} %bitcast.3), channel_id=1, source_target_pairs={{0,16},{16,32},{32,48},{48,0},{1,17},{17,33},{33,49},{49,1},{2,18}... | collective-permute-start | bytes 1572872 | tf_op jit(solution)/shard_map/ppermute | solution.py:149
  57.2 24.9 %collective-permute-start.6 = (bf16[256,1024]{1,0:T(8,128)(2,1)S(1)}, bf16[256,1024]{1,0:T(8,128)(2,1)S(1)}, u32[]{:S(2)}, u32[]{:S(2)}) collective-permute-start(bf16[256,1024]{1,0:T(8,128)(2,1)S(1)} %bitcast.4), channel_id=1, source_target_pairs={{0,8},{8,0},{1,9},{9,1},{2,10},{10,2},{3,11},{11,3},{4,12},{12,4},... | collective-permute-start | bytes 1572872 | tf_op jit(solution)/shard_map/ppermute | solution.py:157
  65.4 11.2 %collective-permute-start.5 = (bf16[128,1024]{1,0:T(8,128)(2,1)S(1)}, bf16[128,1024]{1,0:T(8,128)(2,1)S(1)}, u32[]{:S(2)}, u32[]{:S(2)}) collective-permute-start(bf16[128,1024]{1,0:T(8,128)(2,1)S(1)} %slice.19), channel_id=1, source_target_pairs={{0,48},{16,0},{32,16},{48,32},{1,49},{17,1},{33,17},{49,33},{2,50}... | collective-permute-start | bytes 786440 | tf_op jit(solution)/shard_map/ppermute | solution.py:152
  70.4 9.8 %collective-permute-start.4 = (bf16[128,1024]{1,0:T(8,128)(2,1)S(1)}, bf16[128,1024]{1,0:T(8,128)(2,1)S(1)}, u32[]{:S(2)}, u32[]{:S(2)}) collective-permute-start(bf16[128,1024]{1,0:T(8,128)(2,1)S(1)} %slice.18), channel_id=1, source_target_pairs={{0,16},{16,32},{32,48},{48,0},{1,17},{17,33},{33,49},{49,1},{2,18}... | collective-permute-start | bytes 786440 | tf_op jit(solution)/shard_map/ppermute | solution.py:151
  72.3 12.0 %collective-permute-start.8 = (bf16[256,1024]{1,0:T(8,128)(2,1)S(1)}, bf16[256,1024]{1,0:T(8,128)(2,1)S(1)}, u32[]{:S(2)}, u32[]{:S(2)}) collective-permute-start(bf16[256,1024]{1,0:T(8,128)(2,1)S(1)} %collective-permute-done.3.refs_2_), channel_id=1, source_target_pairs={{0,8},{8,0},{1,9},{9,1},{2,10},{10,2},{3,11},{11,3},{4,12},{12,4},... | collective-permute-start | bytes 1572872 | tf_op jit(solution)/shard_map/ppermute | solution.py:157
  74.2 10.9 %collective-permute-start.7 = (bf16[256,1024]{1,0:T(8,128)(2,1)S(1)}, bf16[256,1024]{1,0:T(8,128)(2,1)S(1)}, u32[]{:S(2)}, u32[]{:S(2)}) collective-permute-start(bf16[256,1024]{1,0:T(8,128)(2,1)S(1)} %collective-permute-done.2.refs_1_), channel_id=1, source_target_pairs={{0,8},{8,0},{1,9},{9,1},{2,10},{10,2},{3,11},{11,3},{4,12},{12,4},... | collective-permute-start | bytes 1572872 | tf_op jit(solution)/shard_map/ppermute | solution.py:157
  76.7 5.4 %collective-permute-start.10 = (bf16[128,1024]{1,0:T(8,128)(2,1)S(1)}, bf16[128,1024]{1,0:T(8,128)(2,1)S(1)}, u32[]{:S(2)}, u32[]{:S(2)}) collective-permute-start(bf16[128,1024]{1,0:T(8,128)(2,1)S(1)} %collective-permute-done.5.refs_4_), channel_id=1, source_target_pairs={{0,8},{8,0},{1,9},{9,1},{2,10},{10,2},{3,11},{11,3},{4,12},{12,4},... | collective-permute-start | bytes 786440 | tf_op jit(solution)/shard_map/ppermute | solution.py:157
  80.2 3.4 %collective-permute-start.9 = (bf16[128,1024]{1,0:T(8,128)(2,1)S(1)}, bf16[128,1024]{1,0:T(8,128)(2,1)S(1)}, u32[]{:S(2)}, u32[]{:S(2)}) collective-permute-start(bf16[128,1024]{1,0:T(8,128)(2,1)S(1)} %collective-permute-done.4.refs_3_), channel_id=1, source_target_pairs={{0,8},{8,0},{1,9},{9,1},{2,10},{10,2},{3,11},{11,3},{4,12},{12,4},... | collective-permute-start | bytes 786440 | tf_op jit(solution)/shard_map/ppermute | solution.py:157
  83.6 0.7 copy-start
  84.3 0.8 copy-start.3
  85.1 1.0 copy-start.1
  86.1 22.2 %slice-start = ((bf16[8,40,1024]{2,1,0:T(8,128)(2,1)}), bf16[8,8,1024]{2,1,0:T(8,128)(2,1)S(1)}, s32[]{:S(2)}) async-start(bf16[8,40,1024]{2,1,0:T(8,128)(2,1)} %copy-done.2), calls=%async_computation.3 | async-start | bytes 262144 | tf_op jit(solution)/shard_map/slice | solution.py:166
  106.3 3.8 %collective-permute-start.11 = (bf16[1024,256]{1,0:T(8,128)(2,1)S(1)}, bf16[1024,256]{1,0:T(8,128)(2,1)S(1)}, u32[]{:S(2)}, u32[]{:S(2)}) collective-permute-start(bf16[1024,256]{1,0:T(8,128)(2,1)S(1)} %all_gather.11.own), channel_id=1, source_target_pairs={{0,8},{8,0},{1,9},{9,1},{2,10},{10,2},{3,11},{11,3},{4,12},{12,4},... | collective-permute-start | bytes 1572872 | tf_op jit(solution)/shard_map/ppermute | solution.py:157
  129.1 14.5 %collective-permute-start.12 = (bf16[64,128]{1,0:T(8,128)(2,1)}, bf16[64,128]{1,0:T(8,128)(2,1)S(1)}, u32[]{:S(2)}, u32[]{:S(2)}) collective-permute-start(bf16[64,128]{1,0:T(8,128)(2,1)} %shard_map.39), channel_id=1, source_target_pairs={{0,0},{1,64},{2,128},{3,192},{4,256},{5,320},{6,384},{7,448},{8,8}... | collective-permute-start | bytes 49160 | tf_op jit(solution)/shard_map/ppermute | solution.py:174
Sparse Core Ops, SparseCore 0:
  9.4 58.5 all-gather.2

commit v6 on v5

--- a/solution.py
+++ b/solution.py
@@ -28,13 +28,18 @@
                 shard = y * 8 + x * 2 + c
                 kind, head, quarter = shard // 32, shard // 4 % 8, shard % 4
                 for z in range(8):
-                    moves.append((place(y, x, c, z), place(kind * 4 + quarter, z // 2, z % 2, head)))
+                    target = place(kind * 4 + quarter, z // 2, z % 2, (head + 4) % 8)
+                    moves.append((place(y, x, c, z), target))
     return moves
 
 
 def query_moves():
     return [
-        (place(y, x, c, z), place(z, x, c, y)) for y in range(8) for x in range(4) for c in range(2) for z in range(8)
+        (place(y, x, c, z), place(z, x, c, (y + 4) % 8))
+        for y in range(8)
+        for x in range(4)
+        for c in range(2)
+        for z in range(8)
     ]
 
 
@@ -47,41 +52,45 @@
 
 
 def project_kernel(mem_ref, *refs):
-    w_refs, (out_ref, held, sems) = refs[:10], refs[10:]
+    w_refs, (out_ref, mem_held, w_held, mem_sems, w_sems) = refs[:10], refs[10:]
     x, core = lax.axis_index("x"), lax.axis_index("c")
     order = [(swapped, away) for away in (0, 3, 1, 2) for swapped in (0, 1)]
     copies = []
     for j, (swapped, away) in enumerate(order):
         half = core if swapped == 0 else 1 - core
         share = lax.rem(x + away, 4) * 2 + half
-        copies.append(pltpu.make_async_copy(mem_ref.at[share], held.at[j], sems.at[j]))
-        copies[j].start()
-    keys = values = None
-    for j, (swapped, away) in enumerate(order):
         own, left, right, opp_k, opp_v = w_refs[5 * swapped : 5 * swapped + 5]
         if away == 2:
-            k_rows, v_rows = opp_k[...], opp_v[...]
+            pairs = [(opp_k, w_held.at[j, pl.ds(0, HD)]), (opp_v, w_held.at[j, pl.ds(HD, HD)])]
         else:
-            ref = {0: own, 3: left, 1: right}[away]
-            k_rows, v_rows = ref[:HD], ref[HD:]
-        copies[j].wait()
-        k_part = lax.dot_general(held[j], k_rows, NT, preferred_element_type=jnp.float32)
-        v_part = lax.dot_general(held[j], v_rows, NT, preferred_element_type=jnp.float32)
-        keys = k_part if keys is None else keys + k_part
-        values = v_part if values is None else values + v_part
-    out_ref[:, :HD] = keys.astype(out_ref.dtype)
-    out_ref[:, HD:] = values.astype(out_ref.dtype)
+            pairs = [({0: own, 3: left, 1: right}[away], w_held.at[j])]
+        moves = [pltpu.make_async_copy(mem_ref.at[share], mem_held.at[j], mem_sems.at[j])]
+        moves += [pltpu.make_async_copy(src, dst, w_sems.at[j, i]) for i, (src, dst) in enumerate(pairs)]
+        for move in moves:
+            move.start()
+        copies.append(moves)
+    total = None
+    for j, moves in enumerate(copies):
+        for move in moves:
+            move.wait()
+        part = lax.dot_general(mem_held[j], w_held[j], NT, preferred_element_type=jnp.float32)
+        total = part if total is None else total + part
+    out_ref[...] = total.astype(out_ref.dtype)
 
 
 def project(mem_all, w_pieces):
-    vmem = pl.BlockSpec(memory_space=pltpu.VMEM)
     return pl.pallas_call(
         project_kernel,
         out_shape=jax.ShapeDtypeStruct((256, 2 * HD), jnp.bfloat16),
-        in_specs=[pl.BlockSpec(memory_space=pl.ANY)] + [vmem] * 10,
-        out_specs=vmem,
-        scratch_shapes=[pltpu.VMEM(mem_all.shape, jnp.bfloat16), pltpu.SemaphoreType.DMA((8,))],
-        compiler_params=pltpu.CompilerParams(vmem_limit_bytes=50 << 20),
+        in_specs=[pl.BlockSpec(memory_space=pl.ANY)] * 11,
+        out_specs=pl.BlockSpec(memory_space=pltpu.VMEM),
+        scratch_shapes=[
+            pltpu.VMEM(mem_all.shape, jnp.bfloat16),
+            pltpu.VMEM(mem_all.shape, jnp.bfloat16),
+            pltpu.SemaphoreType.DMA((8,)),
+            pltpu.SemaphoreType.DMA((8, 2)),
+        ],
+        compiler_params=pltpu.CompilerParams(vmem_limit_bytes=52 << 20),
         cost_estimate=pl.CostEstimate(flops=2 * 256 * 256 * 8192, bytes_accessed=8 << 20, transcendentals=0),
     )(mem_all, *w_pieces)
 
@@ -161,7 +170,7 @@
     mem_all = lax.all_gather(memory, "z", axis=0)
     rows = lax.ppermute(kv_weight, ALL, weight_moves())
     query = lax.ppermute(queries, ALL, query_moves())
-    both = spread(jnp.concatenate([rows, query.reshape(8, 8 * HD)], axis=0), "y")
+    both = lax.all_gather(jnp.concatenate([rows, query.reshape(8, 8 * HD)], axis=0), "y", axis=0)
     rows = both[:, :32].reshape(2 * HD, 8 * HD)
     query = both[:, 32:].reshape(512, HD)
     w_pieces = ring(rows)
@@ -171,7 +180,7 @@
     parts = attend(query, own, swap(own))
     parts = lax.all_to_all(parts, "y", 0, 0, tiled=True)
     result = merge(parts)
-    return lax.ppermute(result, ALL, query_moves())
+    return lax.ppermute(result, ALL, [(b, a) for a, b in query_moves()])
 
 
 def solution(mesh):

time: 152 us -> 153 us (level)
  the two profiles are of different devices: /device:TPU:178 before, /device:TPU:1 now
where the time goes in v6:
time: 153 us
  starting transfers between devices  59.7 us (39%)
  blocking collectives  49.4 us (32%)
  waiting for transfers between devices  19.1 us (12%)
  between operations  13.7 us (9%)
  Pallas kernels  8.94 us (6%)
  local copies, waits for them, and re-layouts  1.88 us (1%)
    ppermute x6, starting transfers between devices, swap(): return lax.ppermute(value, 'c', SWAP)  26.1 us
    all_gather x1, blocking collectives, body(): lax.all_gather(jnp.concatenate([rows, query.reshape(8, 8 * HD)], axis=0),...  23.4 us
    all_to_all x1, blocking collectives, body(): parts = lax.all_to_all(parts, 'y', 0, 0, tiled=True)  16 us
    ppermute x1, starting transfers between devices, body(): rows = lax.ppermute(kv_weight, ALL, weight_moves())  13 us
    all_gather x1, blocking collectives, body(): own = lax.all_gather(own, 'x', axis=0, tiled=True)  9.9 us
    ppermute x1, waiting for transfers between devices, body(): return lax.ppermute(result, ALL, [(b, a) for a, b in query_moves()])  6.72 us
    ppermute x1, waiting for transfers between devices, ring(): opp_a = lax.ppermute(left[:half], 'x', shift(4, 1))  6.12 us
    ppermute x1, starting transfers between devices, ring(): right = lax.ppermute(value, 'x', shift(4, -1))  5.02 us
  transfers between devices with their start and end apart: 14, of which 4 were waited for; matrix products, arithmetic and copies ran while one was open for 0% of the time, Pallas kernels for 0%

profile of v6, /device:TPU:1, one launch (start us, length us, event | category | flops | bytes accessed | tf_op | source)
XLA Modules:
  0.0 152.7 jit_solution(13514701502242813622)
XLA Ops:
  6.5 0.7 all-gather.4.cloned.1.call-update
  7.3 13.0 %collective-permute-start = (bf16[32,1024]{1,0:T(8,128)(2,1)}, bf16[32,1024]{1,0:T(8,128)(2,1)S(1)}, u32[]{:S(2)}, u32[]{:S(2)}) collective-permute-start(bf16[32,1024]{1,0:T(8,128)(2,1)} %param.4), channel_id=1, source_target_pairs={{0,4},{1,12},{2,20},{3,28},{4,36},{5,44},{6,52},{7,60},{8,68},{9,7... | collective-permute-start | bytes 196616 | tf_op jit(solution)/shard_map/ppermute | solution.py:171
  20.3 4.7 %collective-permute-start.1 = (bf16[64,128]{1,0:T(8,128)(2,1)}, bf16[64,128]{1,0:T(8,128)(2,1)S(1)}, u32[]{:S(2)}, u32[]{:S(2)}) collective-permute-start(bf16[64,128]{1,0:T(8,128)(2,1)} %param.5), channel_id=1, source_target_pairs={{0,4},{1,68},{2,132},{3,196},{4,260},{5,324},{6,388},{7,452},{8,12... | collective-permute-start | bytes 49160 | tf_op jit(solution)/shard_map/ppermute | solution.py:172
  25.0 4.1 %collective-permute-done.1 = bf16[64,128]{1,0:T(8,128)(2,1)S(1)} collective-permute-done((bf16[64,128]{1,0:T(8,128)(2,1)}, bf16[64,128]{1,0:T(8,128)(2,1)S(1)}, u32[]{:S(2)}, u32[]{:S(2)}) %collective-permute-start.1) | collective-permute-done | bytes 16416 | tf_op jit(solution)/shard_map/ppermute | solution.py:172
  29.1 0.0 collective-permute-done
  29.1 23.4 %all-gather = bf16[320,1024]{1,0:T(8,128)(2,1)S(1)} all-gather(bf16[40,1024]{1,0:T(8,128)(2,1)S(1)} %pad_maximum_fusion), channel_id=2, replica_groups=mesh['y'=8,'x'=4,'c'=2,'z'=8] {'y'}, dimensions={0}, use_global_device_ids=true | all-gather | bytes 737280 | tf_op jit(solution)/shard_map/all_gather | solution.py:173
  52.6 5.0 %collective-permute-start.3 = (bf16[256,1024]{1,0:T(8,128)(2,1)S(1)}, bf16[256,1024]{1,0:T(8,128)(2,1)S(1)}, u32[]{:S(2)}, u32[]{:S(2)}) collective-permute-start(bf16[256,1024]{1,0:T(8,128)(2,1)S(1)} %bitcast.3), channel_id=1, source_target_pairs={{0,48},{16,0},{32,16},{48,32},{1,49},{17,1},{33,17},{49,33},{2,50}... | collective-permute-start | bytes 1572872 | tf_op jit(solution)/shard_map/ppermute | solution.py:159
  57.6 1.9 %collective-permute-start.2 = (bf16[256,1024]{1,0:T(8,128)(2,1)S(1)}, bf16[256,1024]{1,0:T(8,128)(2,1)S(1)}, u32[]{:S(2)}, u32[]{:S(2)}) collective-permute-start(bf16[256,1024]{1,0:T(8,128)(2,1)S(1)} %bitcast.4), channel_id=1, source_target_pairs={{0,16},{16,32},{32,48},{48,0},{1,17},{17,33},{33,49},{49,1},{2,18}... | collective-permute-start | bytes 1572872 | tf_op jit(solution)/shard_map/ppermute | solution.py:158
  59.5 6.3 %collective-permute-start.6 = (bf16[256,1024]{1,0:T(8,128)(2,1)S(1)}, bf16[256,1024]{1,0:T(8,128)(2,1)S(1)}, u32[]{:S(2)}, u32[]{:S(2)}) collective-permute-start(bf16[256,1024]{1,0:T(8,128)(2,1)S(1)} %bitcast.5), channel_id=1, source_target_pairs={{0,8},{8,0},{1,9},{9,1},{2,10},{10,2},{3,11},{11,3},{4,12},{12,4},... | collective-permute-start | bytes 1572872 | tf_op jit(solution)/shard_map/ppermute | solution.py:166
  65.9 0.0 collective-permute-done.3.refs_2_
  65.9 4.9 %collective-permute-start.5 = (bf16[128,1024]{1,0:T(8,128)(2,1)S(1)}, bf16[128,1024]{1,0:T(8,128)(2,1)S(1)}, u32[]{:S(2)}, u32[]{:S(2)}) collective-permute-start(bf16[128,1024]{1,0:T(8,128)(2,1)S(1)} %slice.19), channel_id=1, source_target_pairs={{0,48},{16,0},{32,16},{48,32},{1,49},{17,1},{33,17},{49,33},{2,50}... | collective-permute-start | bytes 786440 | tf_op jit(solution)/shard_map/ppermute | solution.py:161
  70.8 6.5 %collective-permute-start.8 = (bf16[256,1024]{1,0:T(8,128)(2,1)S(1)}, bf16[256,1024]{1,0:T(8,128)(2,1)S(1)}, u32[]{:S(2)}, u32[]{:S(2)}) collective-permute-start(bf16[256,1024]{1,0:T(8,128)(2,1)S(1)} %collective-permute-done.3.refs_2_), channel_id=1, source_target_pairs={{0,8},{8,0},{1,9},{9,1},{2,10},{10,2},{3,11},{11,3},{4,12},{12,4},... | collective-permute-start | bytes 1572872 | tf_op jit(solution)/shard_map/ppermute | solution.py:166
  77.3 1.9 %collective-permute-start.7 = (bf16[256,1024]{1,0:T(8,128)(2,1)S(1)}, bf16[256,1024]{1,0:T(8,128)(2,1)S(1)}, u32[]{:S(2)}, u32[]{:S(2)}) collective-permute-start(bf16[256,1024]{1,0:T(8,128)(2,1)S(1)} %collective-permute-done.2.refs_1_), channel_id=1, source_target_pairs={{0,8},{8,0},{1,9},{9,1},{2,10},{10,2},{3,11},{11,3},{4,12},{12,4},... | collective-permute-start | bytes 1572872 | tf_op jit(solution)/shard_map/ppermute | solution.py:166
  79.3 1.9 %collective-permute-start.4 = (bf16[128,1024]{1,0:T(8,128)(2,1)S(1)}, bf16[128,1024]{1,0:T(8,128)(2,1)S(1)}, u32[]{:S(2)}, u32[]{:S(2)}) collective-permute-start(bf16[128,1024]{1,0:T(8,128)(2,1)S(1)} %slice.18), channel_id=1, source_target_pairs={{0,16},{16,32},{32,48},{48,0},{1,17},{17,33},{33,49},{49,1},{2,18}... | collective-permute-start | bytes 786440 | tf_op jit(solution)/shard_map/ppermute | solution.py:160
  81.2 0.0 collective-permute-done.5.refs_4_
  81.2 2.4 %collective-permute-start.10 = (bf16[128,1024]{1,0:T(8,128)(2,1)S(1)}, bf16[128,1024]{1,0:T(8,128)(2,1)S(1)}, u32[]{:S(2)}, u32[]{:S(2)}) collective-permute-start(bf16[128,1024]{1,0:T(8,128)(2,1)S(1)} %collective-permute-done.5.refs_4_), channel_id=1, source_target_pairs={{0,8},{8,0},{1,9},{9,1},{2,10},{10,2},{3,11},{11,3},{4,12},{12,4},... | collective-permute-start | bytes 786440 | tf_op jit(solution)/shard_map/ppermute | solution.py:166
  83.6 6.1 %collective-permute-done.4.refs_3_ = bf16[128,1024]{1,0:T(8,128)(2,1)S(1)} collective-permute-done((bf16[128,1024]{1,0:T(8,128)(2,1)S(1)}, bf16[128,1024]{1,0:T(8,128)(2,1)S(1)}, u32[]{:S(2)}, u32[]{:S(2)}) %collective-permute-start.4) | collective-permute-done | bytes 262176 | tf_op jit(solution)/shard_map/ppermute | solution.py:160
  89.7 3.2 %collective-permute-start.9 = (bf16[128,1024]{1,0:T(8,128)(2,1)S(1)}, bf16[128,1024]{1,0:T(8,128)(2,1)S(1)}, u32[]{:S(2)}, u32[]{:S(2)}) collective-permute-start(bf16[128,1024]{1,0:T(8,128)(2,1)S(1)} %collective-permute-done.4.refs_3_), channel_id=1, source_target_pairs={{0,8},{8,0},{1,9},{9,1},{2,10},{10,2},{3,11},{11,3},{4,12},{12,4},... | collective-permute-start | bytes 786440 | tf_op jit(solution)/shard_map/ppermute | solution.py:166
  93.1 0.8 copy-done.2
  93.8 0.2 copy-done.3
  94.0 0.2 copy-done.4
  94.2 4.5 %shard_map.37 = bf16[256,256]{1,0:T(8,128)(2,1)S(1)} custom-call(bf16[8,256,1024]{2,1,0:T(8,128)(2,1)} %bitcast.7, bf16[256,1024]{1,0:T(8,128)(2,1)S(1)} %bitcast.6, bf16[256,1024]{1,0:T(8,128)(2,1)} %copy-done.1, bf16[256,1024]{1,0:T(8,128)(2,1)} %copy-done, bf16[128,1024]{1,0:T(8,128)(2,1)S(1)} %collective-permute-done.4.refs_3_, ...), custom_call_target="tpu_custom_call" | custom-call | flops 1073741824 | bytes 8388608 | tf_op jit(solution)/shard_map/pallas_call | solution.py:82
  98.7 9.9 %all_gather.19.own = bf16[1024,256]{1,0:T(8,128)(2,1)S(1)} all-gather(bf16[256,256]{1,0:T(8,128)(2,1)S(1)} %shard_map.37), channel_id=1, replica_groups=mesh['y'=8,'x'=4,'c'=2,'z'=8] {'x'}, dimensions={0}, use_global_device_ids=true | all-gather | bytes 655360 | tf_op jit(solution)/shard_map/all_gather | solution.py:179
  108.6 5.7 %collective-permute-start.11 = (bf16[1024,256]{1,0:T(8,128)(2,1)S(1)}, bf16[1024,256]{1,0:T(8,128)(2,1)S(1)}, u32[]{:S(2)}, u32[]{:S(2)}) collective-permute-start(bf16[1024,256]{1,0:T(8,128)(2,1)S(1)} %all_gather.19.own), channel_id=1, source_target_pairs={{0,8},{8,0},{1,9},{9,1},{2,10},{10,2},{3,11},{11,3},{4,12},{12,4},... | collective-permute-start | bytes 1572872 | tf_op jit(solution)/shard_map/ppermute | solution.py:166
  114.3 0.1 reshape.10.q_ref
  114.3 1.4 collective-permute-done.11.other
  115.8 2.3 %shard_map.38 = f32[8,72,128]{2,1,0:T(8,128)S(1)} custom-call(bf16[512,128]{1,0:T(8,128)(2,1)S(1)} %reshape.10.q_ref, bf16[1024,256]{1,0:T(8,128)(2,1)S(1)} %all_gather.19.own, bf16[1024,256]{1,0:T(8,128)(2,1)S(1)} %collective-permute-done.11.other), custom_call_target="tpu_custom_call" | custom-call | flops 536870912 | bytes 2097152 | tf_op jit(solution)/shard_map/pallas_call | solution.py:127
  118.1 16.0 %all_to_all.5.part_ref = f32[8,72,128]{2,1,0:T(8,128)} all-to-all(f32[8,72,128]{2,1,0:T(8,128)S(1)} %shard_map.38), channel_id=1, replica_groups=mesh['y'=8,'x'=4,'c'=2,'z'=8] {'y'}, dimensions={0} | all-to-all | bytes 589824 | tf_op jit(solution)/shard_map/all_to_all | solution.py:181
  134.1 2.1 %shard_map.39 = bf16[64,128]{1,0:T(8,128)(2,1)} custom-call(f32[8,72,128]{2,1,0:T(8,128)} %all_to_all.5.part_ref), custom_call_target="tpu_custom_call" | custom-call | tf_op jit(solution)/shard_map/pallas_call | solution.py:150
  136.3 2.2 %collective-permute-start.12 = (bf16[64,128]{1,0:T(8,128)(2,1)}, bf16[64,128]{1,0:T(8,128)(2,1)S(1)}, u32[]{:S(2)}, u32[]{:S(2)}) collective-permute-start(bf16[64,128]{1,0:T(8,128)(2,1)} %shard_map.39), channel_id=1, source_target_pairs={{4,0},{68,1},{132,2},{196,3},{260,4},{324,5},{388,6},{452,7},{12,8... | collective-permute-start | bytes 49160 | tf_op jit(solution)/shard_map/ppermute | solution.py:183
  138.5 6.7 %collective-permute-done.12 = bf16[64,128]{1,0:T(8,128)(2,1)S(1)} collective-permute-done((bf16[64,128]{1,0:T(8,128)(2,1)}, bf16[64,128]{1,0:T(8,128)(2,1)S(1)}, u32[]{:S(2)}, u32[]{:S(2)}) %collective-permute-start.12) | collective-permute-done | bytes 16416 | tf_op jit(solution)/shard_map/ppermute | solution.py:183
  145.2 0.6 copy.5
  (21 shorter events, 0.1 us)
Async XLA Ops:
  6.5 87.6 %all-gather.4.cloned.1.call-start = ((), (), s32[]{:S(2)}) async-start(), calls=%async_computation.1 | async-start | bytes 4718592 | tf_op jit(solution)/shard_map/all_gather | solution.py:170
  7.3 21.8 %collective-permute-start = (bf16[32,1024]{1,0:T(8,128)(2,1)}, bf16[32,1024]{1,0:T(8,128)(2,1)S(1)}, u32[]{:S(2)}, u32[]{:S(2)}) collective-permute-start(bf16[32,1024]{1,0:T(8,128)(2,1)} %param.4), channel_id=1, source_target_pairs={{0,4},{1,12},{2,20},{3,28},{4,36},{5,44},{6,52},{7,60},{8,68},{9,7... | collective-permute-start | bytes 196616 | tf_op jit(solution)/shard_map/ppermute | solution.py:171
  20.3 8.8 %collective-permute-start.1 = (bf16[64,128]{1,0:T(8,128)(2,1)}, bf16[64,128]{1,0:T(8,128)(2,1)S(1)}, u32[]{:S(2)}, u32[]{:S(2)}) collective-permute-start(bf16[64,128]{1,0:T(8,128)(2,1)} %param.5), channel_id=1, source_target_pairs={{0,4},{1,68},{2,132},{3,196},{4,260},{5,324},{6,388},{7,452},{8,12... | collective-permute-start | bytes 49160 | tf_op jit(solution)/shard_map/ppermute | solution.py:172
  52.6 13.3 %collective-permute-start.3 = (bf16[256,1024]{1,0:T(8,128)(2,1)S(1)}, bf16[256,1024]{1,0:T(8,128)(2,1)S(1)}, u32[]{:S(2)}, u32[]{:S(2)}) collective-permute-start(bf16[256,1024]{1,0:T(8,128)(2,1)S(1)} %bitcast.3), channel_id=1, source_target_pairs={{0,48},{16,0},{32,16},{48,32},{1,49},{17,1},{33,17},{49,33},{2,50}... | collective-permute-start | bytes 1572872 | tf_op jit(solution)/shard_map/ppermute | solution.py:159
  57.6 19.7 %collective-permute-start.2 = (bf16[256,1024]{1,0:T(8,128)(2,1)S(1)}, bf16[256,1024]{1,0:T(8,128)(2,1)S(1)}, u32[]{:S(2)}, u32[]{:S(2)}) collective-permute-start(bf16[256,1024]{1,0:T(8,128)(2,1)S(1)} %bitcast.4), channel_id=1, source_target_pairs={{0,16},{16,32},{32,48},{48,0},{1,17},{17,33},{33,49},{49,1},{2,18}... | collective-permute-start | bytes 1572872 | tf_op jit(solution)/shard_map/ppermute | solution.py:158
  59.5 33.4 %collective-permute-start.6 = (bf16[256,1024]{1,0:T(8,128)(2,1)S(1)}, bf16[256,1024]{1,0:T(8,128)(2,1)S(1)}, u32[]{:S(2)}, u32[]{:S(2)}) collective-permute-start(bf16[256,1024]{1,0:T(8,128)(2,1)S(1)} %bitcast.5), channel_id=1, source_target_pairs={{0,8},{8,0},{1,9},{9,1},{2,10},{10,2},{3,11},{11,3},{4,12},{12,4},... | collective-permute-start | bytes 1572872 | tf_op jit(solution)/shard_map/ppermute | solution.py:166
  65.9 28.3 %copy-start = (bf16[256,1024]{1,0:T(8,128)(2,1)}, bf16[256,1024]{1,0:T(8,128)(2,1)S(1)}, u32[]{:S(2)}) copy-start(bf16[256,1024]{1,0:T(8,128)(2,1)S(1)} %collective-permute-done.3.refs_2_) | copy-start | bytes 1572868
  65.9 15.2 %collective-permute-start.5 = (bf16[128,1024]{1,0:T(8,128)(2,1)S(1)}, bf16[128,1024]{1,0:T(8,128)(2,1)S(1)}, u32[]{:S(2)}, u32[]{:S(2)}) collective-permute-start(bf16[128,1024]{1,0:T(8,128)(2,1)S(1)} %slice.19), channel_id=1, source_target_pairs={{0,48},{16,0},{32,16},{48,32},{1,49},{17,1},{33,17},{49,33},{2,50}... | collective-permute-start | bytes 786440 | tf_op jit(solution)/shard_map/ppermute | solution.py:161
  70.8 22.2 %collective-permute-start.8 = (bf16[256,1024]{1,0:T(8,128)(2,1)S(1)}, bf16[256,1024]{1,0:T(8,128)(2,1)S(1)}, u32[]{:S(2)}, u32[]{:S(2)}) collective-permute-start(bf16[256,1024]{1,0:T(8,128)(2,1)S(1)} %collective-permute-done.3.refs_2_), channel_id=1, source_target_pairs={{0,8},{8,0},{1,9},{9,1},{2,10},{10,2},{3,11},{11,3},{4,12},{12,4},... | collective-permute-start | bytes 1572872 | tf_op jit(solution)/shard_map/ppermute | solution.py:166
  77.3 16.9 %copy-start.1 = (bf16[256,1024]{1,0:T(8,128)(2,1)}, bf16[256,1024]{1,0:T(8,128)(2,1)S(1)}, u32[]{:S(2)}) copy-start(bf16[256,1024]{1,0:T(8,128)(2,1)S(1)} %collective-permute-done.2.refs_1_) | copy-start | bytes 1572868
  77.3 15.7 %collective-permute-start.7 = (bf16[256,1024]{1,0:T(8,128)(2,1)S(1)}, bf16[256,1024]{1,0:T(8,128)(2,1)S(1)}, u32[]{:S(2)}, u32[]{:S(2)}) collective-permute-start(bf16[256,1024]{1,0:T(8,128)(2,1)S(1)} %collective-permute-done.2.refs_1_), channel_id=1, source_target_pairs={{0,8},{8,0},{1,9},{9,1},{2,10},{10,2},{3,11},{11,3},{4,12},{12,4},... | collective-permute-start | bytes 1572872 | tf_op jit(solution)/shard_map/ppermute | solution.py:166
  79.3 10.5 %collective-permute-start.4 = (bf16[128,1024]{1,0:T(8,128)(2,1)S(1)}, bf16[128,1024]{1,0:T(8,128)(2,1)S(1)}, u32[]{:S(2)}, u32[]{:S(2)}) collective-permute-start(bf16[128,1024]{1,0:T(8,128)(2,1)S(1)} %slice.18), channel_id=1, source_target_pairs={{0,16},{16,32},{32,48},{48,0},{1,17},{17,33},{33,49},{49,1},{2,18}... | collective-permute-start | bytes 786440 | tf_op jit(solution)/shard_map/ppermute | solution.py:160
  81.2 11.9 %collective-permute-start.10 = (bf16[128,1024]{1,0:T(8,128)(2,1)S(1)}, bf16[128,1024]{1,0:T(8,128)(2,1)S(1)}, u32[]{:S(2)}, u32[]{:S(2)}) collective-permute-start(bf16[128,1024]{1,0:T(8,128)(2,1)S(1)} %collective-permute-done.5.refs_4_), channel_id=1, source_target_pairs={{0,8},{8,0},{1,9},{9,1},{2,10},{10,2},{3,11},{11,3},{4,12},{12,4},... | collective-permute-start | bytes 786440 | tf_op jit(solution)/shard_map/ppermute | solution.py:166
  89.7 4.4 %collective-permute-start.9 = (bf16[128,1024]{1,0:T(8,128)(2,1)S(1)}, bf16[128,1024]{1,0:T(8,128)(2,1)S(1)}, u32[]{:S(2)}, u32[]{:S(2)}) collective-permute-start(bf16[128,1024]{1,0:T(8,128)(2,1)S(1)} %collective-permute-done.4.refs_3_), channel_id=1, source_target_pairs={{0,8},{8,0},{1,9},{9,1},{2,10},{10,2},{3,11},{11,3},{4,12},{12,4},... | collective-permute-start | bytes 786440 | tf_op jit(solution)/shard_map/ppermute | solution.py:166
  93.0 0.8 copy-start.2
  93.0 1.0 copy-start.3
  93.0 1.1 copy-start.4
  108.6 7.2 %collective-permute-start.11 = (bf16[1024,256]{1,0:T(8,128)(2,1)S(1)}, bf16[1024,256]{1,0:T(8,128)(2,1)S(1)}, u32[]{:S(2)}, u32[]{:S(2)}) collective-permute-start(bf16[1024,256]{1,0:T(8,128)(2,1)S(1)} %all_gather.19.own), channel_id=1, source_target_pairs={{0,8},{8,0},{1,9},{9,1},{2,10},{10,2},{3,11},{11,3},{4,12},{12,4},... | collective-permute-start | bytes 1572872 | tf_op jit(solution)/shard_map/ppermute | solution.py:166
  136.3 8.9 %collective-permute-start.12 = (bf16[64,128]{1,0:T(8,128)(2,1)}, bf16[64,128]{1,0:T(8,128)(2,1)S(1)}, u32[]{:S(2)}, u32[]{:S(2)}) collective-permute-start(bf16[64,128]{1,0:T(8,128)(2,1)} %shard_map.39), channel_id=1, source_target_pairs={{4,0},{68,1},{132,2},{196,3},{260,4},{324,5},{388,6},{452,7},{12,8... | collective-permute-start | bytes 49160 | tf_op jit(solution)/shard_map/ppermute | solution.py:183
Sparse Core Ops, SparseCore 0:
  9.4 63.7 all-gather.3

commit v7 on v6

--- a/solution.py
+++ b/solution.py
@@ -52,45 +52,39 @@
 
 
 def project_kernel(mem_ref, *refs):
-    w_refs, (out_ref, mem_held, w_held, mem_sems, w_sems) = refs[:10], refs[10:]
+    w_refs, (out_ref, held, sems) = refs[:8], refs[8:]
     x, core = lax.axis_index("x"), lax.axis_index("c")
-    order = [(swapped, away) for away in (0, 3, 1, 2) for swapped in (0, 1)]
-    copies = []
-    for j, (swapped, away) in enumerate(order):
-        half = core if swapped == 0 else 1 - core
-        share = lax.rem(x + away, 4) * 2 + half
-        own, left, right, opp_k, opp_v = w_refs[5 * swapped : 5 * swapped + 5]
-        if away == 2:
-            pairs = [(opp_k, w_held.at[j, pl.ds(0, HD)]), (opp_v, w_held.at[j, pl.ds(HD, HD)])]
-        else:
-            pairs = [({0: own, 3: left, 1: right}[away], w_held.at[j])]
-        moves = [pltpu.make_async_copy(mem_ref.at[share], mem_held.at[j], mem_sems.at[j])]
-        moves += [pltpu.make_async_copy(src, dst, w_sems.at[j, i]) for i, (src, dst) in enumerate(pairs)]
-        for move in moves:
-            move.start()
-        copies.append(moves)
+    near, far, across = lax.rem(x + 3 + 2 * core, 4), lax.rem(x + 1 + 2 * core, 4), lax.rem(x + 2, 4)
+    shares = [
+        2 * x + core,
+        2 * x + 1 - core,
+        2 * near + core,
+        2 * near + 1 - core,
+        2 * across + core,
+        2 * far + 1 - core,
+        2 * far + core,
+        2 * across + 1 - core,
+    ]
+    copies = [pltpu.make_async_copy(mem_ref.at[share], held.at[j], sems.at[j]) for j, share in enumerate(shares)]
+    for copy in copies:
+        copy.start()
     total = None
-    for j, moves in enumerate(copies):
-        for move in moves:
-            move.wait()
-        part = lax.dot_general(mem_held[j], w_held[j], NT, preferred_element_type=jnp.float32)
+    for j, w_ref in enumerate(w_refs):
+        copies[j].wait()
+        part = lax.dot_general(held[j], w_ref[...], NT, preferred_element_type=jnp.float32)
         total = part if total is None else total + part
     out_ref[...] = total.astype(out_ref.dtype)
 
 
 def project(mem_all, w_pieces):
+    vmem = pl.BlockSpec(memory_space=pltpu.VMEM)
     return pl.pallas_call(
         project_kernel,
         out_shape=jax.ShapeDtypeStruct((256, 2 * HD), jnp.bfloat16),
-        in_specs=[pl.BlockSpec(memory_space=pl.ANY)] * 11,
-        out_specs=pl.BlockSpec(memory_space=pltpu.VMEM),
-        scratch_shapes=[
-            pltpu.VMEM(mem_all.shape, jnp.bfloat16),
-            pltpu.VMEM(mem_all.shape, jnp.bfloat16),
-            pltpu.SemaphoreType.DMA((8,)),
-            pltpu.SemaphoreType.DMA((8, 2)),
-        ],
-        compiler_params=pltpu.CompilerParams(vmem_limit_bytes=52 << 20),
+        in_specs=[pl.BlockSpec(memory_space=pl.ANY)] + [vmem] * 8,
+        out_specs=vmem,
+        scratch_shapes=[pltpu.VMEM(mem_all.shape, jnp.bfloat16), pltpu.SemaphoreType.DMA((8,))],
+        compiler_params=pltpu.CompilerParams(vmem_limit_bytes=50 << 20),
         cost_estimate=pl.CostEstimate(flops=2 * 256 * 256 * 8192, bytes_accessed=8 << 20, transcendentals=0),
     )(mem_all, *w_pieces)
 
@@ -153,13 +147,16 @@
     )(parts)
 
 
-def ring(value):
-    half = value.shape[0] // 2
-    left = lax.ppermute(value, "x", shift(4, 1))
-    right = lax.ppermute(value, "x", shift(4, -1))
-    opp_a = lax.ppermute(left[:half], "x", shift(4, 1))
-    opp_b = lax.ppermute(right[half:], "x", shift(4, -1))
-    return value, left, right, opp_a, opp_b
+def turn(value):
+    return lax.ppermute(value, ("x", "c"), [(2 * i + c, (i + 1 + 2 * c) % 4 * 2 + c) for i in range(4) for c in range(2)])
+
+
+def pieces_over_x(own):
+    first = turn(own)
+    own_swapped = swap(own)
+    across = turn(first)
+    second = turn(own_swapped)
+    return own, own_swapped, first, second, across, swap(first), swap(second), swap(across)
 
 
 def swap(value):
@@ -173,8 +170,8 @@
     both = lax.all_gather(jnp.concatenate([rows, query.reshape(8, 8 * HD)], axis=0), "y", axis=0)
     rows = both[:, :32].reshape(2 * HD, 8 * HD)
     query = both[:, 32:].reshape(512, HD)
-    w_pieces = ring(rows)
-    own = project(mem_all, (*w_pieces, *map(swap, w_pieces)))
+    w_pieces = pieces_over_x(rows)
+    own = project(mem_all, w_pieces)
 
     own = lax.all_gather(own, "x", axis=0, tiled=True)
     parts = attend(query, own, swap(own))

time: 153 us -> 153 us (level)
  waiting for transfers between devices: 19.1 us -> 13.4 us
  local copies, waits for them, and re-layouts: 1.88 us -> 4.26 us
    ppermute x4 -> x3, waiting for transfers between devices: 6.13 us -> 1.02 us  [turn(): lax.ppermute(value, ('x', 'c'), [(2 * i + c, (i + 1 + 2 * c) % 4 * 2 + c)...]
    ppermute x6 -> x5, starting transfers between devices: 26.1 us -> 28.8 us  [swap(): return lax.ppermute(value, 'c', SWAP)]
    unnamed x11 -> x9, local copies, waits for them, and re-layouts: 1.73 us -> 3.24 us
    ppermute x4 -> x3, starting transfers between devices: 13.7 us -> 12.4 us  [turn(): lax.ppermute(value, ('x', 'c'), [(2 * i + c, (i + 1 + 2 * c) % 4 * 2 + c)...]
  transfers between devices with their start and end apart: 14 -> 12, of which waited for: 4 -> 5; matrix products, arithmetic and copies ran while one was open for 0% -> 1% of each run, Pallas kernels for 0% -> 0%
where the time goes in v7:
time: 153 us
  starting transfers between devices  61 us (40%)
  blocking collectives  50.8 us (33%)
  between operations  13.6 us (9%)
  waiting for transfers between devices  13.4 us (9%)
  Pallas kernels  9.65 us (6%)
  local copies, waits for them, and re-layouts  4.26 us (3%)
    ppermute x5, starting transfers between devices, swap(): return lax.ppermute(value, 'c', SWAP)  28.8 us
    all_gather x1, blocking collectives, body(): lax.all_gather(jnp.concatenate([rows, query.reshape(8, 8 * HD)], axis=0),...  23.4 us
    all_to_all x1, blocking collectives, body(): parts = lax.all_to_all(parts, 'y', 0, 0, tiled=True)  17.4 us
    ppermute x1, starting transfers between devices, body(): rows = lax.ppermute(kv_weight, ALL, weight_moves())  13 us
    ppermute x3, starting transfers between devices, turn(): lax.ppermute(value, ('x', 'c'), [(2 * i + c, (i + 1 + 2 * c) % 4 * 2 + c)...  12.4 us
    all_gather x1, blocking collectives, body(): own = lax.all_gather(own, 'x', axis=0, tiled=True)  9.9 us
    ppermute x1, waiting for transfers between devices, body(): return lax.ppermute(result, ALL, [(b, a) for a, b in query_moves()])  6.37 us
    pallas_call x1, Pallas kernels, project(): pl.pallas_call(project_kernel, out_shape=jax.ShapeDtypeStruct((256, 2 * H...  5.18 us
  transfers between devices with their start and end apart: 12, of which 5 were waited for; matrix products, arithmetic and copies ran while one was open for 1% of the time, Pallas kernels for 0%

profile of v7, /device:TPU:1, one launch (start us, length us, event | category | flops | bytes accessed | tf_op | source)
XLA Modules:
  0.0 152.7 jit_solution(2641165722018311855)
XLA Ops:
  6.5 0.7 all-gather.4.cloned.1.call-update
  7.3 13.0 %collective-permute-start = (bf16[32,1024]{1,0:T(8,128)(2,1)}, bf16[32,1024]{1,0:T(8,128)(2,1)S(1)}, u32[]{:S(2)}, u32[]{:S(2)}) collective-permute-start(bf16[32,1024]{1,0:T(8,128)(2,1)} %param.4), channel_id=1, source_target_pairs={{0,4},{1,12},{2,20},{3,28},{4,36},{5,44},{6,52},{7,60},{8,68},{9,7... | collective-permute-start | bytes 196616 | tf_op jit(solution)/shard_map/ppermute | solution.py:168
  20.3 4.7 %collective-permute-start.1 = (bf16[64,128]{1,0:T(8,128)(2,1)}, bf16[64,128]{1,0:T(8,128)(2,1)S(1)}, u32[]{:S(2)}, u32[]{:S(2)}) collective-permute-start(bf16[64,128]{1,0:T(8,128)(2,1)} %param.5), channel_id=1, source_target_pairs={{0,4},{1,68},{2,132},{3,196},{4,260},{5,324},{6,388},{7,452},{8,12... | collective-permute-start | bytes 49160 | tf_op jit(solution)/shard_map/ppermute | solution.py:169
  25.0 4.1 %collective-permute-done.1 = bf16[64,128]{1,0:T(8,128)(2,1)S(1)} collective-permute-done((bf16[64,128]{1,0:T(8,128)(2,1)}, bf16[64,128]{1,0:T(8,128)(2,1)S(1)}, u32[]{:S(2)}, u32[]{:S(2)}) %collective-permute-start.1) | collective-permute-done | bytes 16416 | tf_op jit(solution)/shard_map/ppermute | solution.py:169
  29.1 0.0 collective-permute-done
  29.1 23.4 %all-gather = bf16[320,1024]{1,0:T(8,128)(2,1)S(1)} all-gather(bf16[40,1024]{1,0:T(8,128)(2,1)S(1)} %pad_maximum_fusion), channel_id=2, replica_groups=mesh['y'=8,'x'=4,'c'=2,'z'=8] {'y'}, dimensions={0}, use_global_device_ids=true | all-gather | bytes 737280 | tf_op jit(solution)/shard_map/all_gather | solution.py:170
  52.6 5.0 %collective-permute-start.3 = (bf16[256,1024]{1,0:T(8,128)(2,1)S(1)}, bf16[256,1024]{1,0:T(8,128)(2,1)S(1)}, u32[]{:S(2)}, u32[]{:S(2)}) collective-permute-start(bf16[256,1024]{1,0:T(8,128)(2,1)S(1)} %bitcast.3), channel_id=1, source_target_pairs={{0,16},{8,56},{16,32},{24,8},{32,48},{40,24},{48,0},{56,40},{1,17}... | collective-permute-start | bytes 1572872 | tf_op jit(solution)/shard_map/ppermute | solution.py:151
  57.6 5.1 %collective-permute-start.2 = (bf16[256,1024]{1,0:T(8,128)(2,1)S(1)}, bf16[256,1024]{1,0:T(8,128)(2,1)S(1)}, u32[]{:S(2)}, u32[]{:S(2)}) collective-permute-start(bf16[256,1024]{1,0:T(8,128)(2,1)S(1)} %bitcast.4), channel_id=1, source_target_pairs={{0,8},{8,0},{1,9},{9,1},{2,10},{10,2},{3,11},{11,3},{4,12},{12,4},... | collective-permute-start | bytes 1572872 | tf_op jit(solution)/shard_map/ppermute | solution.py:163
  62.7 1.0 collective-permute-done.3.refs_2_
  63.7 5.4 %collective-permute-start.5 = (bf16[256,1024]{1,0:T(8,128)(2,1)S(1)}, bf16[256,1024]{1,0:T(8,128)(2,1)S(1)}, u32[]{:S(2)}, u32[]{:S(2)}) collective-permute-start(bf16[256,1024]{1,0:T(8,128)(2,1)S(1)} %collective-permute-done.3.refs_2_), channel_id=1, source_target_pairs={{0,16},{8,56},{16,32},{24,8},{32,48},{40,24},{48,0},{56,40},{1,17}... | collective-permute-start | bytes 1572872 | tf_op jit(solution)/shard_map/ppermute | solution.py:151
  69.1 0.0 collective-permute-done.2.refs_1_
  69.2 1.9 %collective-permute-start.4 = (bf16[256,1024]{1,0:T(8,128)(2,1)S(1)}, bf16[256,1024]{1,0:T(8,128)(2,1)S(1)}, u32[]{:S(2)}, u32[]{:S(2)}) collective-permute-start(bf16[256,1024]{1,0:T(8,128)(2,1)S(1)} %collective-permute-done.2.refs_1_), channel_id=1, source_target_pairs={{0,16},{8,56},{16,32},{24,8},{32,48},{40,24},{48,0},{56,40},{1,17}... | collective-permute-start | bytes 1572872 | tf_op jit(solution)/shard_map/ppermute | solution.py:151
  71.1 5.3 %collective-permute-start.6 = (bf16[256,1024]{1,0:T(8,128)(2,1)S(1)}, bf16[256,1024]{1,0:T(8,128)(2,1)S(1)}, u32[]{:S(2)}, u32[]{:S(2)}) collective-permute-start(bf16[256,1024]{1,0:T(8,128)(2,1)S(1)} %collective-permute-done.3.refs_2_), channel_id=1, source_target_pairs={{0,8},{8,0},{1,9},{9,1},{2,10},{10,2},{3,11},{11,3},{4,12},{12,4},... | collective-permute-start | bytes 1572872 | tf_op jit(solution)/shard_map/ppermute | solution.py:163
  76.4 7.0 %collective-permute-start.8 = (bf16[256,1024]{1,0:T(8,128)(2,1)S(1)}, bf16[256,1024]{1,0:T(8,128)(2,1)S(1)}, u32[]{:S(2)}, u32[]{:S(2)}) collective-permute-start(bf16[256,1024]{1,0:T(8,128)(2,1)S(1)} %collective-permute-done.5.refs_4_), channel_id=1, source_target_pairs={{0,8},{8,0},{1,9},{9,1},{2,10},{10,2},{3,11},{11,3},{4,12},{12,4},... | collective-permute-start | bytes 1572872 | tf_op jit(solution)/shard_map/ppermute | solution.py:163
  83.4 5.6 %collective-permute-start.7 = (bf16[256,1024]{1,0:T(8,128)(2,1)S(1)}, bf16[256,1024]{1,0:T(8,128)(2,1)S(1)}, u32[]{:S(2)}, u32[]{:S(2)}) collective-permute-start(bf16[256,1024]{1,0:T(8,128)(2,1)S(1)} %collective-permute-done.4.refs_3_), channel_id=1, source_target_pairs={{0,8},{8,0},{1,9},{9,1},{2,10},{10,2},{3,11},{11,3},{4,12},{12,4},... | collective-permute-start | bytes 1572872 | tf_op jit(solution)/shard_map/ppermute | solution.py:163
  89.0 0.0 collective-permute-done.6.refs_5_
  89.0 0.8 copy-done.3
  89.8 0.7 collective-permute-done.7.refs_6_
  90.5 0.8 copy-done
  91.3 1.0 copy-done.1
  92.3 5.2 %shard_map.37 = bf16[256,256]{1,0:T(8,128)(2,1)S(1)} custom-call(bf16[8,256,1024]{2,1,0:T(8,128)(2,1)} %bitcast.6, bf16[256,1024]{1,0:T(8,128)(2,1)S(1)} %bitcast.5, bf16[256,1024]{1,0:T(8,128)(2,1)S(1)} %collective-permute-done.2.refs_1_, bf16[256,1024]{1,0:T(8,128)(2,1)S(1)} %collective-permute-done.3.refs_2_, ...), custom_call_target="tpu_custom_call" | custom-call | flops 1073741824 | bytes 8388608 | tf_op jit(solution)/shard_map/pallas_call | solution.py:81
  97.5 9.9 %all_gather.19.own = bf16[1024,256]{1,0:T(8,128)(2,1)S(1)} all-gather(bf16[256,256]{1,0:T(8,128)(2,1)S(1)} %shard_map.37), channel_id=1, replica_groups=mesh['y'=8,'x'=4,'c'=2,'z'=8] {'x'}, dimensions={0}, use_global_device_ids=true | all-gather | bytes 655360 | tf_op jit(solution)/shard_map/all_gather | solution.py:176
  107.4 5.8 %collective-permute-start.9 = (bf16[1024,256]{1,0:T(8,128)(2,1)S(1)}, bf16[1024,256]{1,0:T(8,128)(2,1)S(1)}, u32[]{:S(2)}, u32[]{:S(2)}) collective-permute-start(bf16[1024,256]{1,0:T(8,128)(2,1)S(1)} %all_gather.19.own), channel_id=1, source_target_pairs={{0,8},{8,0},{1,9},{9,1},{2,10},{10,2},{3,11},{11,3},{4,12},{12,4},... | collective-permute-start | bytes 1572872 | tf_op jit(solution)/shard_map/ppermute | solution.py:163
  113.3 0.9 slice.8
  114.2 0.1 reshape.10.q_ref
  114.2 0.5 collective-permute-done.9.other
  114.8 2.3 %shard_map.38 = f32[8,72,128]{2,1,0:T(8,128)S(1)} custom-call(bf16[512,128]{1,0:T(8,128)(2,1)S(1)} %reshape.10.q_ref, bf16[1024,256]{1,0:T(8,128)(2,1)S(1)} %all_gather.19.own, bf16[1024,256]{1,0:T(8,128)(2,1)S(1)} %collective-permute-done.9.other), custom_call_target="tpu_custom_call" | custom-call | flops 536870912 | bytes 2097152 | tf_op jit(solution)/shard_map/pallas_call | solution.py:121
  117.1 17.4 %all_to_all.5.part_ref = f32[8,72,128]{2,1,0:T(8,128)} all-to-all(f32[8,72,128]{2,1,0:T(8,128)S(1)} %shard_map.38), channel_id=1, replica_groups=mesh['y'=8,'x'=4,'c'=2,'z'=8] {'y'}, dimensions={0} | all-to-all | bytes 589824 | tf_op jit(solution)/shard_map/all_to_all | solution.py:178
  134.5 2.1 %shard_map.39 = bf16[64,128]{1,0:T(8,128)(2,1)} custom-call(f32[8,72,128]{2,1,0:T(8,128)} %all_to_all.5.part_ref), custom_call_target="tpu_custom_call" | custom-call | tf_op jit(solution)/shard_map/pallas_call | solution.py:144
  136.6 2.2 %collective-permute-start.10 = (bf16[64,128]{1,0:T(8,128)(2,1)}, bf16[64,128]{1,0:T(8,128)(2,1)S(1)}, u32[]{:S(2)}, u32[]{:S(2)}) collective-permute-start(bf16[64,128]{1,0:T(8,128)(2,1)} %shard_map.39), channel_id=1, source_target_pairs={{4,0},{68,1},{132,2},{196,3},{260,4},{324,5},{388,6},{452,7},{12,8... | collective-permute-start | bytes 49160 | tf_op jit(solution)/shard_map/ppermute | solution.py:180
  138.9 6.4 %collective-permute-done.10 = bf16[64,128]{1,0:T(8,128)(2,1)S(1)} collective-permute-done((bf16[64,128]{1,0:T(8,128)(2,1)}, bf16[64,128]{1,0:T(8,128)(2,1)S(1)}, u32[]{:S(2)}, u32[]{:S(2)}) %collective-permute-start.10) | collective-permute-done | bytes 16416 | tf_op jit(solution)/shard_map/ppermute | solution.py:180
  145.2 0.6 copy.5
  (13 shorter events, 0.1 us)
Async XLA Ops:
  6.5 84.8 %all-gather.4.cloned.1.call-start = ((), (), s32[]{:S(2)}) async-start(), calls=%async_computation.1 | async-start | bytes 4718592 | tf_op jit(solution)/shard_map/all_gather | solution.py:167
  7.3 21.8 %collective-permute-start = (bf16[32,1024]{1,0:T(8,128)(2,1)}, bf16[32,1024]{1,0:T(8,128)(2,1)S(1)}, u32[]{:S(2)}, u32[]{:S(2)}) collective-permute-start(bf16[32,1024]{1,0:T(8,128)(2,1)} %param.4), channel_id=1, source_target_pairs={{0,4},{1,12},{2,20},{3,28},{4,36},{5,44},{6,52},{7,60},{8,68},{9,7... | collective-permute-start | bytes 196616 | tf_op jit(solution)/shard_map/ppermute | solution.py:168
  20.3 8.8 %collective-permute-start.1 = (bf16[64,128]{1,0:T(8,128)(2,1)}, bf16[64,128]{1,0:T(8,128)(2,1)S(1)}, u32[]{:S(2)}, u32[]{:S(2)}) collective-permute-start(bf16[64,128]{1,0:T(8,128)(2,1)} %param.5), channel_id=1, source_target_pairs={{0,4},{1,68},{2,132},{3,196},{4,260},{5,324},{6,388},{7,452},{8,12... | collective-permute-start | bytes 49160 | tf_op jit(solution)/shard_map/ppermute | solution.py:169
  52.5 36.5 %copy-start.2 = (bf16[320,1024]{1,0:T(8,128)(2,1)}, bf16[320,1024]{1,0:T(8,128)(2,1)S(1)}, u32[]{:S(2)}) copy-start(bf16[320,1024]{1,0:T(8,128)(2,1)S(1)} %all-gather) | copy-start | bytes 1966084
  52.6 11.1 %collective-permute-start.3 = (bf16[256,1024]{1,0:T(8,128)(2,1)S(1)}, bf16[256,1024]{1,0:T(8,128)(2,1)S(1)}, u32[]{:S(2)}, u32[]{:S(2)}) collective-permute-start(bf16[256,1024]{1,0:T(8,128)(2,1)S(1)} %bitcast.3), channel_id=1, source_target_pairs={{0,16},{8,56},{16,32},{24,8},{32,48},{40,24},{48,0},{56,40},{1,17}... | collective-permute-start | bytes 1572872 | tf_op jit(solution)/shard_map/ppermute | solution.py:151
  57.6 11.5 %collective-permute-start.2 = (bf16[256,1024]{1,0:T(8,128)(2,1)S(1)}, bf16[256,1024]{1,0:T(8,128)(2,1)S(1)}, u32[]{:S(2)}, u32[]{:S(2)}) collective-permute-start(bf16[256,1024]{1,0:T(8,128)(2,1)S(1)} %bitcast.4), channel_id=1, source_target_pairs={{0,8},{8,0},{1,9},{9,1},{2,10},{10,2},{3,11},{11,3},{4,12},{12,4},... | collective-permute-start | bytes 1572872 | tf_op jit(solution)/shard_map/ppermute | solution.py:163
  63.7 12.6 %collective-permute-start.5 = (bf16[256,1024]{1,0:T(8,128)(2,1)S(1)}, bf16[256,1024]{1,0:T(8,128)(2,1)S(1)}, u32[]{:S(2)}, u32[]{:S(2)}) collective-permute-start(bf16[256,1024]{1,0:T(8,128)(2,1)S(1)} %collective-permute-done.3.refs_2_), channel_id=1, source_target_pairs={{0,16},{8,56},{16,32},{24,8},{32,48},{40,24},{48,0},{56,40},{1,17}... | collective-permute-start | bytes 1572872 | tf_op jit(solution)/shard_map/ppermute | solution.py:151
  69.2 14.2 %collective-permute-start.4 = (bf16[256,1024]{1,0:T(8,128)(2,1)S(1)}, bf16[256,1024]{1,0:T(8,128)(2,1)S(1)}, u32[]{:S(2)}, u32[]{:S(2)}) collective-permute-start(bf16[256,1024]{1,0:T(8,128)(2,1)S(1)} %collective-permute-done.2.refs_1_), channel_id=1, source_target_pairs={{0,16},{8,56},{16,32},{24,8},{32,48},{40,24},{48,0},{56,40},{1,17}... | collective-permute-start | bytes 1572872 | tf_op jit(solution)/shard_map/ppermute | solution.py:151
  71.1 17.9 %collective-permute-start.6 = (bf16[256,1024]{1,0:T(8,128)(2,1)S(1)}, bf16[256,1024]{1,0:T(8,128)(2,1)S(1)}, u32[]{:S(2)}, u32[]{:S(2)}) collective-permute-start(bf16[256,1024]{1,0:T(8,128)(2,1)S(1)} %collective-permute-done.3.refs_2_), channel_id=1, source_target_pairs={{0,8},{8,0},{1,9},{9,1},{2,10},{10,2},{3,11},{11,3},{4,12},{12,4},... | collective-permute-start | bytes 1572872 | tf_op jit(solution)/shard_map/ppermute | solution.py:163
  76.4 12.6 %collective-permute-start.8 = (bf16[256,1024]{1,0:T(8,128)(2,1)S(1)}, bf16[256,1024]{1,0:T(8,128)(2,1)S(1)}, u32[]{:S(2)}, u32[]{:S(2)}) collective-permute-start(bf16[256,1024]{1,0:T(8,128)(2,1)S(1)} %collective-permute-done.5.refs_4_), channel_id=1, source_target_pairs={{0,8},{8,0},{1,9},{9,1},{2,10},{10,2},{3,11},{11,3},{4,12},{12,4},... | collective-permute-start | bytes 1572872 | tf_op jit(solution)/shard_map/ppermute | solution.py:163
  83.4 7.1 %collective-permute-start.7 = (bf16[256,1024]{1,0:T(8,128)(2,1)S(1)}, bf16[256,1024]{1,0:T(8,128)(2,1)S(1)}, u32[]{:S(2)}, u32[]{:S(2)}) collective-permute-start(bf16[256,1024]{1,0:T(8,128)(2,1)S(1)} %collective-permute-done.4.refs_3_), channel_id=1, source_target_pairs={{0,8},{8,0},{1,9},{9,1},{2,10},{10,2},{3,11},{11,3},{4,12},{12,4},... | collective-permute-start | bytes 1572872 | tf_op jit(solution)/shard_map/ppermute | solution.py:163
  89.0 0.8 copy-start.3
  90.5 0.8 copy-start
  91.3 1.0 copy-start.1
  107.4 7.3 %collective-permute-start.9 = (bf16[1024,256]{1,0:T(8,128)(2,1)S(1)}, bf16[1024,256]{1,0:T(8,128)(2,1)S(1)}, u32[]{:S(2)}, u32[]{:S(2)}) collective-permute-start(bf16[1024,256]{1,0:T(8,128)(2,1)S(1)} %all_gather.19.own), channel_id=1, source_target_pairs={{0,8},{8,0},{1,9},{9,1},{2,10},{10,2},{3,11},{11,3},{4,12},{12,4},... | collective-permute-start | bytes 1572872 | tf_op jit(solution)/shard_map/ppermute | solution.py:163
  136.6 8.6 %collective-permute-start.10 = (bf16[64,128]{1,0:T(8,128)(2,1)}, bf16[64,128]{1,0:T(8,128)(2,1)S(1)}, u32[]{:S(2)}, u32[]{:S(2)}) collective-permute-start(bf16[64,128]{1,0:T(8,128)(2,1)} %shard_map.39), channel_id=1, source_target_pairs={{4,0},{68,1},{132,2},{196,3},{260,4},{324,5},{388,6},{452,7},{12,8... | collective-permute-start | bytes 49160 | tf_op jit(solution)/shard_map/ppermute | solution.py:180
Sparse Core Ops, SparseCore 0:
  9.4 63.7 all-gather.3

commit v8 on v5

--- a/solution.py
+++ b/solution.py
@@ -28,13 +28,18 @@
                 shard = y * 8 + x * 2 + c
                 kind, head, quarter = shard // 32, shard // 4 % 8, shard % 4
                 for z in range(8):
-                    moves.append((place(y, x, c, z), place(kind * 4 + quarter, z // 2, z % 2, head)))
+                    target = place(kind * 4 + quarter, z // 2, z % 2, (head + 4) % 8)
+                    moves.append((place(y, x, c, z), target))
     return moves
 
 
 def query_moves():
     return [
-        (place(y, x, c, z), place(z, x, c, y)) for y in range(8) for x in range(4) for c in range(2) for z in range(8)
+        (place(y, x, c, z), place(z, x, c, (y + 4) % 8))
+        for y in range(8)
+        for x in range(4)
+        for c in range(2)
+        for z in range(8)
     ]
 
 
@@ -56,21 +61,17 @@
         share = lax.rem(x + away, 4) * 2 + half
         copies.append(pltpu.make_async_copy(mem_ref.at[share], held.at[j], sems.at[j]))
         copies[j].start()
-    keys = values = None
+    total = None
     for j, (swapped, away) in enumerate(order):
         own, left, right, opp_k, opp_v = w_refs[5 * swapped : 5 * swapped + 5]
         if away == 2:
-            k_rows, v_rows = opp_k[...], opp_v[...]
+            w_rows = jnp.concatenate([opp_k[...], opp_v[...]], axis=0)
         else:
-            ref = {0: own, 3: left, 1: right}[away]
-            k_rows, v_rows = ref[:HD], ref[HD:]
+            w_rows = {0: own, 3: left, 1: right}[away][...]
         copies[j].wait()
-        k_part = lax.dot_general(held[j], k_rows, NT, preferred_element_type=jnp.float32)
-        v_part = lax.dot_general(held[j], v_rows, NT, preferred_element_type=jnp.float32)
-        keys = k_part if keys is None else keys + k_part
-        values = v_part if values is None else values + v_part
-    out_ref[:, :HD] = keys.astype(out_ref.dtype)
-    out_ref[:, HD:] = values.astype(out_ref.dtype)
+        part = lax.dot_general(held[j], w_rows, NT, preferred_element_type=jnp.float32)
+        total = part if total is None else total + part
+    out_ref[...] = total.astype(out_ref.dtype)
 
 
 def project(mem_all, w_pieces):
@@ -171,7 +172,7 @@
     parts = attend(query, own, swap(own))
     parts = lax.all_to_all(parts, "y", 0, 0, tiled=True)
     result = merge(parts)
-    return lax.ppermute(result, ALL, query_moves())
+    return lax.ppermute(result, ALL, [(b, a) for a, b in query_moves()])
 
 
 def solution(mesh):

time: 152 us -> 150 us (0.987)
  the two profiles are of different devices: /device:TPU:178 before, /device:TPU:1 now
where the time goes in v8:
time: 150 us; the launch traced here: 148 us
  blocking collectives  52 us (35%)
  starting transfers between devices  51.9 us (35%)
  waiting for transfers between devices  17.3 us (12%)
  between operations  13.6 us (9%)
  Pallas kernels  9.73 us (6%)
  local copies, waits for them, and re-layouts  3.29 us (2%)
    all_to_all x1, blocking collectives, spread(): return lax.all_to_all(copies, axis, 0, 0, tiled=True)  25.8 us
    ppermute x6, starting transfers between devices, swap(): return lax.ppermute(value, 'c', SWAP)  21.5 us
    all_to_all x1, blocking collectives, body(): parts = lax.all_to_all(parts, 'y', 0, 0, tiled=True)  15.6 us
    ppermute x1, starting transfers between devices, body(): rows = lax.ppermute(kv_weight, ALL, weight_moves())  13 us
    all_gather x1, blocking collectives, body(): own = lax.all_gather(own, 'x', axis=0, tiled=True)  10.5 us
    ppermute x1, waiting for transfers between devices, body(): return lax.ppermute(result, ALL, [(b, a) for a, b in query_moves()])  6.38 us
    pallas_call x1, Pallas kernels, project(): pl.pallas_call(project_kernel, out_shape=jax.ShapeDtypeStruct((256, 2 * H...  5.26 us
    ppermute x1, starting transfers between devices, body(): query = lax.ppermute(queries, ALL, query_moves())  4.65 us
  transfers between devices with their start and end apart: 14, of which 5 were waited for; matrix products, arithmetic and copies ran while one was open for 0% of the time, Pallas kernels for 0%

profile of v8, /device:TPU:1, one launch (start us, length us, event | category | flops | bytes accessed | tf_op | source)
XLA Modules:
  0.0 147.9 jit_solution(2601417228157915218)
XLA Ops:
  6.5 0.7 all-gather.3.cloned.1.call-update
  7.3 13.0 %collective-permute-start = (bf16[32,1024]{1,0:T(8,128)(2,1)}, bf16[32,1024]{1,0:T(8,128)(2,1)S(1)}, u32[]{:S(2)}, u32[]{:S(2)}) collective-permute-start(bf16[32,1024]{1,0:T(8,128)(2,1)} %param.4), channel_id=1, source_target_pairs={{0,4},{1,12},{2,20},{3,28},{4,36},{5,44},{6,52},{7,60},{8,68},{9,7... | collective-permute-start | bytes 196616 | tf_op jit(solution)/shard_map/ppermute | solution.py:163
  20.3 4.7 %collective-permute-start.1 = (bf16[64,128]{1,0:T(8,128)(2,1)}, bf16[64,128]{1,0:T(8,128)(2,1)S(1)}, u32[]{:S(2)}, u32[]{:S(2)}) collective-permute-start(bf16[64,128]{1,0:T(8,128)(2,1)} %param.5), channel_id=1, source_target_pairs={{0,4},{1,68},{2,132},{3,196},{4,260},{5,324},{6,388},{7,452},{8,12... | collective-permute-start | bytes 49160 | tf_op jit(solution)/shard_map/ppermute | solution.py:164
  25.0 4.1 %collective-permute-done.1 = bf16[64,128]{1,0:T(8,128)(2,1)S(1)} collective-permute-done((bf16[64,128]{1,0:T(8,128)(2,1)}, bf16[64,128]{1,0:T(8,128)(2,1)S(1)}, u32[]{:S(2)}, u32[]{:S(2)}) %collective-permute-start.1) | collective-permute-done | bytes 16416 | tf_op jit(solution)/shard_map/ppermute | solution.py:164
  29.1 0.0 collective-permute-done
  29.1 0.1 broadcast_in_dim.2
  29.2 25.8 %all_to_all.10 = bf16[8,40,1024]{2,1,0:T(8,128)(2,1)S(1)} all-to-all(bf16[8,40,1024]{2,1,0:T(8,128)(2,1)S(1)} %broadcast_in_dim.2), channel_id=1, replica_groups=mesh['y'=8,'x'=4,'c'=2,'z'=8] {'y'}, dimensions={0} | all-to-all | bytes 1310720 | tf_op jit(solution)/shard_map/all_to_all | solution.py:16
  55.0 2.1 %collective-permute-start.3 = (bf16[256,1024]{1,0:T(8,128)(2,1)S(1)}, bf16[256,1024]{1,0:T(8,128)(2,1)S(1)}, u32[]{:S(2)}, u32[]{:S(2)}) collective-permute-start(bf16[256,1024]{1,0:T(8,128)(2,1)S(1)} %bitcast.2), channel_id=1, source_target_pairs={{0,48},{16,0},{32,16},{48,32},{1,49},{17,1},{33,17},{49,33},{2,50}... | collective-permute-start | bytes 1572872 | tf_op jit(solution)/shard_map/ppermute | solution.py:151
  57.1 3.2 %collective-permute-start.2 = (bf16[256,1024]{1,0:T(8,128)(2,1)S(1)}, bf16[256,1024]{1,0:T(8,128)(2,1)S(1)}, u32[]{:S(2)}, u32[]{:S(2)}) collective-permute-start(bf16[256,1024]{1,0:T(8,128)(2,1)S(1)} %bitcast.3), channel_id=1, source_target_pairs={{0,16},{16,32},{32,48},{48,0},{1,17},{17,33},{33,49},{49,1},{2,18}... | collective-permute-start | bytes 1572872 | tf_op jit(solution)/shard_map/ppermute | solution.py:150
  60.3 4.5 %collective-permute-start.6 = (bf16[256,1024]{1,0:T(8,128)(2,1)S(1)}, bf16[256,1024]{1,0:T(8,128)(2,1)S(1)}, u32[]{:S(2)}, u32[]{:S(2)}) collective-permute-start(bf16[256,1024]{1,0:T(8,128)(2,1)S(1)} %bitcast.4), channel_id=1, source_target_pairs={{0,8},{8,0},{1,9},{9,1},{2,10},{10,2},{3,11},{11,3},{4,12},{12,4},... | collective-permute-start | bytes 1572872 | tf_op jit(solution)/shard_map/ppermute | solution.py:158
  64.8 3.6 %collective-permute-done.3.refs_2_ = bf16[256,1024]{1,0:T(8,128)(2,1)S(1)} collective-permute-done((bf16[256,1024]{1,0:T(8,128)(2,1)S(1)}, bf16[256,1024]{1,0:T(8,128)(2,1)S(1)}, u32[]{:S(2)}, u32[]{:S(2)}) %collective-permute-start.3) | collective-permute-done | bytes 524320 | tf_op jit(solution)/shard_map/ppermute | solution.py:151
  68.4 1.9 %collective-permute-start.5 = (bf16[128,1024]{1,0:T(8,128)(2,1)S(1)}, bf16[128,1024]{1,0:T(8,128)(2,1)S(1)}, u32[]{:S(2)}, u32[]{:S(2)}) collective-permute-start(bf16[128,1024]{1,0:T(8,128)(2,1)S(1)} %slice.19), channel_id=1, source_target_pairs={{0,48},{16,0},{32,16},{48,32},{1,49},{17,1},{33,17},{49,33},{2,50}... | collective-permute-start | bytes 786440 | tf_op jit(solution)/shard_map/ppermute | solution.py:153
  70.4 3.4 %collective-permute-start.4 = (bf16[128,1024]{1,0:T(8,128)(2,1)S(1)}, bf16[128,1024]{1,0:T(8,128)(2,1)S(1)}, u32[]{:S(2)}, u32[]{:S(2)}) collective-permute-start(bf16[128,1024]{1,0:T(8,128)(2,1)S(1)} %slice.18), channel_id=1, source_target_pairs={{0,16},{16,32},{32,48},{48,0},{1,17},{17,33},{33,49},{49,1},{2,18}... | collective-permute-start | bytes 786440 | tf_op jit(solution)/shard_map/ppermute | solution.py:152
  73.7 5.3 %collective-permute-start.8 = (bf16[256,1024]{1,0:T(8,128)(2,1)S(1)}, bf16[256,1024]{1,0:T(8,128)(2,1)S(1)}, u32[]{:S(2)}, u32[]{:S(2)}) collective-permute-start(bf16[256,1024]{1,0:T(8,128)(2,1)S(1)} %collective-permute-done.3.refs_2_), channel_id=1, source_target_pairs={{0,8},{8,0},{1,9},{9,1},{2,10},{10,2},{3,11},{11,3},{4,12},{12,4},... | collective-permute-start | bytes 1572872 | tf_op jit(solution)/shard_map/ppermute | solution.py:158
  79.1 1.9 %collective-permute-start.7 = (bf16[256,1024]{1,0:T(8,128)(2,1)S(1)}, bf16[256,1024]{1,0:T(8,128)(2,1)S(1)}, u32[]{:S(2)}, u32[]{:S(2)}) collective-permute-start(bf16[256,1024]{1,0:T(8,128)(2,1)S(1)} %collective-permute-done.2.refs_1_), channel_id=1, source_target_pairs={{0,8},{8,0},{1,9},{9,1},{2,10},{10,2},{3,11},{11,3},{4,12},{12,4},... | collective-permute-start | bytes 1572872 | tf_op jit(solution)/shard_map/ppermute | solution.py:158
  81.0 2.4 %collective-permute-start.10 = (bf16[128,1024]{1,0:T(8,128)(2,1)S(1)}, bf16[128,1024]{1,0:T(8,128)(2,1)S(1)}, u32[]{:S(2)}, u32[]{:S(2)}) collective-permute-start(bf16[128,1024]{1,0:T(8,128)(2,1)S(1)} %collective-permute-done.5.refs_4_), channel_id=1, source_target_pairs={{0,8},{8,0},{1,9},{9,1},{2,10},{10,2},{3,11},{11,3},{4,12},{12,4},... | collective-permute-start | bytes 786440 | tf_op jit(solution)/shard_map/ppermute | solution.py:158
  83.4 2.8 %collective-permute-start.9 = (bf16[128,1024]{1,0:T(8,128)(2,1)S(1)}, bf16[128,1024]{1,0:T(8,128)(2,1)S(1)}, u32[]{:S(2)}, u32[]{:S(2)}) collective-permute-start(bf16[128,1024]{1,0:T(8,128)(2,1)S(1)} %collective-permute-done.4.refs_3_), channel_id=1, source_target_pairs={{0,8},{8,0},{1,9},{9,1},{2,10},{10,2},{3,11},{11,3},{4,12},{12,4},... | collective-permute-start | bytes 786440 | tf_op jit(solution)/shard_map/ppermute | solution.py:158
  86.3 1.1 collective-permute-done.9.refs_8_
  87.4 0.7 copy-done
  88.1 0.8 copy-done.3
  88.9 0.9 copy-done.1
  89.9 5.3 %shard_map.37 = bf16[256,256]{1,0:T(8,128)(2,1)S(1)} custom-call(bf16[8,256,1024]{2,1,0:T(8,128)(2,1)} %bitcast.6, bf16[256,1024]{1,0:T(8,128)(2,1)S(1)} %bitcast.5, bf16[256,1024]{1,0:T(8,128)(2,1)S(1)} %collective-permute-done.2.refs_1_, bf16[256,1024]{1,0:T(8,128)(2,1)S(1)} %collective-permute-done.3.refs_2_, ...), custom_call_target="tpu_custom_call" | custom-call | flops 1073741824 | bytes 8388608 | tf_op jit(solution)/shard_map/pallas_call | solution.py:79
  95.2 10.5 %all_gather.11.own = bf16[1024,256]{1,0:T(8,128)(2,1)S(1)} all-gather(bf16[256,256]{1,0:T(8,128)(2,1)S(1)} %shard_map.37), channel_id=1, replica_groups=mesh['y'=8,'x'=4,'c'=2,'z'=8] {'x'}, dimensions={0}, use_global_device_ids=true | all-gather | bytes 655360 | tf_op jit(solution)/shard_map/all_gather | solution.py:171
  105.7 4.5 %collective-permute-start.11 = (bf16[1024,256]{1,0:T(8,128)(2,1)S(1)}, bf16[1024,256]{1,0:T(8,128)(2,1)S(1)}, u32[]{:S(2)}, u32[]{:S(2)}) collective-permute-start(bf16[1024,256]{1,0:T(8,128)(2,1)S(1)} %all_gather.11.own), channel_id=1, source_target_pairs={{0,8},{8,0},{1,9},{9,1},{2,10},{10,2},{3,11},{11,3},{4,12},{12,4},... | collective-permute-start | bytes 1572872 | tf_op jit(solution)/shard_map/ppermute | solution.py:158
  110.2 0.1 reshape.11.q_ref
  110.3 1.4 collective-permute-done.11.other
  111.7 2.3 %shard_map.38 = f32[8,72,128]{2,1,0:T(8,128)S(1)} custom-call(bf16[512,128]{1,0:T(8,128)(2,1)S(1)} %reshape.11.q_ref, bf16[1024,256]{1,0:T(8,128)(2,1)S(1)} %all_gather.11.own, bf16[1024,256]{1,0:T(8,128)(2,1)S(1)} %collective-permute-done.11.other), custom_call_target="tpu_custom_call" | custom-call | flops 536870912 | bytes 2097152 | tf_op jit(solution)/shard_map/pallas_call | solution.py:119
  114.1 15.6 %all_to_all.11.part_ref = f32[8,72,128]{2,1,0:T(8,128)} all-to-all(f32[8,72,128]{2,1,0:T(8,128)S(1)} %shard_map.38), channel_id=1, replica_groups=mesh['y'=8,'x'=4,'c'=2,'z'=8] {'y'}, dimensions={0} | all-to-all | bytes 589824 | tf_op jit(solution)/shard_map/all_to_all | solution.py:173
  129.7 2.1 %shard_map.39 = bf16[64,128]{1,0:T(8,128)(2,1)} custom-call(f32[8,72,128]{2,1,0:T(8,128)} %all_to_all.11.part_ref), custom_call_target="tpu_custom_call" | custom-call | tf_op jit(solution)/shard_map/pallas_call | solution.py:142
  131.9 2.2 %collective-permute-start.12 = (bf16[64,128]{1,0:T(8,128)(2,1)}, bf16[64,128]{1,0:T(8,128)(2,1)S(1)}, u32[]{:S(2)}, u32[]{:S(2)}) collective-permute-start(bf16[64,128]{1,0:T(8,128)(2,1)} %shard_map.39), channel_id=1, source_target_pairs={{4,0},{68,1},{132,2},{196,3},{260,4},{324,5},{388,6},{452,7},{12,8... | collective-permute-start | bytes 49160 | tf_op jit(solution)/shard_map/ppermute | solution.py:175
  134.1 6.4 %collective-permute-done.12 = bf16[64,128]{1,0:T(8,128)(2,1)S(1)} collective-permute-done((bf16[64,128]{1,0:T(8,128)(2,1)}, bf16[64,128]{1,0:T(8,128)(2,1)S(1)}, u32[]{:S(2)}, u32[]{:S(2)}) %collective-permute-start.12) | collective-permute-done | bytes 16416 | tf_op jit(solution)/shard_map/ppermute | solution.py:175
  140.4 0.6 copy.5
  (21 shorter events, 0.1 us)
Async XLA Ops:
  6.5 82.4 %all-gather.3.cloned.1.call-start = ((), (), s32[]{:S(2)}) async-start(), calls=%async_computation.2 | async-start | bytes 4718592 | tf_op jit(solution)/shard_map/all_gather | solution.py:162
  7.3 21.8 %collective-permute-start = (bf16[32,1024]{1,0:T(8,128)(2,1)}, bf16[32,1024]{1,0:T(8,128)(2,1)S(1)}, u32[]{:S(2)}, u32[]{:S(2)}) collective-permute-start(bf16[32,1024]{1,0:T(8,128)(2,1)} %param.4), channel_id=1, source_target_pairs={{0,4},{1,12},{2,20},{3,28},{4,36},{5,44},{6,52},{7,60},{8,68},{9,7... | collective-permute-start | bytes 196616 | tf_op jit(solution)/shard_map/ppermute | solution.py:163
  20.3 8.8 %collective-permute-start.1 = (bf16[64,128]{1,0:T(8,128)(2,1)}, bf16[64,128]{1,0:T(8,128)(2,1)S(1)}, u32[]{:S(2)}, u32[]{:S(2)}) collective-permute-start(bf16[64,128]{1,0:T(8,128)(2,1)} %param.5), channel_id=1, source_target_pairs={{0,4},{1,68},{2,132},{3,196},{4,260},{5,324},{6,388},{7,452},{8,12... | collective-permute-start | bytes 49160 | tf_op jit(solution)/shard_map/ppermute | solution.py:164
  55.0 33.2 %copy-start.2 = (bf16[8,40,1024]{2,1,0:T(8,128)(2,1)}, bf16[8,40,1024]{2,1,0:T(8,128)(2,1)S(1)}, u32[]{:S(2)}) copy-start(bf16[8,40,1024]{2,1,0:T(8,128)(2,1)S(1)} %all_to_all.10) | copy-start | bytes 1966084
  55.0 13.4 %collective-permute-start.3 = (bf16[256,1024]{1,0:T(8,128)(2,1)S(1)}, bf16[256,1024]{1,0:T(8,128)(2,1)S(1)}, u32[]{:S(2)}, u32[]{:S(2)}) collective-permute-start(bf16[256,1024]{1,0:T(8,128)(2,1)S(1)} %bitcast.2), channel_id=1, source_target_pairs={{0,48},{16,0},{32,16},{48,32},{1,49},{17,1},{33,17},{49,33},{2,50}... | collective-permute-start | bytes 1572872 | tf_op jit(solution)/shard_map/ppermute | solution.py:151
  57.1 13.2 %collective-permute-start.2 = (bf16[256,1024]{1,0:T(8,128)(2,1)S(1)}, bf16[256,1024]{1,0:T(8,128)(2,1)S(1)}, u32[]{:S(2)}, u32[]{:S(2)}) collective-permute-start(bf16[256,1024]{1,0:T(8,128)(2,1)S(1)} %bitcast.3), channel_id=1, source_target_pairs={{0,16},{16,32},{32,48},{48,0},{1,17},{17,33},{33,49},{49,1},{2,18}... | collective-permute-start | bytes 1572872 | tf_op jit(solution)/shard_map/ppermute | solution.py:150
  60.3 26.0 %collective-permute-start.6 = (bf16[256,1024]{1,0:T(8,128)(2,1)S(1)}, bf16[256,1024]{1,0:T(8,128)(2,1)S(1)}, u32[]{:S(2)}, u32[]{:S(2)}) collective-permute-start(bf16[256,1024]{1,0:T(8,128)(2,1)S(1)} %bitcast.4), channel_id=1, source_target_pairs={{0,8},{8,0},{1,9},{9,1},{2,10},{10,2},{3,11},{11,3},{4,12},{12,4},... | collective-permute-start | bytes 1572872 | tf_op jit(solution)/shard_map/ppermute | solution.py:158
  68.4 12.6 %collective-permute-start.5 = (bf16[128,1024]{1,0:T(8,128)(2,1)S(1)}, bf16[128,1024]{1,0:T(8,128)(2,1)S(1)}, u32[]{:S(2)}, u32[]{:S(2)}) collective-permute-start(bf16[128,1024]{1,0:T(8,128)(2,1)S(1)} %slice.19), channel_id=1, source_target_pairs={{0,48},{16,0},{32,16},{48,32},{1,49},{17,1},{33,17},{49,33},{2,50}... | collective-permute-start | bytes 786440 | tf_op jit(solution)/shard_map/ppermute | solution.py:153
  70.4 13.1 %collective-permute-start.4 = (bf16[128,1024]{1,0:T(8,128)(2,1)S(1)}, bf16[128,1024]{1,0:T(8,128)(2,1)S(1)}, u32[]{:S(2)}, u32[]{:S(2)}) collective-permute-start(bf16[128,1024]{1,0:T(8,128)(2,1)S(1)} %slice.18), channel_id=1, source_target_pairs={{0,16},{16,32},{32,48},{48,0},{1,17},{17,33},{33,49},{49,1},{2,18}... | collective-permute-start | bytes 786440 | tf_op jit(solution)/shard_map/ppermute | solution.py:152
  73.7 14.4 %collective-permute-start.8 = (bf16[256,1024]{1,0:T(8,128)(2,1)S(1)}, bf16[256,1024]{1,0:T(8,128)(2,1)S(1)}, u32[]{:S(2)}, u32[]{:S(2)}) collective-permute-start(bf16[256,1024]{1,0:T(8,128)(2,1)S(1)} %collective-permute-done.3.refs_2_), channel_id=1, source_target_pairs={{0,8},{8,0},{1,9},{9,1},{2,10},{10,2},{3,11},{11,3},{4,12},{12,4},... | collective-permute-start | bytes 1572872 | tf_op jit(solution)/shard_map/ppermute | solution.py:158
  79.1 9.9 %collective-permute-start.7 = (bf16[256,1024]{1,0:T(8,128)(2,1)S(1)}, bf16[256,1024]{1,0:T(8,128)(2,1)S(1)}, u32[]{:S(2)}, u32[]{:S(2)}) collective-permute-start(bf16[256,1024]{1,0:T(8,128)(2,1)S(1)} %collective-permute-done.2.refs_1_), channel_id=1, source_target_pairs={{0,8},{8,0},{1,9},{9,1},{2,10},{10,2},{3,11},{11,3},{4,12},{12,4},... | collective-permute-start | bytes 1572872 | tf_op jit(solution)/shard_map/ppermute | solution.py:158
  81.0 5.3 %collective-permute-start.10 = (bf16[128,1024]{1,0:T(8,128)(2,1)S(1)}, bf16[128,1024]{1,0:T(8,128)(2,1)S(1)}, u32[]{:S(2)}, u32[]{:S(2)}) collective-permute-start(bf16[128,1024]{1,0:T(8,128)(2,1)S(1)} %collective-permute-done.5.refs_4_), channel_id=1, source_target_pairs={{0,8},{8,0},{1,9},{9,1},{2,10},{10,2},{3,11},{11,3},{4,12},{12,4},... | collective-permute-start | bytes 786440 | tf_op jit(solution)/shard_map/ppermute | solution.py:158
  83.4 4.0 %collective-permute-start.9 = (bf16[128,1024]{1,0:T(8,128)(2,1)S(1)}, bf16[128,1024]{1,0:T(8,128)(2,1)S(1)}, u32[]{:S(2)}, u32[]{:S(2)}) collective-permute-start(bf16[128,1024]{1,0:T(8,128)(2,1)S(1)} %collective-permute-done.4.refs_3_), channel_id=1, source_target_pairs={{0,8},{8,0},{1,9},{9,1},{2,10},{10,2},{3,11},{11,3},{4,12},{12,4},... | collective-permute-start | bytes 786440 | tf_op jit(solution)/shard_map/ppermute | solution.py:158
  87.4 0.7 copy-start
  88.1 0.8 copy-start.3
  88.9 1.0 copy-start.1
  89.9 20.3 %slice-start = ((bf16[8,40,1024]{2,1,0:T(8,128)(2,1)}), bf16[8,8,1024]{2,1,0:T(8,128)(2,1)S(1)}, s32[]{:S(2)}) async-start(bf16[8,40,1024]{2,1,0:T(8,128)(2,1)} %copy-done.2), calls=%async_computation.3 | async-start | bytes 262144 | tf_op jit(solution)/shard_map/slice | solution.py:167
  105.7 6.0 %collective-permute-start.11 = (bf16[1024,256]{1,0:T(8,128)(2,1)S(1)}, bf16[1024,256]{1,0:T(8,128)(2,1)S(1)}, u32[]{:S(2)}, u32[]{:S(2)}) collective-permute-start(bf16[1024,256]{1,0:T(8,128)(2,1)S(1)} %all_gather.11.own), channel_id=1, source_target_pairs={{0,8},{8,0},{1,9},{9,1},{2,10},{10,2},{3,11},{11,3},{4,12},{12,4},... | collective-permute-start | bytes 1572872 | tf_op jit(solution)/shard_map/ppermute | solution.py:158
  131.9 8.6 %collective-permute-start.12 = (bf16[64,128]{1,0:T(8,128)(2,1)}, bf16[64,128]{1,0:T(8,128)(2,1)S(1)}, u32[]{:S(2)}, u32[]{:S(2)}) collective-permute-start(bf16[64,128]{1,0:T(8,128)(2,1)} %shard_map.39), channel_id=1, source_target_pairs={{4,0},{68,1},{132,2},{196,3},{260,4},{324,5},{388,6},{452,7},{12,8... | collective-permute-start | bytes 49160 | tf_op jit(solution)/shard_map/ppermute | solution.py:175
Sparse Core Ops, SparseCore 0:
  9.4 63.7 all-gather.2

commit v9 on v8

--- a/solution.py
+++ b/solution.py
@@ -59,8 +59,10 @@
     for j, (swapped, away) in enumerate(order):
         half = core if swapped == 0 else 1 - core
         share = lax.rem(x + away, 4) * 2 + half
-        copies.append(pltpu.make_async_copy(mem_ref.at[share], held.at[j], sems.at[j]))
-        copies[j].start()
+        for i in range(4):
+            part = pl.ds(64 * i, 64)
+            copies.append(pltpu.make_async_copy(mem_ref.at[share, part], held.at[j, part], sems.at[j, i]))
+            copies[-1].start()
     total = None
     for j, (swapped, away) in enumerate(order):
         own, left, right, opp_k, opp_v = w_refs[5 * swapped : 5 * swapped + 5]
@@ -68,7 +70,8 @@
             w_rows = jnp.concatenate([opp_k[...], opp_v[...]], axis=0)
         else:
             w_rows = {0: own, 3: left, 1: right}[away][...]
-        copies[j].wait()
+        for copy in copies[4 * j : 4 * j + 4]:
+            copy.wait()
         part = lax.dot_general(held[j], w_rows, NT, preferred_element_type=jnp.float32)
         total = part if total is None else total + part
     out_ref[...] = total.astype(out_ref.dtype)
@@ -81,8 +84,8 @@
         out_shape=jax.ShapeDtypeStruct((256, 2 * HD), jnp.bfloat16),
         in_specs=[pl.BlockSpec(memory_space=pl.ANY)] + [vmem] * 10,
         out_specs=vmem,
-        scratch_shapes=[pltpu.VMEM(mem_all.shape, jnp.bfloat16), pltpu.SemaphoreType.DMA((8,))],
-        compiler_params=pltpu.CompilerParams(vmem_limit_bytes=50 << 20),
+        scratch_shapes=[pltpu.VMEM(mem_all.shape, jnp.bfloat16), pltpu.SemaphoreType.DMA((8, 4))],
+        compiler_params=pltpu.CompilerParams(vmem_limit_bytes=46 << 20),
         cost_estimate=pl.CostEstimate(flops=2 * 256 * 256 * 8192, bytes_accessed=8 << 20, transcendentals=0),
     )(mem_all, *w_pieces)
 
@@ -165,7 +168,9 @@
     both = spread(jnp.concatenate([rows, query.reshape(8, 8 * HD)], axis=0), "y")
     rows = both[:, :32].reshape(2 * HD, 8 * HD)
     query = both[:, 32:].reshape(512, HD)
-    w_pieces = ring(rows)
+    *w_pieces, opp_k, opp_v = ring(rows)
+    opp_k, opp_v, mem_all = lax.optimization_barrier((opp_k, opp_v, mem_all))
+    w_pieces += [opp_k, opp_v]
     own = project(mem_all, (*w_pieces, *map(swap, w_pieces)))
 
     own = lax.all_gather(own, "x", axis=0, tiled=True)

time: 150 us -> 149 us (level)
  waiting for transfers between devices: 17.3 us -> 22.2 us
  local copies, waits for them, and re-layouts: 3.29 us -> 0.82 us
  starting transfers between devices: 51.9 us -> 49.6 us
    ppermute x1, waiting for transfers between devices: 3.56 us -> 8.08 us  [ring(): right = lax.ppermute(value, 'x', shift(4, -1))]
    unnamed x9 -> x3, local copies, waits for them, and re-layouts: 3.08 us -> 0.61 us
    ppermute x6, starting transfers between devices: 21.5 us -> 19.2 us  [swap(): return lax.ppermute(value, 'c', SWAP)]
where the time goes in v9:
time: 149 us; the launch traced here: 148 us
  blocking collectives  51.8 us (35%)
  starting transfers between devices  49.6 us (33%)
  waiting for transfers between devices  22.2 us (15%)
  between operations  13.6 us (9%)
  Pallas kernels  9.93 us (7%)
    all_to_all x1, blocking collectives, spread(): return lax.all_to_all(copies, axis, 0, 0, tiled=True)  25.8 us
    ppermute x6, starting transfers between devices, swap(): return lax.ppermute(value, 'c', SWAP)  19.2 us
    all_to_all x1, blocking collectives, body(): parts = lax.all_to_all(parts, 'y', 0, 0, tiled=True)  15.6 us
    ppermute x1, starting transfers between devices, body(): rows = lax.ppermute(kv_weight, ALL, weight_moves())  13 us
    all_gather x1, blocking collectives, body(): own = lax.all_gather(own, 'x', axis=0, tiled=True)  10.3 us
    ppermute x1, waiting for transfers between devices, ring(): right = lax.ppermute(value, 'x', shift(4, -1))  8.08 us
    ppermute x1, waiting for transfers between devices, body(): return lax.ppermute(result, ALL, [(b, a) for a, b in query_moves()])  6.36 us
    pallas_call x1, Pallas kernels, project(): pl.pallas_call(project_kernel, out_shape=jax.ShapeDtypeStruct((256, 2 * H...  5.46 us
  transfers between devices with their start and end apart: 14, of which 5 were waited for; matrix products, arithmetic and copies ran while one was open for 0% of the time, Pallas kernels for 0%

profile of v9, /device:TPU:1, one launch (start us, length us, event | category | flops | bytes accessed | tf_op | source)
XLA Modules:
  0.0 148.0 jit_solution(11851690408516843046)
XLA Ops:
  6.5 0.7 all-gather.3.cloned.1.call-update
  7.3 13.0 %collective-permute-start = (bf16[32,1024]{1,0:T(8,128)(2,1)}, bf16[32,1024]{1,0:T(8,128)(2,1)S(1)}, u32[]{:S(2)}, u32[]{:S(2)}) collective-permute-start(bf16[32,1024]{1,0:T(8,128)(2,1)} %param.4), channel_id=1, source_target_pairs={{0,4},{1,12},{2,20},{3,28},{4,36},{5,44},{6,52},{7,60},{8,68},{9,7... | collective-permute-start | bytes 196616 | tf_op jit(solution)/shard_map/ppermute | solution.py:166
  20.3 4.7 %collective-permute-start.1 = (bf16[64,128]{1,0:T(8,128)(2,1)}, bf16[64,128]{1,0:T(8,128)(2,1)S(1)}, u32[]{:S(2)}, u32[]{:S(2)}) collective-permute-start(bf16[64,128]{1,0:T(8,128)(2,1)} %param.5), channel_id=1, source_target_pairs={{0,4},{1,68},{2,132},{3,196},{4,260},{5,324},{6,388},{7,452},{8,12... | collective-permute-start | bytes 49160 | tf_op jit(solution)/shard_map/ppermute | solution.py:167
  25.0 4.1 %collective-permute-done.1 = bf16[64,128]{1,0:T(8,128)(2,1)S(1)} collective-permute-done((bf16[64,128]{1,0:T(8,128)(2,1)}, bf16[64,128]{1,0:T(8,128)(2,1)S(1)}, u32[]{:S(2)}, u32[]{:S(2)}) %collective-permute-start.1) | collective-permute-done | bytes 16416 | tf_op jit(solution)/shard_map/ppermute | solution.py:167
  29.1 0.0 collective-permute-done
  29.1 0.1 broadcast_in_dim.2
  29.2 25.8 %all_to_all.10 = bf16[8,40,1024]{2,1,0:T(8,128)(2,1)S(1)} all-to-all(bf16[8,40,1024]{2,1,0:T(8,128)(2,1)S(1)} %broadcast_in_dim.2), channel_id=1, replica_groups=mesh['y'=8,'x'=4,'c'=2,'z'=8] {'y'}, dimensions={0} | all-to-all | bytes 1310720 | tf_op jit(solution)/shard_map/all_to_all | solution.py:16
  55.0 2.1 %collective-permute-start.4 = (bf16[256,1024]{1,0:T(8,128)(2,1)S(1)}, bf16[256,1024]{1,0:T(8,128)(2,1)S(1)}, u32[]{:S(2)}, u32[]{:S(2)}) collective-permute-start(bf16[256,1024]{1,0:T(8,128)(2,1)S(1)} %bitcast.2), channel_id=1, source_target_pairs={{0,48},{16,0},{32,16},{48,32},{1,49},{17,1},{33,17},{49,33},{2,50}... | collective-permute-start | bytes 1572872 | tf_op jit(solution)/shard_map/ppermute | solution.py:154
  57.1 3.2 %collective-permute-start.2 = (bf16[256,1024]{1,0:T(8,128)(2,1)S(1)}, bf16[256,1024]{1,0:T(8,128)(2,1)S(1)}, u32[]{:S(2)}, u32[]{:S(2)}) collective-permute-start(bf16[256,1024]{1,0:T(8,128)(2,1)S(1)} %bitcast.3), channel_id=1, source_target_pairs={{0,16},{16,32},{32,48},{48,0},{1,17},{17,33},{33,49},{49,1},{2,18}... | collective-permute-start | bytes 1572872 | tf_op jit(solution)/shard_map/ppermute | solution.py:153
  60.3 8.1 %collective-permute-done.4.refs_2_ = bf16[256,1024]{1,0:T(8,128)(2,1)S(1)} collective-permute-done((bf16[256,1024]{1,0:T(8,128)(2,1)S(1)}, bf16[256,1024]{1,0:T(8,128)(2,1)S(1)}, u32[]{:S(2)}, u32[]{:S(2)}) %collective-permute-start.4) | collective-permute-done | bytes 524320 | tf_op jit(solution)/shard_map/ppermute | solution.py:154
  68.4 1.9 %collective-permute-start.5 = (bf16[128,1024]{1,0:T(8,128)(2,1)S(1)}, bf16[128,1024]{1,0:T(8,128)(2,1)S(1)}, u32[]{:S(2)}, u32[]{:S(2)}) collective-permute-start(bf16[128,1024]{1,0:T(8,128)(2,1)S(1)} %slice.19), channel_id=1, source_target_pairs={{0,48},{16,0},{32,16},{48,32},{1,49},{17,1},{33,17},{49,33},{2,50}... | collective-permute-start | bytes 786440 | tf_op jit(solution)/shard_map/ppermute | solution.py:156
  70.3 0.0 collective-permute-done.2.refs_1_
  70.4 3.4 %collective-permute-start.3 = (bf16[128,1024]{1,0:T(8,128)(2,1)S(1)}, bf16[128,1024]{1,0:T(8,128)(2,1)}, u32[]{:S(2)}, u32[]{:S(2)}) collective-permute-start(bf16[128,1024]{1,0:T(8,128)(2,1)S(1)} %slice.18), channel_id=1, source_target_pairs={{0,16},{16,32},{32,48},{48,0},{1,17},{17,33},{33,49},{49,1},{2,18}... | collective-permute-start | bytes 786440 | tf_op jit(solution)/shard_map/ppermute | solution.py:155
  73.7 5.3 %collective-permute-start.6 = (bf16[256,1024]{1,0:T(8,128)(2,1)S(1)}, bf16[256,1024]{1,0:T(8,128)(2,1)S(1)}, u32[]{:S(2)}, u32[]{:S(2)}) collective-permute-start(bf16[256,1024]{1,0:T(8,128)(2,1)S(1)} %bitcast.4), channel_id=1, source_target_pairs={{0,8},{8,0},{1,9},{9,1},{2,10},{10,2},{3,11},{11,3},{4,12},{12,4},... | collective-permute-start | bytes 1572872 | tf_op jit(solution)/shard_map/ppermute | solution.py:161
  79.1 1.9 %collective-permute-start.8 = (bf16[256,1024]{1,0:T(8,128)(2,1)S(1)}, bf16[256,1024]{1,0:T(8,128)(2,1)S(1)}, u32[]{:S(2)}, u32[]{:S(2)}) collective-permute-start(bf16[256,1024]{1,0:T(8,128)(2,1)S(1)} %collective-permute-done.4.refs_2_), channel_id=1, source_target_pairs={{0,8},{8,0},{1,9},{9,1},{2,10},{10,2},{3,11},{11,3},{4,12},{12,4},... | collective-permute-start | bytes 1572872 | tf_op jit(solution)/shard_map/ppermute | solution.py:161
  81.0 2.4 %collective-permute-start.7 = (bf16[256,1024]{1,0:T(8,128)(2,1)S(1)}, bf16[256,1024]{1,0:T(8,128)(2,1)S(1)}, u32[]{:S(2)}, u32[]{:S(2)}) collective-permute-start(bf16[256,1024]{1,0:T(8,128)(2,1)S(1)} %collective-permute-done.2.refs_1_), channel_id=1, source_target_pairs={{0,8},{8,0},{1,9},{9,1},{2,10},{10,2},{3,11},{11,3},{4,12},{12,4},... | collective-permute-start | bytes 1572872 | tf_op jit(solution)/shard_map/ppermute | solution.py:161
  83.4 0.0 collective-permute-done.3.refs_3_
  83.5 0.0 all-gather.3.cloned.1.call-done
  83.5 3.0 %collective-permute-start.9 = (bf16[128,1024]{1,0:T(8,128)(2,1)}, bf16[128,1024]{1,0:T(8,128)(2,1)S(1)}, u32[]{:S(2)}, u32[]{:S(2)}) collective-permute-start(bf16[128,1024]{1,0:T(8,128)(2,1)} %collective-permute-done.3.refs_3_), channel_id=1, source_target_pairs={{0,8},{8,0},{1,9},{9,1},{2,10},{10,2},{3,11},{11,3},{4,12},{12,4},... | collective-permute-start | bytes 786440 | tf_op jit(solution)/shard_map/ppermute | solution.py:161
  86.5 1.9 %collective-permute-start.10 = (bf16[128,1024]{1,0:T(8,128)(2,1)S(1)}, bf16[128,1024]{1,0:T(8,128)(2,1)S(1)}, u32[]{:S(2)}, u32[]{:S(2)}) collective-permute-start(bf16[128,1024]{1,0:T(8,128)(2,1)S(1)} %collective-permute-done.5.refs_4_), channel_id=1, source_target_pairs={{0,8},{8,0},{1,9},{9,1},{2,10},{10,2},{3,11},{11,3},{4,12},{12,4},... | collective-permute-start | bytes 786440 | tf_op jit(solution)/shard_map/ppermute | solution.py:161
  88.5 1.5 collective-permute-done.10.refs_9_
  89.9 5.5 %shard_map.37 = bf16[256,256]{1,0:T(8,128)(2,1)S(1)} custom-call(bf16[8,256,1024]{2,1,0:T(8,128)(2,1)} %bitcast.6, bf16[256,1024]{1,0:T(8,128)(2,1)S(1)} %bitcast.5, bf16[256,1024]{1,0:T(8,128)(2,1)S(1)} %collective-permute-done.2.refs_1_, bf16[256,1024]{1,0:T(8,128)(2,1)S(1)} %collective-permute-done.4.refs_2_, ...), custom_call_target="tpu_custom_call" | custom-call | flops 1073741824 | bytes 8388608 | tf_op jit(solution)/shard_map/pallas_call | solution.py:82
  95.4 10.3 %all_gather.11.own = bf16[1024,256]{1,0:T(8,128)(2,1)S(1)} all-gather(bf16[256,256]{1,0:T(8,128)(2,1)S(1)} %shard_map.37), channel_id=1, replica_groups=mesh['y'=8,'x'=4,'c'=2,'z'=8] {'x'}, dimensions={0}, use_global_device_ids=true | all-gather | bytes 655360 | tf_op jit(solution)/shard_map/all_gather | solution.py:176
  105.7 4.6 %collective-permute-start.11 = (bf16[1024,256]{1,0:T(8,128)(2,1)S(1)}, bf16[1024,256]{1,0:T(8,128)(2,1)S(1)}, u32[]{:S(2)}, u32[]{:S(2)}) collective-permute-start(bf16[1024,256]{1,0:T(8,128)(2,1)S(1)} %all_gather.11.own), channel_id=1, source_target_pairs={{0,8},{8,0},{1,9},{9,1},{2,10},{10,2},{3,11},{11,3},{4,12},{12,4},... | collective-permute-start | bytes 1572872 | tf_op jit(solution)/shard_map/ppermute | solution.py:161
  110.4 0.1 reshape.11.q_ref
  110.4 1.4 collective-permute-done.11.other
  111.9 2.3 %shard_map.38 = f32[8,72,128]{2,1,0:T(8,128)S(1)} custom-call(bf16[512,128]{1,0:T(8,128)(2,1)S(1)} %reshape.11.q_ref, bf16[1024,256]{1,0:T(8,128)(2,1)S(1)} %all_gather.11.own, bf16[1024,256]{1,0:T(8,128)(2,1)S(1)} %collective-permute-done.11.other), custom_call_target="tpu_custom_call" | custom-call | flops 536870912 | bytes 2097152 | tf_op jit(solution)/shard_map/pallas_call | solution.py:122
  114.2 15.6 %all_to_all.11.part_ref = f32[8,72,128]{2,1,0:T(8,128)} all-to-all(f32[8,72,128]{2,1,0:T(8,128)S(1)} %shard_map.38), channel_id=1, replica_groups=mesh['y'=8,'x'=4,'c'=2,'z'=8] {'y'}, dimensions={0} | all-to-all | bytes 589824 | tf_op jit(solution)/shard_map/all_to_all | solution.py:178
  129.8 2.1 %shard_map.39 = bf16[64,128]{1,0:T(8,128)(2,1)} custom-call(f32[8,72,128]{2,1,0:T(8,128)} %all_to_all.11.part_ref), custom_call_target="tpu_custom_call" | custom-call | tf_op jit(solution)/shard_map/pallas_call | solution.py:145
  132.0 2.2 %collective-permute-start.12 = (bf16[64,128]{1,0:T(8,128)(2,1)}, bf16[64,128]{1,0:T(8,128)(2,1)S(1)}, u32[]{:S(2)}, u32[]{:S(2)}) collective-permute-start(bf16[64,128]{1,0:T(8,128)(2,1)} %shard_map.39), channel_id=1, source_target_pairs={{4,0},{68,1},{132,2},{196,3},{260,4},{324,5},{388,6},{452,7},{12,8... | collective-permute-start | bytes 49160 | tf_op jit(solution)/shard_map/ppermute | solution.py:180
  134.2 6.4 %collective-permute-done.12 = bf16[64,128]{1,0:T(8,128)(2,1)S(1)} collective-permute-done((bf16[64,128]{1,0:T(8,128)(2,1)}, bf16[64,128]{1,0:T(8,128)(2,1)S(1)}, u32[]{:S(2)}, u32[]{:S(2)}) %collective-permute-start.12) | collective-permute-done | bytes 16416 | tf_op jit(solution)/shard_map/ppermute | solution.py:180
  140.5 0.6 copy.5
  (15 shorter events, 0.1 us)
Async XLA Ops:
  6.5 76.9 %all-gather.3.cloned.1.call-start = ((), (), s32[]{:S(2)}) async-start(), calls=%async_computation.2 | async-start | bytes 4718592 | tf_op jit(solution)/shard_map/all_gather | solution.py:165
  7.3 21.8 %collective-permute-start = (bf16[32,1024]{1,0:T(8,128)(2,1)}, bf16[32,1024]{1,0:T(8,128)(2,1)S(1)}, u32[]{:S(2)}, u32[]{:S(2)}) collective-permute-start(bf16[32,1024]{1,0:T(8,128)(2,1)} %param.4), channel_id=1, source_target_pairs={{0,4},{1,12},{2,20},{3,28},{4,36},{5,44},{6,52},{7,60},{8,68},{9,7... | collective-permute-start | bytes 196616 | tf_op jit(solution)/shard_map/ppermute | solution.py:166
  20.3 8.8 %collective-permute-start.1 = (bf16[64,128]{1,0:T(8,128)(2,1)}, bf16[64,128]{1,0:T(8,128)(2,1)S(1)}, u32[]{:S(2)}, u32[]{:S(2)}) collective-permute-start(bf16[64,128]{1,0:T(8,128)(2,1)} %param.5), channel_id=1, source_target_pairs={{0,4},{1,68},{2,132},{3,196},{4,260},{5,324},{6,388},{7,452},{8,12... | collective-permute-start | bytes 49160 | tf_op jit(solution)/shard_map/ppermute | solution.py:167
  55.0 28.5 %copy-start = (bf16[8,40,1024]{2,1,0:T(8,128)(2,1)}, bf16[8,40,1024]{2,1,0:T(8,128)(2,1)S(1)}, u32[]{:S(2)}) copy-start(bf16[8,40,1024]{2,1,0:T(8,128)(2,1)S(1)} %all_to_all.10) | copy-start | bytes 1966084
  55.0 13.4 %collective-permute-start.4 = (bf16[256,1024]{1,0:T(8,128)(2,1)S(1)}, bf16[256,1024]{1,0:T(8,128)(2,1)S(1)}, u32[]{:S(2)}, u32[]{:S(2)}) collective-permute-start(bf16[256,1024]{1,0:T(8,128)(2,1)S(1)} %bitcast.2), channel_id=1, source_target_pairs={{0,48},{16,0},{32,16},{48,32},{1,49},{17,1},{33,17},{49,33},{2,50}... | collective-permute-start | bytes 1572872 | tf_op jit(solution)/shard_map/ppermute | solution.py:154
  57.1 13.2 %collective-permute-start.2 = (bf16[256,1024]{1,0:T(8,128)(2,1)S(1)}, bf16[256,1024]{1,0:T(8,128)(2,1)S(1)}, u32[]{:S(2)}, u32[]{:S(2)}) collective-permute-start(bf16[256,1024]{1,0:T(8,128)(2,1)S(1)} %bitcast.3), channel_id=1, source_target_pairs={{0,16},{16,32},{32,48},{48,0},{1,17},{17,33},{33,49},{49,1},{2,18}... | collective-permute-start | bytes 1572872 | tf_op jit(solution)/shard_map/ppermute | solution.py:153
  68.4 15.0 %collective-permute-start.5 = (bf16[128,1024]{1,0:T(8,128)(2,1)S(1)}, bf16[128,1024]{1,0:T(8,128)(2,1)S(1)}, u32[]{:S(2)}, u32[]{:S(2)}) collective-permute-start(bf16[128,1024]{1,0:T(8,128)(2,1)S(1)} %slice.19), channel_id=1, source_target_pairs={{0,48},{16,0},{32,16},{48,32},{1,49},{17,1},{33,17},{49,33},{2,50}... | collective-permute-start | bytes 786440 | tf_op jit(solution)/shard_map/ppermute | solution.py:156
  70.4 13.1 %collective-permute-start.3 = (bf16[128,1024]{1,0:T(8,128)(2,1)S(1)}, bf16[128,1024]{1,0:T(8,128)(2,1)}, u32[]{:S(2)}, u32[]{:S(2)}) collective-permute-start(bf16[128,1024]{1,0:T(8,128)(2,1)S(1)} %slice.18), channel_id=1, source_target_pairs={{0,16},{16,32},{32,48},{48,0},{1,17},{17,33},{33,49},{49,1},{2,18}... | collective-permute-start | bytes 786440 | tf_op jit(solution)/shard_map/ppermute | solution.py:155
  73.7 14.7 %collective-permute-start.6 = (bf16[256,1024]{1,0:T(8,128)(2,1)S(1)}, bf16[256,1024]{1,0:T(8,128)(2,1)S(1)}, u32[]{:S(2)}, u32[]{:S(2)}) collective-permute-start(bf16[256,1024]{1,0:T(8,128)(2,1)S(1)} %bitcast.4), channel_id=1, source_target_pairs={{0,8},{8,0},{1,9},{9,1},{2,10},{10,2},{3,11},{11,3},{4,12},{12,4},... | collective-permute-start | bytes 1572872 | tf_op jit(solution)/shard_map/ppermute | solution.py:161
  79.1 9.4 %collective-permute-start.8 = (bf16[256,1024]{1,0:T(8,128)(2,1)S(1)}, bf16[256,1024]{1,0:T(8,128)(2,1)S(1)}, u32[]{:S(2)}, u32[]{:S(2)}) collective-permute-start(bf16[256,1024]{1,0:T(8,128)(2,1)S(1)} %collective-permute-done.4.refs_2_), channel_id=1, source_target_pairs={{0,8},{8,0},{1,9},{9,1},{2,10},{10,2},{3,11},{11,3},{4,12},{12,4},... | collective-permute-start | bytes 1572872 | tf_op jit(solution)/shard_map/ppermute | solution.py:161
  81.0 7.5 %collective-permute-start.7 = (bf16[256,1024]{1,0:T(8,128)(2,1)S(1)}, bf16[256,1024]{1,0:T(8,128)(2,1)S(1)}, u32[]{:S(2)}, u32[]{:S(2)}) collective-permute-start(bf16[256,1024]{1,0:T(8,128)(2,1)S(1)} %collective-permute-done.2.refs_1_), channel_id=1, source_target_pairs={{0,8},{8,0},{1,9},{9,1},{2,10},{10,2},{3,11},{11,3},{4,12},{12,4},... | collective-permute-start | bytes 1572872 | tf_op jit(solution)/shard_map/ppermute | solution.py:161
  83.5 26.9 %slice-start = ((bf16[8,40,1024]{2,1,0:T(8,128)(2,1)}), bf16[8,8,1024]{2,1,0:T(8,128)(2,1)S(1)}, s32[]{:S(2)}) async-start(bf16[8,40,1024]{2,1,0:T(8,128)(2,1)} %copy-done), calls=%async_computation.3 | async-start | bytes 262144 | tf_op jit(solution)/shard_map/slice | solution.py:170
  83.5 5.0 %collective-permute-start.9 = (bf16[128,1024]{1,0:T(8,128)(2,1)}, bf16[128,1024]{1,0:T(8,128)(2,1)S(1)}, u32[]{:S(2)}, u32[]{:S(2)}) collective-permute-start(bf16[128,1024]{1,0:T(8,128)(2,1)} %collective-permute-done.3.refs_3_), channel_id=1, source_target_pairs={{0,8},{8,0},{1,9},{9,1},{2,10},{10,2},{3,11},{11,3},{4,12},{12,4},... | collective-permute-start | bytes 786440 | tf_op jit(solution)/shard_map/ppermute | solution.py:161
  86.5 3.4 %collective-permute-start.10 = (bf16[128,1024]{1,0:T(8,128)(2,1)S(1)}, bf16[128,1024]{1,0:T(8,128)(2,1)S(1)}, u32[]{:S(2)}, u32[]{:S(2)}) collective-permute-start(bf16[128,1024]{1,0:T(8,128)(2,1)S(1)} %collective-permute-done.5.refs_4_), channel_id=1, source_target_pairs={{0,8},{8,0},{1,9},{9,1},{2,10},{10,2},{3,11},{11,3},{4,12},{12,4},... | collective-permute-start | bytes 786440 | tf_op jit(solution)/shard_map/ppermute | solution.py:161
  105.7 6.1 %collective-permute-start.11 = (bf16[1024,256]{1,0:T(8,128)(2,1)S(1)}, bf16[1024,256]{1,0:T(8,128)(2,1)S(1)}, u32[]{:S(2)}, u32[]{:S(2)}) collective-permute-start(bf16[1024,256]{1,0:T(8,128)(2,1)S(1)} %all_gather.11.own), channel_id=1, source_target_pairs={{0,8},{8,0},{1,9},{9,1},{2,10},{10,2},{3,11},{11,3},{4,12},{12,4},... | collective-permute-start | bytes 1572872 | tf_op jit(solution)/shard_map/ppermute | solution.py:161
  132.0 8.6 %collective-permute-start.12 = (bf16[64,128]{1,0:T(8,128)(2,1)}, bf16[64,128]{1,0:T(8,128)(2,1)S(1)}, u32[]{:S(2)}, u32[]{:S(2)}) collective-permute-start(bf16[64,128]{1,0:T(8,128)(2,1)} %shard_map.39), channel_id=1, source_target_pairs={{4,0},{68,1},{132,2},{196,3},{260,4},{324,5},{388,6},{452,7},{12,8... | collective-permute-start | bytes 49160 | tf_op jit(solution)/shard_map/ppermute | solution.py:180
Sparse Core Ops, SparseCore 0:
  9.4 63.7 all-gather.2

commit v10 on v8

--- a/solution.py
+++ b/solution.py
@@ -51,38 +51,24 @@
 SWAP = [(0, 1), (1, 0)]
 
 
-def project_kernel(mem_ref, *refs):
-    w_refs, (out_ref, held, sems) = refs[:10], refs[10:]
+def project_kernel(mem_ref, own, left, right, opp, own_s, left_s, right_s, opp_s, out_ref):
     x, core = lax.axis_index("x"), lax.axis_index("c")
-    order = [(swapped, away) for away in (0, 3, 1, 2) for swapped in (0, 1)]
-    copies = []
-    for j, (swapped, away) in enumerate(order):
-        half = core if swapped == 0 else 1 - core
-        share = lax.rem(x + away, 4) * 2 + half
-        copies.append(pltpu.make_async_copy(mem_ref.at[share], held.at[j], sems.at[j]))
-        copies[j].start()
+    pairs = []
+    for half, refs in ((core, (own, left, right, opp)), (1 - core, (own_s, left_s, right_s, opp_s))):
+        for away, ref in zip((0, 3, 1, 2), refs):
+            pairs.append((2 * lax.rem(x + away, 4) + half, ref))
     total = None
-    for j, (swapped, away) in enumerate(order):
-        own, left, right, opp_k, opp_v = w_refs[5 * swapped : 5 * swapped + 5]
-        if away == 2:
-            w_rows = jnp.concatenate([opp_k[...], opp_v[...]], axis=0)
-        else:
-            w_rows = {0: own, 3: left, 1: right}[away][...]
-        copies[j].wait()
-        part = lax.dot_general(held[j], w_rows, NT, preferred_element_type=jnp.float32)
+    for share, ref in pairs:
+        part = lax.dot_general(mem_ref[share], ref[...], NT, preferred_element_type=jnp.float32)
         total = part if total is None else total + part
     out_ref[...] = total.astype(out_ref.dtype)
 
 
-def project(mem_all, w_pieces):
-    vmem = pl.BlockSpec(memory_space=pltpu.VMEM)
+def project(mem_all, *w_pieces):
     return pl.pallas_call(
         project_kernel,
         out_shape=jax.ShapeDtypeStruct((256, 2 * HD), jnp.bfloat16),
-        in_specs=[pl.BlockSpec(memory_space=pl.ANY)] + [vmem] * 10,
-        out_specs=vmem,
-        scratch_shapes=[pltpu.VMEM(mem_all.shape, jnp.bfloat16), pltpu.SemaphoreType.DMA((8,))],
-        compiler_params=pltpu.CompilerParams(vmem_limit_bytes=50 << 20),
+        compiler_params=pltpu.CompilerParams(vmem_limit_bytes=16 << 20),
         cost_estimate=pl.CostEstimate(flops=2 * 256 * 256 * 8192, bytes_accessed=8 << 20, transcendentals=0),
     )(mem_all, *w_pieces)
 
@@ -165,8 +151,10 @@
     both = spread(jnp.concatenate([rows, query.reshape(8, 8 * HD)], axis=0), "y")
     rows = both[:, :32].reshape(2 * HD, 8 * HD)
     query = both[:, 32:].reshape(512, HD)
-    w_pieces = ring(rows)
-    own = project(mem_all, (*w_pieces, *map(swap, w_pieces)))
+    rows, left, right, opp_k, opp_v = ring(rows)
+    opp_k, opp_v, mem_all = lax.optimization_barrier((opp_k, opp_v, mem_all))
+    opp = jnp.concatenate([opp_k, opp_v], axis=0)
+    own = project(mem_all, rows, left, right, opp, swap(rows), swap(left), swap(right), swap(opp))
 
     own = lax.all_gather(own, "x", axis=0, tiled=True)
     parts = attend(query, own, swap(own))

time: 150 us -> 147 us (0.980)
  waiting for transfers between devices: 17.3 us -> 22.2 us
  starting transfers between devices: 51.9 us -> 47.8 us
  Pallas kernels: 9.73 us -> 5.74 us
    ppermute x1, waiting for transfers between devices: 3.56 us -> 8.08 us  [ring(): right = lax.ppermute(value, 'x', shift(4, -1))]
    ppermute x6 -> x5, starting transfers between devices: 21.5 us -> 17.3 us  [swap(): return lax.ppermute(value, 'c', SWAP)]
    pallas_call x1, Pallas kernels: 5.26 us -> 1.27 us  [project(): pl.pallas_call(project_kernel, out_shape=jax.ShapeDtypeStruct((256, 2 * H...]
    unnamed x9 -> x6, local copies, waits for them, and re-layouts: 3.08 us -> 3.76 us
  transfers between devices with their start and end apart: 14 -> 13, of which waited for: 5 -> 5; matrix products, arithmetic and copies ran while one was open for 0% -> 1% of each run, Pallas kernels for 0% -> 0%
where the time goes in v10:
time: 147 us; the launch traced here: 145 us
  blocking collectives  51.8 us (35%)
  starting transfers between devices  47.8 us (33%)
  waiting for transfers between devices  22.2 us (15%)
  between operations  13.6 us (9%)
  Pallas kernels  5.74 us (4%)
  local copies, waits for them, and re-layouts  4 us (3%)
    all_to_all x1, blocking collectives, spread(): return lax.all_to_all(copies, axis, 0, 0, tiled=True)  25.8 us
    ppermute x5, starting transfers between devices, swap(): return lax.ppermute(value, 'c', SWAP)  17.3 us
    all_to_all x1, blocking collectives, body(): parts = lax.all_to_all(parts, 'y', 0, 0, tiled=True)  15.6 us
    ppermute x1, starting transfers between devices, body(): rows = lax.ppermute(kv_weight, ALL, weight_moves())  13 us
    all_gather x1, blocking collectives, body(): own = lax.all_gather(own, 'x', axis=0, tiled=True)  10.4 us
    ppermute x1, waiting for transfers between devices, ring(): right = lax.ppermute(value, 'x', shift(4, -1))  8.08 us
    ppermute x1, waiting for transfers between devices, body(): return lax.ppermute(result, ALL, [(b, a) for a, b in query_moves()])  6.38 us
    ppermute x1, starting transfers between devices, body(): query = lax.ppermute(queries, ALL, query_moves())  4.65 us
  transfers between devices with their start and end apart: 13, of which 5 were waited for; matrix products, arithmetic and copies ran while one was open for 1% of the time, Pallas kernels for 0%

profile of v10, /device:TPU:1, one launch (start us, length us, event | category | flops | bytes accessed | tf_op | source)
XLA Modules:
  0.0 145.2 jit_solution(11833963025442411721)
XLA Ops:
  6.5 0.7 all-gather.3.cloned.1.call-update
  7.3 13.0 %collective-permute-start = (bf16[32,1024]{1,0:T(8,128)(2,1)}, bf16[32,1024]{1,0:T(8,128)(2,1)S(1)}, u32[]{:S(2)}, u32[]{:S(2)}) collective-permute-start(bf16[32,1024]{1,0:T(8,128)(2,1)} %param.4), channel_id=1, source_target_pairs={{0,4},{1,12},{2,20},{3,28},{4,36},{5,44},{6,52},{7,60},{8,68},{9,7... | collective-permute-start | bytes 196616 | tf_op jit(solution)/shard_map/ppermute | solution.py:149
  20.3 4.7 %collective-permute-start.1 = (bf16[64,128]{1,0:T(8,128)(2,1)}, bf16[64,128]{1,0:T(8,128)(2,1)S(1)}, u32[]{:S(2)}, u32[]{:S(2)}) collective-permute-start(bf16[64,128]{1,0:T(8,128)(2,1)} %param.5), channel_id=1, source_target_pairs={{0,4},{1,68},{2,132},{3,196},{4,260},{5,324},{6,388},{7,452},{8,12... | collective-permute-start | bytes 49160 | tf_op jit(solution)/shard_map/ppermute | solution.py:150
  25.0 4.1 %collective-permute-done.1 = bf16[64,128]{1,0:T(8,128)(2,1)S(1)} collective-permute-done((bf16[64,128]{1,0:T(8,128)(2,1)}, bf16[64,128]{1,0:T(8,128)(2,1)S(1)}, u32[]{:S(2)}, u32[]{:S(2)}) %collective-permute-start.1) | collective-permute-done | bytes 16416 | tf_op jit(solution)/shard_map/ppermute | solution.py:150
  29.1 0.0 collective-permute-done
  29.1 0.1 broadcast_in_dim.2
  29.2 25.8 %all_to_all.10 = bf16[8,40,1024]{2,1,0:T(8,128)(2,1)S(1)} all-to-all(bf16[8,40,1024]{2,1,0:T(8,128)(2,1)S(1)} %broadcast_in_dim.2), channel_id=1, replica_groups=mesh['y'=8,'x'=4,'c'=2,'z'=8] {'y'}, dimensions={0} | all-to-all | bytes 1310720 | tf_op jit(solution)/shard_map/all_to_all | solution.py:16
  55.0 2.1 %collective-permute-start.4 = (bf16[256,1024]{1,0:T(8,128)(2,1)S(1)}, bf16[256,1024]{1,0:T(8,128)(2,1)S(1)}, u32[]{:S(2)}, u32[]{:S(2)}) collective-permute-start(bf16[256,1024]{1,0:T(8,128)(2,1)S(1)} %bitcast.3), channel_id=1, source_target_pairs={{0,48},{16,0},{32,16},{48,32},{1,49},{17,1},{33,17},{49,33},{2,50}... | collective-permute-start | bytes 1572872 | tf_op jit(solution)/shard_map/ppermute | solution.py:137
  57.1 3.2 %collective-permute-start.2 = (bf16[256,1024]{1,0:T(8,128)(2,1)S(1)}, bf16[256,1024]{1,0:T(8,128)(2,1)S(1)}, u32[]{:S(2)}, u32[]{:S(2)}) collective-permute-start(bf16[256,1024]{1,0:T(8,128)(2,1)S(1)} %bitcast.4), channel_id=1, source_target_pairs={{0,16},{16,32},{32,48},{48,0},{1,17},{17,33},{33,49},{49,1},{2,18}... | collective-permute-start | bytes 1572872 | tf_op jit(solution)/shard_map/ppermute | solution.py:136
  60.3 8.1 %collective-permute-done.4.right = bf16[256,1024]{1,0:T(8,128)(2,1)S(1)} collective-permute-done((bf16[256,1024]{1,0:T(8,128)(2,1)S(1)}, bf16[256,1024]{1,0:T(8,128)(2,1)S(1)}, u32[]{:S(2)}, u32[]{:S(2)}) %collective-permute-start.4) | collective-permute-done | bytes 524320 | tf_op jit(solution)/shard_map/ppermute | solution.py:137
  68.4 1.9 %collective-permute-start.5 = (bf16[128,1024]{1,0:T(8,128)(2,1)S(1)}, bf16[128,1024]{1,0:T(8,128)(2,1)S(1)}, u32[]{:S(2)}, u32[]{:S(2)}) collective-permute-start(bf16[128,1024]{1,0:T(8,128)(2,1)S(1)} %slice.19), channel_id=1, source_target_pairs={{0,48},{16,0},{32,16},{48,32},{1,49},{17,1},{33,17},{49,33},{2,50}... | collective-permute-start | bytes 786440 | tf_op jit(solution)/shard_map/ppermute | solution.py:139
  70.3 0.0 collective-permute-done.2.left
  70.4 3.4 %collective-permute-start.3 = (bf16[128,1024]{1,0:T(8,128)(2,1)S(1)}, bf16[128,1024]{1,0:T(8,128)(2,1)}, u32[]{:S(2)}, u32[]{:S(2)}) collective-permute-start(bf16[128,1024]{1,0:T(8,128)(2,1)S(1)} %slice.18), channel_id=1, source_target_pairs={{0,16},{16,32},{32,48},{48,0},{1,17},{17,33},{33,49},{49,1},{2,18}... | collective-permute-start | bytes 786440 | tf_op jit(solution)/shard_map/ppermute | solution.py:138
  73.7 5.3 %collective-permute-start.6 = (bf16[256,1024]{1,0:T(8,128)(2,1)S(1)}, bf16[256,1024]{1,0:T(8,128)(2,1)S(1)}, u32[]{:S(2)}, u32[]{:S(2)}) collective-permute-start(bf16[256,1024]{1,0:T(8,128)(2,1)S(1)} %bitcast.5), channel_id=1, source_target_pairs={{0,8},{8,0},{1,9},{9,1},{2,10},{10,2},{3,11},{11,3},{4,12},{12,4},... | collective-permute-start | bytes 1572872 | tf_op jit(solution)/shard_map/ppermute | solution.py:144
  79.1 1.9 %collective-permute-start.8 = (bf16[256,1024]{1,0:T(8,128)(2,1)S(1)}, bf16[256,1024]{1,0:T(8,128)(2,1)S(1)}, u32[]{:S(2)}, u32[]{:S(2)}) collective-permute-start(bf16[256,1024]{1,0:T(8,128)(2,1)S(1)} %collective-permute-done.4.right), channel_id=1, source_target_pairs={{0,8},{8,0},{1,9},{9,1},{2,10},{10,2},{3,11},{11,3},{4,12},{12,4},... | collective-permute-start | bytes 1572872 | tf_op jit(solution)/shard_map/ppermute | solution.py:144
  81.0 2.4 %collective-permute-start.7 = (bf16[256,1024]{1,0:T(8,128)(2,1)S(1)}, bf16[256,1024]{1,0:T(8,128)(2,1)S(1)}, u32[]{:S(2)}, u32[]{:S(2)}) collective-permute-start(bf16[256,1024]{1,0:T(8,128)(2,1)S(1)} %collective-permute-done.2.left), channel_id=1, source_target_pairs={{0,8},{8,0},{1,9},{9,1},{2,10},{10,2},{3,11},{11,3},{4,12},{12,4},... | collective-permute-start | bytes 1572872 | tf_op jit(solution)/shard_map/ppermute | solution.py:144
  83.5 0.0 all-gather.3.cloned.1.call-done
  83.5 1.0 constant_dynamic-update-slice_fusion.1
  84.5 3.0 %collective-permute-start.9 = (bf16[256,1024]{1,0:T(8,128)(2,1)S(1)}, bf16[256,1024]{1,0:T(8,128)(2,1)S(1)}, u32[]{:S(2)}, u32[]{:S(2)}) collective-permute-start(bf16[256,1024]{1,0:T(8,128)(2,1)S(1)} %constant_dynamic-update-slice_fusion.opp), channel_id=1, source_target_pairs={{0,8},{8,0},{1,9},{9,1},{2,10},{10,2},{3,11},{11,3},{4,12},{12,4},... | collective-permute-start | bytes 1572872 | tf_op jit(solution)/shard_map/ppermute | solution.py:144
  87.6 1.5 %collective-permute-done.9.opp_s = bf16[256,1024]{1,0:T(8,128)(2,1)S(1)} collective-permute-done((bf16[256,1024]{1,0:T(8,128)(2,1)S(1)}, bf16[256,1024]{1,0:T(8,128)(2,1)S(1)}, u32[]{:S(2)}, u32[]{:S(2)}) %collective-permute-start.9) | collective-permute-done | bytes 524320 | tf_op jit(solution)/shard_map/ppermute | solution.py:144
  89.0 2.2 %copy-done = bf16[2048,1024]{1,0:T(8,128)(2,1)S(1)} copy-done((bf16[2048,1024]{1,0:T(8,128)(2,1)S(1)}, bf16[2048,1024]{1,0:T(8,128)(2,1)}, u32[]{:S(2)}) %copy-start) | copy-done | bytes 4194328
  91.2 1.3 shard_map.37
  92.5 10.4 %all_gather.11.own = bf16[1024,256]{1,0:T(8,128)(2,1)S(1)} all-gather(bf16[256,256]{1,0:T(8,128)(2,1)S(1)} %shard_map.37), channel_id=1, replica_groups=mesh['y'=8,'x'=4,'c'=2,'z'=8] {'x'}, dimensions={0}, use_global_device_ids=true | all-gather | bytes 655360 | tf_op jit(solution)/shard_map/all_gather | solution.py:159
  102.9 4.7 %collective-permute-start.10 = (bf16[1024,256]{1,0:T(8,128)(2,1)S(1)}, bf16[1024,256]{1,0:T(8,128)(2,1)S(1)}, u32[]{:S(2)}, u32[]{:S(2)}) collective-permute-start(bf16[1024,256]{1,0:T(8,128)(2,1)S(1)} %all_gather.11.own), channel_id=1, source_target_pairs={{0,8},{8,0},{1,9},{9,1},{2,10},{10,2},{3,11},{11,3},{4,12},{12,4},... | collective-permute-start | bytes 1572872 | tf_op jit(solution)/shard_map/ppermute | solution.py:144
  107.6 0.1 reshape.11.q_ref
  107.7 1.4 collective-permute-done.10.other
  109.1 2.3 %shard_map.38 = f32[8,72,128]{2,1,0:T(8,128)S(1)} custom-call(bf16[512,128]{1,0:T(8,128)(2,1)S(1)} %reshape.11.q_ref, bf16[1024,256]{1,0:T(8,128)(2,1)S(1)} %all_gather.11.own, bf16[1024,256]{1,0:T(8,128)(2,1)S(1)} %collective-permute-done.10.other), custom_call_target="tpu_custom_call" | custom-call | flops 536870912 | bytes 2097152 | tf_op jit(solution)/shard_map/pallas_call | solution.py:105
  111.4 15.6 %all_to_all.11.part_ref = f32[8,72,128]{2,1,0:T(8,128)} all-to-all(f32[8,72,128]{2,1,0:T(8,128)S(1)} %shard_map.38), channel_id=1, replica_groups=mesh['y'=8,'x'=4,'c'=2,'z'=8] {'y'}, dimensions={0} | all-to-all | bytes 589824 | tf_op jit(solution)/shard_map/all_to_all | solution.py:161
  127.1 2.1 %shard_map.39 = bf16[64,128]{1,0:T(8,128)(2,1)} custom-call(f32[8,72,128]{2,1,0:T(8,128)} %all_to_all.11.part_ref), custom_call_target="tpu_custom_call" | custom-call | tf_op jit(solution)/shard_map/pallas_call | solution.py:128
  129.2 2.2 %collective-permute-start.11 = (bf16[64,128]{1,0:T(8,128)(2,1)}, bf16[64,128]{1,0:T(8,128)(2,1)S(1)}, u32[]{:S(2)}, u32[]{:S(2)}) collective-permute-start(bf16[64,128]{1,0:T(8,128)(2,1)} %shard_map.39), channel_id=1, source_target_pairs={{4,0},{68,1},{132,2},{196,3},{260,4},{324,5},{388,6},{452,7},{12,8... | collective-permute-start | bytes 49160 | tf_op jit(solution)/shard_map/ppermute | solution.py:163
  131.4 6.4 %collective-permute-done.11 = bf16[64,128]{1,0:T(8,128)(2,1)S(1)} collective-permute-done((bf16[64,128]{1,0:T(8,128)(2,1)}, bf16[64,128]{1,0:T(8,128)(2,1)S(1)}, u32[]{:S(2)}, u32[]{:S(2)}) %collective-permute-start.11) | collective-permute-done | bytes 16416 | tf_op jit(solution)/shard_map/ppermute | solution.py:163
  137.8 0.6 copy.6
  (17 shorter events, 0.1 us)
Async XLA Ops:
  6.5 76.9 %all-gather.3.cloned.1.call-start = ((), (), s32[]{:S(2)}) async-start(), calls=%async_computation.2 | async-start | bytes 4718592 | tf_op jit(solution)/shard_map/all_gather | solution.py:148
  7.3 21.8 %collective-permute-start = (bf16[32,1024]{1,0:T(8,128)(2,1)}, bf16[32,1024]{1,0:T(8,128)(2,1)S(1)}, u32[]{:S(2)}, u32[]{:S(2)}) collective-permute-start(bf16[32,1024]{1,0:T(8,128)(2,1)} %param.4), channel_id=1, source_target_pairs={{0,4},{1,12},{2,20},{3,28},{4,36},{5,44},{6,52},{7,60},{8,68},{9,7... | collective-permute-start | bytes 196616 | tf_op jit(solution)/shard_map/ppermute | solution.py:149
  20.3 8.8 %collective-permute-start.1 = (bf16[64,128]{1,0:T(8,128)(2,1)}, bf16[64,128]{1,0:T(8,128)(2,1)S(1)}, u32[]{:S(2)}, u32[]{:S(2)}) collective-permute-start(bf16[64,128]{1,0:T(8,128)(2,1)} %param.5), channel_id=1, source_target_pairs={{0,4},{1,68},{2,132},{3,196},{4,260},{5,324},{6,388},{7,452},{8,12... | collective-permute-start | bytes 49160 | tf_op jit(solution)/shard_map/ppermute | solution.py:150
  55.0 24.1 %copy-start.1 = (bf16[8,40,1024]{2,1,0:T(8,128)(2,1)}, bf16[8,40,1024]{2,1,0:T(8,128)(2,1)S(1)}, u32[]{:S(2)}) copy-start(bf16[8,40,1024]{2,1,0:T(8,128)(2,1)S(1)} %all_to_all.10) | copy-start | bytes 1966084
  55.0 13.4 %collective-permute-start.4 = (bf16[256,1024]{1,0:T(8,128)(2,1)S(1)}, bf16[256,1024]{1,0:T(8,128)(2,1)S(1)}, u32[]{:S(2)}, u32[]{:S(2)}) collective-permute-start(bf16[256,1024]{1,0:T(8,128)(2,1)S(1)} %bitcast.3), channel_id=1, source_target_pairs={{0,48},{16,0},{32,16},{48,32},{1,49},{17,1},{33,17},{49,33},{2,50}... | collective-permute-start | bytes 1572872 | tf_op jit(solution)/shard_map/ppermute | solution.py:137
  57.1 13.2 %collective-permute-start.2 = (bf16[256,1024]{1,0:T(8,128)(2,1)S(1)}, bf16[256,1024]{1,0:T(8,128)(2,1)S(1)}, u32[]{:S(2)}, u32[]{:S(2)}) collective-permute-start(bf16[256,1024]{1,0:T(8,128)(2,1)S(1)} %bitcast.4), channel_id=1, source_target_pairs={{0,16},{16,32},{32,48},{48,0},{1,17},{17,33},{33,49},{49,1},{2,18}... | collective-permute-start | bytes 1572872 | tf_op jit(solution)/shard_map/ppermute | solution.py:136
  68.4 15.0 %collective-permute-start.5 = (bf16[128,1024]{1,0:T(8,128)(2,1)S(1)}, bf16[128,1024]{1,0:T(8,128)(2,1)S(1)}, u32[]{:S(2)}, u32[]{:S(2)}) collective-permute-start(bf16[128,1024]{1,0:T(8,128)(2,1)S(1)} %slice.19), channel_id=1, source_target_pairs={{0,48},{16,0},{32,16},{48,32},{1,49},{17,1},{33,17},{49,33},{2,50}... | collective-permute-start | bytes 786440 | tf_op jit(solution)/shard_map/ppermute | solution.py:139
  70.4 13.1 %collective-permute-start.3 = (bf16[128,1024]{1,0:T(8,128)(2,1)S(1)}, bf16[128,1024]{1,0:T(8,128)(2,1)}, u32[]{:S(2)}, u32[]{:S(2)}) collective-permute-start(bf16[128,1024]{1,0:T(8,128)(2,1)S(1)} %slice.18), channel_id=1, source_target_pairs={{0,16},{16,32},{32,48},{48,0},{1,17},{17,33},{33,49},{49,1},{2,18}... | collective-permute-start | bytes 786440 | tf_op jit(solution)/shard_map/ppermute | solution.py:138
  73.7 13.8 %collective-permute-start.6 = (bf16[256,1024]{1,0:T(8,128)(2,1)S(1)}, bf16[256,1024]{1,0:T(8,128)(2,1)S(1)}, u32[]{:S(2)}, u32[]{:S(2)}) collective-permute-start(bf16[256,1024]{1,0:T(8,128)(2,1)S(1)} %bitcast.5), channel_id=1, source_target_pairs={{0,8},{8,0},{1,9},{9,1},{2,10},{10,2},{3,11},{11,3},{4,12},{12,4},... | collective-permute-start | bytes 1572872 | tf_op jit(solution)/shard_map/ppermute | solution.py:144
  79.1 8.5 %collective-permute-start.8 = (bf16[256,1024]{1,0:T(8,128)(2,1)S(1)}, bf16[256,1024]{1,0:T(8,128)(2,1)S(1)}, u32[]{:S(2)}, u32[]{:S(2)}) collective-permute-start(bf16[256,1024]{1,0:T(8,128)(2,1)S(1)} %collective-permute-done.4.right), channel_id=1, source_target_pairs={{0,8},{8,0},{1,9},{9,1},{2,10},{10,2},{3,11},{11,3},{4,12},{12,4},... | collective-permute-start | bytes 1572872 | tf_op jit(solution)/shard_map/ppermute | solution.py:144
  81.0 6.5 %collective-permute-start.7 = (bf16[256,1024]{1,0:T(8,128)(2,1)S(1)}, bf16[256,1024]{1,0:T(8,128)(2,1)S(1)}, u32[]{:S(2)}, u32[]{:S(2)}) collective-permute-start(bf16[256,1024]{1,0:T(8,128)(2,1)S(1)} %collective-permute-done.2.left), channel_id=1, source_target_pairs={{0,8},{8,0},{1,9},{9,1},{2,10},{10,2},{3,11},{11,3},{4,12},{12,4},... | collective-permute-start | bytes 1572872 | tf_op jit(solution)/shard_map/ppermute | solution.py:144
  84.5 23.1 %slice-start = ((bf16[8,40,1024]{2,1,0:T(8,128)(2,1)}), bf16[8,8,1024]{2,1,0:T(8,128)(2,1)S(1)}, s32[]{:S(2)}) async-start(bf16[8,40,1024]{2,1,0:T(8,128)(2,1)} %copy-done.1), calls=%async_computation.3 | async-start | bytes 262144 | tf_op jit(solution)/shard_map/slice | solution.py:153
  84.5 4.6 %collective-permute-start.9 = (bf16[256,1024]{1,0:T(8,128)(2,1)S(1)}, bf16[256,1024]{1,0:T(8,128)(2,1)S(1)}, u32[]{:S(2)}, u32[]{:S(2)}) collective-permute-start(bf16[256,1024]{1,0:T(8,128)(2,1)S(1)} %constant_dynamic-update-slice_fusion.opp), channel_id=1, source_target_pairs={{0,8},{8,0},{1,9},{9,1},{2,10},{10,2},{3,11},{11,3},{4,12},{12,4},... | collective-permute-start | bytes 1572872 | tf_op jit(solution)/shard_map/ppermute | solution.py:144
  89.0 2.2 %copy-start = (bf16[2048,1024]{1,0:T(8,128)(2,1)S(1)}, bf16[2048,1024]{1,0:T(8,128)(2,1)}, u32[]{:S(2)}) copy-start(bf16[2048,1024]{1,0:T(8,128)(2,1)} %all-gather.3.cloned.1.call-done) | copy-start | bytes 12582916
  102.9 6.2 %collective-permute-start.10 = (bf16[1024,256]{1,0:T(8,128)(2,1)S(1)}, bf16[1024,256]{1,0:T(8,128)(2,1)S(1)}, u32[]{:S(2)}, u32[]{:S(2)}) collective-permute-start(bf16[1024,256]{1,0:T(8,128)(2,1)S(1)} %all_gather.11.own), channel_id=1, source_target_pairs={{0,8},{8,0},{1,9},{9,1},{2,10},{10,2},{3,11},{11,3},{4,12},{12,4},... | collective-permute-start | bytes 1572872 | tf_op jit(solution)/shard_map/ppermute | solution.py:144
  129.2 8.6 %collective-permute-start.11 = (bf16[64,128]{1,0:T(8,128)(2,1)}, bf16[64,128]{1,0:T(8,128)(2,1)S(1)}, u32[]{:S(2)}, u32[]{:S(2)}) collective-permute-start(bf16[64,128]{1,0:T(8,128)(2,1)} %shard_map.39), channel_id=1, source_target_pairs={{4,0},{68,1},{132,2},{196,3},{260,4},{324,5},{388,6},{452,7},{12,8... | collective-permute-start | bytes 49160 | tf_op jit(solution)/shard_map/ppermute | solution.py:163
Sparse Core Ops, SparseCore 0:
  9.4 63.7 all-gather.2

commit v11 on v10

--- a/solution.py
+++ b/solution.py
@@ -1,3 +1,5 @@
+import functools
+
 import jax
 import jax.numpy as jnp
 from jax import lax
@@ -51,26 +53,25 @@
 SWAP = [(0, 1), (1, 0)]
 
 
-def project_kernel(mem_ref, own, left, right, opp, own_s, left_s, right_s, opp_s, out_ref):
+def project_kernel(swapped, mem_ref, own, left, right, opp, *refs):
     x, core = lax.axis_index("x"), lax.axis_index("c")
-    pairs = []
-    for half, refs in ((core, (own, left, right, opp)), (1 - core, (own_s, left_s, right_s, opp_s))):
-        for away, ref in zip((0, 3, 1, 2), refs):
-            pairs.append((2 * lax.rem(x + away, 4) + half, ref))
-    total = None
-    for share, ref in pairs:
-        part = lax.dot_general(mem_ref[share], ref[...], NT, preferred_element_type=jnp.float32)
+    half = 1 - core if swapped else core
+    *before, out_ref = refs
+    total = before[0][...] if before else None
+    for away, ref in zip((0, 3, 1, 2), (own, left, right, opp)):
+        share = mem_ref[2 * lax.rem(x + away, 4) + half]
+        part = lax.dot_general(share, ref[...], NT, preferred_element_type=jnp.float32)
         total = part if total is None else total + part
     out_ref[...] = total.astype(out_ref.dtype)
 
 
-def project(mem_all, *w_pieces):
+def project(dtype, mem_all, *operands):
     return pl.pallas_call(
-        project_kernel,
-        out_shape=jax.ShapeDtypeStruct((256, 2 * HD), jnp.bfloat16),
+        functools.partial(project_kernel, dtype == jnp.bfloat16),
+        out_shape=jax.ShapeDtypeStruct((256, 2 * HD), dtype),
         compiler_params=pltpu.CompilerParams(vmem_limit_bytes=16 << 20),
-        cost_estimate=pl.CostEstimate(flops=2 * 256 * 256 * 8192, bytes_accessed=8 << 20, transcendentals=0),
-    )(mem_all, *w_pieces)
+        cost_estimate=pl.CostEstimate(flops=256 * 256 * 8192, bytes_accessed=4 << 20, transcendentals=0),
+    )(mem_all, *operands)
 
 
 def attend_kernel(q_ref, own, other, out_ref):
@@ -154,7 +155,8 @@
     rows, left, right, opp_k, opp_v = ring(rows)
     opp_k, opp_v, mem_all = lax.optimization_barrier((opp_k, opp_v, mem_all))
     opp = jnp.concatenate([opp_k, opp_v], axis=0)
-    own = project(mem_all, rows, left, right, opp, swap(rows), swap(left), swap(right), swap(opp))
+    near = project(jnp.float32, mem_all, rows, left, right, opp)
+    own = project(jnp.bfloat16, mem_all, swap(rows), swap(left), swap(right), swap(opp), near)
 
     own = lax.all_gather(own, "x", axis=0, tiled=True)
     parts = attend(query, own, swap(own))

time: 147 us -> 146 us (level); the launches traced: 145 us -> 146 us
  starting transfers between devices: 47.8 us -> 49.8 us
    ppermute x1, waiting for transfers between devices: 8.08 us -> 0.01 us  [ring(): right = lax.ppermute(value, 'x', shift(4, -1))]
    ppermute x1, waiting for transfers between devices: 0.01 us -> 8.08 us  [ring(): left = lax.ppermute(value, 'x', shift(4, 1))]
    ppermute x1, starting transfers between devices: 1.92 us -> 4.57 us  [ring(): opp_b = lax.ppermute(right[half:], 'x', shift(4, -1))]
    ppermute x1, starting transfers between devices: 2.08 us -> 4.57 us  [ring(): right = lax.ppermute(value, 'x', shift(4, -1))]
    ppermute x5, waiting for transfers between devices: 2.93 us -> 1.45 us  [swap(): return lax.ppermute(value, 'c', SWAP)]
  transfers between devices with their start and end apart: 13 -> 13, of which waited for: 5 -> 4; matrix products, arithmetic and copies ran while one was open for 1% -> 1% of each run, Pallas kernels for 0% -> 1%
where the time goes in v11:
time: 146 us
  blocking collectives  51.4 us (35%)
  starting transfers between devices  49.8 us (34%)
  waiting for transfers between devices  21 us (14%)
  between operations  13.7 us (9%)
  Pallas kernels  5.94 us (4%)
  local copies, waits for them, and re-layouts  3.99 us (3%)
    all_to_all x1, blocking collectives, spread(): return lax.all_to_all(copies, axis, 0, 0, tiled=True)  25.8 us
    ppermute x5, starting transfers between devices, swap(): return lax.ppermute(value, 'c', SWAP)  17.2 us
    all_to_all x1, blocking collectives, body(): parts = lax.all_to_all(parts, 'y', 0, 0, tiled=True)  15.8 us
    ppermute x1, starting transfers between devices, body(): rows = lax.ppermute(kv_weight, ALL, weight_moves())  13 us
    all_gather x1, blocking collectives, body(): own = lax.all_gather(own, 'x', axis=0, tiled=True)  9.9 us
    ppermute x1, waiting for transfers between devices, ring(): left = lax.ppermute(value, 'x', shift(4, 1))  8.08 us
    ppermute x1, waiting for transfers between devices, body(): return lax.ppermute(result, ALL, [(b, a) for a, b in query_moves()])  6.67 us
    ppermute x1, starting transfers between devices, body(): query = lax.ppermute(queries, ALL, query_moves())  4.65 us
  transfers between devices with their start and end apart: 13, of which 4 were waited for; matrix products, arithmetic and copies ran while one was open for 1% of the time, Pallas kernels for 1%

profile of v11, /device:TPU:1, one launch (start us, length us, event | category | flops | bytes accessed | tf_op | source)
XLA Modules:
  0.0 145.9 jit_solution(12630667784471451625)
XLA Ops:
  6.5 0.7 all-gather.3.cloned.1.call-update
  7.3 13.0 %collective-permute-start = (bf16[32,1024]{1,0:T(8,128)(2,1)}, bf16[32,1024]{1,0:T(8,128)(2,1)S(1)}, u32[]{:S(2)}, u32[]{:S(2)}) collective-permute-start(bf16[32,1024]{1,0:T(8,128)(2,1)} %param.4), channel_id=1, source_target_pairs={{0,4},{1,12},{2,20},{3,28},{4,36},{5,44},{6,52},{7,60},{8,68},{9,7... | collective-permute-start | bytes 196616 | tf_op jit(solution)/shard_map/ppermute | solution.py:150
  20.3 4.7 %collective-permute-start.1 = (bf16[64,128]{1,0:T(8,128)(2,1)}, bf16[64,128]{1,0:T(8,128)(2,1)S(1)}, u32[]{:S(2)}, u32[]{:S(2)}) collective-permute-start(bf16[64,128]{1,0:T(8,128)(2,1)} %param.5), channel_id=1, source_target_pairs={{0,4},{1,68},{2,132},{3,196},{4,260},{5,324},{6,388},{7,452},{8,12... | collective-permute-start | bytes 49160 | tf_op jit(solution)/shard_map/ppermute | solution.py:151
  25.0 4.1 %collective-permute-done.1 = bf16[64,128]{1,0:T(8,128)(2,1)S(1)} collective-permute-done((bf16[64,128]{1,0:T(8,128)(2,1)}, bf16[64,128]{1,0:T(8,128)(2,1)S(1)}, u32[]{:S(2)}, u32[]{:S(2)}) %collective-permute-start.1) | collective-permute-done | bytes 16416 | tf_op jit(solution)/shard_map/ppermute | solution.py:151
  29.1 0.0 collective-permute-done
  29.1 0.1 broadcast_in_dim.2
  29.2 25.8 %all_to_all.10 = bf16[8,40,1024]{2,1,0:T(8,128)(2,1)S(1)} all-to-all(bf16[8,40,1024]{2,1,0:T(8,128)(2,1)S(1)} %broadcast_in_dim.2), channel_id=1, replica_groups=mesh['y'=8,'x'=4,'c'=2,'z'=8] {'y'}, dimensions={0} | all-to-all | bytes 1310720 | tf_op jit(solution)/shard_map/all_to_all | solution.py:18
  55.0 1.9 %collective-permute-start.2 = (bf16[256,1024]{1,0:T(8,128)(2,1)S(1)}, bf16[256,1024]{1,0:T(8,128)(2,1)S(1)}, u32[]{:S(2)}, u32[]{:S(2)}) collective-permute-start(bf16[256,1024]{1,0:T(8,128)(2,1)S(1)} %bitcast.4), channel_id=1, source_target_pairs={{0,16},{16,32},{32,48},{48,0},{1,17},{17,33},{33,49},{49,1},{2,18}... | collective-permute-start | bytes 1572872 | tf_op jit(solution)/shard_map/ppermute | solution.py:137
  56.9 4.6 %collective-permute-start.4 = (bf16[256,1024]{1,0:T(8,128)(2,1)S(1)}, bf16[256,1024]{1,0:T(8,128)(2,1)S(1)}, u32[]{:S(2)}, u32[]{:S(2)}) collective-permute-start(bf16[256,1024]{1,0:T(8,128)(2,1)S(1)} %bitcast.5), channel_id=1, source_target_pairs={{0,48},{16,0},{32,16},{48,32},{1,49},{17,1},{33,17},{49,33},{2,50}... | collective-permute-start | bytes 1572872 | tf_op jit(solution)/shard_map/ppermute | solution.py:138
  61.5 8.1 %collective-permute-done.2.left = bf16[256,1024]{1,0:T(8,128)(2,1)S(1)} collective-permute-done((bf16[256,1024]{1,0:T(8,128)(2,1)S(1)}, bf16[256,1024]{1,0:T(8,128)(2,1)S(1)}, u32[]{:S(2)}, u32[]{:S(2)}) %collective-permute-start.2) | collective-permute-done | bytes 524320 | tf_op jit(solution)/shard_map/ppermute | solution.py:137
  69.6 1.9 %collective-permute-start.3 = (bf16[128,1024]{1,0:T(8,128)(2,1)S(1)}, bf16[128,1024]{1,0:T(8,128)(2,1)S(1)}, u32[]{:S(2)}, u32[]{:S(2)}) collective-permute-start(bf16[128,1024]{1,0:T(8,128)(2,1)S(1)} %slice.18), channel_id=1, source_target_pairs={{0,16},{16,32},{32,48},{48,0},{1,17},{17,33},{33,49},{49,1},{2,18}... | collective-permute-start | bytes 786440 | tf_op jit(solution)/shard_map/ppermute | solution.py:139
  71.6 0.0 collective-permute-done.4.right
  71.6 4.6 %collective-permute-start.5 = (bf16[128,1024]{1,0:T(8,128)(2,1)S(1)}, bf16[128,1024]{1,0:T(8,128)(2,1)}, u32[]{:S(2)}, u32[]{:S(2)}) collective-permute-start(bf16[128,1024]{1,0:T(8,128)(2,1)S(1)} %slice.19), channel_id=1, source_target_pairs={{0,48},{16,0},{32,16},{48,32},{1,49},{17,1},{33,17},{49,33},{2,50}... | collective-permute-start | bytes 786440 | tf_op jit(solution)/shard_map/ppermute | solution.py:140
  76.2 5.3 %collective-permute-start.6 = (bf16[256,1024]{1,0:T(8,128)(2,1)S(1)}, bf16[256,1024]{1,0:T(8,128)(2,1)S(1)}, u32[]{:S(2)}, u32[]{:S(2)}) collective-permute-start(bf16[256,1024]{1,0:T(8,128)(2,1)S(1)} %bitcast.6), channel_id=1, source_target_pairs={{0,8},{8,0},{1,9},{9,1},{2,10},{10,2},{3,11},{11,3},{4,12},{12,4},... | collective-permute-start | bytes 1572872 | tf_op jit(solution)/shard_map/ppermute | solution.py:145
  81.5 1.9 %collective-permute-start.7 = (bf16[256,1024]{1,0:T(8,128)(2,1)S(1)}, bf16[256,1024]{1,0:T(8,128)(2,1)S(1)}, u32[]{:S(2)}, u32[]{:S(2)}) collective-permute-start(bf16[256,1024]{1,0:T(8,128)(2,1)S(1)} %collective-permute-done.2.left), channel_id=1, source_target_pairs={{0,8},{8,0},{1,9},{9,1},{2,10},{10,2},{3,11},{11,3},{4,12},{12,4},... | collective-permute-start | bytes 1572872 | tf_op jit(solution)/shard_map/ppermute | solution.py:145
  83.4 2.4 %collective-permute-start.8 = (bf16[256,1024]{1,0:T(8,128)(2,1)S(1)}, bf16[256,1024]{1,0:T(8,128)(2,1)S(1)}, u32[]{:S(2)}, u32[]{:S(2)}) collective-permute-start(bf16[256,1024]{1,0:T(8,128)(2,1)S(1)} %collective-permute-done.4.right), channel_id=1, source_target_pairs={{0,8},{8,0},{1,9},{9,1},{2,10},{10,2},{3,11},{11,3},{4,12},{12,4},... | collective-permute-start | bytes 1572872 | tf_op jit(solution)/shard_map/ppermute | solution.py:145
  85.9 0.0 all-gather.3.cloned.1.call-done
  85.9 1.0 constant_dynamic-update-slice_fusion.opp
  86.9 1.9 %collective-permute-start.9 = (bf16[256,1024]{1,0:T(8,128)(2,1)S(1)}, bf16[256,1024]{1,0:T(8,128)(2,1)S(1)}, u32[]{:S(2)}, u32[]{:S(2)}) collective-permute-start(bf16[256,1024]{1,0:T(8,128)(2,1)S(1)} %constant_dynamic-update-slice_fusion.opp), channel_id=1, source_target_pairs={{0,8},{8,0},{1,9},{9,1},{2,10},{10,2},{3,11},{11,3},{4,12},{12,4},... | collective-permute-start | bytes 1572872 | tf_op jit(solution)/shard_map/ppermute | solution.py:145
  88.8 2.2 %copy-done = bf16[2048,1024]{1,0:T(8,128)(2,1)S(1)} copy-done((bf16[2048,1024]{1,0:T(8,128)(2,1)S(1)}, bf16[2048,1024]{1,0:T(8,128)(2,1)}, u32[]{:S(2)}) %copy-start) | copy-done | bytes 4194328
  91.0 0.7 shard_map.37.refs_0_
  91.8 0.7 shard_map.38
  92.6 9.9 %all_gather.11.own = bf16[1024,256]{1,0:T(8,128)(2,1)S(1)} all-gather(bf16[256,256]{1,0:T(8,128)(2,1)S(1)} %shard_map.38), channel_id=1, replica_groups=mesh['y'=8,'x'=4,'c'=2,'z'=8] {'x'}, dimensions={0}, use_global_device_ids=true | all-gather | bytes 655360 | tf_op jit(solution)/shard_map/all_gather | solution.py:161
  102.5 5.6 %collective-permute-start.10 = (bf16[1024,256]{1,0:T(8,128)(2,1)S(1)}, bf16[1024,256]{1,0:T(8,128)(2,1)S(1)}, u32[]{:S(2)}, u32[]{:S(2)}) collective-permute-start(bf16[1024,256]{1,0:T(8,128)(2,1)S(1)} %all_gather.11.own), channel_id=1, source_target_pairs={{0,8},{8,0},{1,9},{9,1},{2,10},{10,2},{3,11},{11,3},{4,12},{12,4},... | collective-permute-start | bytes 1572872 | tf_op jit(solution)/shard_map/ppermute | solution.py:145
  108.1 0.1 reshape.11.q_ref
  108.2 1.4 collective-permute-done.10.other
  109.6 2.3 %shard_map.39 = f32[8,72,128]{2,1,0:T(8,128)S(1)} custom-call(bf16[512,128]{1,0:T(8,128)(2,1)S(1)} %reshape.11.q_ref, bf16[1024,256]{1,0:T(8,128)(2,1)S(1)} %all_gather.11.own, bf16[1024,256]{1,0:T(8,128)(2,1)S(1)} %collective-permute-done.10.other), custom_call_target="tpu_custom_call" | custom-call | flops 536870912 | bytes 2097152 | tf_op jit(solution)/shard_map/pallas_call | solution.py:106
  112.0 15.8 %all_to_all.11.part_ref = f32[8,72,128]{2,1,0:T(8,128)} all-to-all(f32[8,72,128]{2,1,0:T(8,128)S(1)} %shard_map.39), channel_id=1, replica_groups=mesh['y'=8,'x'=4,'c'=2,'z'=8] {'y'}, dimensions={0} | all-to-all | bytes 589824 | tf_op jit(solution)/shard_map/all_to_all | solution.py:163
  127.7 2.1 %shard_map.40 = bf16[64,128]{1,0:T(8,128)(2,1)} custom-call(f32[8,72,128]{2,1,0:T(8,128)} %all_to_all.11.part_ref), custom_call_target="tpu_custom_call" | custom-call | tf_op jit(solution)/shard_map/pallas_call | solution.py:129
  129.8 1.9 %collective-permute-start.11 = (bf16[64,128]{1,0:T(8,128)(2,1)}, bf16[64,128]{1,0:T(8,128)(2,1)S(1)}, u32[]{:S(2)}, u32[]{:S(2)}) collective-permute-start(bf16[64,128]{1,0:T(8,128)(2,1)} %shard_map.40), channel_id=1, source_target_pairs={{4,0},{68,1},{132,2},{196,3},{260,4},{324,5},{388,6},{452,7},{12,8... | collective-permute-start | bytes 49160 | tf_op jit(solution)/shard_map/ppermute | solution.py:165
  131.8 6.7 %collective-permute-done.11 = bf16[64,128]{1,0:T(8,128)(2,1)S(1)} collective-permute-done((bf16[64,128]{1,0:T(8,128)(2,1)}, bf16[64,128]{1,0:T(8,128)(2,1)S(1)}, u32[]{:S(2)}, u32[]{:S(2)}) %collective-permute-start.11) | collective-permute-done | bytes 16416 | tf_op jit(solution)/shard_map/ppermute | solution.py:165
  138.4 0.6 copy.6
  (18 shorter events, 0.1 us)
Async XLA Ops:
  6.5 79.4 %all-gather.3.cloned.1.call-start = ((), (), s32[]{:S(2)}) async-start(), calls=%async_computation.2 | async-start | bytes 4718592 | tf_op jit(solution)/shard_map/all_gather | solution.py:149
  7.3 21.8 %collective-permute-start = (bf16[32,1024]{1,0:T(8,128)(2,1)}, bf16[32,1024]{1,0:T(8,128)(2,1)S(1)}, u32[]{:S(2)}, u32[]{:S(2)}) collective-permute-start(bf16[32,1024]{1,0:T(8,128)(2,1)} %param.4), channel_id=1, source_target_pairs={{0,4},{1,12},{2,20},{3,28},{4,36},{5,44},{6,52},{7,60},{8,68},{9,7... | collective-permute-start | bytes 196616 | tf_op jit(solution)/shard_map/ppermute | solution.py:150
  20.3 8.8 %collective-permute-start.1 = (bf16[64,128]{1,0:T(8,128)(2,1)}, bf16[64,128]{1,0:T(8,128)(2,1)S(1)}, u32[]{:S(2)}, u32[]{:S(2)}) collective-permute-start(bf16[64,128]{1,0:T(8,128)(2,1)} %param.5), channel_id=1, source_target_pairs={{0,4},{1,68},{2,132},{3,196},{4,260},{5,324},{6,388},{7,452},{8,12... | collective-permute-start | bytes 49160 | tf_op jit(solution)/shard_map/ppermute | solution.py:151
  55.0 26.5 %copy-start.1 = (bf16[8,40,1024]{2,1,0:T(8,128)(2,1)}, bf16[8,40,1024]{2,1,0:T(8,128)(2,1)S(1)}, u32[]{:S(2)}) copy-start(bf16[8,40,1024]{2,1,0:T(8,128)(2,1)S(1)} %all_to_all.10) | copy-start | bytes 1966084
  55.0 14.6 %collective-permute-start.2 = (bf16[256,1024]{1,0:T(8,128)(2,1)S(1)}, bf16[256,1024]{1,0:T(8,128)(2,1)S(1)}, u32[]{:S(2)}, u32[]{:S(2)}) collective-permute-start(bf16[256,1024]{1,0:T(8,128)(2,1)S(1)} %bitcast.4), channel_id=1, source_target_pairs={{0,16},{16,32},{32,48},{48,0},{1,17},{17,33},{33,49},{49,1},{2,18}... | collective-permute-start | bytes 1572872 | tf_op jit(solution)/shard_map/ppermute | solution.py:137
  56.9 14.6 %collective-permute-start.4 = (bf16[256,1024]{1,0:T(8,128)(2,1)S(1)}, bf16[256,1024]{1,0:T(8,128)(2,1)S(1)}, u32[]{:S(2)}, u32[]{:S(2)}) collective-permute-start(bf16[256,1024]{1,0:T(8,128)(2,1)S(1)} %bitcast.5), channel_id=1, source_target_pairs={{0,48},{16,0},{32,16},{48,32},{1,49},{17,1},{33,17},{49,33},{2,50}... | collective-permute-start | bytes 1572872 | tf_op jit(solution)/shard_map/ppermute | solution.py:138
  69.6 16.2 %collective-permute-start.3 = (bf16[128,1024]{1,0:T(8,128)(2,1)S(1)}, bf16[128,1024]{1,0:T(8,128)(2,1)S(1)}, u32[]{:S(2)}, u32[]{:S(2)}) collective-permute-start(bf16[128,1024]{1,0:T(8,128)(2,1)S(1)} %slice.18), channel_id=1, source_target_pairs={{0,16},{16,32},{32,48},{48,0},{1,17},{17,33},{33,49},{49,1},{2,18}... | collective-permute-start | bytes 786440 | tf_op jit(solution)/shard_map/ppermute | solution.py:139
  71.6 14.3 %collective-permute-start.5 = (bf16[128,1024]{1,0:T(8,128)(2,1)S(1)}, bf16[128,1024]{1,0:T(8,128)(2,1)}, u32[]{:S(2)}, u32[]{:S(2)}) collective-permute-start(bf16[128,1024]{1,0:T(8,128)(2,1)S(1)} %slice.19), channel_id=1, source_target_pairs={{0,48},{16,0},{32,16},{48,32},{1,49},{17,1},{33,17},{49,33},{2,50}... | collective-permute-start | bytes 786440 | tf_op jit(solution)/shard_map/ppermute | solution.py:140
  76.2 15.6 %collective-permute-start.6 = (bf16[256,1024]{1,0:T(8,128)(2,1)S(1)}, bf16[256,1024]{1,0:T(8,128)(2,1)S(1)}, u32[]{:S(2)}, u32[]{:S(2)}) collective-permute-start(bf16[256,1024]{1,0:T(8,128)(2,1)S(1)} %bitcast.6), channel_id=1, source_target_pairs={{0,8},{8,0},{1,9},{9,1},{2,10},{10,2},{3,11},{11,3},{4,12},{12,4},... | collective-permute-start | bytes 1572872 | tf_op jit(solution)/shard_map/ppermute | solution.py:145
  81.5 10.3 %collective-permute-start.7 = (bf16[256,1024]{1,0:T(8,128)(2,1)S(1)}, bf16[256,1024]{1,0:T(8,128)(2,1)S(1)}, u32[]{:S(2)}, u32[]{:S(2)}) collective-permute-start(bf16[256,1024]{1,0:T(8,128)(2,1)S(1)} %collective-permute-done.2.left), channel_id=1, source_target_pairs={{0,8},{8,0},{1,9},{9,1},{2,10},{10,2},{3,11},{11,3},{4,12},{12,4},... | collective-permute-start | bytes 1572872 | tf_op jit(solution)/shard_map/ppermute | solution.py:145
  83.4 8.4 %collective-permute-start.8 = (bf16[256,1024]{1,0:T(8,128)(2,1)S(1)}, bf16[256,1024]{1,0:T(8,128)(2,1)S(1)}, u32[]{:S(2)}, u32[]{:S(2)}) collective-permute-start(bf16[256,1024]{1,0:T(8,128)(2,1)S(1)} %collective-permute-done.4.right), channel_id=1, source_target_pairs={{0,8},{8,0},{1,9},{9,1},{2,10},{10,2},{3,11},{11,3},{4,12},{12,4},... | collective-permute-start | bytes 1572872 | tf_op jit(solution)/shard_map/ppermute | solution.py:145
  86.9 4.9 %collective-permute-start.9 = (bf16[256,1024]{1,0:T(8,128)(2,1)S(1)}, bf16[256,1024]{1,0:T(8,128)(2,1)S(1)}, u32[]{:S(2)}, u32[]{:S(2)}) collective-permute-start(bf16[256,1024]{1,0:T(8,128)(2,1)S(1)} %constant_dynamic-update-slice_fusion.opp), channel_id=1, source_target_pairs={{0,8},{8,0},{1,9},{9,1},{2,10},{10,2},{3,11},{11,3},{4,12},{12,4},... | collective-permute-start | bytes 1572872 | tf_op jit(solution)/shard_map/ppermute | solution.py:145
  88.8 2.2 %copy-start = (bf16[2048,1024]{1,0:T(8,128)(2,1)S(1)}, bf16[2048,1024]{1,0:T(8,128)(2,1)}, u32[]{:S(2)}) copy-start(bf16[2048,1024]{1,0:T(8,128)(2,1)} %all-gather.3.cloned.1.call-done) | copy-start | bytes 12582916
  91.8 16.3 %slice-start = ((bf16[8,40,1024]{2,1,0:T(8,128)(2,1)}), bf16[8,8,1024]{2,1,0:T(8,128)(2,1)S(1)}, s32[]{:S(2)}) async-start(bf16[8,40,1024]{2,1,0:T(8,128)(2,1)} %copy-done.1), calls=%async_computation.3 | async-start | bytes 262144 | tf_op jit(solution)/shard_map/slice | solution.py:154
  102.5 7.2 %collective-permute-start.10 = (bf16[1024,256]{1,0:T(8,128)(2,1)S(1)}, bf16[1024,256]{1,0:T(8,128)(2,1)S(1)}, u32[]{:S(2)}, u32[]{:S(2)}) collective-permute-start(bf16[1024,256]{1,0:T(8,128)(2,1)S(1)} %all_gather.11.own), channel_id=1, source_target_pairs={{0,8},{8,0},{1,9},{9,1},{2,10},{10,2},{3,11},{11,3},{4,12},{12,4},... | collective-permute-start | bytes 1572872 | tf_op jit(solution)/shard_map/ppermute | solution.py:145
  129.8 8.6 %collective-permute-start.11 = (bf16[64,128]{1,0:T(8,128)(2,1)}, bf16[64,128]{1,0:T(8,128)(2,1)S(1)}, u32[]{:S(2)}, u32[]{:S(2)}) collective-permute-start(bf16[64,128]{1,0:T(8,128)(2,1)} %shard_map.40), channel_id=1, source_target_pairs={{4,0},{68,1},{132,2},{196,3},{260,4},{324,5},{388,6},{452,7},{12,8... | collective-permute-start | bytes 49160 | tf_op jit(solution)/shard_map/ppermute | solution.py:165
Sparse Core Ops, SparseCore 0:
  9.4 63.7 all-gather.2

commit v12 on v11

--- a/solution.py
+++ b/solution.py
@@ -136,9 +136,11 @@
     half = value.shape[0] // 2
     left = lax.ppermute(value, "x", shift(4, 1))
     right = lax.ppermute(value, "x", shift(4, -1))
+    swapped = swap(value)
     opp_a = lax.ppermute(left[:half], "x", shift(4, 1))
     opp_b = lax.ppermute(right[half:], "x", shift(4, -1))
-    return value, left, right, opp_a, opp_b
+    left, right, swapped = lax.optimization_barrier((left, right, swapped))
+    return swapped, left, right, opp_a, opp_b
 
 
 def swap(value):
@@ -152,11 +154,11 @@
     both = spread(jnp.concatenate([rows, query.reshape(8, 8 * HD)], axis=0), "y")
     rows = both[:, :32].reshape(2 * HD, 8 * HD)
     query = both[:, 32:].reshape(512, HD)
-    rows, left, right, opp_k, opp_v = ring(rows)
+    rows_s, left, right, opp_k, opp_v = ring(rows)
     opp_k, opp_v, mem_all = lax.optimization_barrier((opp_k, opp_v, mem_all))
     opp = jnp.concatenate([opp_k, opp_v], axis=0)
     near = project(jnp.float32, mem_all, rows, left, right, opp)
-    own = project(jnp.bfloat16, mem_all, swap(rows), swap(left), swap(right), swap(opp), near)
+    own = project(jnp.bfloat16, mem_all, rows_s, swap(left), swap(right), swap(opp), near)
 
     own = lax.all_gather(own, "x", axis=0, tiled=True)
     parts = attend(query, own, swap(own))

time: 146 us -> 145 us (level)
  waiting for transfers between devices: 21 us -> 16.2 us
  starting transfers between devices: 49.8 us -> 52.4 us
    ppermute x1, waiting for transfers between devices: 8.08 us -> 0.01 us  [ring(): left = lax.ppermute(value, 'x', shift(4, 1))]
    ppermute x5, starting transfers between devices: 17.2 us -> 21.9 us  [swap(): return lax.ppermute(value, 'c', SWAP)]
    ppermute x1, waiting for transfers between devices: 0.01 us -> 3.56 us  [ring(): right = lax.ppermute(value, 'x', shift(4, -1))]
    ppermute x1, starting transfers between devices: 4.57 us -> 1.92 us  [ring(): opp_b = lax.ppermute(right[half:], 'x', shift(4, -1))]
    ppermute x1, starting transfers between devices: 4.57 us -> 2.08 us  [ring(): right = lax.ppermute(value, 'x', shift(4, -1))]
where the time goes in v12:
time: 145 us; the launch traced here: 144 us
  starting transfers between devices  52.4 us (36%)
  blocking collectives  51.9 us (36%)
  waiting for transfers between devices  16.2 us (11%)
  between operations  13.7 us (9%)
  Pallas kernels  5.94 us (4%)
  local copies, waits for them, and re-layouts  3.99 us (3%)
    all_to_all x1, blocking collectives, spread(): return lax.all_to_all(copies, axis, 0, 0, tiled=True)  25.8 us
    ppermute x5, starting transfers between devices, swap(): return lax.ppermute(value, 'c', SWAP)  21.9 us
    all_to_all x1, blocking collectives, body(): parts = lax.all_to_all(parts, 'y', 0, 0, tiled=True)  15.6 us
    ppermute x1, starting transfers between devices, body(): rows = lax.ppermute(kv_weight, ALL, weight_moves())  13 us
    all_gather x1, blocking collectives, body(): own = lax.all_gather(own, 'x', axis=0, tiled=True)  10.5 us
    ppermute x1, waiting for transfers between devices, body(): return lax.ppermute(result, ALL, [(b, a) for a, b in query_moves()])  6.36 us
    ppermute x1, starting transfers between devices, body(): query = lax.ppermute(queries, ALL, query_moves())  4.65 us
    ppermute x1, waiting for transfers between devices, body(): query = lax.ppermute(queries, ALL, query_moves())  4.09 us
  transfers between devices with their start and end apart: 13, of which 4 were waited for; matrix products, arithmetic and copies ran while one was open for 1% of the time, Pallas kernels for 1%

profile of v12, /device:TPU:1, one launch (start us, length us, event | category | flops | bytes accessed | tf_op | source)
XLA Modules:
  0.0 144.1 jit_solution(6065591637891484919)
XLA Ops:
  6.5 0.7 all-gather.3.cloned.1.call-update
  7.3 13.0 %collective-permute-start = (bf16[32,1024]{1,0:T(8,128)(2,1)}, bf16[32,1024]{1,0:T(8,128)(2,1)S(1)}, u32[]{:S(2)}, u32[]{:S(2)}) collective-permute-start(bf16[32,1024]{1,0:T(8,128)(2,1)} %param.4), channel_id=1, source_target_pairs={{0,4},{1,12},{2,20},{3,28},{4,36},{5,44},{6,52},{7,60},{8,68},{9,7... | collective-permute-start | bytes 196616 | tf_op jit(solution)/shard_map/ppermute | solution.py:152
  20.3 4.7 %collective-permute-start.1 = (bf16[64,128]{1,0:T(8,128)(2,1)}, bf16[64,128]{1,0:T(8,128)(2,1)S(1)}, u32[]{:S(2)}, u32[]{:S(2)}) collective-permute-start(bf16[64,128]{1,0:T(8,128)(2,1)} %param.5), channel_id=1, source_target_pairs={{0,4},{1,68},{2,132},{3,196},{4,260},{5,324},{6,388},{7,452},{8,12... | collective-permute-start | bytes 49160 | tf_op jit(solution)/shard_map/ppermute | solution.py:153
  25.0 4.1 %collective-permute-done.1 = bf16[64,128]{1,0:T(8,128)(2,1)S(1)} collective-permute-done((bf16[64,128]{1,0:T(8,128)(2,1)}, bf16[64,128]{1,0:T(8,128)(2,1)S(1)}, u32[]{:S(2)}, u32[]{:S(2)}) %collective-permute-start.1) | collective-permute-done | bytes 16416 | tf_op jit(solution)/shard_map/ppermute | solution.py:153
  29.1 0.0 collective-permute-done
  29.1 0.1 broadcast_in_dim.2
  29.2 25.8 %all_to_all.10 = bf16[8,40,1024]{2,1,0:T(8,128)(2,1)S(1)} all-to-all(bf16[8,40,1024]{2,1,0:T(8,128)(2,1)S(1)} %broadcast_in_dim.2), channel_id=1, replica_groups=mesh['y'=8,'x'=4,'c'=2,'z'=8] {'y'}, dimensions={0} | all-to-all | bytes 1310720 | tf_op jit(solution)/shard_map/all_to_all | solution.py:18
  55.0 2.1 %collective-permute-start.4 = (bf16[256,1024]{1,0:T(8,128)(2,1)S(1)}, bf16[256,1024]{1,0:T(8,128)(2,1)S(1)}, u32[]{:S(2)}, u32[]{:S(2)}) collective-permute-start(bf16[256,1024]{1,0:T(8,128)(2,1)S(1)} %bitcast.4), channel_id=1, source_target_pairs={{0,48},{16,0},{32,16},{48,32},{1,49},{17,1},{33,17},{49,33},{2,50}... | collective-permute-start | bytes 1572872 | tf_op jit(solution)/shard_map/ppermute | solution.py:138
  57.1 3.2 %collective-permute-start.2 = (bf16[256,1024]{1,0:T(8,128)(2,1)S(1)}, bf16[256,1024]{1,0:T(8,128)(2,1)S(1)}, u32[]{:S(2)}, u32[]{:S(2)}) collective-permute-start(bf16[256,1024]{1,0:T(8,128)(2,1)S(1)} %bitcast.5), channel_id=1, source_target_pairs={{0,16},{16,32},{32,48},{48,0},{1,17},{17,33},{33,49},{49,1},{2,18}... | collective-permute-start | bytes 1572872 | tf_op jit(solution)/shard_map/ppermute | solution.py:137
  60.3 4.5 %collective-permute-start.6 = (bf16[256,1024]{1,0:T(8,128)(2,1)S(1)}, bf16[256,1024]{1,0:T(8,128)(2,1)S(1)}, u32[]{:S(2)}, u32[]{:S(2)}) collective-permute-start(bf16[256,1024]{1,0:T(8,128)(2,1)S(1)} %bitcast.6), channel_id=1, source_target_pairs={{0,8},{8,0},{1,9},{9,1},{2,10},{10,2},{3,11},{11,3},{4,12},{12,4},... | collective-permute-start | bytes 1572872 | tf_op jit(solution)/shard_map/ppermute | solution.py:147
  64.8 3.6 %collective-permute-done.4.right = bf16[256,1024]{1,0:T(8,128)(2,1)S(1)} collective-permute-done((bf16[256,1024]{1,0:T(8,128)(2,1)S(1)}, bf16[256,1024]{1,0:T(8,128)(2,1)S(1)}, u32[]{:S(2)}, u32[]{:S(2)}) %collective-permute-start.4) | collective-permute-done | bytes 524320 | tf_op jit(solution)/shard_map/ppermute | solution.py:138
  68.4 1.9 %collective-permute-start.5 = (bf16[128,1024]{1,0:T(8,128)(2,1)S(1)}, bf16[128,1024]{1,0:T(8,128)(2,1)S(1)}, u32[]{:S(2)}, u32[]{:S(2)}) collective-permute-start(bf16[128,1024]{1,0:T(8,128)(2,1)S(1)} %slice.19), channel_id=1, source_target_pairs={{0,48},{16,0},{32,16},{48,32},{1,49},{17,1},{33,17},{49,33},{2,50}... | collective-permute-start | bytes 786440 | tf_op jit(solution)/shard_map/ppermute | solution.py:141
  70.3 0.0 collective-permute-done.2.left
  70.4 3.4 %collective-permute-start.3 = (bf16[128,1024]{1,0:T(8,128)(2,1)S(1)}, bf16[128,1024]{1,0:T(8,128)(2,1)}, u32[]{:S(2)}, u32[]{:S(2)}) collective-permute-start(bf16[128,1024]{1,0:T(8,128)(2,1)S(1)} %slice.18), channel_id=1, source_target_pairs={{0,16},{16,32},{32,48},{48,0},{1,17},{17,33},{33,49},{49,1},{2,18}... | collective-permute-start | bytes 786440 | tf_op jit(solution)/shard_map/ppermute | solution.py:140
  73.8 5.3 %collective-permute-start.7 = (bf16[256,1024]{1,0:T(8,128)(2,1)S(1)}, bf16[256,1024]{1,0:T(8,128)(2,1)S(1)}, u32[]{:S(2)}, u32[]{:S(2)}) collective-permute-start(bf16[256,1024]{1,0:T(8,128)(2,1)S(1)} %collective-permute-done.2.left), channel_id=1, source_target_pairs={{0,8},{8,0},{1,9},{9,1},{2,10},{10,2},{3,11},{11,3},{4,12},{12,4},... | collective-permute-start | bytes 1572872 | tf_op jit(solution)/shard_map/ppermute | solution.py:147
  79.1 1.9 %collective-permute-start.8 = (bf16[256,1024]{1,0:T(8,128)(2,1)S(1)}, bf16[256,1024]{1,0:T(8,128)(2,1)S(1)}, u32[]{:S(2)}, u32[]{:S(2)}) collective-permute-start(bf16[256,1024]{1,0:T(8,128)(2,1)S(1)} %collective-permute-done.4.right), channel_id=1, source_target_pairs={{0,8},{8,0},{1,9},{9,1},{2,10},{10,2},{3,11},{11,3},{4,12},{12,4},... | collective-permute-start | bytes 1572872 | tf_op jit(solution)/shard_map/ppermute | solution.py:147
  81.1 0.0 all-gather.3.cloned.1.call-done
  81.1 1.0 constant_dynamic-update-slice_fusion.1
  82.1 5.3 %collective-permute-start.9 = (bf16[256,1024]{1,0:T(8,128)(2,1)S(1)}, bf16[256,1024]{1,0:T(8,128)(2,1)S(1)}, u32[]{:S(2)}, u32[]{:S(2)}) collective-permute-start(bf16[256,1024]{1,0:T(8,128)(2,1)S(1)} %constant_dynamic-update-slice_fusion.opp), channel_id=1, source_target_pairs={{0,8},{8,0},{1,9},{9,1},{2,10},{10,2},{3,11},{11,3},{4,12},{12,4},... | collective-permute-start | bytes 1572872 | tf_op jit(solution)/shard_map/ppermute | solution.py:147
  87.4 2.2 %copy-done = bf16[2048,1024]{1,0:T(8,128)(2,1)S(1)} copy-done((bf16[2048,1024]{1,0:T(8,128)(2,1)S(1)}, bf16[2048,1024]{1,0:T(8,128)(2,1)}, u32[]{:S(2)}) %copy-start) | copy-done | bytes 4194328
  89.6 0.7 shard_map.37.refs_0_
  90.4 0.7 shard_map.38
  91.1 10.5 %all_gather.11.own = bf16[1024,256]{1,0:T(8,128)(2,1)S(1)} all-gather(bf16[256,256]{1,0:T(8,128)(2,1)S(1)} %shard_map.38), channel_id=1, replica_groups=mesh['y'=8,'x'=4,'c'=2,'z'=8] {'x'}, dimensions={0}, use_global_device_ids=true | all-gather | bytes 655360 | tf_op jit(solution)/shard_map/all_gather | solution.py:163
  101.6 4.8 %collective-permute-start.10 = (bf16[1024,256]{1,0:T(8,128)(2,1)S(1)}, bf16[1024,256]{1,0:T(8,128)(2,1)S(1)}, u32[]{:S(2)}, u32[]{:S(2)}) collective-permute-start(bf16[1024,256]{1,0:T(8,128)(2,1)S(1)} %all_gather.11.own), channel_id=1, source_target_pairs={{0,8},{8,0},{1,9},{9,1},{2,10},{10,2},{3,11},{11,3},{4,12},{12,4},... | collective-permute-start | bytes 1572872 | tf_op jit(solution)/shard_map/ppermute | solution.py:147
  106.4 0.1 reshape.11.q_ref
  106.5 1.4 collective-permute-done.10.other
  108.0 2.3 %shard_map.39 = f32[8,72,128]{2,1,0:T(8,128)S(1)} custom-call(bf16[512,128]{1,0:T(8,128)(2,1)S(1)} %reshape.11.q_ref, bf16[1024,256]{1,0:T(8,128)(2,1)S(1)} %all_gather.11.own, bf16[1024,256]{1,0:T(8,128)(2,1)S(1)} %collective-permute-done.10.other), custom_call_target="tpu_custom_call" | custom-call | flops 536870912 | bytes 2097152 | tf_op jit(solution)/shard_map/pallas_call | solution.py:106
  110.3 15.6 %all_to_all.11.part_ref = f32[8,72,128]{2,1,0:T(8,128)} all-to-all(f32[8,72,128]{2,1,0:T(8,128)S(1)} %shard_map.39), channel_id=1, replica_groups=mesh['y'=8,'x'=4,'c'=2,'z'=8] {'y'}, dimensions={0} | all-to-all | bytes 589824 | tf_op jit(solution)/shard_map/all_to_all | solution.py:165
  125.9 2.1 %shard_map.40 = bf16[64,128]{1,0:T(8,128)(2,1)} custom-call(f32[8,72,128]{2,1,0:T(8,128)} %all_to_all.11.part_ref), custom_call_target="tpu_custom_call" | custom-call | tf_op jit(solution)/shard_map/pallas_call | solution.py:129
  128.0 2.2 %collective-permute-start.11 = (bf16[64,128]{1,0:T(8,128)(2,1)}, bf16[64,128]{1,0:T(8,128)(2,1)S(1)}, u32[]{:S(2)}, u32[]{:S(2)}) collective-permute-start(bf16[64,128]{1,0:T(8,128)(2,1)} %shard_map.40), channel_id=1, source_target_pairs={{4,0},{68,1},{132,2},{196,3},{260,4},{324,5},{388,6},{452,7},{12,8... | collective-permute-start | bytes 49160 | tf_op jit(solution)/shard_map/ppermute | solution.py:167
  130.3 6.4 %collective-permute-done.11 = bf16[64,128]{1,0:T(8,128)(2,1)S(1)} collective-permute-done((bf16[64,128]{1,0:T(8,128)(2,1)}, bf16[64,128]{1,0:T(8,128)(2,1)S(1)}, u32[]{:S(2)}, u32[]{:S(2)}) %collective-permute-start.11) | collective-permute-done | bytes 16416 | tf_op jit(solution)/shard_map/ppermute | solution.py:167
  136.6 0.6 copy.6
  (18 shorter events, 0.1 us)
Async XLA Ops:
  6.5 74.5 %all-gather.3.cloned.1.call-start = ((), (), s32[]{:S(2)}) async-start(), calls=%async_computation.2 | async-start | bytes 4718592 | tf_op jit(solution)/shard_map/all_gather | solution.py:151
  7.3 21.8 %collective-permute-start = (bf16[32,1024]{1,0:T(8,128)(2,1)}, bf16[32,1024]{1,0:T(8,128)(2,1)S(1)}, u32[]{:S(2)}, u32[]{:S(2)}) collective-permute-start(bf16[32,1024]{1,0:T(8,128)(2,1)} %param.4), channel_id=1, source_target_pairs={{0,4},{1,12},{2,20},{3,28},{4,36},{5,44},{6,52},{7,60},{8,68},{9,7... | collective-permute-start | bytes 196616 | tf_op jit(solution)/shard_map/ppermute | solution.py:152
  20.3 8.8 %collective-permute-start.1 = (bf16[64,128]{1,0:T(8,128)(2,1)}, bf16[64,128]{1,0:T(8,128)(2,1)S(1)}, u32[]{:S(2)}, u32[]{:S(2)}) collective-permute-start(bf16[64,128]{1,0:T(8,128)(2,1)} %param.5), channel_id=1, source_target_pairs={{0,4},{1,68},{2,132},{3,196},{4,260},{5,324},{6,388},{7,452},{8,12... | collective-permute-start | bytes 49160 | tf_op jit(solution)/shard_map/ppermute | solution.py:153
  55.0 18.8 %copy-start.1 = (bf16[8,40,1024]{2,1,0:T(8,128)(2,1)}, bf16[8,40,1024]{2,1,0:T(8,128)(2,1)S(1)}, u32[]{:S(2)}) copy-start(bf16[8,40,1024]{2,1,0:T(8,128)(2,1)S(1)} %all_to_all.10) | copy-start | bytes 1966084
  55.0 13.4 %collective-permute-start.4 = (bf16[256,1024]{1,0:T(8,128)(2,1)S(1)}, bf16[256,1024]{1,0:T(8,128)(2,1)S(1)}, u32[]{:S(2)}, u32[]{:S(2)}) collective-permute-start(bf16[256,1024]{1,0:T(8,128)(2,1)S(1)} %bitcast.4), channel_id=1, source_target_pairs={{0,48},{16,0},{32,16},{48,32},{1,49},{17,1},{33,17},{49,33},{2,50}... | collective-permute-start | bytes 1572872 | tf_op jit(solution)/shard_map/ppermute | solution.py:138
  57.1 13.2 %collective-permute-start.2 = (bf16[256,1024]{1,0:T(8,128)(2,1)S(1)}, bf16[256,1024]{1,0:T(8,128)(2,1)S(1)}, u32[]{:S(2)}, u32[]{:S(2)}) collective-permute-start(bf16[256,1024]{1,0:T(8,128)(2,1)S(1)} %bitcast.5), channel_id=1, source_target_pairs={{0,16},{16,32},{32,48},{48,0},{1,17},{17,33},{33,49},{49,1},{2,18}... | collective-permute-start | bytes 1572872 | tf_op jit(solution)/shard_map/ppermute | solution.py:137
  60.3 13.4 %collective-permute-start.6 = (bf16[256,1024]{1,0:T(8,128)(2,1)S(1)}, bf16[256,1024]{1,0:T(8,128)(2,1)S(1)}, u32[]{:S(2)}, u32[]{:S(2)}) collective-permute-start(bf16[256,1024]{1,0:T(8,128)(2,1)S(1)} %bitcast.6), channel_id=1, source_target_pairs={{0,8},{8,0},{1,9},{9,1},{2,10},{10,2},{3,11},{11,3},{4,12},{12,4},... | collective-permute-start | bytes 1572872 | tf_op jit(solution)/shard_map/ppermute | solution.py:147
  68.4 12.6 %collective-permute-start.5 = (bf16[128,1024]{1,0:T(8,128)(2,1)S(1)}, bf16[128,1024]{1,0:T(8,128)(2,1)S(1)}, u32[]{:S(2)}, u32[]{:S(2)}) collective-permute-start(bf16[128,1024]{1,0:T(8,128)(2,1)S(1)} %slice.19), channel_id=1, source_target_pairs={{0,48},{16,0},{32,16},{48,32},{1,49},{17,1},{33,17},{49,33},{2,50}... | collective-permute-start | bytes 786440 | tf_op jit(solution)/shard_map/ppermute | solution.py:141
  70.4 10.7 %collective-permute-start.3 = (bf16[128,1024]{1,0:T(8,128)(2,1)S(1)}, bf16[128,1024]{1,0:T(8,128)(2,1)}, u32[]{:S(2)}, u32[]{:S(2)}) collective-permute-start(bf16[128,1024]{1,0:T(8,128)(2,1)S(1)} %slice.18), channel_id=1, source_target_pairs={{0,16},{16,32},{32,48},{48,0},{1,17},{17,33},{33,49},{49,1},{2,18}... | collective-permute-start | bytes 786440 | tf_op jit(solution)/shard_map/ppermute | solution.py:140
  73.8 16.6 %collective-permute-start.7 = (bf16[256,1024]{1,0:T(8,128)(2,1)S(1)}, bf16[256,1024]{1,0:T(8,128)(2,1)S(1)}, u32[]{:S(2)}, u32[]{:S(2)}) collective-permute-start(bf16[256,1024]{1,0:T(8,128)(2,1)S(1)} %collective-permute-done.2.left), channel_id=1, source_target_pairs={{0,8},{8,0},{1,9},{9,1},{2,10},{10,2},{3,11},{11,3},{4,12},{12,4},... | collective-permute-start | bytes 1572872 | tf_op jit(solution)/shard_map/ppermute | solution.py:147
  79.1 11.2 %collective-permute-start.8 = (bf16[256,1024]{1,0:T(8,128)(2,1)S(1)}, bf16[256,1024]{1,0:T(8,128)(2,1)S(1)}, u32[]{:S(2)}, u32[]{:S(2)}) collective-permute-start(bf16[256,1024]{1,0:T(8,128)(2,1)S(1)} %collective-permute-done.4.right), channel_id=1, source_target_pairs={{0,8},{8,0},{1,9},{9,1},{2,10},{10,2},{3,11},{11,3},{4,12},{12,4},... | collective-permute-start | bytes 1572872 | tf_op jit(solution)/shard_map/ppermute | solution.py:147
  82.1 8.3 %collective-permute-start.9 = (bf16[256,1024]{1,0:T(8,128)(2,1)S(1)}, bf16[256,1024]{1,0:T(8,128)(2,1)S(1)}, u32[]{:S(2)}, u32[]{:S(2)}) collective-permute-start(bf16[256,1024]{1,0:T(8,128)(2,1)S(1)} %constant_dynamic-update-slice_fusion.opp), channel_id=1, source_target_pairs={{0,8},{8,0},{1,9},{9,1},{2,10},{10,2},{3,11},{11,3},{4,12},{12,4},... | collective-permute-start | bytes 1572872 | tf_op jit(solution)/shard_map/ppermute | solution.py:147
  87.4 2.2 %copy-start = (bf16[2048,1024]{1,0:T(8,128)(2,1)S(1)}, bf16[2048,1024]{1,0:T(8,128)(2,1)}, u32[]{:S(2)}) copy-start(bf16[2048,1024]{1,0:T(8,128)(2,1)} %all-gather.3.cloned.1.call-done) | copy-start | bytes 12582916
  90.3 16.1 %slice-start = ((bf16[8,40,1024]{2,1,0:T(8,128)(2,1)}), bf16[8,8,1024]{2,1,0:T(8,128)(2,1)S(1)}, s32[]{:S(2)}) async-start(bf16[8,40,1024]{2,1,0:T(8,128)(2,1)} %copy-done.1), calls=%async_computation.3 | async-start | bytes 262144 | tf_op jit(solution)/shard_map/slice | solution.py:156
  101.6 6.3 %collective-permute-start.10 = (bf16[1024,256]{1,0:T(8,128)(2,1)S(1)}, bf16[1024,256]{1,0:T(8,128)(2,1)S(1)}, u32[]{:S(2)}, u32[]{:S(2)}) collective-permute-start(bf16[1024,256]{1,0:T(8,128)(2,1)S(1)} %all_gather.11.own), channel_id=1, source_target_pairs={{0,8},{8,0},{1,9},{9,1},{2,10},{10,2},{3,11},{11,3},{4,12},{12,4},... | collective-permute-start | bytes 1572872 | tf_op jit(solution)/shard_map/ppermute | solution.py:147
  128.0 8.6 %collective-permute-start.11 = (bf16[64,128]{1,0:T(8,128)(2,1)}, bf16[64,128]{1,0:T(8,128)(2,1)S(1)}, u32[]{:S(2)}, u32[]{:S(2)}) collective-permute-start(bf16[64,128]{1,0:T(8,128)(2,1)} %shard_map.40), channel_id=1, source_target_pairs={{4,0},{68,1},{132,2},{196,3},{260,4},{324,5},{388,6},{452,7},{12,8... | collective-permute-start | bytes 49160 | tf_op jit(solution)/shard_map/ppermute | solution.py:167
Sparse Core Ops, SparseCore 0:
  9.4 63.7 all-gather.2

commit v13 on v12

--- a/solution.py
+++ b/solution.py
@@ -160,7 +160,7 @@
     near = project(jnp.float32, mem_all, rows, left, right, opp)
     own = project(jnp.bfloat16, mem_all, rows_s, swap(left), swap(right), swap(opp), near)
 
-    own = lax.all_gather(own, "x", axis=0, tiled=True)
+    own = spread(own, "x").reshape(1024, 2 * HD)
     parts = attend(query, own, swap(own))
     parts = lax.all_to_all(parts, "y", 0, 0, tiled=True)
     result = merge(parts)

time: 145 us -> 144 us (level)
  starting transfers between devices: 52.4 us -> 50.5 us
    all_to_all x1 -> x2, blocking collectives: 25.8 us -> 37.5 us  [spread(): return lax.all_to_all(copies, axis, 0, 0, tiled=True)]
    all_gather x1 -> x0, blocking collectives: 10.5 us -> none  [body(): own = lax.all_gather(own, 'x', axis=0, tiled=True)]
    ppermute x5, starting transfers between devices: 21.9 us -> 20 us  [swap(): return lax.ppermute(value, 'c', SWAP)]
where the time goes in v13:
time: 144 us
  blocking collectives  53.2 us (37%)
  starting transfers between devices  50.5 us (35%)
  waiting for transfers between devices  16.2 us (11%)
  between operations  13.7 us (10%)
  Pallas kernels  5.94 us (4%)
  local copies, waits for them, and re-layouts  4.03 us (3%)
    all_to_all x2, blocking collectives, spread(): return lax.all_to_all(copies, axis, 0, 0, tiled=True)  37.5 us
    ppermute x5, starting transfers between devices, swap(): return lax.ppermute(value, 'c', SWAP)  20 us
    all_to_all x1, blocking collectives, body(): parts = lax.all_to_all(parts, 'y', 0, 0, tiled=True)  15.6 us
    ppermute x1, starting transfers between devices, body(): rows = lax.ppermute(kv_weight, ALL, weight_moves())  13 us
    ppermute x1, waiting for transfers between devices, body(): return lax.ppermute(result, ALL, [(b, a) for a, b in query_moves()])  6.37 us
    ppermute x1, starting transfers between devices, body(): query = lax.ppermute(queries, ALL, query_moves())  4.65 us
    ppermute x1, waiting for transfers between devices, body(): query = lax.ppermute(queries, ALL, query_moves())  4.09 us
    unnamed x6, local copies, waits for them, and re-layouts  3.76 us
  transfers between devices with their start and end apart: 13, of which 4 were waited for; matrix products, arithmetic and copies ran while one was open for 1% of the time, Pallas kernels for 1%

profile of v13, /device:TPU:1, one launch (start us, length us, event | category | flops | bytes accessed | tf_op | source)
XLA Modules:
  0.0 143.6 jit_solution(6354986386147972619)
XLA Ops:
  6.5 0.7 all-gather.3.cloned.1.call-update
  7.3 13.0 %collective-permute-start = (bf16[32,1024]{1,0:T(8,128)(2,1)}, bf16[32,1024]{1,0:T(8,128)(2,1)S(1)}, u32[]{:S(2)}, u32[]{:S(2)}) collective-permute-start(bf16[32,1024]{1,0:T(8,128)(2,1)} %param.4), channel_id=1, source_target_pairs={{0,4},{1,12},{2,20},{3,28},{4,36},{5,44},{6,52},{7,60},{8,68},{9,7... | collective-permute-start | bytes 196616 | tf_op jit(solution)/shard_map/ppermute | solution.py:152
  20.3 4.7 %collective-permute-start.1 = (bf16[64,128]{1,0:T(8,128)(2,1)}, bf16[64,128]{1,0:T(8,128)(2,1)S(1)}, u32[]{:S(2)}, u32[]{:S(2)}) collective-permute-start(bf16[64,128]{1,0:T(8,128)(2,1)} %param.5), channel_id=1, source_target_pairs={{0,4},{1,68},{2,132},{3,196},{4,260},{5,324},{6,388},{7,452},{8,12... | collective-permute-start | bytes 49160 | tf_op jit(solution)/shard_map/ppermute | solution.py:153
  25.0 4.1 %collective-permute-done.1 = bf16[64,128]{1,0:T(8,128)(2,1)S(1)} collective-permute-done((bf16[64,128]{1,0:T(8,128)(2,1)}, bf16[64,128]{1,0:T(8,128)(2,1)S(1)}, u32[]{:S(2)}, u32[]{:S(2)}) %collective-permute-start.1) | collective-permute-done | bytes 16416 | tf_op jit(solution)/shard_map/ppermute | solution.py:153
  29.1 0.0 collective-permute-done
  29.1 0.1 broadcast_in_dim.4
  29.2 25.8 %all_to_all.15 = bf16[8,40,1024]{2,1,0:T(8,128)(2,1)S(1)} all-to-all(bf16[8,40,1024]{2,1,0:T(8,128)(2,1)S(1)} %broadcast_in_dim.4), channel_id=1, replica_groups=mesh['y'=8,'x'=4,'c'=2,'z'=8] {'y'}, dimensions={0} | all-to-all | bytes 1310720 | tf_op jit(solution)/shard_map/all_to_all | solution.py:18
  55.0 2.1 %collective-permute-start.4 = (bf16[256,1024]{1,0:T(8,128)(2,1)S(1)}, bf16[256,1024]{1,0:T(8,128)(2,1)S(1)}, u32[]{:S(2)}, u32[]{:S(2)}) collective-permute-start(bf16[256,1024]{1,0:T(8,128)(2,1)S(1)} %bitcast.5), channel_id=1, source_target_pairs={{0,48},{16,0},{32,16},{48,32},{1,49},{17,1},{33,17},{49,33},{2,50}... | collective-permute-start | bytes 1572872 | tf_op jit(solution)/shard_map/ppermute | solution.py:138
  57.1 3.2 %collective-permute-start.2 = (bf16[256,1024]{1,0:T(8,128)(2,1)S(1)}, bf16[256,1024]{1,0:T(8,128)(2,1)S(1)}, u32[]{:S(2)}, u32[]{:S(2)}) collective-permute-start(bf16[256,1024]{1,0:T(8,128)(2,1)S(1)} %bitcast.6), channel_id=1, source_target_pairs={{0,16},{16,32},{32,48},{48,0},{1,17},{17,33},{33,49},{49,1},{2,18}... | collective-permute-start | bytes 1572872 | tf_op jit(solution)/shard_map/ppermute | solution.py:137
  60.3 4.5 %collective-permute-start.6 = (bf16[256,1024]{1,0:T(8,128)(2,1)S(1)}, bf16[256,1024]{1,0:T(8,128)(2,1)S(1)}, u32[]{:S(2)}, u32[]{:S(2)}) collective-permute-start(bf16[256,1024]{1,0:T(8,128)(2,1)S(1)} %bitcast.7), channel_id=1, source_target_pairs={{0,8},{8,0},{1,9},{9,1},{2,10},{10,2},{3,11},{11,3},{4,12},{12,4},... | collective-permute-start | bytes 1572872 | tf_op jit(solution)/shard_map/ppermute | solution.py:147
  64.8 3.6 %collective-permute-done.4.right = bf16[256,1024]{1,0:T(8,128)(2,1)S(1)} collective-permute-done((bf16[256,1024]{1,0:T(8,128)(2,1)S(1)}, bf16[256,1024]{1,0:T(8,128)(2,1)S(1)}, u32[]{:S(2)}, u32[]{:S(2)}) %collective-permute-start.4) | collective-permute-done | bytes 524320 | tf_op jit(solution)/shard_map/ppermute | solution.py:138
  68.4 1.9 %collective-permute-start.5 = (bf16[128,1024]{1,0:T(8,128)(2,1)S(1)}, bf16[128,1024]{1,0:T(8,128)(2,1)S(1)}, u32[]{:S(2)}, u32[]{:S(2)}) collective-permute-start(bf16[128,1024]{1,0:T(8,128)(2,1)S(1)} %slice.19), channel_id=1, source_target_pairs={{0,48},{16,0},{32,16},{48,32},{1,49},{17,1},{33,17},{49,33},{2,50}... | collective-permute-start | bytes 786440 | tf_op jit(solution)/shard_map/ppermute | solution.py:141
  70.3 0.0 collective-permute-done.2.left
  70.4 3.4 %collective-permute-start.3 = (bf16[128,1024]{1,0:T(8,128)(2,1)S(1)}, bf16[128,1024]{1,0:T(8,128)(2,1)}, u32[]{:S(2)}, u32[]{:S(2)}) collective-permute-start(bf16[128,1024]{1,0:T(8,128)(2,1)S(1)} %slice.18), channel_id=1, source_target_pairs={{0,16},{16,32},{32,48},{48,0},{1,17},{17,33},{33,49},{49,1},{2,18}... | collective-permute-start | bytes 786440 | tf_op jit(solution)/shard_map/ppermute | solution.py:140
  73.8 5.3 %collective-permute-start.7 = (bf16[256,1024]{1,0:T(8,128)(2,1)S(1)}, bf16[256,1024]{1,0:T(8,128)(2,1)S(1)}, u32[]{:S(2)}, u32[]{:S(2)}) collective-permute-start(bf16[256,1024]{1,0:T(8,128)(2,1)S(1)} %collective-permute-done.2.left), channel_id=1, source_target_pairs={{0,8},{8,0},{1,9},{9,1},{2,10},{10,2},{3,11},{11,3},{4,12},{12,4},... | collective-permute-start | bytes 1572872 | tf_op jit(solution)/shard_map/ppermute | solution.py:147
  79.1 1.9 %collective-permute-start.8 = (bf16[256,1024]{1,0:T(8,128)(2,1)S(1)}, bf16[256,1024]{1,0:T(8,128)(2,1)S(1)}, u32[]{:S(2)}, u32[]{:S(2)}) collective-permute-start(bf16[256,1024]{1,0:T(8,128)(2,1)S(1)} %collective-permute-done.4.right), channel_id=1, source_target_pairs={{0,8},{8,0},{1,9},{9,1},{2,10},{10,2},{3,11},{11,3},{4,12},{12,4},... | collective-permute-start | bytes 1572872 | tf_op jit(solution)/shard_map/ppermute | solution.py:147
  81.1 0.0 all-gather.3.cloned.1.call-done
  81.1 1.0 constant_dynamic-update-slice_fusion.1
  82.1 5.3 %collective-permute-start.9 = (bf16[256,1024]{1,0:T(8,128)(2,1)S(1)}, bf16[256,1024]{1,0:T(8,128)(2,1)S(1)}, u32[]{:S(2)}, u32[]{:S(2)}) collective-permute-start(bf16[256,1024]{1,0:T(8,128)(2,1)S(1)} %constant_dynamic-update-slice_fusion.opp), channel_id=1, source_target_pairs={{0,8},{8,0},{1,9},{9,1},{2,10},{10,2},{3,11},{11,3},{4,12},{12,4},... | collective-permute-start | bytes 1572872 | tf_op jit(solution)/shard_map/ppermute | solution.py:147
  87.4 2.2 %copy-done = bf16[2048,1024]{1,0:T(8,128)(2,1)S(1)} copy-done((bf16[2048,1024]{1,0:T(8,128)(2,1)S(1)}, bf16[2048,1024]{1,0:T(8,128)(2,1)}, u32[]{:S(2)}) %copy-start) | copy-done | bytes 4194328
  89.6 0.7 shard_map.37.refs_0_
  90.4 0.7 shard_map.38
  91.2 11.7 %all_to_all.16 = bf16[4,256,256]{2,1,0:T(8,128)(2,1)S(1)} all-to-all(bf16[4,256,256]{2,1,0:T(8,128)(2,1)S(1)} %broadcast_in_dim.5), channel_id=1, replica_groups=mesh['y'=8,'x'=4,'c'=2,'z'=8] {'x'}, dimensions={0} | all-to-all | bytes 1048576 | tf_op jit(solution)/shard_map/all_to_all | solution.py:18
  102.9 3.0 %collective-permute-start.10 = (bf16[1024,256]{1,0:T(8,128)(2,1)S(1)}, bf16[1024,256]{1,0:T(8,128)(2,1)S(1)}, u32[]{:S(2)}, u32[]{:S(2)}) collective-permute-start(bf16[1024,256]{1,0:T(8,128)(2,1)S(1)} %bitcast.9), channel_id=1, source_target_pairs={{0,8},{8,0},{1,9},{9,1},{2,10},{10,2},{3,11},{11,3},{4,12},{12,4},... | collective-permute-start | bytes 1572872 | tf_op jit(solution)/shard_map/ppermute | solution.py:147
  105.9 0.1 reshape.15.q_ref
  106.0 1.4 %collective-permute-done.10.other = bf16[1024,256]{1,0:T(8,128)(2,1)S(1)} collective-permute-done((bf16[1024,256]{1,0:T(8,128)(2,1)S(1)}, bf16[1024,256]{1,0:T(8,128)(2,1)S(1)}, u32[]{:S(2)}, u32[]{:S(2)}) %collective-permute-start.10) | collective-permute-done | bytes 524320 | tf_op jit(solution)/shard_map/ppermute | solution.py:147
  107.4 2.3 %shard_map.39 = f32[8,72,128]{2,1,0:T(8,128)S(1)} custom-call(bf16[512,128]{1,0:T(8,128)(2,1)S(1)} %reshape.15.q_ref, bf16[1024,256]{1,0:T(8,128)(2,1)S(1)} %bitcast.10, bf16[1024,256]{1,0:T(8,128)(2,1)S(1)} %collective-permute-done.10.other), custom_call_target="tpu_custom_call" | custom-call | flops 536870912 | bytes 2097152 | tf_op jit(solution)/shard_map/pallas_call | solution.py:106
  109.7 15.6 %all_to_all.17.part_ref = f32[8,72,128]{2,1,0:T(8,128)} all-to-all(f32[8,72,128]{2,1,0:T(8,128)S(1)} %shard_map.39), channel_id=1, replica_groups=mesh['y'=8,'x'=4,'c'=2,'z'=8] {'y'}, dimensions={0} | all-to-all | bytes 589824 | tf_op jit(solution)/shard_map/all_to_all | solution.py:165
  125.4 2.1 %shard_map.40 = bf16[64,128]{1,0:T(8,128)(2,1)} custom-call(f32[8,72,128]{2,1,0:T(8,128)} %all_to_all.17.part_ref), custom_call_target="tpu_custom_call" | custom-call | tf_op jit(solution)/shard_map/pallas_call | solution.py:129
  127.5 2.2 %collective-permute-start.11 = (bf16[64,128]{1,0:T(8,128)(2,1)}, bf16[64,128]{1,0:T(8,128)(2,1)S(1)}, u32[]{:S(2)}, u32[]{:S(2)}) collective-permute-start(bf16[64,128]{1,0:T(8,128)(2,1)} %shard_map.40), channel_id=1, source_target_pairs={{4,0},{68,1},{132,2},{196,3},{260,4},{324,5},{388,6},{452,7},{12,8... | collective-permute-start | bytes 49160 | tf_op jit(solution)/shard_map/ppermute | solution.py:167
  129.7 6.4 %collective-permute-done.11 = bf16[64,128]{1,0:T(8,128)(2,1)S(1)} collective-permute-done((bf16[64,128]{1,0:T(8,128)(2,1)}, bf16[64,128]{1,0:T(8,128)(2,1)S(1)}, u32[]{:S(2)}, u32[]{:S(2)}) %collective-permute-start.11) | collective-permute-done | bytes 16416 | tf_op jit(solution)/shard_map/ppermute | solution.py:167
  136.1 0.6 copy.6
  (19 shorter events, 0.2 us)
Async XLA Ops:
  6.5 74.5 %all-gather.3.cloned.1.call-start = ((), (), s32[]{:S(2)}) async-start(), calls=%async_computation.3 | async-start | bytes 4718592 | tf_op jit(solution)/shard_map/all_gather | solution.py:151
  7.3 21.8 %collective-permute-start = (bf16[32,1024]{1,0:T(8,128)(2,1)}, bf16[32,1024]{1,0:T(8,128)(2,1)S(1)}, u32[]{:S(2)}, u32[]{:S(2)}) collective-permute-start(bf16[32,1024]{1,0:T(8,128)(2,1)} %param.4), channel_id=1, source_target_pairs={{0,4},{1,12},{2,20},{3,28},{4,36},{5,44},{6,52},{7,60},{8,68},{9,7... | collective-permute-start | bytes 196616 | tf_op jit(solution)/shard_map/ppermute | solution.py:152
  20.3 8.8 %collective-permute-start.1 = (bf16[64,128]{1,0:T(8,128)(2,1)}, bf16[64,128]{1,0:T(8,128)(2,1)S(1)}, u32[]{:S(2)}, u32[]{:S(2)}) collective-permute-start(bf16[64,128]{1,0:T(8,128)(2,1)} %param.5), channel_id=1, source_target_pairs={{0,4},{1,68},{2,132},{3,196},{4,260},{5,324},{6,388},{7,452},{8,12... | collective-permute-start | bytes 49160 | tf_op jit(solution)/shard_map/ppermute | solution.py:153
  55.0 18.8 %copy-start.1 = (bf16[8,40,1024]{2,1,0:T(8,128)(2,1)}, bf16[8,40,1024]{2,1,0:T(8,128)(2,1)S(1)}, u32[]{:S(2)}) copy-start(bf16[8,40,1024]{2,1,0:T(8,128)(2,1)S(1)} %all_to_all.15) | copy-start | bytes 1966084
  55.0 13.4 %collective-permute-start.4 = (bf16[256,1024]{1,0:T(8,128)(2,1)S(1)}, bf16[256,1024]{1,0:T(8,128)(2,1)S(1)}, u32[]{:S(2)}, u32[]{:S(2)}) collective-permute-start(bf16[256,1024]{1,0:T(8,128)(2,1)S(1)} %bitcast.5), channel_id=1, source_target_pairs={{0,48},{16,0},{32,16},{48,32},{1,49},{17,1},{33,17},{49,33},{2,50}... | collective-permute-start | bytes 1572872 | tf_op jit(solution)/shard_map/ppermute | solution.py:138
  57.1 13.2 %collective-permute-start.2 = (bf16[256,1024]{1,0:T(8,128)(2,1)S(1)}, bf16[256,1024]{1,0:T(8,128)(2,1)S(1)}, u32[]{:S(2)}, u32[]{:S(2)}) collective-permute-start(bf16[256,1024]{1,0:T(8,128)(2,1)S(1)} %bitcast.6), channel_id=1, source_target_pairs={{0,16},{16,32},{32,48},{48,0},{1,17},{17,33},{33,49},{49,1},{2,18}... | collective-permute-start | bytes 1572872 | tf_op jit(solution)/shard_map/ppermute | solution.py:137
  60.3 13.4 %collective-permute-start.6 = (bf16[256,1024]{1,0:T(8,128)(2,1)S(1)}, bf16[256,1024]{1,0:T(8,128)(2,1)S(1)}, u32[]{:S(2)}, u32[]{:S(2)}) collective-permute-start(bf16[256,1024]{1,0:T(8,128)(2,1)S(1)} %bitcast.7), channel_id=1, source_target_pairs={{0,8},{8,0},{1,9},{9,1},{2,10},{10,2},{3,11},{11,3},{4,12},{12,4},... | collective-permute-start | bytes 1572872 | tf_op jit(solution)/shard_map/ppermute | solution.py:147
  68.4 12.6 %collective-permute-start.5 = (bf16[128,1024]{1,0:T(8,128)(2,1)S(1)}, bf16[128,1024]{1,0:T(8,128)(2,1)S(1)}, u32[]{:S(2)}, u32[]{:S(2)}) collective-permute-start(bf16[128,1024]{1,0:T(8,128)(2,1)S(1)} %slice.19), channel_id=1, source_target_pairs={{0,48},{16,0},{32,16},{48,32},{1,49},{17,1},{33,17},{49,33},{2,50}... | collective-permute-start | bytes 786440 | tf_op jit(solution)/shard_map/ppermute | solution.py:141
  70.4 10.7 %collective-permute-start.3 = (bf16[128,1024]{1,0:T(8,128)(2,1)S(1)}, bf16[128,1024]{1,0:T(8,128)(2,1)}, u32[]{:S(2)}, u32[]{:S(2)}) collective-permute-start(bf16[128,1024]{1,0:T(8,128)(2,1)S(1)} %slice.18), channel_id=1, source_target_pairs={{0,16},{16,32},{32,48},{48,0},{1,17},{17,33},{33,49},{49,1},{2,18}... | collective-permute-start | bytes 786440 | tf_op jit(solution)/shard_map/ppermute | solution.py:140
  73.8 16.6 %collective-permute-start.7 = (bf16[256,1024]{1,0:T(8,128)(2,1)S(1)}, bf16[256,1024]{1,0:T(8,128)(2,1)S(1)}, u32[]{:S(2)}, u32[]{:S(2)}) collective-permute-start(bf16[256,1024]{1,0:T(8,128)(2,1)S(1)} %collective-permute-done.2.left), channel_id=1, source_target_pairs={{0,8},{8,0},{1,9},{9,1},{2,10},{10,2},{3,11},{11,3},{4,12},{12,4},... | collective-permute-start | bytes 1572872 | tf_op jit(solution)/shard_map/ppermute | solution.py:147
  79.1 11.2 %collective-permute-start.8 = (bf16[256,1024]{1,0:T(8,128)(2,1)S(1)}, bf16[256,1024]{1,0:T(8,128)(2,1)S(1)}, u32[]{:S(2)}, u32[]{:S(2)}) collective-permute-start(bf16[256,1024]{1,0:T(8,128)(2,1)S(1)} %collective-permute-done.4.right), channel_id=1, source_target_pairs={{0,8},{8,0},{1,9},{9,1},{2,10},{10,2},{3,11},{11,3},{4,12},{12,4},... | collective-permute-start | bytes 1572872 | tf_op jit(solution)/shard_map/ppermute | solution.py:147
  82.1 8.3 %collective-permute-start.9 = (bf16[256,1024]{1,0:T(8,128)(2,1)S(1)}, bf16[256,1024]{1,0:T(8,128)(2,1)S(1)}, u32[]{:S(2)}, u32[]{:S(2)}) collective-permute-start(bf16[256,1024]{1,0:T(8,128)(2,1)S(1)} %constant_dynamic-update-slice_fusion.opp), channel_id=1, source_target_pairs={{0,8},{8,0},{1,9},{9,1},{2,10},{10,2},{3,11},{11,3},{4,12},{12,4},... | collective-permute-start | bytes 1572872 | tf_op jit(solution)/shard_map/ppermute | solution.py:147
  87.4 2.2 %copy-start = (bf16[2048,1024]{1,0:T(8,128)(2,1)S(1)}, bf16[2048,1024]{1,0:T(8,128)(2,1)}, u32[]{:S(2)}) copy-start(bf16[2048,1024]{1,0:T(8,128)(2,1)} %all-gather.3.cloned.1.call-done) | copy-start | bytes 12582916
  90.3 15.6 %slice-start = ((bf16[8,40,1024]{2,1,0:T(8,128)(2,1)}), bf16[8,8,1024]{2,1,0:T(8,128)(2,1)S(1)}, s32[]{:S(2)}) async-start(bf16[8,40,1024]{2,1,0:T(8,128)(2,1)} %copy-done.1), calls=%async_computation.4 | async-start | bytes 262144 | tf_op jit(solution)/shard_map/slice | solution.py:156
  102.9 4.5 %collective-permute-start.10 = (bf16[1024,256]{1,0:T(8,128)(2,1)S(1)}, bf16[1024,256]{1,0:T(8,128)(2,1)S(1)}, u32[]{:S(2)}, u32[]{:S(2)}) collective-permute-start(bf16[1024,256]{1,0:T(8,128)(2,1)S(1)} %bitcast.9), channel_id=1, source_target_pairs={{0,8},{8,0},{1,9},{9,1},{2,10},{10,2},{3,11},{11,3},{4,12},{12,4},... | collective-permute-start | bytes 1572872 | tf_op jit(solution)/shard_map/ppermute | solution.py:147
  127.5 8.6 %collective-permute-start.11 = (bf16[64,128]{1,0:T(8,128)(2,1)}, bf16[64,128]{1,0:T(8,128)(2,1)S(1)}, u32[]{:S(2)}, u32[]{:S(2)}) collective-permute-start(bf16[64,128]{1,0:T(8,128)(2,1)} %shard_map.40), channel_id=1, source_target_pairs={{4,0},{68,1},{132,2},{196,3},{260,4},{324,5},{388,6},{452,7},{12,8... | collective-permute-start | bytes 49160 | tf_op jit(solution)/shard_map/ppermute | solution.py:167
Sparse Core Ops, SparseCore 0:
  9.4 63.7 all-gather.2

commit v14 on v13

--- a/solution.py
+++ b/solution.py
@@ -53,14 +53,15 @@
 SWAP = [(0, 1), (1, 0)]
 
 
-def project_kernel(swapped, mem_ref, own, left, right, opp, *refs):
+def project_kernel(swapped, mem_ref, own, left, right, opp_k, opp_v, *refs):
     x, core = lax.axis_index("x"), lax.axis_index("c")
     half = 1 - core if swapped else core
     *before, out_ref = refs
     total = before[0][...] if before else None
-    for away, ref in zip((0, 3, 1, 2), (own, left, right, opp)):
+    opp = jnp.concatenate([opp_k[...], opp_v[...]], axis=0)
+    for away, rows in zip((0, 3, 1, 2), (own[...], left[...], right[...], opp)):
         share = mem_ref[2 * lax.rem(x + away, 4) + half]
-        part = lax.dot_general(share, ref[...], NT, preferred_element_type=jnp.float32)
+        part = lax.dot_general(share, rows, NT, preferred_element_type=jnp.float32)
         total = part if total is None else total + part
     out_ref[...] = total.astype(out_ref.dtype)
 
@@ -155,10 +156,10 @@
     rows = both[:, :32].reshape(2 * HD, 8 * HD)
     query = both[:, 32:].reshape(512, HD)
     rows_s, left, right, opp_k, opp_v = ring(rows)
-    opp_k, opp_v, mem_all = lax.optimization_barrier((opp_k, opp_v, mem_all))
-    opp = jnp.concatenate([opp_k, opp_v], axis=0)
-    near = project(jnp.float32, mem_all, rows, left, right, opp)
-    own = project(jnp.bfloat16, mem_all, rows_s, swap(left), swap(right), swap(opp), near)
+    opp_k, mem_all = lax.optimization_barrier((opp_k, mem_all))
+    near = project(jnp.float32, mem_all, rows, left, right, opp_k, opp_v)
+    swapped = [rows_s, *map(swap, (left, right, opp_k, opp_v))]
+    own = project(jnp.bfloat16, mem_all, *swapped, near)
 
     own = spread(own, "x").reshape(1024, 2 * HD)
     parts = attend(query, own, swap(own))

time: 144 us -> 146 us (1.014)
  Pallas kernels: 5.94 us -> 7.87 us
    pallas_call x2, Pallas kernels: 1.47 us -> 3.4 us  [project(): pl.pallas_call(functools.partial(project_kernel, dtype == jnp.bfloat16),...]
    unnamed x6 -> x5, local copies, waits for them, and re-layouts: 3.76 us -> 2.79 us
    ppermute x5 -> x6, starting transfers between devices: 20 us -> 20.8 us  [swap(): return lax.ppermute(value, 'c', SWAP)]
  transfers between devices with their start and end apart: 13 -> 14, of which waited for: 4 -> 4; matrix products, arithmetic and copies ran while one was open for 1% -> 0% of each run, Pallas kernels for 1% -> 1%
where the time goes in v14:
time: 146 us; the launch traced here: 145 us
  blocking collectives  52.8 us (36%)
  starting transfers between devices  51.2 us (35%)
  waiting for transfers between devices  16.2 us (11%)
  between operations  13.7 us (9%)
  Pallas kernels  7.87 us (5%)
  local copies, waits for them, and re-layouts  3.04 us (2%)
    all_to_all x2, blocking collectives, spread(): return lax.all_to_all(copies, axis, 0, 0, tiled=True)  37.1 us
    ppermute x6, starting transfers between devices, swap(): return lax.ppermute(value, 'c', SWAP)  20.8 us
    all_to_all x1, blocking collectives, body(): parts = lax.all_to_all(parts, 'y', 0, 0, tiled=True)  15.6 us
    ppermute x1, starting transfers between devices, body(): rows = lax.ppermute(kv_weight, ALL, weight_moves())  13 us
    ppermute x1, waiting for transfers between devices, body(): return lax.ppermute(result, ALL, [(b, a) for a, b in query_moves()])  6.38 us
    ppermute x1, starting transfers between devices, body(): query = lax.ppermute(queries, ALL, query_moves())  4.65 us
    ppermute x1, waiting for transfers between devices, body(): query = lax.ppermute(queries, ALL, query_moves())  4.09 us
    ppermute x1, waiting for transfers between devices, ring(): right = lax.ppermute(value, 'x', shift(4, -1))  3.56 us
  transfers between devices with their start and end apart: 14, of which 4 were waited for; matrix products, arithmetic and copies ran while one was open for 0% of the time, Pallas kernels for 1%

profile of v14, /device:TPU:1, one launch (start us, length us, event | category | flops | bytes accessed | tf_op | source)
XLA Modules:
  0.0 144.8 jit_solution(6111380446802088961)
XLA Ops:
  6.5 0.7 all-gather.3.cloned.1.call-update
  7.3 13.0 %collective-permute-start = (bf16[32,1024]{1,0:T(8,128)(2,1)}, bf16[32,1024]{1,0:T(8,128)(2,1)S(1)}, u32[]{:S(2)}, u32[]{:S(2)}) collective-permute-start(bf16[32,1024]{1,0:T(8,128)(2,1)} %param.4), channel_id=1, source_target_pairs={{0,4},{1,12},{2,20},{3,28},{4,36},{5,44},{6,52},{7,60},{8,68},{9,7... | collective-permute-start | bytes 196616 | tf_op jit(solution)/shard_map/ppermute | solution.py:153
  20.3 4.7 %collective-permute-start.1 = (bf16[64,128]{1,0:T(8,128)(2,1)}, bf16[64,128]{1,0:T(8,128)(2,1)S(1)}, u32[]{:S(2)}, u32[]{:S(2)}) collective-permute-start(bf16[64,128]{1,0:T(8,128)(2,1)} %param.5), channel_id=1, source_target_pairs={{0,4},{1,68},{2,132},{3,196},{4,260},{5,324},{6,388},{7,452},{8,12... | collective-permute-start | bytes 49160 | tf_op jit(solution)/shard_map/ppermute | solution.py:154
  25.0 4.1 %collective-permute-done.1 = bf16[64,128]{1,0:T(8,128)(2,1)S(1)} collective-permute-done((bf16[64,128]{1,0:T(8,128)(2,1)}, bf16[64,128]{1,0:T(8,128)(2,1)S(1)}, u32[]{:S(2)}, u32[]{:S(2)}) %collective-permute-start.1) | collective-permute-done | bytes 16416 | tf_op jit(solution)/shard_map/ppermute | solution.py:154
  29.1 0.0 collective-permute-done
  29.1 0.1 broadcast_in_dim.4
  29.2 25.8 %all_to_all.15 = bf16[8,40,1024]{2,1,0:T(8,128)(2,1)S(1)} all-to-all(bf16[8,40,1024]{2,1,0:T(8,128)(2,1)S(1)} %broadcast_in_dim.4), channel_id=1, replica_groups=mesh['y'=8,'x'=4,'c'=2,'z'=8] {'y'}, dimensions={0} | all-to-all | bytes 1310720 | tf_op jit(solution)/shard_map/all_to_all | solution.py:18
  55.0 2.1 %collective-permute-start.4 = (bf16[256,1024]{1,0:T(8,128)(2,1)S(1)}, bf16[256,1024]{1,0:T(8,128)(2,1)S(1)}, u32[]{:S(2)}, u32[]{:S(2)}) collective-permute-start(bf16[256,1024]{1,0:T(8,128)(2,1)S(1)} %bitcast.5), channel_id=1, source_target_pairs={{0,48},{16,0},{32,16},{48,32},{1,49},{17,1},{33,17},{49,33},{2,50}... | collective-permute-start | bytes 1572872 | tf_op jit(solution)/shard_map/ppermute | solution.py:139
  57.1 3.2 %collective-permute-start.2 = (bf16[256,1024]{1,0:T(8,128)(2,1)S(1)}, bf16[256,1024]{1,0:T(8,128)(2,1)S(1)}, u32[]{:S(2)}, u32[]{:S(2)}) collective-permute-start(bf16[256,1024]{1,0:T(8,128)(2,1)S(1)} %bitcast.6), channel_id=1, source_target_pairs={{0,16},{16,32},{32,48},{48,0},{1,17},{17,33},{33,49},{49,1},{2,18}... | collective-permute-start | bytes 1572872 | tf_op jit(solution)/shard_map/ppermute | solution.py:138
  60.3 4.5 %collective-permute-start.5 = (bf16[256,1024]{1,0:T(8,128)(2,1)S(1)}, bf16[256,1024]{1,0:T(8,128)(2,1)S(1)}, u32[]{:S(2)}, u32[]{:S(2)}) collective-permute-start(bf16[256,1024]{1,0:T(8,128)(2,1)S(1)} %bitcast.7), channel_id=1, source_target_pairs={{0,8},{8,0},{1,9},{9,1},{2,10},{10,2},{3,11},{11,3},{4,12},{12,4},... | collective-permute-start | bytes 1572872 | tf_op jit(solution)/shard_map/ppermute | solution.py:148
  64.8 3.6 %collective-permute-done.4.right = bf16[256,1024]{1,0:T(8,128)(2,1)S(1)} collective-permute-done((bf16[256,1024]{1,0:T(8,128)(2,1)S(1)}, bf16[256,1024]{1,0:T(8,128)(2,1)S(1)}, u32[]{:S(2)}, u32[]{:S(2)}) %collective-permute-start.4) | collective-permute-done | bytes 524320 | tf_op jit(solution)/shard_map/ppermute | solution.py:139
  68.4 1.9 %collective-permute-start.9 = (bf16[128,1024]{1,0:T(8,128)(2,1)S(1)}, bf16[128,1024]{1,0:T(8,128)(2,1)}, u32[]{:S(2)}, u32[]{:S(2)}) collective-permute-start(bf16[128,1024]{1,0:T(8,128)(2,1)S(1)} %slice.19), channel_id=1, source_target_pairs={{0,48},{16,0},{32,16},{48,32},{1,49},{17,1},{33,17},{49,33},{2,50}... | collective-permute-start | bytes 786440 | tf_op jit(solution)/shard_map/ppermute | solution.py:142
  70.4 3.4 %collective-permute-start.3 = (bf16[128,1024]{1,0:T(8,128)(2,1)S(1)}, bf16[128,1024]{1,0:T(8,128)(2,1)S(1)}, u32[]{:S(2)}, u32[]{:S(2)}) collective-permute-start(bf16[128,1024]{1,0:T(8,128)(2,1)S(1)} %slice.18), channel_id=1, source_target_pairs={{0,16},{16,32},{32,48},{48,0},{1,17},{17,33},{33,49},{49,1},{2,18}... | collective-permute-start | bytes 786440 | tf_op jit(solution)/shard_map/ppermute | solution.py:141
  73.7 0.0 collective-permute-done.5.own
  73.8 5.3 %collective-permute-start.6 = (bf16[256,1024]{1,0:T(8,128)(2,1)S(1)}, bf16[256,1024]{1,0:T(8,128)(2,1)S(1)}, u32[]{:S(2)}, u32[]{:S(2)}) collective-permute-start(bf16[256,1024]{1,0:T(8,128)(2,1)S(1)} %collective-permute-done.2.left), channel_id=1, source_target_pairs={{0,8},{8,0},{1,9},{9,1},{2,10},{10,2},{3,11},{11,3},{4,12},{12,4},... | collective-permute-start | bytes 1572872 | tf_op jit(solution)/shard_map/ppermute | solution.py:148
  79.1 1.9 %collective-permute-start.7 = (bf16[256,1024]{1,0:T(8,128)(2,1)S(1)}, bf16[256,1024]{1,0:T(8,128)(2,1)S(1)}, u32[]{:S(2)}, u32[]{:S(2)}) collective-permute-start(bf16[256,1024]{1,0:T(8,128)(2,1)S(1)} %collective-permute-done.4.right), channel_id=1, source_target_pairs={{0,8},{8,0},{1,9},{9,1},{2,10},{10,2},{3,11},{11,3},{4,12},{12,4},... | collective-permute-start | bytes 1572872 | tf_op jit(solution)/shard_map/ppermute | solution.py:148
  81.0 2.4 %collective-permute-start.10 = (bf16[128,1024]{1,0:T(8,128)(2,1)}, bf16[128,1024]{1,0:T(8,128)(2,1)}, u32[]{:S(2)}, u32[]{:S(2)}) collective-permute-start(bf16[128,1024]{1,0:T(8,128)(2,1)} %collective-permute-done.9.opp_v), channel_id=1, source_target_pairs={{0,8},{8,0},{1,9},{9,1},{2,10},{10,2},{3,11},{11,3},{4,12},{12,4},... | collective-permute-start | bytes 786440 | tf_op jit(solution)/shard_map/ppermute | solution.py:148
  83.5 0.0 all-gather.3.cloned.1.call-done
  83.5 2.8 %collective-permute-start.8 = (bf16[128,1024]{1,0:T(8,128)(2,1)S(1)}, bf16[128,1024]{1,0:T(8,128)(2,1)S(1)}, u32[]{:S(2)}, u32[]{:S(2)}) collective-permute-start(bf16[128,1024]{1,0:T(8,128)(2,1)S(1)} %collective-permute-done.3.opp_k), channel_id=1, source_target_pairs={{0,8},{8,0},{1,9},{9,1},{2,10},{10,2},{3,11},{11,3},{4,12},{12,4},... | collective-permute-start | bytes 786440 | tf_op jit(solution)/shard_map/ppermute | solution.py:148
  86.3 2.2 %copy-done = bf16[2048,1024]{1,0:T(8,128)(2,1)S(1)} copy-done((bf16[2048,1024]{1,0:T(8,128)(2,1)S(1)}, bf16[2048,1024]{1,0:T(8,128)(2,1)}, u32[]{:S(2)}) %copy-start) | copy-done | bytes 4194328
  88.5 1.7 %shard_map.37.refs_0_ = f32[256,256]{1,0:T(8,128)S(1)} custom-call(bf16[8,256,1024]{2,1,0:T(8,128)(2,1)S(1)} %bitcast.3, bf16[256,1024]{1,0:T(8,128)(2,1)S(1)} %bitcast.8, bf16[256,1024]{1,0:T(8,128)(2,1)S(1)} %collective-permute-done.2.left, bf16[256,1024]{1,0:T(8,128)(2,1)S(1)} %collective-permute-done.4.right, ...), custom_call_target="tpu_custom_call" | custom-call | flops 536870912 | bytes 4194304 | tf_op jit(solution)/shard_map/pallas_call | solution.py:70
  90.2 1.7 %shard_map.38 = bf16[256,256]{1,0:T(8,128)(2,1)S(1)} custom-call(bf16[8,256,1024]{2,1,0:T(8,128)(2,1)S(1)} %bitcast.4, bf16[256,1024]{1,0:T(8,128)(2,1)S(1)} %collective-permute-done.5.own, bf16[256,1024]{1,0:T(8,128)(2,1)S(1)} %collective-permute-done.6.left, bf16[256,1024]{1,0:T(8,128)(2,1)S(1)} %collective-permute-done.7.right, ...), custom_call_target="tpu_custom_call" | custom-call | flops 536870912 | bytes 4194304 | tf_op jit(solution)/shard_map/pallas_call | solution.py:70
  92.0 11.3 %all_to_all.16 = bf16[4,256,256]{2,1,0:T(8,128)(2,1)S(1)} all-to-all(bf16[4,256,256]{2,1,0:T(8,128)(2,1)S(1)} %broadcast_in_dim.5), channel_id=1, replica_groups=mesh['y'=8,'x'=4,'c'=2,'z'=8] {'x'}, dimensions={0} | all-to-all | bytes 1048576 | tf_op jit(solution)/shard_map/all_to_all | solution.py:18
  103.3 3.8 %collective-permute-start.11 = (bf16[1024,256]{1,0:T(8,128)(2,1)S(1)}, bf16[1024,256]{1,0:T(8,128)(2,1)S(1)}, u32[]{:S(2)}, u32[]{:S(2)}) collective-permute-start(bf16[1024,256]{1,0:T(8,128)(2,1)S(1)} %bitcast.9), channel_id=1, source_target_pairs={{0,8},{8,0},{1,9},{9,1},{2,10},{10,2},{3,11},{11,3},{4,12},{12,4},... | collective-permute-start | bytes 1572872 | tf_op jit(solution)/shard_map/ppermute | solution.py:148
  107.1 0.1 reshape.15.q_ref
  107.2 1.4 collective-permute-done.11.other
  108.6 2.3 %shard_map.39 = f32[8,72,128]{2,1,0:T(8,128)S(1)} custom-call(bf16[512,128]{1,0:T(8,128)(2,1)S(1)} %reshape.15.q_ref, bf16[1024,256]{1,0:T(8,128)(2,1)S(1)} %bitcast.10, bf16[1024,256]{1,0:T(8,128)(2,1)S(1)} %collective-permute-done.11.other), custom_call_target="tpu_custom_call" | custom-call | flops 536870912 | bytes 2097152 | tf_op jit(solution)/shard_map/pallas_call | solution.py:107
  111.0 15.6 %all_to_all.17.part_ref = f32[8,72,128]{2,1,0:T(8,128)} all-to-all(f32[8,72,128]{2,1,0:T(8,128)S(1)} %shard_map.39), channel_id=1, replica_groups=mesh['y'=8,'x'=4,'c'=2,'z'=8] {'y'}, dimensions={0} | all-to-all | bytes 589824 | tf_op jit(solution)/shard_map/all_to_all | solution.py:166
  126.6 2.1 %shard_map.40 = bf16[64,128]{1,0:T(8,128)(2,1)} custom-call(f32[8,72,128]{2,1,0:T(8,128)} %all_to_all.17.part_ref), custom_call_target="tpu_custom_call" | custom-call | tf_op jit(solution)/shard_map/pallas_call | solution.py:130
  128.8 2.2 %collective-permute-start.12 = (bf16[64,128]{1,0:T(8,128)(2,1)}, bf16[64,128]{1,0:T(8,128)(2,1)S(1)}, u32[]{:S(2)}, u32[]{:S(2)}) collective-permute-start(bf16[64,128]{1,0:T(8,128)(2,1)} %shard_map.40), channel_id=1, source_target_pairs={{4,0},{68,1},{132,2},{196,3},{260,4},{324,5},{388,6},{452,7},{12,8... | collective-permute-start | bytes 49160 | tf_op jit(solution)/shard_map/ppermute | solution.py:168
  131.0 6.4 %collective-permute-done.12 = bf16[64,128]{1,0:T(8,128)(2,1)S(1)} collective-permute-done((bf16[64,128]{1,0:T(8,128)(2,1)}, bf16[64,128]{1,0:T(8,128)(2,1)S(1)}, u32[]{:S(2)}, u32[]{:S(2)}) %collective-permute-start.12) | collective-permute-done | bytes 16416 | tf_op jit(solution)/shard_map/ppermute | solution.py:168
  137.3 0.6 copy.5
  (19 shorter events, 0.2 us)
Async XLA Ops:
  6.5 77.0 %all-gather.3.cloned.1.call-start = ((), (), s32[]{:S(2)}) async-start(), calls=%async_computation.3 | async-start | bytes 4718592 | tf_op jit(solution)/shard_map/all_gather | solution.py:152
  7.3 21.8 %collective-permute-start = (bf16[32,1024]{1,0:T(8,128)(2,1)}, bf16[32,1024]{1,0:T(8,128)(2,1)S(1)}, u32[]{:S(2)}, u32[]{:S(2)}) collective-permute-start(bf16[32,1024]{1,0:T(8,128)(2,1)} %param.4), channel_id=1, source_target_pairs={{0,4},{1,12},{2,20},{3,28},{4,36},{5,44},{6,52},{7,60},{8,68},{9,7... | collective-permute-start | bytes 196616 | tf_op jit(solution)/shard_map/ppermute | solution.py:153
  20.3 8.8 %collective-permute-start.1 = (bf16[64,128]{1,0:T(8,128)(2,1)}, bf16[64,128]{1,0:T(8,128)(2,1)S(1)}, u32[]{:S(2)}, u32[]{:S(2)}) collective-permute-start(bf16[64,128]{1,0:T(8,128)(2,1)} %param.5), channel_id=1, source_target_pairs={{0,4},{1,68},{2,132},{3,196},{4,260},{5,324},{6,388},{7,452},{8,12... | collective-permute-start | bytes 49160 | tf_op jit(solution)/shard_map/ppermute | solution.py:154
  55.0 26.1 %copy-start.1 = (bf16[8,40,1024]{2,1,0:T(8,128)(2,1)}, bf16[8,40,1024]{2,1,0:T(8,128)(2,1)S(1)}, u32[]{:S(2)}) copy-start(bf16[8,40,1024]{2,1,0:T(8,128)(2,1)S(1)} %all_to_all.15) | copy-start | bytes 1966084
  55.0 13.4 %collective-permute-start.4 = (bf16[256,1024]{1,0:T(8,128)(2,1)S(1)}, bf16[256,1024]{1,0:T(8,128)(2,1)S(1)}, u32[]{:S(2)}, u32[]{:S(2)}) collective-permute-start(bf16[256,1024]{1,0:T(8,128)(2,1)S(1)} %bitcast.5), channel_id=1, source_target_pairs={{0,48},{16,0},{32,16},{48,32},{1,49},{17,1},{33,17},{49,33},{2,50}... | collective-permute-start | bytes 1572872 | tf_op jit(solution)/shard_map/ppermute | solution.py:139
  57.1 13.2 %collective-permute-start.2 = (bf16[256,1024]{1,0:T(8,128)(2,1)S(1)}, bf16[256,1024]{1,0:T(8,128)(2,1)S(1)}, u32[]{:S(2)}, u32[]{:S(2)}) collective-permute-start(bf16[256,1024]{1,0:T(8,128)(2,1)S(1)} %bitcast.6), channel_id=1, source_target_pairs={{0,16},{16,32},{32,48},{48,0},{1,17},{17,33},{33,49},{49,1},{2,18}... | collective-permute-start | bytes 1572872 | tf_op jit(solution)/shard_map/ppermute | solution.py:138
  60.3 13.4 %collective-permute-start.5 = (bf16[256,1024]{1,0:T(8,128)(2,1)S(1)}, bf16[256,1024]{1,0:T(8,128)(2,1)S(1)}, u32[]{:S(2)}, u32[]{:S(2)}) collective-permute-start(bf16[256,1024]{1,0:T(8,128)(2,1)S(1)} %bitcast.7), channel_id=1, source_target_pairs={{0,8},{8,0},{1,9},{9,1},{2,10},{10,2},{3,11},{11,3},{4,12},{12,4},... | collective-permute-start | bytes 1572872 | tf_op jit(solution)/shard_map/ppermute | solution.py:148
  68.4 12.6 %collective-permute-start.9 = (bf16[128,1024]{1,0:T(8,128)(2,1)S(1)}, bf16[128,1024]{1,0:T(8,128)(2,1)}, u32[]{:S(2)}, u32[]{:S(2)}) collective-permute-start(bf16[128,1024]{1,0:T(8,128)(2,1)S(1)} %slice.19), channel_id=1, source_target_pairs={{0,48},{16,0},{32,16},{48,32},{1,49},{17,1},{33,17},{49,33},{2,50}... | collective-permute-start | bytes 786440 | tf_op jit(solution)/shard_map/ppermute | solution.py:142
  70.4 13.1 %collective-permute-start.3 = (bf16[128,1024]{1,0:T(8,128)(2,1)S(1)}, bf16[128,1024]{1,0:T(8,128)(2,1)S(1)}, u32[]{:S(2)}, u32[]{:S(2)}) collective-permute-start(bf16[128,1024]{1,0:T(8,128)(2,1)S(1)} %slice.18), channel_id=1, source_target_pairs={{0,16},{16,32},{32,48},{48,0},{1,17},{17,33},{33,49},{49,1},{2,18}... | collective-permute-start | bytes 786440 | tf_op jit(solution)/shard_map/ppermute | solution.py:141
  73.8 16.4 %collective-permute-start.6 = (bf16[256,1024]{1,0:T(8,128)(2,1)S(1)}, bf16[256,1024]{1,0:T(8,128)(2,1)S(1)}, u32[]{:S(2)}, u32[]{:S(2)}) collective-permute-start(bf16[256,1024]{1,0:T(8,128)(2,1)S(1)} %collective-permute-done.2.left), channel_id=1, source_target_pairs={{0,8},{8,0},{1,9},{9,1},{2,10},{10,2},{3,11},{11,3},{4,12},{12,4},... | collective-permute-start | bytes 1572872 | tf_op jit(solution)/shard_map/ppermute | solution.py:148
  79.1 11.1 %collective-permute-start.7 = (bf16[256,1024]{1,0:T(8,128)(2,1)S(1)}, bf16[256,1024]{1,0:T(8,128)(2,1)S(1)}, u32[]{:S(2)}, u32[]{:S(2)}) collective-permute-start(bf16[256,1024]{1,0:T(8,128)(2,1)S(1)} %collective-permute-done.4.right), channel_id=1, source_target_pairs={{0,8},{8,0},{1,9},{9,1},{2,10},{10,2},{3,11},{11,3},{4,12},{12,4},... | collective-permute-start | bytes 1572872 | tf_op jit(solution)/shard_map/ppermute | solution.py:148
  81.0 9.1 %collective-permute-start.10 = (bf16[128,1024]{1,0:T(8,128)(2,1)}, bf16[128,1024]{1,0:T(8,128)(2,1)}, u32[]{:S(2)}, u32[]{:S(2)}) collective-permute-start(bf16[128,1024]{1,0:T(8,128)(2,1)} %collective-permute-done.9.opp_v), channel_id=1, source_target_pairs={{0,8},{8,0},{1,9},{9,1},{2,10},{10,2},{3,11},{11,3},{4,12},{12,4},... | collective-permute-start | bytes 786440 | tf_op jit(solution)/shard_map/ppermute | solution.py:148
  83.5 6.7 %collective-permute-start.8 = (bf16[128,1024]{1,0:T(8,128)(2,1)S(1)}, bf16[128,1024]{1,0:T(8,128)(2,1)S(1)}, u32[]{:S(2)}, u32[]{:S(2)}) collective-permute-start(bf16[128,1024]{1,0:T(8,128)(2,1)S(1)} %collective-permute-done.3.opp_k), channel_id=1, source_target_pairs={{0,8},{8,0},{1,9},{9,1},{2,10},{10,2},{3,11},{11,3},{4,12},{12,4},... | collective-permute-start | bytes 786440 | tf_op jit(solution)/shard_map/ppermute | solution.py:148
  86.3 2.2 %copy-start = (bf16[2048,1024]{1,0:T(8,128)(2,1)S(1)}, bf16[2048,1024]{1,0:T(8,128)(2,1)}, u32[]{:S(2)}) copy-start(bf16[2048,1024]{1,0:T(8,128)(2,1)} %all-gather.3.cloned.1.call-done) | copy-start | bytes 12582916
  90.2 17.0 %slice-start = ((bf16[8,40,1024]{2,1,0:T(8,128)(2,1)}), bf16[8,8,1024]{2,1,0:T(8,128)(2,1)S(1)}, s32[]{:S(2)}) async-start(bf16[8,40,1024]{2,1,0:T(8,128)(2,1)} %copy-done.1), calls=%async_computation.4 | async-start | bytes 262144 | tf_op jit(solution)/shard_map/slice | solution.py:157
  103.3 5.4 %collective-permute-start.11 = (bf16[1024,256]{1,0:T(8,128)(2,1)S(1)}, bf16[1024,256]{1,0:T(8,128)(2,1)S(1)}, u32[]{:S(2)}, u32[]{:S(2)}) collective-permute-start(bf16[1024,256]{1,0:T(8,128)(2,1)S(1)} %bitcast.9), channel_id=1, source_target_pairs={{0,8},{8,0},{1,9},{9,1},{2,10},{10,2},{3,11},{11,3},{4,12},{12,4},... | collective-permute-start | bytes 1572872 | tf_op jit(solution)/shard_map/ppermute | solution.py:148
  128.8 8.6 %collective-permute-start.12 = (bf16[64,128]{1,0:T(8,128)(2,1)}, bf16[64,128]{1,0:T(8,128)(2,1)S(1)}, u32[]{:S(2)}, u32[]{:S(2)}) collective-permute-start(bf16[64,128]{1,0:T(8,128)(2,1)} %shard_map.40), channel_id=1, source_target_pairs={{4,0},{68,1},{132,2},{196,3},{260,4},{324,5},{388,6},{452,7},{12,8... | collective-permute-start | bytes 49160 | tf_op jit(solution)/shard_map/ppermute | solution.py:168
Sparse Core Ops, SparseCore 0:
  9.4 63.7 all-gather.2

commit v15 on v13

--- a/solution.py
+++ b/solution.py
@@ -114,7 +114,7 @@
 
 
 def merge_kernel(part_ref, out_ref):
-    stats = jnp.concatenate([part_ref[j, 64:65, :] for j in range(8)], axis=0).T
+    stats = part_ref[:, 64, :].T
     tops, totals = stats[:64], stats[64:]
     top = jnp.max(tops, axis=1, keepdims=True)
     factor = jnp.exp(tops - top)

time: 144 us -> 144 us (level)
  no operation moved by 1% of the time
where the time goes in v15:
time: 144 us
  blocking collectives  53.2 us (37%)
  starting transfers between devices  50.5 us (35%)
  waiting for transfers between devices  16.2 us (11%)
  between operations  13.7 us (10%)
  Pallas kernels  5.94 us (4%)
  local copies, waits for them, and re-layouts  4.03 us (3%)
    all_to_all x2, blocking collectives, spread(): return lax.all_to_all(copies, axis, 0, 0, tiled=True)  37.5 us
    ppermute x5, starting transfers between devices, swap(): return lax.ppermute(value, 'c', SWAP)  20 us
    all_to_all x1, blocking collectives, body(): parts = lax.all_to_all(parts, 'y', 0, 0, tiled=True)  15.6 us
    ppermute x1, starting transfers between devices, body(): rows = lax.ppermute(kv_weight, ALL, weight_moves())  13 us
    ppermute x1, waiting for transfers between devices, body(): return lax.ppermute(result, ALL, [(b, a) for a, b in query_moves()])  6.37 us
    ppermute x1, starting transfers between devices, body(): query = lax.ppermute(queries, ALL, query_moves())  4.65 us
    ppermute x1, waiting for transfers between devices, body(): query = lax.ppermute(queries, ALL, query_moves())  4.09 us
    unnamed x6, local copies, waits for them, and re-layouts  3.76 us
  transfers between devices with their start and end apart: 13, of which 4 were waited for; matrix products, arithmetic and copies ran while one was open for 1% of the time, Pallas kernels for 1%

profile of v15, /device:TPU:1, one launch (start us, length us, event | category | flops | bytes accessed | tf_op | source)
XLA Modules:
  0.0 143.6 jit_solution(4899773803799957739)
XLA Ops:
  6.5 0.7 all-gather.3.cloned.1.call-update
  7.3 13.0 %collective-permute-start = (bf16[32,1024]{1,0:T(8,128)(2,1)}, bf16[32,1024]{1,0:T(8,128)(2,1)S(1)}, u32[]{:S(2)}, u32[]{:S(2)}) collective-permute-start(bf16[32,1024]{1,0:T(8,128)(2,1)} %param.4), channel_id=1, source_target_pairs={{0,4},{1,12},{2,20},{3,28},{4,36},{5,44},{6,52},{7,60},{8,68},{9,7... | collective-permute-start | bytes 196616 | tf_op jit(solution)/shard_map/ppermute | solution.py:152
  20.3 4.7 %collective-permute-start.1 = (bf16[64,128]{1,0:T(8,128)(2,1)}, bf16[64,128]{1,0:T(8,128)(2,1)S(1)}, u32[]{:S(2)}, u32[]{:S(2)}) collective-permute-start(bf16[64,128]{1,0:T(8,128)(2,1)} %param.5), channel_id=1, source_target_pairs={{0,4},{1,68},{2,132},{3,196},{4,260},{5,324},{6,388},{7,452},{8,12... | collective-permute-start | bytes 49160 | tf_op jit(solution)/shard_map/ppermute | solution.py:153
  25.0 4.1 %collective-permute-done.1 = bf16[64,128]{1,0:T(8,128)(2,1)S(1)} collective-permute-done((bf16[64,128]{1,0:T(8,128)(2,1)}, bf16[64,128]{1,0:T(8,128)(2,1)S(1)}, u32[]{:S(2)}, u32[]{:S(2)}) %collective-permute-start.1) | collective-permute-done | bytes 16416 | tf_op jit(solution)/shard_map/ppermute | solution.py:153
  29.1 0.0 collective-permute-done
  29.1 0.1 broadcast_in_dim.4
  29.2 25.8 %all_to_all.15 = bf16[8,40,1024]{2,1,0:T(8,128)(2,1)S(1)} all-to-all(bf16[8,40,1024]{2,1,0:T(8,128)(2,1)S(1)} %broadcast_in_dim.4), channel_id=1, replica_groups=mesh['y'=8,'x'=4,'c'=2,'z'=8] {'y'}, dimensions={0} | all-to-all | bytes 1310720 | tf_op jit(solution)/shard_map/all_to_all | solution.py:18
  55.0 2.1 %collective-permute-start.4 = (bf16[256,1024]{1,0:T(8,128)(2,1)S(1)}, bf16[256,1024]{1,0:T(8,128)(2,1)S(1)}, u32[]{:S(2)}, u32[]{:S(2)}) collective-permute-start(bf16[256,1024]{1,0:T(8,128)(2,1)S(1)} %bitcast.5), channel_id=1, source_target_pairs={{0,48},{16,0},{32,16},{48,32},{1,49},{17,1},{33,17},{49,33},{2,50}... | collective-permute-start | bytes 1572872 | tf_op jit(solution)/shard_map/ppermute | solution.py:138
  57.1 3.2 %collective-permute-start.2 = (bf16[256,1024]{1,0:T(8,128)(2,1)S(1)}, bf16[256,1024]{1,0:T(8,128)(2,1)S(1)}, u32[]{:S(2)}, u32[]{:S(2)}) collective-permute-start(bf16[256,1024]{1,0:T(8,128)(2,1)S(1)} %bitcast.6), channel_id=1, source_target_pairs={{0,16},{16,32},{32,48},{48,0},{1,17},{17,33},{33,49},{49,1},{2,18}... | collective-permute-start | bytes 1572872 | tf_op jit(solution)/shard_map/ppermute | solution.py:137
  60.3 4.5 %collective-permute-start.6 = (bf16[256,1024]{1,0:T(8,128)(2,1)S(1)}, bf16[256,1024]{1,0:T(8,128)(2,1)S(1)}, u32[]{:S(2)}, u32[]{:S(2)}) collective-permute-start(bf16[256,1024]{1,0:T(8,128)(2,1)S(1)} %bitcast.7), channel_id=1, source_target_pairs={{0,8},{8,0},{1,9},{9,1},{2,10},{10,2},{3,11},{11,3},{4,12},{12,4},... | collective-permute-start | bytes 1572872 | tf_op jit(solution)/shard_map/ppermute | solution.py:147
  64.8 3.6 %collective-permute-done.4.right = bf16[256,1024]{1,0:T(8,128)(2,1)S(1)} collective-permute-done((bf16[256,1024]{1,0:T(8,128)(2,1)S(1)}, bf16[256,1024]{1,0:T(8,128)(2,1)S(1)}, u32[]{:S(2)}, u32[]{:S(2)}) %collective-permute-start.4) | collective-permute-done | bytes 524320 | tf_op jit(solution)/shard_map/ppermute | solution.py:138
  68.4 1.9 %collective-permute-start.5 = (bf16[128,1024]{1,0:T(8,128)(2,1)S(1)}, bf16[128,1024]{1,0:T(8,128)(2,1)S(1)}, u32[]{:S(2)}, u32[]{:S(2)}) collective-permute-start(bf16[128,1024]{1,0:T(8,128)(2,1)S(1)} %slice.19), channel_id=1, source_target_pairs={{0,48},{16,0},{32,16},{48,32},{1,49},{17,1},{33,17},{49,33},{2,50}... | collective-permute-start | bytes 786440 | tf_op jit(solution)/shard_map/ppermute | solution.py:141
  70.3 0.0 collective-permute-done.2.left
  70.4 3.4 %collective-permute-start.3 = (bf16[128,1024]{1,0:T(8,128)(2,1)S(1)}, bf16[128,1024]{1,0:T(8,128)(2,1)}, u32[]{:S(2)}, u32[]{:S(2)}) collective-permute-start(bf16[128,1024]{1,0:T(8,128)(2,1)S(1)} %slice.18), channel_id=1, source_target_pairs={{0,16},{16,32},{32,48},{48,0},{1,17},{17,33},{33,49},{49,1},{2,18}... | collective-permute-start | bytes 786440 | tf_op jit(solution)/shard_map/ppermute | solution.py:140
  73.8 5.3 %collective-permute-start.7 = (bf16[256,1024]{1,0:T(8,128)(2,1)S(1)}, bf16[256,1024]{1,0:T(8,128)(2,1)S(1)}, u32[]{:S(2)}, u32[]{:S(2)}) collective-permute-start(bf16[256,1024]{1,0:T(8,128)(2,1)S(1)} %collective-permute-done.2.left), channel_id=1, source_target_pairs={{0,8},{8,0},{1,9},{9,1},{2,10},{10,2},{3,11},{11,3},{4,12},{12,4},... | collective-permute-start | bytes 1572872 | tf_op jit(solution)/shard_map/ppermute | solution.py:147
  79.1 1.9 %collective-permute-start.8 = (bf16[256,1024]{1,0:T(8,128)(2,1)S(1)}, bf16[256,1024]{1,0:T(8,128)(2,1)S(1)}, u32[]{:S(2)}, u32[]{:S(2)}) collective-permute-start(bf16[256,1024]{1,0:T(8,128)(2,1)S(1)} %collective-permute-done.4.right), channel_id=1, source_target_pairs={{0,8},{8,0},{1,9},{9,1},{2,10},{10,2},{3,11},{11,3},{4,12},{12,4},... | collective-permute-start | bytes 1572872 | tf_op jit(solution)/shard_map/ppermute | solution.py:147
  81.1 0.0 all-gather.3.cloned.1.call-done
  81.1 1.0 constant_dynamic-update-slice_fusion.1
  82.1 5.3 %collective-permute-start.9 = (bf16[256,1024]{1,0:T(8,128)(2,1)S(1)}, bf16[256,1024]{1,0:T(8,128)(2,1)S(1)}, u32[]{:S(2)}, u32[]{:S(2)}) collective-permute-start(bf16[256,1024]{1,0:T(8,128)(2,1)S(1)} %constant_dynamic-update-slice_fusion.opp), channel_id=1, source_target_pairs={{0,8},{8,0},{1,9},{9,1},{2,10},{10,2},{3,11},{11,3},{4,12},{12,4},... | collective-permute-start | bytes 1572872 | tf_op jit(solution)/shard_map/ppermute | solution.py:147
  87.4 2.2 %copy-done = bf16[2048,1024]{1,0:T(8,128)(2,1)S(1)} copy-done((bf16[2048,1024]{1,0:T(8,128)(2,1)S(1)}, bf16[2048,1024]{1,0:T(8,128)(2,1)}, u32[]{:S(2)}) %copy-start) | copy-done | bytes 4194328
  89.6 0.7 shard_map.37.refs_0_
  90.4 0.7 shard_map.38
  91.2 11.7 %all_to_all.16 = bf16[4,256,256]{2,1,0:T(8,128)(2,1)S(1)} all-to-all(bf16[4,256,256]{2,1,0:T(8,128)(2,1)S(1)} %broadcast_in_dim.5), channel_id=1, replica_groups=mesh['y'=8,'x'=4,'c'=2,'z'=8] {'x'}, dimensions={0} | all-to-all | bytes 1048576 | tf_op jit(solution)/shard_map/all_to_all | solution.py:18
  102.9 3.0 %collective-permute-start.10 = (bf16[1024,256]{1,0:T(8,128)(2,1)S(1)}, bf16[1024,256]{1,0:T(8,128)(2,1)S(1)}, u32[]{:S(2)}, u32[]{:S(2)}) collective-permute-start(bf16[1024,256]{1,0:T(8,128)(2,1)S(1)} %bitcast.9), channel_id=1, source_target_pairs={{0,8},{8,0},{1,9},{9,1},{2,10},{10,2},{3,11},{11,3},{4,12},{12,4},... | collective-permute-start | bytes 1572872 | tf_op jit(solution)/shard_map/ppermute | solution.py:147
  105.9 0.1 reshape.15.q_ref
  106.0 1.4 %collective-permute-done.10.other = bf16[1024,256]{1,0:T(8,128)(2,1)S(1)} collective-permute-done((bf16[1024,256]{1,0:T(8,128)(2,1)S(1)}, bf16[1024,256]{1,0:T(8,128)(2,1)S(1)}, u32[]{:S(2)}, u32[]{:S(2)}) %collective-permute-start.10) | collective-permute-done | bytes 524320 | tf_op jit(solution)/shard_map/ppermute | solution.py:147
  107.4 2.3 %shard_map.39 = f32[8,72,128]{2,1,0:T(8,128)S(1)} custom-call(bf16[512,128]{1,0:T(8,128)(2,1)S(1)} %reshape.15.q_ref, bf16[1024,256]{1,0:T(8,128)(2,1)S(1)} %bitcast.10, bf16[1024,256]{1,0:T(8,128)(2,1)S(1)} %collective-permute-done.10.other), custom_call_target="tpu_custom_call" | custom-call | flops 536870912 | bytes 2097152 | tf_op jit(solution)/shard_map/pallas_call | solution.py:106
  109.7 15.6 %all_to_all.17.part_ref = f32[8,72,128]{2,1,0:T(8,128)} all-to-all(f32[8,72,128]{2,1,0:T(8,128)S(1)} %shard_map.39), channel_id=1, replica_groups=mesh['y'=8,'x'=4,'c'=2,'z'=8] {'y'}, dimensions={0} | all-to-all | bytes 589824 | tf_op jit(solution)/shard_map/all_to_all | solution.py:165
  125.4 2.1 %shard_map.40 = bf16[64,128]{1,0:T(8,128)(2,1)} custom-call(f32[8,72,128]{2,1,0:T(8,128)} %all_to_all.17.part_ref), custom_call_target="tpu_custom_call" | custom-call | tf_op jit(solution)/shard_map/pallas_call | solution.py:129
  127.5 2.2 %collective-permute-start.11 = (bf16[64,128]{1,0:T(8,128)(2,1)}, bf16[64,128]{1,0:T(8,128)(2,1)S(1)}, u32[]{:S(2)}, u32[]{:S(2)}) collective-permute-start(bf16[64,128]{1,0:T(8,128)(2,1)} %shard_map.40), channel_id=1, source_target_pairs={{4,0},{68,1},{132,2},{196,3},{260,4},{324,5},{388,6},{452,7},{12,8... | collective-permute-start | bytes 49160 | tf_op jit(solution)/shard_map/ppermute | solution.py:167
  129.7 6.4 %collective-permute-done.11 = bf16[64,128]{1,0:T(8,128)(2,1)S(1)} collective-permute-done((bf16[64,128]{1,0:T(8,128)(2,1)}, bf16[64,128]{1,0:T(8,128)(2,1)S(1)}, u32[]{:S(2)}, u32[]{:S(2)}) %collective-permute-start.11) | collective-permute-done | bytes 16416 | tf_op jit(solution)/shard_map/ppermute | solution.py:167
  136.1 0.6 copy.6
  (19 shorter events, 0.2 us)
Async XLA Ops:
  6.5 74.5 %all-gather.3.cloned.1.call-start = ((), (), s32[]{:S(2)}) async-start(), calls=%async_computation.3 | async-start | bytes 4718592 | tf_op jit(solution)/shard_map/all_gather | solution.py:151
  7.3 21.8 %collective-permute-start = (bf16[32,1024]{1,0:T(8,128)(2,1)}, bf16[32,1024]{1,0:T(8,128)(2,1)S(1)}, u32[]{:S(2)}, u32[]{:S(2)}) collective-permute-start(bf16[32,1024]{1,0:T(8,128)(2,1)} %param.4), channel_id=1, source_target_pairs={{0,4},{1,12},{2,20},{3,28},{4,36},{5,44},{6,52},{7,60},{8,68},{9,7... | collective-permute-start | bytes 196616 | tf_op jit(solution)/shard_map/ppermute | solution.py:152
  20.3 8.8 %collective-permute-start.1 = (bf16[64,128]{1,0:T(8,128)(2,1)}, bf16[64,128]{1,0:T(8,128)(2,1)S(1)}, u32[]{:S(2)}, u32[]{:S(2)}) collective-permute-start(bf16[64,128]{1,0:T(8,128)(2,1)} %param.5), channel_id=1, source_target_pairs={{0,4},{1,68},{2,132},{3,196},{4,260},{5,324},{6,388},{7,452},{8,12... | collective-permute-start | bytes 49160 | tf_op jit(solution)/shard_map/ppermute | solution.py:153
  55.0 18.8 %copy-start.1 = (bf16[8,40,1024]{2,1,0:T(8,128)(2,1)}, bf16[8,40,1024]{2,1,0:T(8,128)(2,1)S(1)}, u32[]{:S(2)}) copy-start(bf16[8,40,1024]{2,1,0:T(8,128)(2,1)S(1)} %all_to_all.15) | copy-start | bytes 1966084
  55.0 13.4 %collective-permute-start.4 = (bf16[256,1024]{1,0:T(8,128)(2,1)S(1)}, bf16[256,1024]{1,0:T(8,128)(2,1)S(1)}, u32[]{:S(2)}, u32[]{:S(2)}) collective-permute-start(bf16[256,1024]{1,0:T(8,128)(2,1)S(1)} %bitcast.5), channel_id=1, source_target_pairs={{0,48},{16,0},{32,16},{48,32},{1,49},{17,1},{33,17},{49,33},{2,50}... | collective-permute-start | bytes 1572872 | tf_op jit(solution)/shard_map/ppermute | solution.py:138
  57.1 13.2 %collective-permute-start.2 = (bf16[256,1024]{1,0:T(8,128)(2,1)S(1)}, bf16[256,1024]{1,0:T(8,128)(2,1)S(1)}, u32[]{:S(2)}, u32[]{:S(2)}) collective-permute-start(bf16[256,1024]{1,0:T(8,128)(2,1)S(1)} %bitcast.6), channel_id=1, source_target_pairs={{0,16},{16,32},{32,48},{48,0},{1,17},{17,33},{33,49},{49,1},{2,18}... | collective-permute-start | bytes 1572872 | tf_op jit(solution)/shard_map/ppermute | solution.py:137
  60.3 13.4 %collective-permute-start.6 = (bf16[256,1024]{1,0:T(8,128)(2,1)S(1)}, bf16[256,1024]{1,0:T(8,128)(2,1)S(1)}, u32[]{:S(2)}, u32[]{:S(2)}) collective-permute-start(bf16[256,1024]{1,0:T(8,128)(2,1)S(1)} %bitcast.7), channel_id=1, source_target_pairs={{0,8},{8,0},{1,9},{9,1},{2,10},{10,2},{3,11},{11,3},{4,12},{12,4},... | collective-permute-start | bytes 1572872 | tf_op jit(solution)/shard_map/ppermute | solution.py:147
  68.4 12.6 %collective-permute-start.5 = (bf16[128,1024]{1,0:T(8,128)(2,1)S(1)}, bf16[128,1024]{1,0:T(8,128)(2,1)S(1)}, u32[]{:S(2)}, u32[]{:S(2)}) collective-permute-start(bf16[128,1024]{1,0:T(8,128)(2,1)S(1)} %slice.19), channel_id=1, source_target_pairs={{0,48},{16,0},{32,16},{48,32},{1,49},{17,1},{33,17},{49,33},{2,50}... | collective-permute-start | bytes 786440 | tf_op jit(solution)/shard_map/ppermute | solution.py:141
  70.4 10.7 %collective-permute-start.3 = (bf16[128,1024]{1,0:T(8,128)(2,1)S(1)}, bf16[128,1024]{1,0:T(8,128)(2,1)}, u32[]{:S(2)}, u32[]{:S(2)}) collective-permute-start(bf16[128,1024]{1,0:T(8,128)(2,1)S(1)} %slice.18), channel_id=1, source_target_pairs={{0,16},{16,32},{32,48},{48,0},{1,17},{17,33},{33,49},{49,1},{2,18}... | collective-permute-start | bytes 786440 | tf_op jit(solution)/shard_map/ppermute | solution.py:140
  73.8 16.6 %collective-permute-start.7 = (bf16[256,1024]{1,0:T(8,128)(2,1)S(1)}, bf16[256,1024]{1,0:T(8,128)(2,1)S(1)}, u32[]{:S(2)}, u32[]{:S(2)}) collective-permute-start(bf16[256,1024]{1,0:T(8,128)(2,1)S(1)} %collective-permute-done.2.left), channel_id=1, source_target_pairs={{0,8},{8,0},{1,9},{9,1},{2,10},{10,2},{3,11},{11,3},{4,12},{12,4},... | collective-permute-start | bytes 1572872 | tf_op jit(solution)/shard_map/ppermute | solution.py:147
  79.1 11.2 %collective-permute-start.8 = (bf16[256,1024]{1,0:T(8,128)(2,1)S(1)}, bf16[256,1024]{1,0:T(8,128)(2,1)S(1)}, u32[]{:S(2)}, u32[]{:S(2)}) collective-permute-start(bf16[256,1024]{1,0:T(8,128)(2,1)S(1)} %collective-permute-done.4.right), channel_id=1, source_target_pairs={{0,8},{8,0},{1,9},{9,1},{2,10},{10,2},{3,11},{11,3},{4,12},{12,4},... | collective-permute-start | bytes 1572872 | tf_op jit(solution)/shard_map/ppermute | solution.py:147
  82.1 8.3 %collective-permute-start.9 = (bf16[256,1024]{1,0:T(8,128)(2,1)S(1)}, bf16[256,1024]{1,0:T(8,128)(2,1)S(1)}, u32[]{:S(2)}, u32[]{:S(2)}) collective-permute-start(bf16[256,1024]{1,0:T(8,128)(2,1)S(1)} %constant_dynamic-update-slice_fusion.opp), channel_id=1, source_target_pairs={{0,8},{8,0},{1,9},{9,1},{2,10},{10,2},{3,11},{11,3},{4,12},{12,4},... | collective-permute-start | bytes 1572872 | tf_op jit(solution)/shard_map/ppermute | solution.py:147
  87.4 2.2 %copy-start = (bf16[2048,1024]{1,0:T(8,128)(2,1)S(1)}, bf16[2048,1024]{1,0:T(8,128)(2,1)}, u32[]{:S(2)}) copy-start(bf16[2048,1024]{1,0:T(8,128)(2,1)} %all-gather.3.cloned.1.call-done) | copy-start | bytes 12582916
  90.3 15.6 %slice-start = ((bf16[8,40,1024]{2,1,0:T(8,128)(2,1)}), bf16[8,8,1024]{2,1,0:T(8,128)(2,1)S(1)}, s32[]{:S(2)}) async-start(bf16[8,40,1024]{2,1,0:T(8,128)(2,1)} %copy-done.1), calls=%async_computation.4 | async-start | bytes 262144 | tf_op jit(solution)/shard_map/slice | solution.py:156
  102.9 4.5 %collective-permute-start.10 = (bf16[1024,256]{1,0:T(8,128)(2,1)S(1)}, bf16[1024,256]{1,0:T(8,128)(2,1)S(1)}, u32[]{:S(2)}, u32[]{:S(2)}) collective-permute-start(bf16[1024,256]{1,0:T(8,128)(2,1)S(1)} %bitcast.9), channel_id=1, source_target_pairs={{0,8},{8,0},{1,9},{9,1},{2,10},{10,2},{3,11},{11,3},{4,12},{12,4},... | collective-permute-start | bytes 1572872 | tf_op jit(solution)/shard_map/ppermute | solution.py:147
  127.5 8.6 %collective-permute-start.11 = (bf16[64,128]{1,0:T(8,128)(2,1)}, bf16[64,128]{1,0:T(8,128)(2,1)S(1)}, u32[]{:S(2)}, u32[]{:S(2)}) collective-permute-start(bf16[64,128]{1,0:T(8,128)(2,1)} %shard_map.40), channel_id=1, source_target_pairs={{4,0},{68,1},{132,2},{196,3},{260,4},{324,5},{388,6},{452,7},{12,8... | collective-permute-start | bytes 49160 | tf_op jit(solution)/shard_map/ppermute | solution.py:167
Sparse Core Ops, SparseCore 0:
  9.4 63.7 all-gather.2
